TPU v7x, 32 devices: a whole 2x2x4 slice. The times are simulated.
32 devices in a mesh: dp: 8 (over z, y), tensor: 4 (over x, core).
Axes of the slice: x: 2, y: 2, z: 4, core: 2. Of those that a mesh axis runs over, the one named last changes fastest.
Arguments:
- tokens: bfloat16 [8, 1024, 512], P('dp', None, 'tensor'), may hold values from -6 to 6
- cotangent: bfloat16 [8, 1024, 512], P('dp', None, 'tensor'), may hold values from -6 to 6
- lengths: int32 [8], P('dp'), may hold values from 1 to 1024, as said below
- norm_gains: float32 [2, 512], replicated, may hold values from 0.5 to 1.5
- conv_kernel: float32 [5, 32, 512], P(None, None, 'tensor'), may hold values from -0.75 to 0.75
- mixer_weights: bfloat16 [3, 512, 512], P(None, None, 'tensor'), may hold values from -0.25 to 0.25
- mlp_weights: bfloat16 [2, 512, 2048], P(None, None, 'tensor'), may hold values from -0.25 to 0.25
- gain_moment: float32 [2, 512], replicated, may hold values from -0.0625 to 0.0625
- kernel_moment: float32 [5, 32, 512], P(None, None, 'tensor'), may hold values from -0.0625 to 0.0625
- mixer_moment: float32 [3, 512, 512], P(None, 'dp', 'tensor'), may hold values from -0.0625 to 0.0625
- mlp_moment: float32 [2, 512, 2048], P(None, 'dp', 'tensor'), may hold values from -0.0625 to 0.0625
Outputs:
- block_out: bfloat16 [8, 1024, 512], P('dp', None, 'tensor')
- input_grad: float32 [8, 1024, 512], P('dp', None, 'tensor')
- gain_moment_new: float32 [2, 512], replicated
- gains_new: float32 [2, 512], replicated
- kernel_moment_new: float32 [5, 32, 512], P(None, None, 'tensor')
- kernel_new: float32 [5, 32, 512], P(None, None, 'tensor')
- mixer_moment_new: float32 [3, 512, 512], P(None, 'dp', 'tensor')
- mixer_new: float32 [3, 512, 512], P(None, 'dp', 'tensor')
- mlp_moment_new: float32 [2, 512, 2048], P(None, 'dp', 'tensor')
- mlp_new: float32 [2, 512, 2048], P(None, 'dp', 'tensor')
Inputs may be any that keep to these rules, and one draw needn't show every extreme that they name: `lengths`: valid tokens of each sequence; the last sequence is full.
All inputs are finite; a program needn't handle non-finite values.
Results may differ from a plain program's by a relative error of at most 0.011.
Values may be sent and summed in bfloat16 or wider, within the bound.
No kernel may reach another device: no remote copies, remote signals or barrier semaphores. Data moves between devices by JAX's collectives and lax.ppermute only.
A program may use at most 192 MiB of HBM per device.

v0:
```python
import functools
import math

import jax
import jax.numpy as jnp
import ml_dtypes
import numpy as np
from jax import lax
from jax.experimental import pallas as pl
from jax.experimental.pallas import tpu as pltpu
from jax.sharding import PartitionSpec as P

NS_STEPS = 5
EPSILON = 1e-05
NS_COEF_A = 3.4445
NS_COEF_B = -4.775
NS_COEF_C = 2.0315
MOMENT_DECAY = 0.5
MATRIX_RATE = 1.0
GAIN_RATE = 0.1
KERNEL_RATE = 0.125
SCALE = 10**10
BF16 = jnp.bfloat16
F32 = jnp.float32


def conv_tables(bucket, levels, taps, dp, slot):
    half = bucket // 4
    size = 2 * half
    t = np.arange(half)
    k = np.arange(half)
    phase = 2 * np.pi * ((k[:, None] * t[None, :]) % size) / size
    forward = np.concatenate([np.cos(phase), -np.sin(phase)], 0)
    forward[half] = (-1.0) ** t
    scale = np.full((half,), 2.0 / size)
    scale[0] = 1.0 / size
    inverse = np.concatenate(
        [np.cos(phase).T * scale[None, :], -np.sin(phase).T * scale[None, :]], 1
    )
    inverse[:, half] = ((-1.0) ** t) / size
    spread = np.zeros((bucket, levels * taps))
    at = 0
    for level in range(levels):
        for tap in range(taps):
            width = 2**level
            spread[at : at + width, level * taps + tap] = 0.5**level
            at += width
    kernel_forward = np.concatenate(
        [forward @ spread[m * half : (m + 1) * half] for m in range(4)], 0
    )
    kernel_inverse = np.concatenate(
        [spread[m * half : (m + 1) * half].T @ inverse for m in range(4)], 1
    )
    share = -(-levels * taps // dp)
    kernel_inverse = np.pad(kernel_inverse, ((0, dp * share - levels * taps), (0, 0)))
    kernel_inverse = kernel_inverse.reshape(dp, share, -1)
    kernel_inverse = np.pad(kernel_inverse, ((0, 0), (0, slot - share), (0, 0))).reshape(dp * slot, -1)
    tables = []
    for table in (forward, inverse, kernel_forward, kernel_inverse):
        high = table.astype(ml_dtypes.bfloat16)
        low = (table - high.astype(np.float64)).astype(ml_dtypes.bfloat16)
        tables.append(np.stack([high, low]))
    return tables


def cross(a, b):
    return a[0] * b[0] - a[1] * b[1], a[0] * b[1] + a[1] * b[2]


def cross_conj(a, b):
    return a[0] * b[0] + a[1] * b[1], a[1] * b[2] - a[0] * b[1]


def with_edge(spec, first):
    real, imag = spec
    return real, jnp.where(first, 0.0, imag), jnp.where(first, imag, real)


def add_pairs(pairs):
    return functools.reduce(lambda p, q: (p[0] + q[0], p[1] + q[1]), pairs)


def spectral_blocks(left, right, conj, store):
    for step in range(4):
        rows = step * 64
        index = lax.broadcasted_iota(jnp.int32, (64, 128), 0)
        first = index + rows == 0
        sign = 1.0 - 2.0 * (index % 2).astype(F32)
        a = [left(r, rows) for r in range(4)]
        b = [with_edge(right(m, rows), first) for m in range(4)]
        if conj:
            sums = [add_pairs([cross_conj(a[r], b[r - q]) for r in range(q, 4)]) for q in range(4)]
        else:
            sums = [add_pairs([cross(a[r], b[q - r]) for r in range(q + 1)]) for q in range(4)]
        for q in range(4):
            other = q + 1 if conj else q - 1
            if 0 <= other < 4:
                real = sums[q][0] + sign * sums[other][0]
                imag = sums[q][1] + sign * sums[other][1]
            else:
                real, imag = sums[q]
            store(q, rows, real, imag)


def lane_pair(ref, half):
    return lambda r, rows: (
        ref[rows : rows + 64, r * 128 : (r + 1) * 128],
        ref[half + rows : half + rows + 64, r * 128 : (r + 1) * 128],
    )


def row_pair(ref, half):
    return lambda r, rows: (
        ref[2 * half * r + rows : 2 * half * r + rows + 64, :],
        ref[2 * half * r + half + rows : 2 * half * r + half + rows + 64, :],
    )


def gelu_both(x):
    c = math.sqrt(2.0 / math.pi)
    t = jnp.tanh(c * (x + 0.044715 * x * x * x))
    value = 0.5 * x * (1.0 + t)
    slope = 0.5 * (1.0 + t) + 0.5 * x * (1.0 - t * t) * (c * (1.0 + 3 * 0.044715 * x * x))
    return value, slope


def after(value, *others):
    return lax.optimization_barrier((value, *others))[0]


def swap(value, axis, k):
    size = lax.axis_size(axis)
    return lax.ppermute(value, axis, [(i, i ^ k) for i in range(size)])


def gather_tensor(value, *meanwhile):
    far = swap(value, "tensor", 2)
    near = swap(value, "tensor", 1)
    if meanwhile:
        far = after(far, *meanwhile)
    far_near = swap(far, "tensor", 1)
    return [value, near, far, far_near]


def gather_dp(value, me, low=0):
    size = lax.axis_size("dp")
    whole = value[None]
    while (1 << low) < size:
        bits = min(3, size.bit_length() - 1 - low)
        mine = (me >> low) & ((1 << bits) - 1)
        out = jnp.zeros((1 << bits,) + whole.shape, whole.dtype)
        for k in range(1 << bits):
            piece = whole if k == 0 else swap(whole, "dp", k << low)
            out = lax.dynamic_update_index_in_dim(out, piece, mine ^ k, 0)
        whole = out.reshape((-1,) + value.shape)
        low += bits
    return whole


def dot(a, b, contract):
    return lax.dot_general(a, b, ((contract[0], contract[1]), ((), ())), preferred_element_type=F32)


NN = ((1,), (0,))
NT = ((1,), (1,))
TN = ((0,), (0,))


def split(value):
    high = value.astype(BF16)
    return high, (value - high.astype(F32)).astype(BF16)


def dot3(a, b):
    a_high, a_low = split(a)
    b_high, b_low = split(b)
    mm = functools.partial(jnp.dot, preferred_element_type=F32)
    return mm(a_high, b_high) + (mm(a_high, b_low) + mm(a_low, b_high))


def table_dot(table, value):
    high, low = split(value)
    return dot(table[0], high, NN) + (dot(table[1], high, NN) + dot(table[0], low, NN))


def newton_schulz(matrix, a_ref, q_ref, p_ref, start, out_rows):
    size = a_ref.shape[0]
    row = lax.broadcasted_iota(jnp.int32, (size, size), 0)
    col = lax.broadcasted_iota(jnp.int32, (size, size), 1)
    unit = (row == col).astype(F32)
    gram = dot(matrix, matrix, NT)
    scale = 1.0 / (jnp.sqrt(jnp.sum(gram * unit)) + 1e-07)
    a_ref[...] = gram * (scale * scale)

    def advance(first):
        a = a_ref[...]
        square = dot3(a, a)
        cube = dot3(a, square)
        poly = NS_COEF_A * unit + NS_COEF_B * a + NS_COEF_C * square
        half = NS_COEF_A * a + NS_COEF_B * square + NS_COEF_C * cube
        a_ref[...] = dot3(poly, half)
        q_ref[...] = poly if first else dot3(poly, q_ref[...])

    advance(True)
    pl.loop(0, NS_STEPS - 2)(lambda _: advance(False))
    a = a_ref[...]
    p_ref[...] = NS_COEF_A * unit + NS_COEF_B * a + NS_COEF_C * dot3(a, a)
    high, low = split(dot3(p_ref[pl.ds(start, out_rows), :], q_ref[...]))
    return scale * (dot(high, matrix, NN) + dot(low, matrix, NN))


VMEM = pl.BlockSpec(memory_space=pltpu.VMEM)
SMEM = pl.BlockSpec(memory_space=pltpu.SMEM)


HBM = pl.BlockSpec(memory_space=pltpu.HBM)


class Late:
    def __init__(self, array):
        self.shape, self.dtype = array.shape, array.dtype
        self.array = pltpu.with_memory_space_constraint(array, pltpu.HBM)


class Store:
    def __init__(self, shape, dtype):
        self.shape, self.dtype = shape, dtype


class Waiting:
    def __init__(self, copy, ref):
        self.copy, self.ref, self.started = copy, ref, False

    def ready(self):
        self.copy.wait()
        return self.ref

    def send(self):
        self.copy.start()
        self.started = True


def call(kernel, outs, scratch, args, time, limit):
    outs = [o if isinstance(o, Store) else jax.ShapeDtypeStruct(*o) for o in outs]
    late = [a for a in (*args, *outs) if isinstance(a, (Late, Store))]
    n_in, n_out = len(args), len(outs)

    def body(*refs):
        given, rest = refs[: n_in + n_out], refs[n_in + n_out :]
        buffers, rest = rest[: len(late)], rest[len(late) :]
        semaphores = rest[-1] if late else None
        passed, stores, at = [], [], 0
        for what, ref in zip((*args, *outs), given):
            if isinstance(what, Late):
                copy = pltpu.make_async_copy(ref, buffers[at], semaphores.at[at])
                copy.start()
            elif isinstance(what, Store):
                copy = pltpu.make_async_copy(buffers[at], ref, semaphores.at[at])
            else:
                passed.append(ref)
                continue
            passed.append(Waiting(copy, buffers[at]))
            if isinstance(what, Store):
                stores.append(passed[-1])
            at += 1
        kernel(*passed, *(rest[:-1] if late else rest))
        for store in stores:
            if not store.started:
                store.send()
        for store in stores:
            store.copy.wait()

    moved = sum(math.prod(a.shape) * jnp.dtype(a.dtype).itemsize for a in (*args, *outs))
    return pl.pallas_call(
        body,
        out_shape=tuple(pltpu.HBM(o.shape, o.dtype) if isinstance(o, Store) else o for o in outs),
        in_specs=[SMEM] + [HBM if isinstance(a, Late) else VMEM for a in args[1:]],
        out_specs=tuple(HBM if isinstance(o, Store) else VMEM for o in outs),
        scratch_shapes=[pltpu.VMEM(a.shape, a.dtype) for a in late]
        + [pltpu.VMEM(shape, dtype) for shape, dtype in scratch]
        + ([pltpu.SemaphoreType.DMA((len(late),))] if late else []),
        compiler_params=pltpu.CompilerParams(vmem_limit_bytes=limit * 2**20),
        cost_estimate=pl.CostEstimate(flops=max(time * SCALE, 10**6), bytes_accessed=moved, transcendentals=0),
    )(*(a.array if isinstance(a, Late) else a for a in args))


def fetch(token, *arrays):
    arrays = [a if isinstance(a, tuple) else (a,) for a in arrays]
    shapes = [
        jax.ShapeDtypeStruct((sum(p.shape[0] for p in a), *a[0].shape[1:]), a[0].dtype) for a in arrays
    ]
    flat = [pltpu.with_memory_space_constraint(p, pltpu.HBM) for a in arrays for p in a]

    def body(token_ref, *refs):
        outs, semaphores, copies, at = refs[len(flat) : -1], refs[-1], [], 0
        for a, out in zip(arrays, outs):
            row = 0
            for p in a:
                target = out if len(a) == 1 else out.at[row : row + p.shape[0]]
                copies.append(pltpu.make_async_copy(refs[at], target, semaphores.at[at]))
                copies[-1].start()
                row, at = row + p.shape[0], at + 1
        for copy in copies:
            copy.wait()

    return pl.pallas_call(
        body,
        out_shape=tuple(shapes),
        in_specs=[SMEM] + [HBM] * len(flat),
        out_specs=(VMEM,) * len(shapes),
        scratch_shapes=[pltpu.SemaphoreType.DMA((len(flat),))],
        compiler_params=pltpu.CompilerParams(vmem_limit_bytes=2 * 2**20),
        cost_estimate=pl.CostEstimate(flops=10**10, bytes_accessed=2 * sum(a.size * a.dtype.itemsize for a in flat), transcendentals=0),
    )(token, *flat)


def block_at(index, size):
    return pl.ds(pl.multiple_of(index * size, size), size)


def row_mask(info, start, rows):
    return (start + lax.broadcasted_iota(jnp.int32, (rows, 1), 0) < info[1]).astype(F32)


def spectrum_kernel(info, table, taps, spec_k):
    taps = taps.ready()[...]
    spec_k[...] = table_dot(table.ready(), taps)


def entry_kernel(info, p0, p1, p2, p3, weights, gains, forward, inverse, spec_k,
                 x, normed, n_own, inv, spec_v, conv, act, slope, branch, gains_kept, wide, spec_y):
    me = info[0]
    part = p1.shape[1]
    for k, piece in enumerate((p0, p1, p2, p3)):
        x[:, block_at(me ^ k, part)] = piece[...]
    gains_kept[...] = gains[...]
    gain = gains[0:1, :]
    half = x.shape[0] // 4
    for c in range(4):
        r = slice(c * half, (c + 1) * half)
        v = x[r, :].astype(F32)
        mean = jnp.mean(v, 1, keepdims=True)
        centred = v - mean
        scale = lax.rsqrt(jnp.mean(centred * centred, 1, keepdims=True) + EPSILON)
        normed[r, :] = (centred * scale * gain).astype(BF16)
        inv.ref[r, :] = scale
        n_own.ref[r, :] = (p0[r, :].astype(F32) - mean) * scale
    n_own.send()
    inv.send()
    for c in range(4):
        r = slice(c * half, (c + 1) * half)
        normal = normed[r, :]
        wide[:, c * part : (c + 1) * part] = dot(normal, weights[0], NN)
        act[r, :], slope[r, :] = gelu_both(dot(normal, weights[1], NN))
    spec_v[...] = table_dot(forward, wide[...])

    def store(q, rows, real, imag):
        spec_y[rows : rows + 64, q * part : (q + 1) * part] = real
        spec_y[half + rows : half + rows + 64, q * part : (q + 1) * part] = imag

    spectral_blocks(lane_pair(spec_v, half), row_pair(spec_k, half), False, store)
    wide[...] = table_dot(inverse, spec_y[...])
    for c in range(4):
        r = slice(c * half, (c + 1) * half)
        out = wide[:, c * part : (c + 1) * part]
        conv[r, :] = out
        out = (act[r, :] * out * row_mask(info, c * half, half)).astype(BF16)
        branch[r, :] = out


def cotangent_kernel(info, p0, p1, p2, p3, weights, cot, out_w, delta, weights_kept):
    part = p0.shape[1]
    for k, piece in enumerate((p0, p1, p2, p3)):
        cot[:, block_at(info[0] ^ k, part)] = piece[: cot.shape[0], :]
        out_w[:, block_at(info[0] ^ k, part)] = piece[cot.shape[0] :, :]
    step = cot.shape[0] // 4
    weights = weights.ready()
    weights_kept[...] = weights[...]
    for c in range(4):
        r = slice(c * step, (c + 1) * step)
        delta[r, :] = dot(cot[r, :], weights[1], NN)


def middle_kernel(info, b0, b1, b2, b3, out_w, x, gains, weights, delta_active,
                  near, kept, normed, active, delta_hidden, n_mine, inv_mine, middle_own, branch, middle):
    me = info[0]
    part = b0.shape[1]
    step = x.shape[0] // 4
    for k, piece in enumerate((b0, b1, b2, b3)):
        branch[:, block_at(me ^ k, part)] = piece[...]
    gain = gains[1:2, :]
    for k in (1, 3, 0, 2):
        block = me ^ k
        r = block_at(block, step)
        mid = x[r, :].astype(F32) + dot(branch[r, :], out_w[...], NT)
        middle[r, :] = mid
        centred = mid - jnp.mean(mid, 1, keepdims=True)
        scale = lax.rsqrt(jnp.mean(centred * centred, 1, keepdims=True) + EPSILON)
        normal = centred * scale
        if k == 0:
            n_mine[...] = normal
            inv_mine[...] = scale
        normal = (normal * gain).astype(BF16)
        normed[r, :] = normal
        value, slope = gelu_both(dot(normal, weights[0], NN))
        mask = row_mask(info, block * step, step)
        active[r, :] = (value * mask).astype(BF16)
        back = (delta_active[r, :] * mask * slope).astype(BF16)
        delta_hidden[r, :] = back
        share = dot(back, weights[0], NT)
        if k % 2:
            near[(k // 2) * step : (k // 2 + 1) * step, :] = share.astype(BF16)
        else:
            kept[(k // 2) * step : (k // 2 + 1) * step, :] = share
    middle_own.ref[...] = middle[:, block_at(me, part)]


def mlp_kernel(info, normed, active, delta_hidden, cot, weights, moment, keep, send, moment_send, near, kept, part_out):
    me = info[0]
    size = normed.shape[1]
    side = info[2] % 2
    for which, (a, b) in enumerate(((normed, delta_hidden), (cot, active))):
        grad = dot(a[...], b[...], TN)

        @pl.when(side == which)
        def _(grad=grad):
            keep[:size, :] = grad

        @pl.when(side != which)
        def _(grad=grad):
            send[:size, :] = grad.astype(BF16)

    length = jnp.full((16, grad.shape[1]), 1, jnp.int32) * info[1]
    first = lax.broadcasted_iota(jnp.int32, length.shape, 0) == 0
    length = jnp.where(first, length // 32, length % 32).astype(F32)
    keep[size:, :] = length
    send[size:, :] = length.astype(BF16)
    moment_send[...] = moment.ready()[1 - side]
    step = active.shape[0] // 4
    part = near.ref.shape[2]
    for c in range(4):
        r = slice(c * step, (c + 1) * step)
        part_out[r, :] = dot(active[r, :], weights[1], NT)
    for k in range(4):
        share = part_out[:, block_at(me ^ k, part)]
        if k % 2:
            near.ref[k // 2] = share.astype(BF16)
        else:
            kept.ref[k // 2] = share


def mlp_rows_kernel(info, keep, came, *outs):
    size = came.shape[0] - 16
    pairs = outs[0].shape[0] if len(outs) == 1 else len(outs)
    rows = size // pairs
    length = keep[size:, :] + came[size:, :].astype(F32)
    for k in range(pairs):
        if len(outs) == 1:
            r, out = pl.ds(k * rows, rows), outs[0].at[k]
        else:
            r, out = block_at((info[2] // 2) ^ k, rows), outs[k]
        out[:rows, :] = (keep[r, :] + came[r, :].astype(F32)).astype(out.dtype)
        out[rows:, :] = length.astype(out.dtype)


def mlp_moment_kernel(info, moment, other_moment, *refs):
    *pieces, matrix, mine, other, count = refs
    rows = moment.shape[1]
    side = info[2] % 2
    if len(pieces) == 1:
        pieces = [pieces[0].at[k] for k in range(pieces[0].shape[0])]
    total = pieces[0][...].astype(F32)
    for piece in pieces[1:]:
        total = total + piece[...].astype(F32)
    tokens = 32.0 * total[2 * rows : 2 * rows + 1, :] + total[2 * rows + 1 : 2 * rows + 2, :]
    count[...] = jnp.broadcast_to(tokens[:, : count.shape[1]], count.shape)
    old = moment[side]
    for which in range(2):
        new = total[which * rows : (which + 1) * rows, :] / tokens

        @pl.when(side == which)
        def _(new=new, which=which):
            now = MOMENT_DECAY * old + new
            mine.ref[...] = now
            matrix[which * rows : (which + 1) * rows, :] = now.astype(matrix.dtype)

        @pl.when(side != which)
        def _(new=new, which=which):
            now = MOMENT_DECAY * other_moment[...] + new
            other.ref[...] = now
            matrix[which * rows : (which + 1) * rows, :] = now.astype(matrix.dtype)


def columns_kernel(info, *refs):
    *pieces, out = refs
    rows = pieces[0].shape[0]
    for k, piece in enumerate(pieces):
        out[block_at((info[2] // 2) ^ k, rows), :] = piece[...]


def join_kernel(info, kept, came, mine, far):
    mine[...] = kept[0] + came[0].astype(F32)
    far[...] = (kept[1] + came[1].astype(F32)).astype(BF16)


def join_late_kernel(info, kept, came, mine, far):
    join_kernel(info, kept.ready(), came, mine, far)


def norm_back_kernel(info, mine, came, cot, n_mine, inv_mine, gains, delta, grad_gain):
    size = mine.shape[0]
    total = mine[...] + came[...].astype(F32)
    n = n_mine[...]
    q = total * gains[1:2, :]
    back = inv_mine[...] * (q - jnp.mean(q, 1, keepdims=True) - n * jnp.mean(q * n, 1, keepdims=True))
    delta[...] = (cot[block_at(info[0], size), :].astype(F32) + back).astype(BF16)
    grad_gain[...] = jnp.sum(total * n, 0, keepdims=True)


def mixer_back_kernel(info, d0, d1, d2, d3, weights, act, slope, conv, branch, normed, spec_v, spec_k, forward, inverse,
                      kernel_inverse, gains,
                      slots, near, kept, sums, delta_own,
                      delta, wide, spec_d, spec_y, spec_u, back, share):
    me = info[0]
    step, width = d0.shape
    part = slots.ref.shape[2]
    half = step
    for k, piece in enumerate((d0, d1, d2, d3)):
        block = me ^ k
        r = block_at(block, step)
        delta[r, :] = piece[...]
        down = dot(piece[...], weights[2], NN) * row_mask(info, block * step, step)
        back[r, part:] = (down * conv[r, :] * slope[r, :]).astype(BF16)
        wide[:, block_at(block, part)] = down * act[r, :]
    delta_own.ref[...] = delta[:, block_at(me, part)]
    delta_own.send()
    spec_d[...] = table_dot(forward, wide[...])

    def store(q, rows, real, imag):
        spec_y[rows : rows + 64, q * part : (q + 1) * part] = real
        spec_y[half + rows : half + rows + 64, q * part : (q + 1) * part] = imag

    def store_rows(q, rows, real, imag):
        spec_u[2 * half * q + rows : 2 * half * q + rows + 64, :] = real
        spec_u[2 * half * q + half + rows : 2 * half * q + half + rows + 64, :] = imag

    spectral_blocks(lane_pair(spec_d, half), row_pair(spec_k, half), True, store)
    wide[...] = table_dot(inverse, spec_y[...])
    for c in range(4):
        back[c * half : (c + 1) * half, :part] = wide[:, c * part : (c + 1) * part].astype(BF16)
    spectral_blocks(lane_pair(spec_d, half), lane_pair(spec_v, half), True, store_rows)
    grad_kernel = table_dot(kernel_inverse, spec_u[...])
    grads = dot(normed[...], back[...], TN)
    grad_out = dot(delta[...], branch[...], TN)
    dp = slots.ref.shape[0]
    rows = width // dp
    taps = grad_kernel.shape[0] // dp
    for i in range(dp):
        r = slice(i * rows, (i + 1) * rows)
        slots.ref[i, :rows, :] = grads[r, :part].astype(slots.ref.dtype)
        slots.ref[i, rows : 2 * rows, :] = grads[r, part:].astype(slots.ref.dtype)
        slots.ref[i, 2 * rows : 3 * rows, :] = grad_out[r, :].astype(slots.ref.dtype)
        slots.ref[i, 3 * rows :, :] = grad_kernel[i * taps : (i + 1) * taps, :].astype(slots.ref.dtype)
    slots.send()
    ones = jnp.ones((8, width), BF16)
    gain = jnp.broadcast_to(gains[0:1, :], (8, width)).astype(BF16)
    for c in range(4):
        r = slice(c * step, (c + 1) * step)
        out = dot(back[r, :part], weights[0], NT) + dot(back[r, part:], weights[1], NT)
        share[r, :] = out
        first = dot(gain, out.astype(BF16), NT)
        second = dot(ones, (out * normed[r, :].astype(F32)).astype(BF16), NT)
        for h in range(step // part):
            at = c * (step // part) + h
            sums[at : at + 1, :] = first[0:1, h * part : (h + 1) * part]
            sums[8 + at : 9 + at, :] = second[0:1, h * part : (h + 1) * part]
    for k in range(4):
        block = share[:, block_at(me ^ k, part)]
        if k % 2:
            near.ref[k // 2] = block.astype(BF16)
        else:
            kept.ref[k // 2] = block


def moment_kernel(info, arrived, moment, count, sums, moment_new, kernel_total, o0, o1, o2, o3, new):
    me = info[0]
    dp = arrived.shape[0]
    _, rows, _ = moment.ref.shape
    total = arrived[0].astype(F32)
    for i in range(1, dp):
        total = total + arrived[i].astype(F32)
    moment = moment.ready()
    for which in range(3):
        value = MOMENT_DECAY * moment[which] + total[which * rows : (which + 1) * rows, :] / count[0:1, :]
        moment_new.ref[which] = value
        new[which] = value.astype(new.dtype)
    kernel_total[...] = total[3 * rows :, :]
    for k, out in enumerate((o0, o1, o2, o3)):
        out[:rows, :] = new[jnp.minimum(me ^ k, 2)]
        out[rows:, :] = sums[...].astype(out.dtype)


def payload_kernel(info, mine, came, n_own, g0, g1, g2, g3, kernel_total, gain_two, payload, extra):
    me = info[0]
    part = mine.shape[1]
    rows = g0.shape[0] - 16
    total = mine[...] + came[...].astype(F32)
    for k, piece in enumerate((g0, g1, g2, g3)):
        payload[0, :rows, block_at(me ^ k, part)] = piece[:rows, :]
    extra[...] = jnp.zeros_like(extra)
    for g in range(min(3, kernel_total.shape[0] // 8)):
        extra[:, g * part : (g + 1) * part] = kernel_total[8 * g : 8 * g + 8, :]
    extra[0:1, 3 * part :] = jnp.sum(total * n_own.ready()[...], 0, keepdims=True)
    for q in range(4):
        extra[1 + q : 2 + q, 3 * part :] = gain_two[:, q * part : (q + 1) * part]
    high, low = split(extra[...])
    payload[0, rows:, :] = jnp.concatenate([high.astype(F32), low.astype(F32)], 0).astype(payload.dtype)
    for i in range(1, payload.shape[0]):
        payload[i] = payload[0]


def output_kernel(info, mine, came, out_mine, out_came, delta_own, n_own, inv, middle_own, gains, g0, g1, g2, g3, input_grad, block_out):
    part = mine.shape[1]
    width = 4 * part
    rows = g0.shape[0] - 16
    gain = gains[0:1, block_at(info[0], part)]
    sums = 0.0
    for piece in (g0, g1, g2, g3):
        sums = sums + piece[rows:, :].astype(F32)
    sums = sums / width
    middle_own = middle_own.ready()
    n_own, inv, delta_own = n_own.ready(), inv.ready(), delta_own.ready()
    for h in range(mine.shape[0] // part):
        r = slice(h * part, (h + 1) * part)
        block_out.ref[r, :] = (middle_own[r, :] + (out_mine[r, :] + out_came[r, :].astype(F32))).astype(BF16)
        column = lambda at: jnp.broadcast_to(sums[at : at + 1, :], (part, part)).T
        total = mine[r, :] + came[r, :].astype(F32)
        back = total * gain - column(h) - n_own[r, :] * column(8 + h)
        input_grad.ref[r, :] = delta_own[r, :].astype(F32) + inv[r, :] * back


def step_kernel(info, pieces, m0, m1, m2, m3, out, kernel_all, matrix, large, a, q, p, gains, small):
    me, row = info[0], info[2]
    dp = gains.shape[0]
    rows = small.shape[0]
    part = kernel_all.shape[1]
    hidden = m0.shape[1]
    for i in range(dp):
        matrix[i * rows : (i + 1) * rows, :] = pieces[i, :rows, :]
        both = pieces[i, rows:, :].astype(F32)
        both = both[:8, :] + both[8:, :]
        for g in range(3):
            kernel_all[i * 24 + 8 * g : i * 24 + 8 * g + 8, :] = both[:, g * part : (g + 1) * part]
        gains[i] = both[:, 3 * part :]
    gain = gains[0]
    for i in range(1, dp):
        gain = gain + gains[i]
    high, low = split(gain)
    gain = jnp.concatenate([high.astype(F32), low.astype(F32)], 0).astype(out.dtype)
    for k in range(8):
        out[k, rows:, :part] = gain
        out[k, rows:, part:] = jnp.zeros((16, out.shape[2] - part), out.dtype)

    @pl.when(me < 3)
    def _():
        small[...] = newton_schulz(matrix[...], a, q, p, pl.multiple_of(row * rows, rows), rows)
        for k in range(8):

            @pl.when(row % 2 == k // 4)
            def _(k=k):
                out[k, :rows, :part] = small[:, (k % 4) * part : (k % 4 + 1) * part].astype(out.dtype)

    @pl.when(me == 3)
    def _():
        for k, piece in enumerate((m0, m1, m2, m3)):
            large[:, block_at(3 ^ k, hidden)] = piece[...]
        start = pl.multiple_of((row // 2) * (2 * rows), 2 * rows)
        result = newton_schulz(large[...], a, q, p, start, 2 * rows)
        for k in range(8):
            lanes = slice((k % 4) * hidden, (k % 4 + 1) * hidden)
            out[k, :rows, :] = result[(k // 4) * rows : (k // 4 + 1) * rows, lanes].astype(out.dtype)


def final_kernel(info, got, moment_mine, moment_back, mixer_weights, mlp_weights, norm_gains, gain_moment, count,
                 mixer_new, mlp_new, mlp_moment_new, gain_moment_new, gains_new, gains):
    row = info[2]
    _, rows, part = mixer_new.ref.shape
    hidden = mlp_new.ref.shape[2]
    width = 4 * part
    side = row % 2
    for t in range(4):
        both = got[4 * side + t, rows:, :part].astype(F32)
        gains[t] = both[:8, :] + both[8:, :]
    for t in range(3):
        old = mixer_weights[t, block_at(row, rows), :].astype(F32)
        mixer_new.ref[t] = old - MATRIX_RATE * got[4 * side + t, :rows, :part].astype(F32)
    mixer_new.send()
    mlp_moment_new.ref[side] = moment_mine.ready()[...]
    mlp_moment_new.ref[1 - side] = moment_back.ready()[...]
    mlp_moment_new.send()
    rate = MATRIX_RATE * math.sqrt(4 * hidden / width)
    for which in range(2):
        old = mlp_weights[which, block_at(row, rows), :].astype(F32)
        mlp_new.ref[which] = old - rate * got[4 * which + 3, :rows, :].astype(F32)

    mlp_new.send()
    two = gains[0] + gains[1] + gains[2] + gains[3]
    for t in range(4):
        lanes = slice(t * part, (t + 1) * part)
        totals = (gains[t][0:1, :], two[1 + t : 2 + t, :])
        for which in range(2):
            gain_moment_new[which : which + 1, lanes] = (
                MOMENT_DECAY * gain_moment[which : which + 1, lanes] + totals[which] / count[0:1, :]
            )
    new = gain_moment_new[...]
    scale = jnp.sqrt(jnp.mean(new * new, 1, keepdims=True)) + 1e-08
    gains_new[...] = norm_gains[...] - GAIN_RATE * new / scale


def per_device(
    tokens,
    cotangent,
    lengths,
    norm_gains,
    conv_kernel,
    mixer_weights,
    mlp_weights,
    gain_moment,
    kernel_moment,
    mixer_moment,
    mlp_moment,
):
    _, bucket, part = tokens.shape
    levels, taps, _ = conv_kernel.shape
    hidden = mlp_weights.shape[2]
    me = lax.axis_index("tensor")
    row = lax.axis_index("dp")
    dp = lax.axis_size("dp")
    width = 4 * part
    rows = width // dp
    half = bucket // 4
    piece_type = BF16 if rows % 16 == 0 else F32
    share = -(-levels * taps // dp)
    slot = -(-share // 8) * 8
    slot += (3 * rows + slot) % 16
    forward, inverse, kernel_forward, kernel_inverse = conv_tables(bucket, levels, taps, dp, slot)
    info = jnp.stack([me, lengths[0], row]).astype(jnp.int32)

    (spec_k,) = call(
        spectrum_kernel,
        [((8 * half, part), F32)],
        [],
        (info, Late(kernel_forward), Late(conv_kernel.reshape(levels * taps, part))),
        2, 10,
    )
    x_own, in_weights, in_gains, forward_one, inverse_one, late = fetch(
        info, tokens[0], mixer_weights, norm_gains, forward, inverse, (cotangent[0], mixer_weights[2])
    )
    x_pieces = gather_tensor(tokens[0], spec_k, x_own)

    act_like = ((bucket, part), F32)
    wide_like = ((half, width), F32)
    spec_like = ((2 * half, width), F32)
    whole_like = ((bucket, width), BF16)
    quarter_like = ((half, width), BF16)
    x, normed, n_own, inv_one, spec_v, conv, gate_act, gate_slope, branch, gains = call(
        entry_kernel,
        [whole_like, whole_like, Store(*act_like), Store((bucket, 1), F32), spec_like, act_like, act_like, act_like,
         ((bucket, part), BF16), ((2, width), F32)],
        [wide_like, spec_like],
        (info, x_own, *x_pieces[1:], in_weights, in_gains, forward_one, inverse_one, spec_k),
        0, 24,
    )
    late = gather_tensor(late, branch)
    cot, out_weights, delta_active, mlp_kept = call(
        cotangent_kernel,
        [whole_like, ((width, width), BF16), ((bucket, hidden), F32), (mlp_weights.shape, BF16)],
        [],
        (after(info, branch), *late, Late(mlp_weights)),
        3, 8,
    )
    branch_pieces = gather_tensor(branch, delta_active)
    near, kept, normed_two, active, delta_hidden, n_mine, inv_mine, middle_own = call(
        middle_kernel,
        [((width, width), BF16), ((width, width), F32), whole_like, ((bucket, hidden), BF16),
         ((bucket, hidden), BF16), wide_like, ((half, 1), F32), Store(*act_like)],
        [whole_like, ((bucket, width), F32)],
        (info, *branch_pieces, out_weights, x, gains, mlp_kept, delta_active),
        6, 24,
    )
    split_blocks = lambda v: v.reshape(2, -1, v.shape[-1])
    came = swap(split_blocks(near), "tensor", 1)
    mine, far = call(join_kernel, [wide_like, quarter_like], [], (info, split_blocks(kept), came), 1, 4)
    mlp_keep, mlp_send, moment_send, out_near, out_kept = call(
        mlp_kernel,
        [((width + 16, hidden), F32), ((width + 16, hidden), BF16), ((rows, hidden), F32), Store((2, bucket, part), BF16),
         Store((2, bucket, part), F32)],
        [((bucket, width), F32)],
        (after(info, far), normed_two, active, delta_hidden, cot, mlp_kept, Late(mlp_moment)),
        4, 20,
    )
    mlp_came = swap(mlp_send, "dp", 1)
    moment_came = swap(moment_send, "dp", 1)
    came = swap(far, "tensor", 2)
    delta_mid, grad_gain_two = call(
        norm_back_kernel,
        [quarter_like, ((1, width), F32)],
        [],
        (after(info, out_near), mine, came, cot, n_mine, inv_mine, gains),
        1000, 6,
    )
    (kernel_inverse_one,) = fetch(after(info, delta_mid), kernel_inverse)
    delta_pieces = gather_tensor(delta_mid, kernel_inverse_one)

    slots, one_near, one_kept, sums, delta_own = call(
        mixer_back_kernel,
        [Store((dp, 3 * rows + slot, part), piece_type), Store((2, bucket, part), BF16), Store((2, bucket, part), F32),
         ((16, part), F32), Store((bucket, part), BF16)],
        [whole_like, wide_like, spec_like, spec_like, ((8 * half, part), F32), ((bucket, 2 * part), BF16),
         ((bucket, width), F32)],
        (info, *delta_pieces, in_weights, gate_act, gate_slope, conv, branch, normed, spec_v, spec_k, forward_one, inverse_one,
         kernel_inverse_one, gains),
        0, 32,
    )
    arrived = lax.all_to_all(slots.astype(BF16), "dp", 0, 0, tiled=True)
    one_mine, far = call(
        join_late_kernel,
        [act_like, ((bucket, part), BF16)],
        [],
        (info, Late(one_kept), swap(one_near, "tensor", 1)),
        0, 4,
    )
    one_came = swap(far, "tensor", 2)
    out_mine, out_far = call(
        join_late_kernel,
        [act_like, ((bucket, part), BF16)],
        [],
        (info, Late(out_kept), swap(after(out_near, far), "tensor", 1)),
        1000, 4,
    )
    out_came = swap(out_far, "tensor", 2)
    pairs = dp // 2
    block = (2 * rows + 16, hidden)
    if dp == 8:
        blocks = call(mlp_rows_kernel, [(block, BF16)] * pairs, [], (info, mlp_keep, mlp_came), 1, 6)
        blocks = [blocks[0]] + [swap(blocks[k], "dp", 2 * k) for k in range(1, pairs)]
    else:
        (blocks,) = call(mlp_rows_kernel, [((pairs, *block), BF16)], [], (info, mlp_keep, mlp_came), 1, 6)
        parities = [[i for i in range(dp) if i % 2 == y] for y in range(2)]
        blocks = [lax.all_to_all(blocks, "dp", 0, 0, tiled=True, axis_index_groups=parities)]
    pair, moment_mine, moment_other, count = call(
        mlp_moment_kernel,
        [((2 * rows, hidden), BF16), Store((rows, hidden), F32), Store((rows, hidden), F32), ((8, part), F32)],
        [],
        (info, mlp_moment, moment_came, *blocks),
        1, 8,
    )
    if dp == 8:
        pair_pieces = [pair] + [swap(pair, "dp", 2 * k) for k in range(1, pairs)]
    else:
        pair_pieces = [lax.all_gather(pair, "dp", axis=0, tiled=True, axis_index_groups=parities)]
    mixer_moment_new, kernel_total, *sends = call(
        moment_kernel,
        [Store((3, rows, part), F32), ((slot, part), F32)] + [((rows + 16, part), piece_type)] * 4,
        [((3, rows, part), piece_type)],
        (after(info, out_far), arrived, Late(mixer_moment), count, sums),
        0, 6,
    )
    got = [sends[0]] + [swap(sends[k].astype(BF16), "tensor", k) for k in (1, 2, 3)]
    (payload,) = call(
        payload_kernel,
        [((dp, rows + 16, width), piece_type)],
        [((8, width), F32)],
        (info, one_mine, one_came, Late(n_own), *(g.astype(piece_type) for g in got), kernel_total, grad_gain_two),
        0, 4,
    )
    everything = lax.all_to_all(payload.astype(BF16), "dp", 0, 0, tiled=True)
    (mlp_columns,) = call(
        columns_kernel, [((width, hidden), BF16)], [], (after(info, payload), *pair_pieces), 0, 4
    )
    mlp_pieces = [mlp_columns] + [lax.ppermute(mlp_columns, "tensor", [(3 ^ k, 3)]) for k in (1, 2, 3)]
    input_grad, block_out = call(
        output_kernel,
        [Store(*act_like), Store((bucket, part), BF16)],
        [],
        (after(info, payload), one_mine, one_came, out_mine, out_came, Late(delta_own), Late(n_own), Late(inv_one), Late(middle_own), gains,
         *(g.astype(piece_type) for g in got)),
        1000, 8,
    )
    square = ((width, width), F32)
    sends, kernel_all = call(
        step_kernel,
        [((8, rows + 16, hidden), piece_type), ((dp * 24, part), F32)],
        [((width, width), piece_type), ((width, 4 * hidden), BF16), square, square, square, ((dp, 8, part), F32),
         ((rows, width), F32)],
        (after(info, block_out), everything.astype(piece_type), *mlp_pieces),
        18, 24,
    )
    groups = [[8 * z + q for q in range(8)] for z in range(dp // 2)]
    got = lax.all_to_all(sends.astype(BF16), ("dp", "tensor"), 0, 0, tiled=True, axis_index_groups=groups)
    moment_back = swap(after(moment_other, payload), "dp", 1)
    old = fetch(after(info, kernel_all), mixer_weights, mlp_weights, norm_gains, gain_moment)
    mixer_new, mlp_new, mlp_moment_new, gain_moment_new, gains_new = call(
        final_kernel,
        [Store((3, rows, part), F32), Store((2, rows, hidden), F32), Store((2, rows, hidden), F32), ((2, width), F32),
         ((2, width), F32)],
        [((4, 8, part), F32)],
        (info, got.astype(piece_type), Late(moment_mine), Late(moment_back), *old, count),
        3, 10,
    )
    grad_kernel = kernel_all.reshape(dp, 24, part)[:, :share].reshape(-1, part)[: levels * taps]
    kernel_moment_new = MOMENT_DECAY * kernel_moment + grad_kernel.reshape(levels, taps, part) / count[0]
    kernel_scale = (
        jnp.sqrt(jnp.mean(kernel_moment_new * kernel_moment_new, axis=(0, 1), keepdims=True)) + 1e-08
    )
    kernel_new = conv_kernel - KERNEL_RATE * kernel_moment_new / kernel_scale
    return (
        block_out[None],
        input_grad[None],
        gain_moment_new,
        gains_new,
        kernel_moment_new,
        kernel_new,
        mixer_moment_new,
        mixer_new,
        mlp_moment_new,
        mlp_new,
    )


def solution(mesh):
    tokens = P("dp", None, "tensor")
    columns = P(None, None, "tensor")
    blocks = P(None, "dp", "tensor")
    return jax.shard_map(
        per_device,
        mesh=mesh,
        in_specs=(tokens, tokens, P("dp"), P(), columns, columns, columns, P(), columns, blocks, blocks),
        out_specs=(tokens, tokens, P(), P(), columns, columns, blocks, blocks, blocks, blocks),
        check_vma=False,
    )
```

profile of v0, /device:TPU:0, one launch (start us, length us, event | category | flops | bytes accessed | tf_op | source)
XLA Modules:
  0.0 173.1 jit_solution(1459901749689170494)
XLA Ops:
  0.6 3.0 %collective-permute-start.1 = (bf16[1024,128]{1,0:T(8,128)(2,1)}, bf16[1024,128]{1,0:T(8,128)(2,1)S(1)}, u32[]{:S(2)}, u32[]{:S(2)}) collective-permute-start(bf16[1024,128]{1,0:T(8,128)(2,1)} %bitcast.20), channel_id=1, source_target_pairs={{0,2},{1,3},{2,0},{3,1},{4,6},{5,7},{6,4},{7,5},{8,10},{9,11},{10,... | collective-permute-start | bytes 786440 | tf_op jit(solution)/shard_map/ppermute | solution.py:133
  4.3 1.6 slice_bitcast_fusion.refs_6_
  5.9 2.1 %shard_map.222 = (bf16[1024,128]{1,0:T(8,128)(2,1)S(1)}, bf16[3,512,128]{2,1,0:T(8,128)(2,1)S(1)}, f32[2,512]{1,0:T(2,128)S(1)}, bf16[2,512,256]{2,1,0:T(8,128)(...) custom-call(s32[3]{0:T(128)S(1)} %pad_add_fusion.token_ref.refs_0_, ...), custom_call_target="tpu_custom_call" | custom-call | flops 10000000000 | bytes 4202496 | tf_op jit(solution)/shard_map/pallas_call | solution.py:306
  8.3 3.1 %shard_map.223.refs_9_.refs_12_ = f32[2048,128]{1,0:T(8,128)S(1)} custom-call(s32[3]{0:T(128)S(1)} %pad_add_fusion.token_ref.refs_0_, bf16[2,2048,160]{2,1,0:T(8,128)(2,1)} %constant.28.clone.refs_1_, f32[160,128]{1,0:T(8,128)} %bitcast.18), custom_call_target="tpu_custom_call" | custom-call | flops 20000000000 | bytes 2441228 | tf_op jit(solution)/shard_map/pallas_call | solution.py:274
  11.4 0.5 collective-permute-start.2
  12.0 1.1 collective-permute-done.2.refs_4_
  13.1 3.6 %shard_map.224 = (bf16[1024,512]{1,0:T(8,128)(2,1)S(1)}, bf16[1024,512]{1,0:T(8,128)(2,1)S(1)}, f32[1024,128]{1,0:T(8,128)}, f32[1024,1]{1,0:T(8,128)}, f32[512,...) custom-call(s32[3]{0:T(128)S(1)} %pad_add_fusion.token_ref.refs_0_, ...), custom_call_target="tpu_custom_call" | custom-call | flops 1000000 | bytes 9056268 | tf_op jit(solution)/shard_map/pallas_call | solution.py:274
  16.7 3.0 %collective-permute-done.6.refs_3_ = bf16[1536,128]{1,0:T(8,128)(2,1)S(1)} collective-permute-done((bf16[1536,128]{1,0:T(8,128)(2,1)S(1)}, bf16[1536,128]{1,0:T(8,128)(2,1)S(1)}, u32[]{:S(2)}, u32[]{:S(2)}) %collective-permute-start.6) | collective-permute-done | bytes 393248 | tf_op jit(solution)/shard_map/ppermute | solution.py:133
  19.7 0.6 collective-permute-start.4
  20.6 0.9 collective-permute-done.7.refs_4_
  21.4 2.7 %shard_map.225 = (bf16[1024,512]{1,0:T(8,128)(2,1)S(1)}, bf16[512,512]{1,0:T(8,128)(2,1)S(1)}, f32[1024,512]{1,0:T(8,128)S(1)}, bf16[2,512,512]{2,1,0:T(8,128)(2,1)S(1)}) custom-call(s32[3]{0:T(128)S(1)} %pad_add_fusion.token_ref.refs_0_, bf16[1536,128]{1,0:T(8,128)(2,1)S(1)} %get-tuple-element.105.refs_1_, ...), custom_call_target="tpu_custom_call" | custom-call | flops 30000001024 | bytes 7340044 | tf_op jit(solution)/shard_map/pallas_call | solution.py:274
  24.2 4.3 %collective-permute-done.4.refs_3_ = bf16[1024,128]{1,0:T(8,128)(2,1)S(1)} collective-permute-done((bf16[1024,128]{1,0:T(8,128)(2,1)S(1)}, bf16[1024,128]{1,0:T(8,128)(2,1)S(1)}, u32[]{:S(2)}, u32[]{:S(2)}) %collective-permute-start.4) | collective-permute-done | bytes 262176 | tf_op jit(solution)/shard_map/ppermute | solution.py:133
  28.4 1.5 collective-permute-done.8.refs_4_
  30.0 5.9 %shard_map.226 = (bf16[512,512]{1,0:T(8,128)(2,1)S(1)}, f32[512,512]{1,0:T(8,128)S(1)}, bf16[1024,512]{1,0:T(8,128)(2,1)S(1)}, bf16[1024,512]{1,0:T(8,128)(2,1)S...) custom-call(s32[3]{0:T(128)S(1)} %pad_add_fusion.token_ref.refs_0_, ...), custom_call_target="tpu_custom_call" | custom-call | flops 60000002048 | bytes 11539468 | tf_op jit(solution)/shard_map/pallas_call | solution.py:274
  36.0 1.8 %collective-permute-done.9.refs_2_ = bf16[2,256,512]{2,1,0:T(8,128)(2,1)S(1)} collective-permute-done((bf16[2,256,512]{2,1,0:T(8,128)(2,1)S(1)}, bf16[2,256,512]{2,1,0:T(8,128)(2,1)S(1)}, u32[]{:S(2)}, u32[]{:S(2)}) %collective-permute-start.9) | collective-permute-done | bytes 524320 | tf_op jit(solution)/shard_map/ppermute | solution.py:133
  37.8 0.6 shard_map.227
  38.5 0.7 collective-permute-start.10
  39.2 5.0 %shard_map.228 = (f32[528,512]{1,0:T(8,128)S(1)}, bf16[528,512]{1,0:T(8,128)(2,1)S(1)}, f32[64,512]{1,0:T(8,128)}, bf16[2,1024,128]{2,1,0:T(8,128)(2,1)}, f32[2,1024,128]{2,1,0:T(8,128)}) custom-call(s32[3]{0:T(128)S(1)} %pad_add_fusion.token_ref.refs_0_, bf16[1024,512]{1,0:T(8,128)(2,1)S(1)} %get-tuple-element.117.refs_1_, ...), custom_call_target="tpu_custom_call" | custom-call | flops 40000000000 | bytes 8830988 | tf_op jit(solution)/shard_map/pallas_call | solution.py:274
  44.2 2.7 %collective-permute-done.10.refs_2_ = bf16[256,512]{1,0:T(8,128)(2,1)S(1)} collective-permute-done((bf16[256,512]{1,0:T(8,128)(2,1)S(1)}, bf16[256,512]{1,0:T(8,128)(2,1)S(1)}, u32[]{:S(2)}, u32[]{:S(2)}) %collective-permute-start.10) | collective-permute-done | bytes 262176 | tf_op jit(solution)/shard_map/ppermute | solution.py:133
  46.9 0.9 shard_map.229
  47.8 0.7 collective-permute-start.12
  48.5 2.1 %shard_map.230.refs_15_ = bf16[2,256,2048]{2,1,0:T(8,128)(2,1)S(1)} custom-call(s32[3]{0:T(128)S(1)} %pad_add_fusion.token_ref.refs_0_, bf16[2,256,2048]{2,1,0:T(8,128)(2,1)} %constant.31.clone.refs_0_), custom_call_target="tpu_custom_call" | custom-call | flops 10000000000 | bytes 4194304 | tf_op jit(solution)/shard_map/pallas_call | solution.py:306
  50.7 4.7 %collective-permute-done.12.refs_3_ = bf16[256,512]{1,0:T(8,128)(2,1)S(1)} collective-permute-done((bf16[256,512]{1,0:T(8,128)(2,1)S(1)}, bf16[256,512]{1,0:T(8,128)(2,1)S(1)}, u32[]{:S(2)}, u32[]{:S(2)}) %collective-permute-start.12) | collective-permute-done | bytes 262176 | tf_op jit(solution)/shard_map/ppermute | solution.py:133
  55.4 1.5 collective-permute-start.18
  57.0 7.1 %shard_map.231 = (bf16[8,224,128]{2,1,0:T(8,128)(2,1)}, bf16[2,1024,128]{2,1,0:T(8,128)(2,1)}, f32[2,1024,128]{2,1,0:T(8,128)}, f32[16,128]{1,0:T(8,128)S(1)}, bf16[1024,128]{1,0:T(8,128)(2,1)}) custom-call(s32[3]{0:T(128)S(1)} %pad_add_fusion.token_ref.refs_0_, bf16[256,512]{1,0:T(8,128)(2,1)S(1)} %get-tuple-element.126.refs_1_, ...), custom_call_target="tpu_custom_call" | custom-call | flops 1000000 | bytes 11874316 | tf_op jit(solution)/shard_map/pallas_call | solution.py:274
  64.1 0.3 collective-permute-start.14
  64.4 1.4 collective-permute-start.17
  65.8 0.5 collective-permute-done.14.refs_2_
  66.3 2.6 %shard_map.232 = (f32[1024,128]{1,0:T(8,128)S(1)}, bf16[1024,128]{1,0:T(8,128)(2,1)}) custom-call(s32[3]{0:T(128)S(1)} %pad_add_fusion.token_ref.refs_0_, f32[2,1024,128]{2,1,0:T(8,128)} %get-tuple-element.134.refs_1_, bf16[2,1024,128]{2,1,0:T(8,128)(2,1)S(1)} %collective-permute-done.14.refs_2_), custom_call_target="tpu_custom_call" | custom-call | flops 1000000 | bytes 2359308 | tf_op jit(solution)/shard_map/pallas_call | solution.py:274
  68.9 0.3 collective-permute-start.16
  69.2 1.3 collective-permute-done.18.refs_2_
  70.5 1.3 shard_map.234
  71.8 1.6 collective-permute-start.19
  73.4 2.6 %collective-permute-start.20 = (bf16[144,512]{1,0:T(8,128)(2,1)}, bf16[144,512]{1,0:T(8,128)(2,1)}, u32[]{:S(2)}, u32[]{:S(2)}) collective-permute-start(bf16[144,512]{1,0:T(8,128)(2,1)} %get-tuple-element.149), channel_id=1, source_target_pairs={{0,16},{4,20},{8,24},{12,28},{16,0},{20,4},{24,8},{28,12},{1,17},{... | collective-permute-start | bytes 442376 | tf_op jit(solution)/shard_map/ppermute | solution.py:133
  76.2 5.8 %all-to-all-start = ((bf16[8,224,128]{2,1,0:T(8,128)(2,1)}), bf16[8,224,128]{2,1,0:T(8,128)(2,1)}, u32[]{:S(2)}, u32[]{:S(2)}) async-start(bf16[8,224,128]{2,1,0:T(8,128)(2,1)} %get-tuple-element.143), calls=%async_computation | async-start | bytes 917504 | tf_op jit(solution)/shard_map/all_to_all | solution.py:825
  82.1 0.7 collective-permute-start.15
  82.8 1.9 %shard_map.233 = (f32[1024,128]{1,0:T(8,128)S(1)}, bf16[1024,128]{1,0:T(8,128)(2,1)S(1)}) custom-call(s32[3]{0:T(128)S(1)} %pad_add_fusion.token_ref.refs_0_, f32[2,1024,128]{2,1,0:T(8,128)} %get-tuple-element.139.refs_1_, bf16[2,1024,128]{2,1,0:T(8,128)(2,1)S(1)} %collective-permute-done.16.refs_2_), custom_call_target="tpu_custom_call" | custom-call | flops 9999999827968 | bytes 2359308 | tf_op jit(solution)/shard_map/pallas_call | solution.py:274
  84.7 1.4 collective-permute-start.25
  86.1 2.9 %collective-permute-done.20.refs_5_ = bf16[144,512]{1,0:T(8,128)(2,1)} collective-permute-done((bf16[144,512]{1,0:T(8,128)(2,1)}, bf16[144,512]{1,0:T(8,128)(2,1)}, u32[]{:S(2)}, u32[]{:S(2)}) %collective-permute-start.20) | collective-permute-done | bytes 147488 | tf_op jit(solution)/shard_map/ppermute | solution.py:133
  89.0 2.0 %shard_map.235 = (bf16[128,512]{1,0:T(8,128)(2,1)S(1)}, f32[64,512]{1,0:T(8,128)}, f32[64,512]{1,0:T(8,128)}, f32[8,128]{1,0:T(8,128)S(1)}) custom-call(s32[3]{0:T(128)S(1)} %pad_add_fusion.token_ref.refs_0_, f32[2,64,512]{2,1,0:T(8,128)S(1)} %copy-done.10, f32[64,512]{1,0:T(8,128)} %collective-permute-done.17.refs_2_, ...), custom_call_target="tpu_custom_call" | custom-call | flops 10000000000 | bytes 1380364 | tf_op jit(solution)/shard_map/pallas_call | solution.py:274
  91.0 7.8 %all-to-all-done.refs_1_ = bf16[8,224,128]{2,1,0:T(8,128)(2,1)} async-done(((bf16[8,224,128]{2,1,0:T(8,128)(2,1)}), bf16[8,224,128]{2,1,0:T(8,128)(2,1)}, u32[]{:S(2)}, u32[]{:S(2)}) %all-to-all-start) | async-done | bytes 458784 | tf_op jit(solution)/shard_map/all_to_all | solution.py:825
  98.8 2.6 %shard_map.236 = (f32[3,64,128]{2,1,0:T(8,128)}, f32[32,128]{1,0:T(8,128)S(1)}, bf16[80,128]{1,0:T(8,128)(2,1)S(1)}, bf16[80,128]{1,0:T(8,128)(2,1)S(1)}, bf16[8...) custom-call(s32[3]{0:T(128)S(1)} %pad_add_fusion.token_ref.refs_0_, bf16[8,224,128]{2,1,0:T(8,128)(2,1)} %all-to-all-done.refs_1_, ...), custom_call_target="tpu_custom_call" | custom-call | flops 1000000 | bytes 765964 | tf_op jit(solution)/shard_map/pallas_call | solution.py:274
  101.5 0.7 collective-permute-start.23
  102.2 2.5 %collective-permute-start.28 = (bf16[128,512]{1,0:T(8,128)(2,1)S(1)}, bf16[128,512]{1,0:T(8,128)(2,1)S(1)}, u32[]{:S(2)}, u32[]{:S(2)}) collective-permute-start(bf16[128,512]{1,0:T(8,128)(2,1)S(1)} %get-tuple-element.167.refs_1_), channel_id=1, source_target_pairs={{0,24},{4,28},{8,16},{12,20},{16,8},{20,12},{24,0},{28,4},{1,25},{... | collective-permute-start | bytes 393224 | tf_op jit(solution)/shard_map/ppermute | solution.py:133
  104.7 1.9 %collective-permute-start.26 = (bf16[128,512]{1,0:T(8,128)(2,1)S(1)}, bf16[128,512]{1,0:T(8,128)(2,1)S(1)}, u32[]{:S(2)}, u32[]{:S(2)}) collective-permute-start(bf16[128,512]{1,0:T(8,128)(2,1)S(1)} %get-tuple-element.167.refs_1_), channel_id=1, source_target_pairs={{0,8},{4,12},{8,0},{12,4},{16,24},{20,28},{24,16},{28,20},{1,9},{5... | collective-permute-start | bytes 393224 | tf_op jit(solution)/shard_map/ppermute | solution.py:133
  106.6 0.3 collective-permute-start.24
  106.9 0.5 slice_bitcast_fusion.1
  107.4 2.5 %collective-permute-done.24.refs_7_.refs_13_ = bf16[80,128]{1,0:T(8,128)(2,1)S(1)} collective-permute-done((bf16[80,128]{1,0:T(8,128)(2,1)S(1)}, bf16[80,128]{1,0:T(8,128)(2,1)S(1)}, u32[]{:S(2)}, u32[]{:S(2)}) %collective-permute-start.24) | collective-permute-done | bytes 20512 | tf_op jit(solution)/shard_map/ppermute | solution.py:133
  110.0 3.0 %shard_map.237 = bf16[8,80,512]{2,1,0:T(8,128)(2,1)} custom-call(s32[3]{0:T(128)S(1)} %pad_add_fusion.token_ref.refs_0_, f32[1024,128]{1,0:T(8,128)S(1)} %get-tuple-element.136.refs_1_, bf16[1024,128]{1,0:T(8,128)(2,1)} %collective-permute-done.15.refs_2_, f32[1024,128]{1,0:T(8,128)} %get-tuple-element.138.refs_3_.refs_6_, ...), custom_call_target="tpu_custom_call" | custom-call | flops 1000000 | bytes 2066444 | tf_op jit(solution)/shard_map/pallas_call | solution.py:274
  113.0 4.7 %all-to-all-start.1 = ((bf16[8,80,512]{2,1,0:T(8,128)(2,1)}), bf16[8,80,512]{2,1,0:T(8,128)(2,1)}, u32[]{:S(2)}, u32[]{:S(2)}) async-start(bf16[8,80,512]{2,1,0:T(8,128)(2,1)} %shard_map.237), calls=%async_computation.1 | async-start | bytes 1310720 | tf_op jit(solution)/shard_map/all_to_all | solution.py:877
  117.7 1.4 shard_map.239.refs_2_
  119.1 2.9 %collective-permute-start.31 = (bf16[512,512]{1,0:T(8,128)(2,1)}, bf16[512,512]{1,0:T(8,128)(2,1)}, u32[]{:S(2)}, u32[]{:S(2)}) collective-permute-start(bf16[512,512]{1,0:T(8,128)(2,1)} %shard_map.239.refs_2_), channel_id=1, source_target_pairs={{0,3},{4,7},{8,11},{12,15},{16,19},{20,23},{24,27},{28,31}} | collective-permute-start | bytes 1572872 | tf_op jit(solution)/shard_map/ppermute | solution.py:881
  122.0 1.5 collective-permute-start.30
  123.4 1.5 collective-permute-start.29
  124.9 1.7 %collective-permute-start.32 = (f32[64,512]{1,0:T(8,128)}, f32[64,512]{1,0:T(8,128)}, u32[]{:S(2)}, u32[]{:S(2)}) collective-permute-start(f32[64,512]{1,0:T(8,128)} %get-tuple-element.171), channel_id=1, source_target_pairs={{0,4},{4,0},{8,12},{12,8},{16,20},{20,16},{24,28},{28,24},{1,5},{5... | collective-permute-start | bytes 393224 | tf_op jit(solution)/shard_map/ppermute | solution.py:133
  126.6 3.8 %shard_map.238 = (f32[1024,128]{1,0:T(8,128)}, bf16[1024,128]{1,0:T(8,128)(2,1)}) custom-call(s32[3]{0:T(128)S(1)} %pad_add_fusion.token_ref.refs_0_, f32[1024,128]{1,0:T(8,128)S(1)} %get-tuple-element.136.refs_1_, bf16[1024,128]{1,0:T(8,128)(2,1)} %collective-permute-done.15.refs_2_, f32[1024,128]{1,0:T(8,128)S(1)} %get-tuple-element.160.refs_3_, ...), custom_call_target="tpu_custom_call" | custom-call | flops 9999999827968 | bytes 3760140 | tf_op jit(solution)/shard_map/pallas_call | solution.py:274
  130.5 2.6 %collective-permute-done.31.refs_5_ = bf16[512,512]{1,0:T(8,128)(2,1)} collective-permute-done((bf16[512,512]{1,0:T(8,128)(2,1)}, bf16[512,512]{1,0:T(8,128)(2,1)}, u32[]{:S(2)}, u32[]{:S(2)}) %collective-permute-start.31) | collective-permute-done | bytes 524320 | tf_op jit(solution)/shard_map/ppermute | solution.py:881
  133.1 2.2 %all-to-all-done.1.refs_1_ = bf16[8,80,512]{2,1,0:T(8,128)(2,1)} async-done(((bf16[8,80,512]{2,1,0:T(8,128)(2,1)}), bf16[8,80,512]{2,1,0:T(8,128)(2,1)}, u32[]{:S(2)}, u32[]{:S(2)}) %all-to-all-start.1) | async-done | bytes 655392 | tf_op jit(solution)/shard_map/all_to_all | solution.py:877
  135.3 19.4 %shard_map.240 = (bf16[8,80,512]{2,1,0:T(8,128)(2,1)}, f32[192,128]{1,0:T(8,128)S(1)}) custom-call(s32[3]{0:T(128)S(1)} %pad_add_fusion.token_ref.refs_0_, bf16[8,80,512]{2,1,0:T(8,128)(2,1)} %all-to-all-done.1.refs_1_, bf16[512,512]{1,0:T(8,128)(2,1)} %shard_map.239.refs_2_, bf16[512,512]{1,0:T(8,128)(2,1)} %collective-permute-done.29.refs_3_, ...), custom_call_target="tpu_custom_call" | custom-call | flops 179999997952 | bytes 3506188 | tf_op jit(solution)/shard_map/pallas_call | solution.py:274
  154.7 4.1 %all-to-all-start.2 = ((bf16[8,80,512]{2,1,0:T(8,128)(2,1)}), bf16[8,80,512]{2,1,0:T(8,128)(2,1)S(1)}, u32[]{:S(2)}, u32[]{:S(2)}) async-start(bf16[8,80,512]{2,1,0:T(8,128)(2,1)} %get-tuple-element.168), calls=%async_computation.2 | async-start | bytes 1310720 | tf_op jit(solution)/shard_map/all_to_all | solution.py:900
  158.8 1.9 %shard_map.241 = (bf16[3,512,128]{2,1,0:T(8,128)(2,1)S(1)}, bf16[2,512,512]{2,1,0:T(8,128)(2,1)S(1)}, f32[2,512]{1,0:T(2,128)S(1)}, f32[2,512]{1,0:T(2,128)S(1)}) custom-call(s32[3]{0:T(128)S(1)} %pad_add_fusion.token_ref.refs_0_, bf16[3,512,128]{2,1,0:T(8,128)(2,1)} %refs_0_.2, bf16[2,512,512]{2,1,0:T(8,128)(2,1)} %refs_1_.6, f32[2,512]{1,0:T(2,128)} %refs_2_.5, ...), custom_call_target="tpu_custom_call" | custom-call | flops 10000000000 | bytes 2899968 | tf_op jit(solution)/shard_map/pallas_call | solution.py:306
  160.8 0.7 divide_subtract_fusion
  161.5 8.4 %all-to-all-done.2.refs_1_ = bf16[8,80,512]{2,1,0:T(8,128)(2,1)S(1)} async-done(((bf16[8,80,512]{2,1,0:T(8,128)(2,1)}), bf16[8,80,512]{2,1,0:T(8,128)(2,1)S(1)}, u32[]{:S(2)}, u32[]{:S(2)}) %all-to-all-start.2) | async-done | bytes 655392 | tf_op jit(solution)/shard_map/all_to_all | solution.py:900
  169.9 3.0 %shard_map.242 = (f32[3,64,128]{2,1,0:T(8,128)}, f32[2,64,512]{2,1,0:T(8,128)}, f32[2,64,512]{2,1,0:T(8,128)}, f32[2,512]{1,0:T(2,128)}, f32[2,512]{1,0:T(2,128)}) custom-call(s32[3]{0:T(128)S(1)} %pad_add_fusion.token_ref.refs_0_, bf16[8,80,512]{2,1,0:T(8,128)(2,1)S(1)} %all-to-all-done.2.refs_1_, f32[64,512]{1,0:T(8,128)} %get-tuple-element.169.refs_2_, ...), custom_call_target="tpu_custom_call" | custom-call | flops 30000001024 | bytes 3002380 | tf_op jit(solution)/shard_map/pallas_call | solution.py:274
  (68 shorter events, 1.2 us)
Async XLA Ops:
  0.6 10.8 %collective-permute-start.1 = (bf16[1024,128]{1,0:T(8,128)(2,1)}, bf16[1024,128]{1,0:T(8,128)(2,1)S(1)}, u32[]{:S(2)}, u32[]{:S(2)}) collective-permute-start(bf16[1024,128]{1,0:T(8,128)(2,1)} %bitcast.20), channel_id=1, source_target_pairs={{0,2},{1,3},{2,0},{3,1},{4,6},{5,7},{6,4},{7,5},{8,10},{9,11},{10,... | collective-permute-start | bytes 786440 | tf_op jit(solution)/shard_map/ppermute | solution.py:133
  3.6 8.3 %collective-permute-start = (bf16[1024,128]{1,0:T(8,128)(2,1)}, bf16[1024,128]{1,0:T(8,128)(2,1)S(1)}, u32[]{:S(2)}, u32[]{:S(2)}) collective-permute-start(bf16[1024,128]{1,0:T(8,128)(2,1)} %bitcast.21), channel_id=1, source_target_pairs={{0,1},{1,0},{2,3},{3,2},{4,5},{5,4},{6,7},{7,6},{8,9},{9,8},{10,11... | collective-permute-start | bytes 786440 | tf_op jit(solution)/shard_map/ppermute | solution.py:133
  8.1 5.0 %copy-start.2 = (bf16[2,512,256]{2,1,0:T(8,128)(2,1)}, bf16[2,512,256]{2,1,0:T(8,128)(2,1)S(1)}, u32[]{:S(2)}) copy-start(bf16[2,512,256]{2,1,0:T(8,128)(2,1)S(1)} %get-tuple-element.101.refs_7_.refs_13_) | copy-start | bytes 1572868
  8.1 5.0 %copy-start.4 = (bf16[2,256,512]{2,1,0:T(8,128)(2,1)}, bf16[2,256,512]{2,1,0:T(8,128)(2,1)S(1)}, u32[]{:S(2)}) copy-start(bf16[2,256,512]{2,1,0:T(8,128)(2,1)S(1)} %get-tuple-element.102.refs_8_.refs_14_) | copy-start | bytes 1572868
  8.1 5.0 %copy-start.6 = (bf16[3,512,128]{2,1,0:T(8,128)(2,1)}, bf16[3,512,128]{2,1,0:T(8,128)(2,1)S(1)}, u32[]{:S(2)}) copy-start(bf16[3,512,128]{2,1,0:T(8,128)(2,1)S(1)} %get-tuple-element.99.refs_5_) | copy-start | bytes 1179652
  8.1 11.6 %collective-permute-start.6 = (bf16[1536,128]{1,0:T(8,128)(2,1)S(1)}, bf16[1536,128]{1,0:T(8,128)(2,1)S(1)}, u32[]{:S(2)}, u32[]{:S(2)}) collective-permute-start(bf16[1536,128]{1,0:T(8,128)(2,1)S(1)} %get-tuple-element.105.refs_1_), channel_id=1, source_target_pairs={{0,2},{1,3},{2,0},{3,1},{4,6},{5,7},{6,4},{7,5},{8,10},{9,11},{10,... | collective-permute-start | bytes 1179656 | tf_op jit(solution)/shard_map/ppermute | solution.py:133
  11.4 12.8 %copy-start = (f32[2048,128]{1,0:T(8,128)}, f32[2048,128]{1,0:T(8,128)S(1)}, u32[]{:S(2)}) copy-start(f32[2048,128]{1,0:T(8,128)S(1)} %shard_map.223.refs_9_.refs_12_) | copy-start | bytes 3145732
  11.4 1.7 collective-permute-start.2
  11.9 8.7 %collective-permute-start.5 = (bf16[1536,128]{1,0:T(8,128)(2,1)S(1)}, bf16[1536,128]{1,0:T(8,128)(2,1)S(1)}, u32[]{:S(2)}, u32[]{:S(2)}) collective-permute-start(bf16[1536,128]{1,0:T(8,128)(2,1)S(1)} %get-tuple-element.105.refs_1_), channel_id=1, source_target_pairs={{0,1},{1,0},{2,3},{3,2},{4,5},{5,4},{6,7},{7,6},{8,9},{9,8},{10,11... | collective-permute-start | bytes 1179656 | tf_op jit(solution)/shard_map/ppermute | solution.py:133
  16.7 40.2 %copy-start.8 = (f32[2,512]{1,0:T(2,128)}, f32[2,512]{1,0:T(2,128)S(1)}, u32[]{:S(2)}) copy-start(f32[2,512]{1,0:T(2,128)S(1)} %get-tuple-element.111.refs_7_.refs_6_.refs_16_.refs_9_) | copy-start | bytes 12292
  19.7 1.7 collective-permute-start.7
  19.7 8.7 %collective-permute-start.4 = (bf16[1024,128]{1,0:T(8,128)(2,1)S(1)}, bf16[1024,128]{1,0:T(8,128)(2,1)S(1)}, u32[]{:S(2)}, u32[]{:S(2)}) collective-permute-start(bf16[1024,128]{1,0:T(8,128)(2,1)S(1)} %get-tuple-element.103.refs_1_.refs_9_), channel_id=1, source_target_pairs={{0,2},{1,3},{2,0},{3,1},{4,6},{5,7},{6,4},{7,5},{8,10},{9,11},{10,... | collective-permute-start | bytes 786440 | tf_op jit(solution)/shard_map/ppermute | solution.py:133
  20.3 8.1 %collective-permute-start.3 = (bf16[1024,128]{1,0:T(8,128)(2,1)S(1)}, bf16[1024,128]{1,0:T(8,128)(2,1)S(1)}, u32[]{:S(2)}, u32[]{:S(2)}) collective-permute-start(bf16[1024,128]{1,0:T(8,128)(2,1)S(1)} %get-tuple-element.103.refs_1_.refs_9_), channel_id=1, source_target_pairs={{0,1},{1,0},{2,3},{3,2},{4,5},{5,4},{6,7},{7,6},{8,9},{9,8},{10,11... | collective-permute-start | bytes 786440 | tf_op jit(solution)/shard_map/ppermute | solution.py:133
  28.4 1.5 collective-permute-start.8
  35.8 2.0 %collective-permute-start.9 = (bf16[2,256,512]{2,1,0:T(8,128)(2,1)S(1)}, bf16[2,256,512]{2,1,0:T(8,128)(2,1)S(1)}, u32[]{:S(2)}, u32[]{:S(2)}) collective-permute-start(bf16[2,256,512]{2,1,0:T(8,128)(2,1)S(1)} %bitcast.16), channel_id=1, source_target_pairs={{0,1},{1,0},{2,3},{3,2},{4,5},{5,4},{6,7},{7,6},{8,9},{9,8},{10,11... | collective-permute-start | bytes 1572872 | tf_op jit(solution)/shard_map/ppermute | solution.py:133
  38.5 8.4 %collective-permute-start.10 = (bf16[256,512]{1,0:T(8,128)(2,1)S(1)}, bf16[256,512]{1,0:T(8,128)(2,1)S(1)}, u32[]{:S(2)}, u32[]{:S(2)}) collective-permute-start(bf16[256,512]{1,0:T(8,128)(2,1)S(1)} %get-tuple-element.115), channel_id=1, source_target_pairs={{0,2},{1,3},{2,0},{3,1},{4,6},{5,7},{6,4},{7,5},{8,10},{9,11},{10,... | collective-permute-start | bytes 786440 | tf_op jit(solution)/shard_map/ppermute | solution.py:133
  47.8 9.2 %copy-start.1 = (f32[2048,128]{1,0:T(8,128)S(1)}, f32[2048,128]{1,0:T(8,128)}, u32[]{:S(2)}) copy-start(f32[2048,128]{1,0:T(8,128)} %copy-done) | copy-start | bytes 3145732
  47.8 9.2 %copy-start.3 = (bf16[2,512,256]{2,1,0:T(8,128)(2,1)S(1)}, bf16[2,512,256]{2,1,0:T(8,128)(2,1)}, u32[]{:S(2)}) copy-start(bf16[2,512,256]{2,1,0:T(8,128)(2,1)} %copy-done.2) | copy-start | bytes 1572868
  47.8 9.2 %copy-start.5 = (bf16[2,256,512]{2,1,0:T(8,128)(2,1)S(1)}, bf16[2,256,512]{2,1,0:T(8,128)(2,1)}, u32[]{:S(2)}) copy-start(bf16[2,256,512]{2,1,0:T(8,128)(2,1)} %copy-done.4) | copy-start | bytes 1572868
  47.8 9.2 %copy-start.7 = (bf16[3,512,128]{2,1,0:T(8,128)(2,1)S(1)}, bf16[3,512,128]{2,1,0:T(8,128)(2,1)}, u32[]{:S(2)}) copy-start(bf16[3,512,128]{2,1,0:T(8,128)(2,1)} %copy-done.6) | copy-start | bytes 1179652
  47.8 7.6 %collective-permute-start.12 = (bf16[256,512]{1,0:T(8,128)(2,1)S(1)}, bf16[256,512]{1,0:T(8,128)(2,1)S(1)}, u32[]{:S(2)}, u32[]{:S(2)}) collective-permute-start(bf16[256,512]{1,0:T(8,128)(2,1)S(1)} %get-tuple-element.126.refs_1_), channel_id=1, source_target_pairs={{0,2},{1,3},{2,0},{3,1},{4,6},{5,7},{6,4},{7,5},{8,10},{9,11},{10,... | collective-permute-start | bytes 786440 | tf_op jit(solution)/shard_map/ppermute | solution.py:133
  48.5 8.4 %collective-permute-start.11 = (bf16[256,512]{1,0:T(8,128)(2,1)S(1)}, bf16[256,512]{1,0:T(8,128)(2,1)S(1)}, u32[]{:S(2)}, u32[]{:S(2)}) collective-permute-start(bf16[256,512]{1,0:T(8,128)(2,1)S(1)} %get-tuple-element.126.refs_1_), channel_id=1, source_target_pairs={{0,1},{1,0},{2,3},{3,2},{4,5},{5,4},{6,7},{7,6},{8,9},{9,8},{10,11... | collective-permute-start | bytes 786440 | tf_op jit(solution)/shard_map/ppermute | solution.py:133
  55.4 1.5 collective-permute-start.13
  55.4 15.1 %collective-permute-start.18 = (bf16[528,512]{1,0:T(8,128)(2,1)S(1)}, bf16[528,512]{1,0:T(8,128)(2,1)S(1)}, u32[]{:S(2)}, u32[]{:S(2)}) collective-permute-start(bf16[528,512]{1,0:T(8,128)(2,1)S(1)} %get-tuple-element.146), channel_id=1, source_target_pairs={{0,4},{4,0},{8,12},{12,8},{16,20},{20,16},{24,28},{28,24},{1,5},{5... | collective-permute-start | bytes 1622024 | tf_op jit(solution)/shard_map/ppermute | solution.py:133
  57.0 11.9 %copy-start.15 = (bf16[2,1024,128]{2,1,0:T(8,128)(2,1)S(1)}, bf16[2,1024,128]{2,1,0:T(8,128)(2,1)}, u32[]{:S(2)}) copy-start(bf16[2,1024,128]{2,1,0:T(8,128)(2,1)} %get-tuple-element.140) | copy-start | bytes 1572868
  64.1 2.2 %collective-permute-start.14 = (bf16[2,1024,128]{2,1,0:T(8,128)(2,1)}, bf16[2,1024,128]{2,1,0:T(8,128)(2,1)S(1)}, u32[]{:S(2)}, u32[]{:S(2)}) collective-permute-start(bf16[2,1024,128]{2,1,0:T(8,128)(2,1)} %get-tuple-element.135), channel_id=1, source_target_pairs={{0,1},{1,0},{2,3},{3,2},{4,5},{5,4},{6,7},{7,6},{8,9},{9,8},{10,11... | collective-permute-start | bytes 1572872 | tf_op jit(solution)/shard_map/ppermute | solution.py:133
  64.4 20.2 %collective-permute-start.17 = (f32[64,512]{1,0:T(8,128)}, f32[64,512]{1,0:T(8,128)}, u32[]{:S(2)}, u32[]{:S(2)}) collective-permute-start(f32[64,512]{1,0:T(8,128)} %get-tuple-element.144), channel_id=1, source_target_pairs={{0,4},{4,0},{8,12},{12,8},{16,20},{20,16},{24,28},{28,24},{1,5},{5... | collective-permute-start | bytes 393224 | tf_op jit(solution)/shard_map/ppermute | solution.py:133
  68.9 13.2 %collective-permute-start.16 = (bf16[2,1024,128]{2,1,0:T(8,128)(2,1)S(1)}, bf16[2,1024,128]{2,1,0:T(8,128)(2,1)S(1)}, u32[]{:S(2)}, u32[]{:S(2)}) collective-permute-start(bf16[2,1024,128]{2,1,0:T(8,128)(2,1)S(1)} %copy-done.15), channel_id=1, source_target_pairs={{0,1},{1,0},{2,3},{3,2},{4,5},{5,4},{6,7},{7,6},{8,9},{9,8},{10,11... | collective-permute-start | bytes 1572872 | tf_op jit(solution)/shard_map/ppermute | solution.py:133
  71.8 14.3 %collective-permute-start.19 = (bf16[144,512]{1,0:T(8,128)(2,1)}, bf16[144,512]{1,0:T(8,128)(2,1)}, u32[]{:S(2)}, u32[]{:S(2)}) collective-permute-start(bf16[144,512]{1,0:T(8,128)(2,1)} %get-tuple-element.148), channel_id=1, source_target_pairs={{0,8},{4,12},{8,0},{12,4},{16,24},{20,28},{24,16},{28,20},{1,9},{5... | collective-permute-start | bytes 442376 | tf_op jit(solution)/shard_map/ppermute | solution.py:133
  73.4 15.6 %collective-permute-start.20 = (bf16[144,512]{1,0:T(8,128)(2,1)}, bf16[144,512]{1,0:T(8,128)(2,1)}, u32[]{:S(2)}, u32[]{:S(2)}) collective-permute-start(bf16[144,512]{1,0:T(8,128)(2,1)} %get-tuple-element.149), channel_id=1, source_target_pairs={{0,16},{4,20},{8,24},{12,28},{16,0},{20,4},{24,8},{28,12},{1,17},{... | collective-permute-start | bytes 442376 | tf_op jit(solution)/shard_map/ppermute | solution.py:133
  76.0 13.0 %collective-permute-start.21 = (bf16[144,512]{1,0:T(8,128)(2,1)}, bf16[144,512]{1,0:T(8,128)(2,1)}, u32[]{:S(2)}, u32[]{:S(2)}) collective-permute-start(bf16[144,512]{1,0:T(8,128)(2,1)} %get-tuple-element.150), channel_id=1, source_target_pairs={{0,24},{4,28},{8,16},{12,20},{16,8},{20,12},{24,0},{28,4},{1,25},{... | collective-permute-start | bytes 442376 | tf_op jit(solution)/shard_map/ppermute | solution.py:133
  76.2 22.6 %all-to-all-start = ((bf16[8,224,128]{2,1,0:T(8,128)(2,1)}), bf16[8,224,128]{2,1,0:T(8,128)(2,1)}, u32[]{:S(2)}, u32[]{:S(2)}) async-start(bf16[8,224,128]{2,1,0:T(8,128)(2,1)} %get-tuple-element.143), calls=%async_computation | async-start | bytes 917504 | tf_op jit(solution)/shard_map/all_to_all | solution.py:825
  82.1 22.6 %collective-permute-start.15 = (bf16[1024,128]{1,0:T(8,128)(2,1)}, bf16[1024,128]{1,0:T(8,128)(2,1)}, u32[]{:S(2)}, u32[]{:S(2)}) collective-permute-start(bf16[1024,128]{1,0:T(8,128)(2,1)} %get-tuple-element.137), channel_id=1, source_target_pairs={{0,2},{1,3},{2,0},{3,1},{4,6},{5,7},{6,4},{7,5},{8,10},{9,11},{10,... | collective-permute-start | bytes 786440 | tf_op jit(solution)/shard_map/ppermute | solution.py:133
  82.8 6.2 %copy-start.10 = (f32[2,64,512]{2,1,0:T(8,128)S(1)}, f32[2,64,512]{2,1,0:T(8,128)}, u32[]{:S(2)}) copy-start(f32[2,64,512]{2,1,0:T(8,128)} %refs_1_.5) | copy-start | bytes 786436
  84.7 42.0 %collective-permute-start.25 = (bf16[1024,128]{1,0:T(8,128)(2,1)S(1)}, bf16[1024,128]{1,0:T(8,128)(2,1)S(1)}, u32[]{:S(2)}, u32[]{:S(2)}) collective-permute-start(bf16[1024,128]{1,0:T(8,128)(2,1)S(1)} %get-tuple-element.141), channel_id=1, source_target_pairs={{0,2},{1,3},{2,0},{3,1},{4,6},{5,7},{6,4},{7,5},{8,10},{9,11},{10,... | collective-permute-start | bytes 786440 | tf_op jit(solution)/shard_map/ppermute | solution.py:133
  101.4 25.2 %copy-start.9 = (f32[2,512]{1,0:T(2,128)S(1)}, f32[2,512]{1,0:T(2,128)}, u32[]{:S(2)}) copy-start(f32[2,512]{1,0:T(2,128)} %copy-done.8) | copy-start | bytes 12292
  101.4 3.3 %collective-permute-start.22 = (bf16[80,128]{1,0:T(8,128)(2,1)S(1)}, bf16[80,128]{1,0:T(8,128)(2,1)S(1)}, u32[]{:S(2)}, u32[]{:S(2)}) collective-permute-start(bf16[80,128]{1,0:T(8,128)(2,1)S(1)} %get-tuple-element.154), channel_id=1, source_target_pairs={{0,1},{1,0},{2,3},{3,2},{4,5},{5,4},{6,7},{7,6},{8,9},{9,8},{10,11... | collective-permute-start | bytes 61448 | tf_op jit(solution)/shard_map/ppermute | solution.py:133
  101.5 5.1 %collective-permute-start.23 = (bf16[80,128]{1,0:T(8,128)(2,1)S(1)}, bf16[80,128]{1,0:T(8,128)(2,1)S(1)}, u32[]{:S(2)}, u32[]{:S(2)}) collective-permute-start(bf16[80,128]{1,0:T(8,128)(2,1)S(1)} %get-tuple-element.155), channel_id=1, source_target_pairs={{0,2},{1,3},{2,0},{3,1},{4,6},{5,7},{6,4},{7,5},{8,10},{9,11},{10,... | collective-permute-start | bytes 61448 | tf_op jit(solution)/shard_map/ppermute | solution.py:133
  102.2 15.5 %collective-permute-start.28 = (bf16[128,512]{1,0:T(8,128)(2,1)S(1)}, bf16[128,512]{1,0:T(8,128)(2,1)S(1)}, u32[]{:S(2)}, u32[]{:S(2)}) collective-permute-start(bf16[128,512]{1,0:T(8,128)(2,1)S(1)} %get-tuple-element.167.refs_1_), channel_id=1, source_target_pairs={{0,24},{4,28},{8,16},{12,20},{16,8},{20,12},{24,0},{28,4},{1,25},{... | collective-permute-start | bytes 393224 | tf_op jit(solution)/shard_map/ppermute | solution.py:133
  104.7 13.0 %collective-permute-start.27 = (bf16[128,512]{1,0:T(8,128)(2,1)S(1)}, bf16[128,512]{1,0:T(8,128)(2,1)S(1)}, u32[]{:S(2)}, u32[]{:S(2)}) collective-permute-start(bf16[128,512]{1,0:T(8,128)(2,1)S(1)} %get-tuple-element.167.refs_1_), channel_id=1, source_target_pairs={{0,16},{4,20},{8,24},{12,28},{16,0},{20,4},{24,8},{28,12},{1,17},{... | collective-permute-start | bytes 393224 | tf_op jit(solution)/shard_map/ppermute | solution.py:133
  104.7 13.0 %collective-permute-start.26 = (bf16[128,512]{1,0:T(8,128)(2,1)S(1)}, bf16[128,512]{1,0:T(8,128)(2,1)S(1)}, u32[]{:S(2)}, u32[]{:S(2)}) collective-permute-start(bf16[128,512]{1,0:T(8,128)(2,1)S(1)} %get-tuple-element.167.refs_1_), channel_id=1, source_target_pairs={{0,8},{4,12},{8,0},{12,4},{16,24},{20,28},{24,16},{28,20},{1,9},{5... | collective-permute-start | bytes 393224 | tf_op jit(solution)/shard_map/ppermute | solution.py:133
  106.6 3.4 %collective-permute-start.24 = (bf16[80,128]{1,0:T(8,128)(2,1)S(1)}, bf16[80,128]{1,0:T(8,128)(2,1)S(1)}, u32[]{:S(2)}, u32[]{:S(2)}) collective-permute-start(bf16[80,128]{1,0:T(8,128)(2,1)S(1)} %get-tuple-element.156), channel_id=1, source_target_pairs={{0,3},{1,2},{2,1},{3,0},{4,7},{5,6},{6,5},{7,4},{8,11},{9,10},{10,... | collective-permute-start | bytes 61448 | tf_op jit(solution)/shard_map/ppermute | solution.py:133
  113.0 22.3 %all-to-all-start.1 = ((bf16[8,80,512]{2,1,0:T(8,128)(2,1)}), bf16[8,80,512]{2,1,0:T(8,128)(2,1)}, u32[]{:S(2)}, u32[]{:S(2)}) async-start(bf16[8,80,512]{2,1,0:T(8,128)(2,1)} %shard_map.237), calls=%async_computation.1 | async-start | bytes 1310720 | tf_op jit(solution)/shard_map/all_to_all | solution.py:877
  119.1 14.0 %collective-permute-start.31 = (bf16[512,512]{1,0:T(8,128)(2,1)}, bf16[512,512]{1,0:T(8,128)(2,1)}, u32[]{:S(2)}, u32[]{:S(2)}) collective-permute-start(bf16[512,512]{1,0:T(8,128)(2,1)} %shard_map.239.refs_2_), channel_id=1, source_target_pairs={{0,3},{4,7},{8,11},{12,15},{16,19},{20,23},{24,27},{28,31}} | collective-permute-start | bytes 1572872 | tf_op jit(solution)/shard_map/ppermute | solution.py:881
  122.0 11.1 %collective-permute-start.30 = (bf16[512,512]{1,0:T(8,128)(2,1)}, bf16[512,512]{1,0:T(8,128)(2,1)}, u32[]{:S(2)}, u32[]{:S(2)}) collective-permute-start(bf16[512,512]{1,0:T(8,128)(2,1)} %shard_map.239.refs_2_), channel_id=1, source_target_pairs={{1,3},{5,7},{9,11},{13,15},{17,19},{21,23},{25,27},{29,31}} | collective-permute-start | bytes 1572872 | tf_op jit(solution)/shard_map/ppermute | solution.py:881
  123.4 9.7 %collective-permute-start.29 = (bf16[512,512]{1,0:T(8,128)(2,1)}, bf16[512,512]{1,0:T(8,128)(2,1)}, u32[]{:S(2)}, u32[]{:S(2)}) collective-permute-start(bf16[512,512]{1,0:T(8,128)(2,1)} %shard_map.239.refs_2_), channel_id=1, source_target_pairs={{2,3},{6,7},{10,11},{14,15},{18,19},{22,23},{26,27},{30,31}} | collective-permute-start | bytes 1572872 | tf_op jit(solution)/shard_map/ppermute | solution.py:881
  124.9 36.6 %collective-permute-start.32 = (f32[64,512]{1,0:T(8,128)}, f32[64,512]{1,0:T(8,128)}, u32[]{:S(2)}, u32[]{:S(2)}) collective-permute-start(f32[64,512]{1,0:T(8,128)} %get-tuple-element.171), channel_id=1, source_target_pairs={{0,4},{4,0},{8,12},{12,8},{16,20},{20,16},{24,28},{28,24},{1,5},{5... | collective-permute-start | bytes 393224 | tf_op jit(solution)/shard_map/ppermute | solution.py:133
  154.7 15.2 %all-to-all-start.2 = ((bf16[8,80,512]{2,1,0:T(8,128)(2,1)}), bf16[8,80,512]{2,1,0:T(8,128)(2,1)S(1)}, u32[]{:S(2)}, u32[]{:S(2)}) async-start(bf16[8,80,512]{2,1,0:T(8,128)(2,1)} %get-tuple-element.168), calls=%async_computation.2 | async-start | bytes 1310720 | tf_op jit(solution)/shard_map/all_to_all | solution.py:900
  158.8 2.0 %copy-start.12 = (f32[5,32,128]{2,1,0:T(8,128)S(1)}, f32[5,32,128]{2,1,0:T(8,128)}, u32[]{:S(2)}) copy-start(f32[5,32,128]{2,1,0:T(8,128)} %param.23) | copy-start | bytes 245764
  158.8 2.0 %copy-start.14 = (f32[128]{0:T(128)S(1)}, f32[128]{0:T(128)}, u32[]{:S(2)}) copy-start(f32[128]{0:T(128)} %slice_bitcast_fusion.1) | copy-start | bytes 1540
  158.8 2.0 %copy-start.13 = (f32[5,32,128]{2,1,0:T(8,128)S(1)}, f32[5,32,128]{2,1,0:T(8,128)}, u32[]{:S(2)}) copy-start(f32[5,32,128]{2,1,0:T(8,128)} %param.19) | copy-start | bytes 245764
  160.8 12.1 %copy-start.11 = (f32[5,32,128]{2,1,0:T(8,128)}, f32[5,32,128]{2,1,0:T(8,128)S(1)}, u32[]{:S(2)}) copy-start(f32[5,32,128]{2,1,0:T(8,128)S(1)} %get-tuple-element.185) | copy-start | bytes 245764
where the time goes:
time: 174 us; the launch traced here: 173 us
  Pallas kernels  76.1 us (44%)
  waiting for transfers between devices  48.2 us (28%)
  starting transfers between devices  43.9 us (25%)
  local copies, waits for them, and re-layouts  2.17 us (1%)
  between operations  1.9 us (1%)
    pallas_call x18, Pallas kernels, call(): pl.pallas_call(body, out_shape=tuple((pltpu.HBM(o.shape, o.dtype) if isin...  70 us
    ppermute x30, waiting for transfers between devices, swap(): return lax.ppermute(value, axis, [(i, i ^ k) for i in range(size)])  27.1 us
    ppermute x30, starting transfers between devices, swap(): return lax.ppermute(value, axis, [(i, i ^ k) for i in range(size)])  23.5 us
    all_to_all x1, waiting for transfers between devices, per_device(): lax.all_to_all(sends.astype(BF16), ('dp', 'tensor'), 0, 0, tiled=True, ax...  8.41 us
    all_to_all x1, waiting for transfers between devices, per_device(): arrived = lax.all_to_all(slots.astype(BF16), 'dp', 0, 0, tiled=True)  7.82 us
    pallas_call x3, Pallas kernels, fetch(): pl.pallas_call(body, out_shape=tuple(shapes), in_specs=[SMEM] + [HBM] * l...  6.18 us
    all_to_all x1, starting transfers between devices, per_device(): arrived = lax.all_to_all(slots.astype(BF16), 'dp', 0, 0, tiled=True)  5.84 us
    ppermute x3, starting transfers between devices, per_device(): lax.ppermute(mlp_columns, 'tensor', [(3 ^ k, 3)])  5.79 us
  transfers between devices with their start and end apart: 36, of which 16 were waited for; matrix products, arithmetic and copies ran while one was open for 2% of the time, Pallas kernels for 38%

commit v1 on v0

--- a/solution.py
+++ b/solution.py
@@ -171,41 +171,51 @@
     return high, (value - high.astype(F32)).astype(BF16)
 
 
-def dot3(a, b):
-    a_high, a_low = split(a)
-    b_high, b_low = split(b)
-    mm = functools.partial(jnp.dot, preferred_element_type=F32)
-    return mm(a_high, b_high) + (mm(a_high, b_low) + mm(a_low, b_high))
-
-
 def table_dot(table, value):
     high, low = split(value)
     return dot(table[0], high, NN) + (dot(table[1], high, NN) + dot(table[0], low, NN))
 
 
-def newton_schulz(matrix, a_ref, q_ref, p_ref, start, out_rows):
+def symmetric(left, right, product):
+    half = left[0].shape[0] // 2
+    top = product([v[:half] for v in left], right, None)
+    low = product([v[half:] for v in left], right, half)
+    return jnp.concatenate([top, jnp.concatenate([top[:, half:].T, low], 1)], 0)
+
+
+def three_terms(left, right, cut=None):
+    right = right if cut is None else [v[:, cut:] for v in right]
+    return dot(left[0], right[0], NN) + (dot(left[0], right[1], NN) + dot(left[1], right[0], NN))
+
+
+def newton_schulz(matrix, a_ref, p_ref, r_ref, start):
     size = a_ref.shape[0]
     row = lax.broadcasted_iota(jnp.int32, (size, size), 0)
     col = lax.broadcasted_iota(jnp.int32, (size, size), 1)
     unit = (row == col).astype(F32)
-    gram = dot(matrix, matrix, NT)
+    gram = symmetric([matrix], [matrix], lambda a, b, cut: dot(a[0], b[0] if cut is None else b[0][cut:], NT))
     scale = 1.0 / (jnp.sqrt(jnp.sum(gram * unit)) + 1e-07)
     a_ref[...] = gram * (scale * scale)
 
     def advance(first):
         a = a_ref[...]
-        square = dot3(a, a)
-        cube = dot3(a, square)
-        poly = NS_COEF_A * unit + NS_COEF_B * a + NS_COEF_C * square
-        half = NS_COEF_A * a + NS_COEF_B * square + NS_COEF_C * cube
-        a_ref[...] = dot3(poly, half)
-        q_ref[...] = poly if first else dot3(poly, q_ref[...])
+        terms = split(a)
+        poly = NS_COEF_A * unit + NS_COEF_B * a + NS_COEF_C * symmetric(terms, terms, three_terms)
+        poly_terms = split(poly)
+        if first:
+            p_ref[...] = poly
+            r_ref[...] = p_ref[pl.ds(start, r_ref.shape[0]), :]
+        else:
+            r_ref[...] = three_terms(split(r_ref[...]), poly_terms)
+        half = symmetric(terms, poly_terms, three_terms)
+        a_ref[...] = symmetric(poly_terms, split(half), three_terms)
 
     advance(True)
     pl.loop(0, NS_STEPS - 2)(lambda _: advance(False))
-    a = a_ref[...]
-    p_ref[...] = NS_COEF_A * unit + NS_COEF_B * a + NS_COEF_C * dot3(a, a)
-    high, low = split(dot3(p_ref[pl.ds(start, out_rows), :], q_ref[...]))
+    rows, terms = r_ref[...], split(a_ref[...])
+    once = three_terms(split(rows), terms)
+    rows = NS_COEF_A * rows + NS_COEF_B * once + NS_COEF_C * three_terms(split(once), terms)
+    high, low = split(rows)
     return scale * (dot(high, matrix, NN) + dot(low, matrix, NN))
 
 
@@ -270,7 +280,6 @@
         for store in stores:
             store.copy.wait()
 
-    moved = sum(math.prod(a.shape) * jnp.dtype(a.dtype).itemsize for a in (*args, *outs))
     return pl.pallas_call(
         body,
         out_shape=tuple(pltpu.HBM(o.shape, o.dtype) if isinstance(o, Store) else o for o in outs),
@@ -280,26 +289,28 @@
         + [pltpu.VMEM(shape, dtype) for shape, dtype in scratch]
         + ([pltpu.SemaphoreType.DMA((len(late),))] if late else []),
         compiler_params=pltpu.CompilerParams(vmem_limit_bytes=limit * 2**20),
-        cost_estimate=pl.CostEstimate(flops=max(time * SCALE, 10**6), bytes_accessed=moved, transcendentals=0),
+        cost_estimate=pl.CostEstimate(flops=max(time * SCALE, 10**6), bytes_accessed=0, transcendentals=0),
     )(*(a.array if isinstance(a, Late) else a for a in args))
 
 
-def fetch(token, *arrays):
-    arrays = [a if isinstance(a, tuple) else (a,) for a in arrays]
-    shapes = [
-        jax.ShapeDtypeStruct((sum(p.shape[0] for p in a), *a[0].shape[1:]), a[0].dtype) for a in arrays
-    ]
-    flat = [pltpu.with_memory_space_constraint(p, pltpu.HBM) for a in arrays for p in a]
+def fetch(token, time, *arrays):
+    arrays = [a if isinstance(a, list) else [(a, None)] for a in arrays]
+    shapes = []
+    for a in arrays:
+        cuts = [p.shape if index is None else p.shape[1:] for p, index in a]
+        shapes.append(jax.ShapeDtypeStruct((sum(c[0] for c in cuts), *cuts[0][1:]), a[0][0].dtype))
+    flat = [pltpu.with_memory_space_constraint(p, pltpu.HBM) for a in arrays for p, _ in a]
 
     def body(token_ref, *refs):
         outs, semaphores, copies, at = refs[len(flat) : -1], refs[-1], [], 0
         for a, out in zip(arrays, outs):
             row = 0
-            for p in a:
-                target = out if len(a) == 1 else out.at[row : row + p.shape[0]]
-                copies.append(pltpu.make_async_copy(refs[at], target, semaphores.at[at]))
+            for _, index in a:
+                source = refs[at] if index is None else refs[at].at[index]
+                target = out if len(a) == 1 else out.at[row : row + source.shape[0]]
+                copies.append(pltpu.make_async_copy(source, target, semaphores.at[at]))
                 copies[-1].start()
-                row, at = row + p.shape[0], at + 1
+                row, at = row + source.shape[0], at + 1
         for copy in copies:
             copy.wait()
 
@@ -310,7 +321,7 @@
         out_specs=(VMEM,) * len(shapes),
         scratch_shapes=[pltpu.SemaphoreType.DMA((len(flat),))],
         compiler_params=pltpu.CompilerParams(vmem_limit_bytes=2 * 2**20),
-        cost_estimate=pl.CostEstimate(flops=10**10, bytes_accessed=2 * sum(a.size * a.dtype.itemsize for a in flat), transcendentals=0),
+        cost_estimate=pl.CostEstimate(flops=max(time * SCALE, 10**6), bytes_accessed=0, transcendentals=0),
     )(token, *flat)
 
 
@@ -415,27 +426,35 @@
     middle_own.ref[...] = middle[:, block_at(me, part)]
 
 
-def mlp_kernel(info, normed, active, delta_hidden, cot, weights, moment, keep, send, moment_send, near, kept, part_out):
+def mlp_kernel(info, normed, active, delta_hidden, cot, moment, out, moment_send, away):
+    size = normed.shape[1]
+    wanted = (info[2] + away) % 2
+
+    @pl.when(wanted == 0)
+    def _():
+        out[:size, :] = dot(normed[...], delta_hidden[...], TN).astype(out.dtype)
+
+    @pl.when(wanted == 1)
+    def _():
+        out[:size, :] = dot(cot[...], active[...], TN).astype(out.dtype)
+
+    length = jnp.full((16, out.shape[1]), 1, jnp.int32) * info[1]
+    first = lax.broadcasted_iota(jnp.int32, length.shape, 0) == 0
+    out[size:, :] = jnp.where(first, length // 32, length % 32).astype(F32).astype(out.dtype)
+    if away:
+        moment_send[...] = moment.ready()[wanted]
+
+
+def mlp_away_kernel(info, normed, active, delta_hidden, cot, moment, out, moment_send):
+    mlp_kernel(info, normed, active, delta_hidden, cot, moment, out, moment_send, 1)
+
+
+def mlp_here_kernel(info, normed, active, delta_hidden, cot, out):
+    mlp_kernel(info, normed, active, delta_hidden, cot, None, out, None, 0)
+
+
+def mlp_out_kernel(info, active, weights, near, kept, part_out):
     me = info[0]
-    size = normed.shape[1]
-    side = info[2] % 2
-    for which, (a, b) in enumerate(((normed, delta_hidden), (cot, active))):
-        grad = dot(a[...], b[...], TN)
-
-        @pl.when(side == which)
-        def _(grad=grad):
-            keep[:size, :] = grad
-
-        @pl.when(side != which)
-        def _(grad=grad):
-            send[:size, :] = grad.astype(BF16)
-
-    length = jnp.full((16, grad.shape[1]), 1, jnp.int32) * info[1]
-    first = lax.broadcasted_iota(jnp.int32, length.shape, 0) == 0
-    length = jnp.where(first, length // 32, length % 32).astype(F32)
-    keep[size:, :] = length
-    send[size:, :] = length.astype(BF16)
-    moment_send[...] = moment.ready()[1 - side]
     step = active.shape[0] // 4
     part = near.ref.shape[2]
     for c in range(4):
@@ -473,7 +492,7 @@
     for piece in pieces[1:]:
         total = total + piece[...].astype(F32)
     tokens = 32.0 * total[2 * rows : 2 * rows + 1, :] + total[2 * rows + 1 : 2 * rows + 2, :]
-    count[...] = jnp.broadcast_to(tokens[:, : count.shape[1]], count.shape)
+    count.ref[...] = jnp.broadcast_to(tokens[:, : count.ref.shape[1]], count.ref.shape)
     old = moment[side]
     for which in range(2):
         new = total[which * rows : (which + 1) * rows, :] / tokens
@@ -503,8 +522,18 @@
     far[...] = (kept[1] + came[1].astype(F32)).astype(BF16)
 
 
-def join_late_kernel(info, kept, came, mine, far):
-    join_kernel(info, kept.ready(), came, mine, far)
+def join_late_kernel(info, one_kept, one_came, out_kept, out_came, one_mine, tail, out_mine, far):
+    one_kept, out_kept = one_kept.ready(), out_kept.ready()
+    size = out_mine.shape[0]
+    one_mine[...] = one_kept[0, :size, :] + one_came[0, :size, :].astype(F32)
+    far[:size, :] = (one_kept[1, :size, :] + one_came[1, :size, :].astype(F32)).astype(BF16)
+    below = one_kept[0, size:, :] + one_came[0, size:, :].astype(F32)
+    high, low = split(below[16:24, :] + below[24:, :])
+    below = jnp.concatenate([below[:16, :], high.astype(F32), low.astype(F32)], 0)
+    tail[...] = below
+    far[size : size + 32, :] = below.astype(BF16)
+    out_mine[...] = out_kept[0] + out_came[0].astype(F32)
+    far[size + 32 :, :] = (out_kept[1] + out_came[1].astype(F32)).astype(BF16)
 
 
 def norm_back_kernel(info, mine, came, cot, n_mine, inv_mine, gains, delta, grad_gain):
@@ -518,8 +547,8 @@
 
 
 def mixer_back_kernel(info, d0, d1, d2, d3, weights, act, slope, conv, branch, normed, spec_v, spec_k, forward, inverse,
-                      kernel_inverse, gains,
-                      slots, near, kept, sums, delta_own,
+                      kernel_inverse, gains, gain_two,
+                      slots, near, kept, delta_own,
                       delta, wide, spec_d, spec_y, spec_u, back, share):
     me = info[0]
     step, width = d0.shape
@@ -563,154 +592,168 @@
         slots.ref[i, 3 * rows :, :] = grad_kernel[i * taps : (i + 1) * taps, :].astype(slots.ref.dtype)
     slots.send()
     ones = jnp.ones((8, width), BF16)
+    gain_one = jnp.zeros((1, width), F32)
+    sums = [[], []]
     gain = jnp.broadcast_to(gains[0:1, :], (8, width)).astype(BF16)
     for c in range(4):
         r = slice(c * step, (c + 1) * step)
         out = dot(back[r, :part], weights[0], NT) + dot(back[r, part:], weights[1], NT)
         share[r, :] = out
         first = dot(gain, out.astype(BF16), NT)
-        second = dot(ones, (out * normed[r, :].astype(F32)).astype(BF16), NT)
+        both = out * normed[r, :].astype(F32)
+        gain_one = gain_one + jnp.sum(both, 0, keepdims=True)
+        second = dot(ones, both.astype(BF16), NT)
         for h in range(step // part):
-            at = c * (step // part) + h
-            sums[at : at + 1, :] = first[0:1, h * part : (h + 1) * part]
-            sums[8 + at : 9 + at, :] = second[0:1, h * part : (h + 1) * part]
+            sums[0].append(first[0:1, h * part : (h + 1) * part])
+            sums[1].append(second[0:1, h * part : (h + 1) * part])
+    gain_one = gain_one / gains[0:1, :]
+    gain = [g[:, q * part : (q + 1) * part] for g in (gain_one, gain_two[...]) for q in range(4)]
+    gain_high, gain_low = split(jnp.concatenate(gain, 0))
+    tail = jnp.concatenate([*sums[0], *sums[1], gain_high.astype(F32), gain_low.astype(F32)], 0)
     for k in range(4):
         block = share[:, block_at(me ^ k, part)]
         if k % 2:
-            near.ref[k // 2] = block.astype(BF16)
+            near.ref[k // 2, : share.shape[0], :] = block.astype(BF16)
+            near.ref[k // 2, share.shape[0] :, :] = tail.astype(BF16)
         else:
-            kept.ref[k // 2] = block
-
-
-def moment_kernel(info, arrived, moment, count, sums, moment_new, kernel_total, o0, o1, o2, o3, new):
+            kept.ref[k // 2, : share.shape[0], :] = block
+            kept.ref[k // 2, share.shape[0] :, :] = tail
+
+
+def keeper(t):
+    return 4 * (1 - t // 2) + t
+
+
+def moment_kernel(info, arrived, moment, count, tail, came, moment_new, slots, came_kept):
     me = info[0]
     dp = arrived.shape[0]
-    _, rows, _ = moment.ref.shape
+    _, rows, part = moment.ref.shape
+    taps = arrived.shape[1] - 3 * rows
     total = arrived[0].astype(F32)
     for i in range(1, dp):
         total = total + arrived[i].astype(F32)
-    moment = moment.ready()
+    size = (came.shape[0] - 32) // 2
+    below = tail[16:, :] + came[size + 16 : size + 32, :].astype(F32)
+    came_kept.ref[...] = came[...]
+    high, low = split(below[:8, :] + below[8:, :])
+    rest = jnp.concatenate([total[3 * rows :, :], high.astype(F32), low.astype(F32)], 0).astype(slots.ref.dtype)
+    moment, count = moment.ready(), count.ready()
     for which in range(3):
         value = MOMENT_DECAY * moment[which] + total[which * rows : (which + 1) * rows, :] / count[0:1, :]
         moment_new.ref[which] = value
-        new[which] = value.astype(new.dtype)
-    kernel_total[...] = total[3 * rows :, :]
-    for k, out in enumerate((o0, o1, o2, o3)):
-        out[:rows, :] = new[jnp.minimum(me ^ k, 2)]
-        out[rows:, :] = sums[...].astype(out.dtype)
-
-
-def payload_kernel(info, mine, came, n_own, g0, g1, g2, g3, kernel_total, gain_two, payload, extra):
-    me = info[0]
+        for z in range(dp // 2):
+            slots.ref[8 * z + keeper(which), :rows, :] = value.astype(slots.ref.dtype)
+    for t in range(4):
+        for z in range(dp // 2):
+            slots.ref[8 * z + (keeper(t) ^ 4), : taps + 16, :] = rest
+    slots.send()
+
+
+def output_kernel(info, mine, came, out_mine, delta_own, n_own, inv, middle_own, gains, tail, input_grad, block_out):
     part = mine.shape[1]
-    rows = g0.shape[0] - 16
-    total = mine[...] + came[...].astype(F32)
-    for k, piece in enumerate((g0, g1, g2, g3)):
-        payload[0, :rows, block_at(me ^ k, part)] = piece[:rows, :]
-    extra[...] = jnp.zeros_like(extra)
-    for g in range(min(3, kernel_total.shape[0] // 8)):
-        extra[:, g * part : (g + 1) * part] = kernel_total[8 * g : 8 * g + 8, :]
-    extra[0:1, 3 * part :] = jnp.sum(total * n_own.ready()[...], 0, keepdims=True)
-    for q in range(4):
-        extra[1 + q : 2 + q, 3 * part :] = gain_two[:, q * part : (q + 1) * part]
-    high, low = split(extra[...])
-    payload[0, rows:, :] = jnp.concatenate([high.astype(F32), low.astype(F32)], 0).astype(payload.dtype)
-    for i in range(1, payload.shape[0]):
-        payload[i] = payload[0]
-
-
-def output_kernel(info, mine, came, out_mine, out_came, delta_own, n_own, inv, middle_own, gains, g0, g1, g2, g3, input_grad, block_out):
-    part = mine.shape[1]
-    width = 4 * part
-    rows = g0.shape[0] - 16
-    gain = gains[0:1, block_at(info[0], part)]
-    sums = 0.0
-    for piece in (g0, g1, g2, g3):
-        sums = sums + piece[rows:, :].astype(F32)
-    sums = sums / width
+    came = came.ready()
+    gain = gains.ready()[0:1, block_at(info[0], part)]
+    size = mine.shape[0]
+    sums = (tail[:16, :] + came[size : size + 16, :].astype(F32)) / (4 * part)
     middle_own = middle_own.ready()
     n_own, inv, delta_own = n_own.ready(), inv.ready(), delta_own.ready()
     for h in range(mine.shape[0] // part):
         r = slice(h * part, (h + 1) * part)
-        block_out.ref[r, :] = (middle_own[r, :] + (out_mine[r, :] + out_came[r, :].astype(F32))).astype(BF16)
+        block_out.ref[r, :] = (middle_own[r, :] + (out_mine[r, :] + came[size + 32 + h * part : size + 32 + (h + 1) * part, :].astype(F32))).astype(BF16)
         column = lambda at: jnp.broadcast_to(sums[at : at + 1, :], (part, part)).T
         total = mine[r, :] + came[r, :].astype(F32)
         back = total * gain - column(h) - n_own[r, :] * column(8 + h)
         input_grad.ref[r, :] = delta_own[r, :].astype(F32) + inv[r, :] * back
 
 
-def step_kernel(info, pieces, m0, m1, m2, m3, out, kernel_all, matrix, large, a, q, p, gains, small):
+def step_kernel(info, got, m0, m1, m2, m3, out, extra, matrix, large, a, p, r, result):
     me, row = info[0], info[2]
-    dp = gains.shape[0]
-    rows = small.shape[0]
-    part = kernel_all.shape[1]
-    hidden = m0.shape[1]
-    for i in range(dp):
-        matrix[i * rows : (i + 1) * rows, :] = pieces[i, :rows, :]
-        both = pieces[i, rows:, :].astype(F32)
-        both = both[:8, :] + both[8:, :]
-        for g in range(3):
-            kernel_all[i * 24 + 8 * g : i * 24 + 8 * g + 8, :] = both[:, g * part : (g + 1) * part]
-        gains[i] = both[:, 3 * part :]
-    gain = gains[0]
-    for i in range(1, dp):
-        gain = gain + gains[i]
-    high, low = split(gain)
-    gain = jnp.concatenate([high.astype(F32), low.astype(F32)], 0).astype(out.dtype)
-    for k in range(8):
-        out[k, rows:, :part] = gain
-        out[k, rows:, part:] = jnp.zeros((16, out.shape[2] - part), out.dtype)
-
-    @pl.when(me < 3)
+    side = row % 2
+    size, width = matrix.shape
+    rows = r.shape[0] // 2
+    part = width // 4
+    hidden = m0.ref.shape[1]
+    start = pl.multiple_of((row // 2) * (2 * rows), 2 * rows)
+    for i in range(extra.shape[0]):
+        extra[i] = got[4 * i + me, : extra.shape[1], :].astype(BF16)
+
+    @pl.when(jnp.logical_and(side == 1 - me // 2, me < 3))
     def _():
-        small[...] = newton_schulz(matrix[...], a, q, p, pl.multiple_of(row * rows, rows), rows)
-        for k in range(8):
-
-            @pl.when(row % 2 == k // 4)
-            def _(k=k):
-                out[k, :rows, :part] = small[:, (k % 4) * part : (k % 4 + 1) * part].astype(out.dtype)
-
-    @pl.when(me == 3)
+        for i in range(size // rows):
+            for t in range(4):
+                matrix[i * rows : (i + 1) * rows, t * part : (t + 1) * part] = got[4 * i + t, :rows, :].astype(BF16)
+        result[...] = newton_schulz(matrix[...], a, p, r, start)
+        for q in range(8):
+            lanes = slice((q % 4) * part, (q % 4 + 1) * part)
+            out[q, :, :part] = result[(q // 4) * rows : (q // 4 + 1) * rows, lanes].astype(out.dtype)
+
+    @pl.when(me == side + 1)
     def _():
         for k, piece in enumerate((m0, m1, m2, m3)):
-            large[:, block_at(3 ^ k, hidden)] = piece[...]
-        start = pl.multiple_of((row // 2) * (2 * rows), 2 * rows)
-        result = newton_schulz(large[...], a, q, p, start, 2 * rows)
-        for k in range(8):
-            lanes = slice((k % 4) * hidden, (k % 4 + 1) * hidden)
-            out[k, :rows, :] = result[(k // 4) * rows : (k // 4 + 1) * rows, lanes].astype(out.dtype)
-
-
-def final_kernel(info, got, moment_mine, moment_back, mixer_weights, mlp_weights, norm_gains, gain_moment, count,
-                 mixer_new, mlp_new, mlp_moment_new, gain_moment_new, gains_new, gains):
-    row = info[2]
+            large[:, block_at(me ^ k, hidden)] = piece.ready()[...]
+        steps = newton_schulz(large[...], a, p, r, start)
+        for q in range(8):
+            lanes = slice((q % 4) * hidden, (q % 4 + 1) * hidden)
+            out[q] = steps[(q // 4) * rows : (q // 4 + 1) * rows, lanes].astype(out.dtype)
+
+    @pl.when(me != side + 1)
+    def _():
+        for piece in (m0, m1, m2, m3):
+            piece.ready()
+
+
+def aside_kernel(info, moment_mine, moment_back, moment_new):
+    side = info[2] % 2
+    moment_new.ref[side] = moment_mine.ready()[...]
+    moment_new.ref[1 - side] = moment_back.ready()[...]
+
+
+def final_kernel(info, got, extra_mine, extra_came, mixer_weights, mlp_weights, norm_gains, gain_moment, taps, taps_moment, count,
+                 mixer_new, mlp_new, gain_moment_new, gains_new, taps_moment_new, taps_new, extra, packed):
+    me, row = info[0], info[2]
+    side = row % 2
+    count = count.ready()
     _, rows, part = mixer_new.ref.shape
     hidden = mlp_new.ref.shape[2]
     width = 4 * part
-    side = row % 2
-    for t in range(4):
-        both = got[4 * side + t, rows:, :part].astype(F32)
-        gains[t] = both[:8, :] + both[8:, :]
     for t in range(3):
         old = mixer_weights[t, block_at(row, rows), :].astype(F32)
-        mixer_new.ref[t] = old - MATRIX_RATE * got[4 * side + t, :rows, :part].astype(F32)
+        mixer_new.ref[t] = old - MATRIX_RATE * got[keeper(t), :rows, :part].astype(F32)
     mixer_new.send()
-    mlp_moment_new.ref[side] = moment_mine.ready()[...]
-    mlp_moment_new.ref[1 - side] = moment_back.ready()[...]
-    mlp_moment_new.send()
     rate = MATRIX_RATE * math.sqrt(4 * hidden / width)
     for which in range(2):
         old = mlp_weights[which, block_at(row, rows), :].astype(F32)
-        mlp_new.ref[which] = old - rate * got[4 * which + 3, :rows, :].astype(F32)
-
+        mlp_new.ref[which] = old - rate * got[4 * which + 1 + which, :rows, :].astype(F32)
     mlp_new.send()
-    two = gains[0] + gains[1] + gains[2] + gains[3]
-    for t in range(4):
-        lanes = slice(t * part, (t + 1) * part)
-        totals = (gains[t][0:1, :], two[1 + t : 2 + t, :])
-        for which in range(2):
+    here = side != 1 - me // 2
+
+    @pl.when(here)
+    def _():
+        extra[...] = extra_mine[...].astype(F32)
+
+    @pl.when(jnp.logical_not(here))
+    def _():
+        extra[...] = extra_came[...].astype(F32)
+
+    dp, height, _ = extra.shape
+    total = taps.shape[0]
+    share = -(-total // dp)
+    gain = 0.0
+    for i in range(dp):
+        size = min(share, total - i * share)
+        if size > 0:
+            packed[i * share : i * share + size, :] = extra[i, :size, :]
+        gain = gain + (extra[i, height - 16 : height - 8, :] + extra[i, height - 8 :, :])
+    new = MOMENT_DECAY * taps_moment[...] + packed[...] / count[0:1, :]
+    taps_moment_new[...] = new
+    scale = jnp.sqrt(jnp.mean(new * new, 0, keepdims=True)) + 1e-08
+    taps_new[...] = taps[...] - KERNEL_RATE * new / scale
+    for which in range(2):
+        for t in range(4):
+            lanes = slice(t * part, (t + 1) * part)
             gain_moment_new[which : which + 1, lanes] = (
-                MOMENT_DECAY * gain_moment[which : which + 1, lanes] + totals[which] / count[0:1, :]
+                MOMENT_DECAY * gain_moment[which : which + 1, lanes]
+                + gain[4 * which + t : 4 * which + t + 1, :] / count[0:1, :]
             )
     new = gain_moment_new[...]
     scale = jnp.sqrt(jnp.mean(new * new, 1, keepdims=True)) + 1e-08
@@ -746,15 +789,15 @@
     forward, inverse, kernel_forward, kernel_inverse = conv_tables(bucket, levels, taps, dp, slot)
     info = jnp.stack([me, lengths[0], row]).astype(jnp.int32)
 
+    x_own, in_weights, in_gains, forward_one, inverse_one, late = fetch(
+        info, 1, tokens[0], mixer_weights, norm_gains, forward, inverse, [(cotangent, 0), (mixer_weights, 2)]
+    )
     (spec_k,) = call(
         spectrum_kernel,
         [((8 * half, part), F32)],
         [],
-        (info, Late(kernel_forward), Late(conv_kernel.reshape(levels * taps, part))),
+        (after(info, x_own), Late(kernel_forward), Late(conv_kernel.reshape(levels * taps, part))),
         2, 10,
-    )
-    x_own, in_weights, in_gains, forward_one, inverse_one, late = fetch(
-        info, tokens[0], mixer_weights, norm_gains, forward, inverse, (cotangent[0], mixer_weights[2])
     )
     x_pieces = gather_tensor(tokens[0], spec_k, x_own)
 
@@ -769,7 +812,7 @@
          ((bucket, part), BF16), ((2, width), F32)],
         [wide_like, spec_like],
         (info, x_own, *x_pieces[1:], in_weights, in_gains, forward_one, inverse_one, spec_k),
-        0, 24,
+        0, 12,
     )
     late = gather_tensor(late, branch)
     cot, out_weights, delta_active, mlp_kept = call(
@@ -777,7 +820,7 @@
         [whole_like, ((width, width), BF16), ((bucket, hidden), F32), (mlp_weights.shape, BF16)],
         [],
         (after(info, branch), *late, Late(mlp_weights)),
-        3, 8,
+        3, 5,
     )
     branch_pieces = gather_tensor(branch, delta_active)
     near, kept, normed_two, active, delta_hidden, n_mine, inv_mine, middle_own = call(
@@ -786,18 +829,21 @@
          ((bucket, hidden), BF16), wide_like, ((half, 1), F32), Store(*act_like)],
         [whole_like, ((bucket, width), F32)],
         (info, *branch_pieces, out_weights, x, gains, mlp_kept, delta_active),
-        6, 24,
+        6, 12,
     )
     split_blocks = lambda v: v.reshape(2, -1, v.shape[-1])
     came = swap(split_blocks(near), "tensor", 1)
     mine, far = call(join_kernel, [wide_like, quarter_like], [], (info, split_blocks(kept), came), 1, 4)
-    mlp_keep, mlp_send, moment_send, out_near, out_kept = call(
-        mlp_kernel,
-        [((width + 16, hidden), F32), ((width + 16, hidden), BF16), ((rows, hidden), F32), Store((2, bucket, part), BF16),
-         Store((2, bucket, part), F32)],
-        [((bucket, width), F32)],
-        (after(info, far), normed_two, active, delta_hidden, cot, mlp_kept, Late(mlp_moment)),
-        4, 20,
+    mlp_inputs = (normed_two, active, delta_hidden, cot)
+    mlp_send, moment_send = call(
+        mlp_away_kernel,
+        [((width + 16, hidden), BF16), ((rows, hidden), F32)],
+        [],
+        (after(info, far), *mlp_inputs, Late(mlp_moment)),
+        2, 5,
+    )
+    (mlp_keep,) = call(
+        mlp_here_kernel, [((width + 16, hidden), F32)], [], (after(info, mlp_send), *mlp_inputs), 1000, 8
     )
     mlp_came = swap(mlp_send, "dp", 1)
     moment_came = swap(moment_send, "dp", 1)
@@ -806,51 +852,52 @@
         norm_back_kernel,
         [quarter_like, ((1, width), F32)],
         [],
-        (after(info, out_near), mine, came, cot, n_mine, inv_mine, gains),
-        1000, 6,
-    )
-    (kernel_inverse_one,) = fetch(after(info, delta_mid), kernel_inverse)
-    delta_pieces = gather_tensor(delta_mid, kernel_inverse_one)
-
-    slots, one_near, one_kept, sums, delta_own = call(
+        (after(info, mlp_keep), mine, came, cot, n_mine, inv_mine, gains),
+        1000, 4,
+    )
+    (kernel_inverse_one,) = fetch(after(info, delta_mid), 0, kernel_inverse)
+    out_near, out_kept = call(
+        mlp_out_kernel,
+        [Store((2, bucket, part), BF16), Store((2, bucket, part), F32)],
+        [((bucket, width), F32)],
+        (after(info, kernel_inverse_one), active, mlp_kept),
+        1, 8,
+    )
+    delta_pieces = gather_tensor(delta_mid, kernel_inverse_one, out_near)
+
+    pairs = dp // 2
+    parities = [[i for i in range(dp) if i % 2 == y] for y in range(2)]
+    groups = [[8 * z + q for q in range(8)] for z in range(pairs)]
+    block = (2 * rows + 16, hidden)
+    if dp == 8:
+        blocks = call(mlp_rows_kernel, [(block, BF16)] * pairs, [], (info, mlp_keep, mlp_came), 0, 6)
+        blocks = [blocks[0]] + [swap(blocks[k], "dp", 2 * k) for k in range(1, pairs)]
+    else:
+        (blocks,) = call(mlp_rows_kernel, [((pairs, *block), BF16)], [], (info, mlp_keep, mlp_came), 0, 6)
+        blocks = [lax.all_to_all(blocks, "dp", 0, 0, tiled=True, axis_index_groups=parities)]
+
+    slots, one_near, one_kept, delta_own = call(
         mixer_back_kernel,
-        [Store((dp, 3 * rows + slot, part), piece_type), Store((2, bucket, part), BF16), Store((2, bucket, part), F32),
-         ((16, part), F32), Store((bucket, part), BF16)],
+        [Store((dp, 3 * rows + slot, part), piece_type), Store((2, bucket + 32, part), BF16),
+         Store((2, bucket + 32, part), F32), Store((bucket, part), BF16)],
         [whole_like, wide_like, spec_like, spec_like, ((8 * half, part), F32), ((bucket, 2 * part), BF16),
          ((bucket, width), F32)],
-        (info, *delta_pieces, in_weights, gate_act, gate_slope, conv, branch, normed, spec_v, spec_k, forward_one, inverse_one,
-         kernel_inverse_one, gains),
-        0, 32,
+        (after(info, blocks[0]), *delta_pieces, in_weights, gate_act, gate_slope, conv, branch, normed, spec_v, spec_k, forward_one, inverse_one,
+         kernel_inverse_one, gains, grad_gain_two),
+        1000, 18,
     )
     arrived = lax.all_to_all(slots.astype(BF16), "dp", 0, 0, tiled=True)
-    one_mine, far = call(
+    one_mine, one_tail, out_mine, far = call(
         join_late_kernel,
-        [act_like, ((bucket, part), BF16)],
+        [act_like, ((32, part), F32), act_like, ((2 * bucket + 32, part), BF16)],
         [],
-        (info, Late(one_kept), swap(one_near, "tensor", 1)),
-        0, 4,
-    )
-    one_came = swap(far, "tensor", 2)
-    out_mine, out_far = call(
-        join_late_kernel,
-        [act_like, ((bucket, part), BF16)],
-        [],
-        (info, Late(out_kept), swap(after(out_near, far), "tensor", 1)),
-        1000, 4,
-    )
-    out_came = swap(out_far, "tensor", 2)
-    pairs = dp // 2
-    block = (2 * rows + 16, hidden)
-    if dp == 8:
-        blocks = call(mlp_rows_kernel, [(block, BF16)] * pairs, [], (info, mlp_keep, mlp_came), 1, 6)
-        blocks = [blocks[0]] + [swap(blocks[k], "dp", 2 * k) for k in range(1, pairs)]
-    else:
-        (blocks,) = call(mlp_rows_kernel, [((pairs, *block), BF16)], [], (info, mlp_keep, mlp_came), 1, 6)
-        parities = [[i for i in range(dp) if i % 2 == y] for y in range(2)]
-        blocks = [lax.all_to_all(blocks, "dp", 0, 0, tiled=True, axis_index_groups=parities)]
+        (info, Late(one_kept), swap(one_near, "tensor", 1), Late(out_kept), swap(out_near, "tensor", 1)),
+        0, 6,
+    )
+    far_came = swap(far, "tensor", 2)
     pair, moment_mine, moment_other, count = call(
         mlp_moment_kernel,
-        [((2 * rows, hidden), BF16), Store((rows, hidden), F32), Store((rows, hidden), F32), ((8, part), F32)],
+        [((2 * rows, hidden), BF16), Store((rows, hidden), F32), Store((rows, hidden), F32), Store((8, part), F32)],
         [],
         (info, mlp_moment, moment_came, *blocks),
         1, 8,
@@ -859,61 +906,63 @@
         pair_pieces = [pair] + [swap(pair, "dp", 2 * k) for k in range(1, pairs)]
     else:
         pair_pieces = [lax.all_gather(pair, "dp", axis=0, tiled=True, axis_index_groups=parities)]
-    mixer_moment_new, kernel_total, *sends = call(
+    height = -(-max(rows, slot + 16) // 16) * 16
+    mixer_moment_new, slots, far_kept = call(
         moment_kernel,
-        [Store((3, rows, part), F32), ((slot, part), F32)] + [((rows + 16, part), piece_type)] * 4,
-        [((3, rows, part), piece_type)],
-        (after(info, out_far), arrived, Late(mixer_moment), count, sums),
-        0, 6,
-    )
-    got = [sends[0]] + [swap(sends[k].astype(BF16), "tensor", k) for k in (1, 2, 3)]
-    (payload,) = call(
-        payload_kernel,
-        [((dp, rows + 16, width), piece_type)],
-        [((8, width), F32)],
-        (info, one_mine, one_came, Late(n_own), *(g.astype(piece_type) for g in got), kernel_total, grad_gain_two),
-        0, 4,
-    )
-    everything = lax.all_to_all(payload.astype(BF16), "dp", 0, 0, tiled=True)
+        [Store((3, rows, part), F32), Store((4 * dp, height, part), piece_type), Store((2 * bucket + 32, part), BF16)],
+        [],
+        (info, arrived, Late(mixer_moment), Late(count), one_tail, far_came),
+        1000, 8,
+    )
+    got = lax.all_to_all(slots.astype(BF16), ("dp", "tensor"), 0, 0, tiled=True)
     (mlp_columns,) = call(
-        columns_kernel, [((width, hidden), BF16)], [], (after(info, payload), *pair_pieces), 0, 4
-    )
-    mlp_pieces = [mlp_columns] + [lax.ppermute(mlp_columns, "tensor", [(3 ^ k, 3)]) for k in (1, 2, 3)]
+        columns_kernel, [((width, hidden), BF16)], [], (after(info, slots), *pair_pieces), 1000, 4
+    )
+    mlp_pieces = [mlp_columns] + [
+        lax.ppermute(
+            mlp_columns,
+            ("dp", "tensor"),
+            [(8 * z + 4 * y + ((1 + y) ^ k), 8 * z + 4 * y + 1 + y) for z in range(pairs) for y in range(2)],
+        )
+        for k in (1, 2, 3)
+    ]
+    moment_back = swap(moment_other, "dp", 1)
     input_grad, block_out = call(
         output_kernel,
         [Store(*act_like), Store((bucket, part), BF16)],
         [],
-        (after(info, payload), one_mine, one_came, out_mine, out_came, Late(delta_own), Late(n_own), Late(inv_one), Late(middle_own), gains,
-         *(g.astype(piece_type) for g in got)),
-        1000, 8,
+        (after(info, slots), one_mine, Late(far_kept), out_mine, Late(delta_own), Late(n_own), Late(inv_one),
+         Late(middle_own), Late(norm_gains), one_tail),
+        0, 8,
+    )
+    (mlp_moment_new,) = call(
+        aside_kernel, [Store((2, rows, hidden), F32)], [], (after(info, slots), Late(moment_mine), Late(moment_back)), 1, 4
     )
     square = ((width, width), F32)
-    sends, kernel_all = call(
+    sends, extra = call(
         step_kernel,
-        [((8, rows + 16, hidden), piece_type), ((dp * 24, part), F32)],
-        [((width, width), piece_type), ((width, 4 * hidden), BF16), square, square, square, ((dp, 8, part), F32),
-         ((rows, width), F32)],
-        (after(info, block_out), everything.astype(piece_type), *mlp_pieces),
+        [((8, rows, hidden), piece_type), ((dp, slot + 16, part), BF16)],
+        [((width, width), BF16), ((width, 4 * hidden), BF16), square, square, ((2 * rows, width), F32),
+         ((2 * rows, width), F32)],
+        (after(info, block_out, mlp_moment_new), got, *(Late(v) for v in mlp_pieces)),
         18, 24,
     )
-    groups = [[8 * z + q for q in range(8)] for z in range(dp // 2)]
     got = lax.all_to_all(sends.astype(BF16), ("dp", "tensor"), 0, 0, tiled=True, axis_index_groups=groups)
-    moment_back = swap(after(moment_other, payload), "dp", 1)
-    old = fetch(after(info, kernel_all), mixer_weights, mlp_weights, norm_gains, gain_moment)
-    mixer_new, mlp_new, mlp_moment_new, gain_moment_new, gains_new = call(
+    extra_came = swap(extra, "dp", 1)
+    flat = (levels * taps, part)
+    old = fetch(
+        after(info, extra), 0, mixer_weights, mlp_weights, norm_gains, gain_moment, conv_kernel.reshape(flat),
+        kernel_moment.reshape(flat),
+    )
+    mixer_new, mlp_new, gain_moment_new, gains_new, kernel_moment_new, kernel_new = call(
         final_kernel,
-        [Store((3, rows, part), F32), Store((2, rows, hidden), F32), Store((2, rows, hidden), F32), ((2, width), F32),
-         ((2, width), F32)],
-        [((4, 8, part), F32)],
-        (info, got.astype(piece_type), Late(moment_mine), Late(moment_back), *old, count),
-        3, 10,
-    )
-    grad_kernel = kernel_all.reshape(dp, 24, part)[:, :share].reshape(-1, part)[: levels * taps]
-    kernel_moment_new = MOMENT_DECAY * kernel_moment + grad_kernel.reshape(levels, taps, part) / count[0]
-    kernel_scale = (
-        jnp.sqrt(jnp.mean(kernel_moment_new * kernel_moment_new, axis=(0, 1), keepdims=True)) + 1e-08
-    )
-    kernel_new = conv_kernel - KERNEL_RATE * kernel_moment_new / kernel_scale
+        [Store((3, rows, part), F32), Store((2, rows, hidden), F32), ((2, width), F32), ((2, width), F32), (flat, F32),
+         (flat, F32)],
+        [((dp, slot + 16, part), F32), (flat, F32)],
+        (info, got.astype(piece_type), extra, extra_came, *old, Late(count)),
+        0, 8,
+    )
+    kernel_moment_new, kernel_new = (v.reshape(conv_kernel.shape) for v in (kernel_moment_new, kernel_new))
     return (
         block_out[None],
         input_grad[None],

time: 174 us -> 162 us (0.931)
  starting transfers between devices: 43.9 us -> 71.2 us
  waiting for transfers between devices: 48.2 us -> 27.8 us
  Pallas kernels: 76.1 us -> 59.9 us
  local copies, waits for them, and re-layouts: 2.17 us -> 0.08 us
    all_to_all x1, starting transfers between devices: 4.06 us -> 23 us  [per_device(): lax.all_to_all(sends.astype(BF16), ('dp', 'tensor'), 0, 0, tiled=True, ax...]
    pallas_call x18 -> x19, Pallas kernels: 70 us -> 53.7 us  [call(): pl.pallas_call(body, out_shape=tuple((pltpu.HBM(o.shape, o.dtype) if isin...]
    ppermute x30 -> x27, starting transfers between devices: 23.5 us -> 33.8 us  [swap(): return lax.ppermute(value, axis, [(i, i ^ k) for i in range(size)])]
    all_to_all x1, waiting for transfers between devices: 8.41 us -> 0.01 us  [per_device(): lax.all_to_all(sends.astype(BF16), ('dp', 'tensor'), 0, 0, tiled=True, ax...]
    all_to_all x1, waiting for transfers between devices: 7.82 us -> 1.27 us  [per_device(): arrived = lax.all_to_all(slots.astype(BF16), 'dp', 0, 0, tiled=True)]
    ppermute x30 -> x27, waiting for transfers between devices: 27.1 us -> 22.9 us  [swap(): return lax.ppermute(value, axis, [(i, i ^ k) for i in range(size)])]
    ppermute x3, waiting for transfers between devices: 2.63 us -> 0.01 us  [per_device(): lax.ppermute(mlp_columns, ('dp', 'tensor'), [(8 * z + 4 * y + (1 + y ^ k)...]
  transfers between devices with their start and end apart: 36 -> 33, of which waited for: 16 -> 13; matrix products, arithmetic and copies ran while one was open for 2% -> 0% of each run, Pallas kernels for 38% -> 29%
where the time goes in v1:
time: 162 us; the launch traced here: 161 us
  starting transfers between devices  71.2 us (44%)
  Pallas kernels  59.9 us (37%)
  waiting for transfers between devices  27.8 us (17%)
  between operations  1.96 us (1%)
    pallas_call x19, Pallas kernels, call(): pl.pallas_call(body, out_shape=tuple((pltpu.HBM(o.shape, o.dtype) if isin...  53.7 us
    ppermute x27, starting transfers between devices, swap(): return lax.ppermute(value, axis, [(i, i ^ k) for i in range(size)])  33.8 us
    all_to_all x1, starting transfers between devices, per_device(): lax.all_to_all(sends.astype(BF16), ('dp', 'tensor'), 0, 0, tiled=True, ax...  23 us
    ppermute x27, waiting for transfers between devices, swap(): return lax.ppermute(value, axis, [(i, i ^ k) for i in range(size)])  22.9 us
    pallas_call x3, Pallas kernels, fetch(): pl.pallas_call(body, out_shape=tuple(shapes), in_specs=[SMEM] + [HBM] * l...  6.22 us
    all_to_all x1, starting transfers between devices, per_device(): arrived = lax.all_to_all(slots.astype(BF16), 'dp', 0, 0, tiled=True)  4.86 us
    all_to_all x1, starting transfers between devices, per_device(): got = lax.all_to_all(slots.astype(BF16), ('dp', 'tensor'), 0, 0, tiled=True)  4.81 us
    ppermute x3, starting transfers between devices, per_device(): lax.ppermute(mlp_columns, ('dp', 'tensor'), [(8 * z + 4 * y + (1 + y ^ k)...  4.7 us
  transfers between devices with their start and end apart: 33, of which 13 were waited for; matrix products, arithmetic and copies ran while one was open for 0% of the time, Pallas kernels for 29%

profile of v1, /device:TPU:0, one launch (start us, length us, event | category | flops | bytes accessed | tf_op | source)
XLA Modules:
  0.0 161.0 jit_solution(9163754731490908023)
XLA Ops:
  0.6 3.0 %collective-permute-start.1 = (bf16[1024,128]{1,0:T(8,128)(2,1)}, bf16[1024,128]{1,0:T(8,128)(2,1)S(1)}, u32[]{:S(2)}, u32[]{:S(2)}) collective-permute-start(bf16[1024,128]{1,0:T(8,128)(2,1)} %bitcast.17), channel_id=1, source_target_pairs={{0,2},{1,3},{2,0},{3,1},{4,6},{5,7},{6,4},{7,5},{8,10},{9,11},{10,... | collective-permute-start | bytes 786440 | tf_op jit(solution)/shard_map/ppermute | solution.py:133
  4.3 0.1 pad_add_fusion.token_ref.refs_0_
  4.4 2.1 %shard_map.222 = (bf16[1024,128]{1,0:T(8,128)(2,1)S(1)}, bf16[3,512,128]{2,1,0:T(8,128)(2,1)S(1)}, f32[2,512]{1,0:T(2,128)S(1)}, bf16[2,512,256]{2,1,0:T(8,128)(...) custom-call(s32[3]{0:T(128)S(1)} %pad_add_fusion.token_ref.refs_0_, ...), custom_call_target="tpu_custom_call" | custom-call | flops 10000000000 | tf_op jit(solution)/shard_map/pallas_call | solution.py:317
  6.5 0.0 copy-start.2
  6.5 0.2 collective-permute-start.6
  6.7 3.1 %shard_map.223.refs_9_.refs_12_ = f32[2048,128]{1,0:T(8,128)S(1)} custom-call(s32[3]{0:T(128)S(1)} %pad_add_fusion.token_ref.refs_0_, bf16[2,2048,160]{2,1,0:T(8,128)(2,1)} %constant.19.clone.refs_1_, f32[160,128]{1,0:T(8,128)} %bitcast.13), custom_call_target="tpu_custom_call" | custom-call | flops 20000000000 | tf_op jit(solution)/shard_map/pallas_call | solution.py:283
  9.8 0.8 collective-permute-done.1.refs_3_
  10.7 0.5 collective-permute-start.5
  11.2 1.0 collective-permute-done.2.refs_4_
  12.2 3.6 %shard_map.224 = (bf16[1024,512]{1,0:T(8,128)(2,1)S(1)}, bf16[1024,512]{1,0:T(8,128)(2,1)S(1)}, f32[1024,128]{1,0:T(8,128)}, f32[1024,1]{1,0:T(8,128)}, f32[512,...) custom-call(s32[3]{0:T(128)S(1)} %pad_add_fusion.token_ref.refs_0_, ...), custom_call_target="tpu_custom_call" | custom-call | flops 1000000 | tf_op jit(solution)/shard_map/pallas_call | solution.py:283
  15.9 2.7 %collective-permute-done.6.refs_3_ = bf16[1536,128]{1,0:T(8,128)(2,1)S(1)} collective-permute-done((bf16[1536,128]{1,0:T(8,128)(2,1)S(1)}, bf16[1536,128]{1,0:T(8,128)(2,1)S(1)}, u32[]{:S(2)}, u32[]{:S(2)}) %collective-permute-start.6) | collective-permute-done | bytes 393248 | tf_op jit(solution)/shard_map/ppermute | solution.py:133
  18.6 1.7 %collective-permute-start.4 = (bf16[1024,128]{1,0:T(8,128)(2,1)S(1)}, bf16[1024,128]{1,0:T(8,128)(2,1)S(1)}, u32[]{:S(2)}, u32[]{:S(2)}) collective-permute-start(bf16[1024,128]{1,0:T(8,128)(2,1)S(1)} %get-tuple-element.103.refs_1_.refs_9_), channel_id=1, source_target_pairs={{0,2},{1,3},{2,0},{3,1},{4,6},{5,7},{6,4},{7,5},{8,10},{9,11},{10,... | collective-permute-start | bytes 786440 | tf_op jit(solution)/shard_map/ppermute | solution.py:133
  20.3 0.2 collective-permute-start.3
  20.6 2.7 %shard_map.225 = (bf16[1024,512]{1,0:T(8,128)(2,1)S(1)}, bf16[512,512]{1,0:T(8,128)(2,1)S(1)}, f32[1024,512]{1,0:T(8,128)S(1)}, bf16[2,512,512]{2,1,0:T(8,128)(2,1)S(1)}) custom-call(s32[3]{0:T(128)S(1)} %pad_add_fusion.token_ref.refs_0_, bf16[1536,128]{1,0:T(8,128)(2,1)S(1)} %get-tuple-element.105.refs_1_, ...), custom_call_target="tpu_custom_call" | custom-call | flops 30000001024 | tf_op jit(solution)/shard_map/pallas_call | solution.py:283
  23.3 4.0 %collective-permute-done.4.refs_3_ = bf16[1024,128]{1,0:T(8,128)(2,1)S(1)} collective-permute-done((bf16[1024,128]{1,0:T(8,128)(2,1)S(1)}, bf16[1024,128]{1,0:T(8,128)(2,1)S(1)}, u32[]{:S(2)}, u32[]{:S(2)}) %collective-permute-start.4) | collective-permute-done | bytes 262176 | tf_op jit(solution)/shard_map/ppermute | solution.py:133
  27.3 1.5 collective-permute-done.8.refs_4_
  28.9 5.9 %shard_map.226 = (bf16[512,512]{1,0:T(8,128)(2,1)S(1)}, f32[512,512]{1,0:T(8,128)S(1)}, bf16[1024,512]{1,0:T(8,128)(2,1)S(1)}, bf16[1024,512]{1,0:T(8,128)(2,1)S...) custom-call(s32[3]{0:T(128)S(1)} %pad_add_fusion.token_ref.refs_0_, ...), custom_call_target="tpu_custom_call" | custom-call | flops 60000002048 | tf_op jit(solution)/shard_map/pallas_call | solution.py:283
  34.7 0.2 collective-permute-start.9
  34.9 1.8 %collective-permute-done.9.refs_2_ = bf16[2,256,512]{2,1,0:T(8,128)(2,1)S(1)} collective-permute-done((bf16[2,256,512]{2,1,0:T(8,128)(2,1)S(1)}, bf16[2,256,512]{2,1,0:T(8,128)(2,1)S(1)}, u32[]{:S(2)}, u32[]{:S(2)}) %collective-permute-start.9) | collective-permute-done | bytes 524320 | tf_op jit(solution)/shard_map/ppermute | solution.py:133
  36.7 1.3 shard_map.227
  38.0 1.8 %collective-permute-start.11 = (bf16[256,512]{1,0:T(8,128)(2,1)}, bf16[256,512]{1,0:T(8,128)(2,1)}, u32[]{:S(2)}, u32[]{:S(2)}) collective-permute-start(bf16[256,512]{1,0:T(8,128)(2,1)} %get-tuple-element.115), channel_id=1, source_target_pairs={{0,2},{1,3},{2,0},{3,1},{4,6},{5,7},{6,4},{7,5},{8,10},{9,11},{10,... | collective-permute-start | bytes 786440 | tf_op jit(solution)/shard_map/ppermute | solution.py:133
  39.8 2.3 %shard_map.228 = (bf16[528,512]{1,0:T(8,128)(2,1)}, f32[64,512]{1,0:T(8,128)}) custom-call(s32[3]{0:T(128)S(1)} %pad_add_fusion.token_ref.refs_0_, bf16[1024,512]{1,0:T(8,128)(2,1)S(1)} %get-tuple-element.117.refs_1_, bf16[1024,512]{1,0:T(8,128)(2,1)S(1)} %get-tuple-element.118.refs_2_.refs_1_, bf16[1024,512]{1,0:T(8,128)(2,1)S(1)} %get-tuple-element.119.refs_3_, ...), custom_call_target="tpu_custom_call" | custom-call | flops 20000000000 | tf_op jit(solution)/shard_map/pallas_call | solution.py:283
  42.1 1.6 collective-permute-start.10
  43.7 1.5 shard_map.229.refs_1_
  45.2 1.5 collective-permute-done.11.refs_2_
  46.7 1.3 shard_map.231
  48.1 1.8 %collective-permute-start.13 = (bf16[256,512]{1,0:T(8,128)(2,1)S(1)}, bf16[256,512]{1,0:T(8,128)(2,1)S(1)}, u32[]{:S(2)}, u32[]{:S(2)}) collective-permute-start(bf16[256,512]{1,0:T(8,128)(2,1)S(1)} %get-tuple-element.129.refs_1_), channel_id=1, source_target_pairs={{0,2},{1,3},{2,0},{3,1},{4,6},{5,7},{6,4},{7,5},{8,10},{9,11},{10,... | collective-permute-start | bytes 786440 | tf_op jit(solution)/shard_map/ppermute | solution.py:133
  49.9 2.1 %shard_map.232.refs_15_ = bf16[2,256,2048]{2,1,0:T(8,128)(2,1)S(1)} custom-call(s32[3]{0:T(128)S(1)} %pad_add_fusion.token_ref.refs_0_, bf16[2,256,2048]{2,1,0:T(8,128)(2,1)} %constant.20.clone.refs_0_), custom_call_target="tpu_custom_call" | custom-call | flops 1000000 | tf_op jit(solution)/shard_map/pallas_call | solution.py:317
  52.1 2.6 %shard_map.233 = (bf16[2,1024,128]{2,1,0:T(8,128)(2,1)}, f32[2,1024,128]{2,1,0:T(8,128)}) custom-call(s32[3]{0:T(128)S(1)} %pad_add_fusion.token_ref.refs_0_, bf16[1024,512]{1,0:T(8,128)(2,1)S(1)} %copy-done.13, bf16[2,512,512]{2,1,0:T(8,128)(2,1)S(1)} %get-tuple-element.112.refs_8_.refs_2_), custom_call_target="tpu_custom_call" | custom-call | flops 10000000000 | tf_op jit(solution)/shard_map/pallas_call | solution.py:283
  54.7 1.0 collective-permute-done.13.refs_3_
  55.7 0.5 collective-permute-start.20
  56.2 0.4 collective-permute-done.10.refs_2_
  56.6 1.2 shard_map.230
  57.8 7.1 %shard_map.234 = (bf16[8,224,128]{2,1,0:T(8,128)(2,1)}, bf16[2,1056,128]{2,1,0:T(8,128)(2,1)}, f32[2,1056,128]{2,1,0:T(8,128)}, bf16[1024,128]{1,0:T(8,128)(2,1)}) custom-call(s32[3]{0:T(128)S(1)} %pad_add_fusion.token_ref.refs_0_, bf16[256,512]{1,0:T(8,128)(2,1)S(1)} %get-tuple-element.129.refs_1_, bf16[256,512]{1,0:T(8,128)(2,1)S(1)} %collective-permute-done.12.refs_2_, ...), custom_call_target="tpu_custom_call" | custom-call | flops 9999999827968 | tf_op jit(solution)/shard_map/pallas_call | solution.py:283
  64.9 0.1 collective-permute-start.19
  65.0 1.7 %collective-permute-start.16 = (bf16[144,512]{1,0:T(8,128)(2,1)S(1)}, bf16[144,512]{1,0:T(8,128)(2,1)}, u32[]{:S(2)}, u32[]{:S(2)}) collective-permute-start(bf16[144,512]{1,0:T(8,128)(2,1)S(1)} %get-tuple-element.142), channel_id=1, source_target_pairs={{0,8},{4,12},{8,0},{12,4},{16,24},{20,28},{24,16},{28,20},{1,9},{5... | collective-permute-start | bytes 442376 | tf_op jit(solution)/shard_map/ppermute | solution.py:133
  66.7 2.5 %collective-permute-start.17 = (bf16[144,512]{1,0:T(8,128)(2,1)S(1)}, bf16[144,512]{1,0:T(8,128)(2,1)}, u32[]{:S(2)}, u32[]{:S(2)}) collective-permute-start(bf16[144,512]{1,0:T(8,128)(2,1)S(1)} %get-tuple-element.143), channel_id=1, source_target_pairs={{0,16},{4,20},{8,24},{12,28},{16,0},{20,4},{24,8},{28,12},{1,17},{... | collective-permute-start | bytes 442376 | tf_op jit(solution)/shard_map/ppermute | solution.py:133
  69.2 0.2 collective-permute-start.18
  69.4 1.6 collective-permute-start.15
  71.0 4.9 %all-to-all-start = ((bf16[8,224,128]{2,1,0:T(8,128)(2,1)}), bf16[8,224,128]{2,1,0:T(8,128)(2,1)S(1)}, u32[]{:S(2)}, u32[]{:S(2)}) async-start(bf16[8,224,128]{2,1,0:T(8,128)(2,1)} %get-tuple-element.140), calls=%async_computation | async-start | bytes 917504 | tf_op jit(solution)/shard_map/all_to_all | solution.py:889
  75.9 2.8 %shard_map.236 = (f32[1024,128]{1,0:T(8,128)S(1)}, f32[32,128]{1,0:T(8,128)S(1)}, f32[1024,128]{1,0:T(8,128)S(1)}, bf16[2080,128]{1,0:T(8,128)(2,1)S(1)}) custom-call(s32[3]{0:T(128)S(1)} %pad_add_fusion.token_ref.refs_0_, f32[2,1056,128]{2,1,0:T(8,128)} %get-tuple-element.146.refs_1_, bf16[2,1056,128]{2,1,0:T(8,128)(2,1)S(1)} %collective-permute-done.19.refs_2_, ...), custom_call_target="tpu_custom_call" | custom-call | flops 1000000 | tf_op jit(solution)/shard_map/pallas_call | solution.py:283
  78.7 1.5 collective-permute-start.21
  80.3 1.2 collective-permute-done.17.refs_5_
  81.4 2.6 %shard_map.235 = (bf16[128,512]{1,0:T(8,128)(2,1)}, f32[64,512]{1,0:T(8,128)}, f32[64,512]{1,0:T(8,128)}, f32[8,128]{1,0:T(8,128)}) custom-call(s32[3]{0:T(128)S(1)} %pad_add_fusion.token_ref.refs_0_, f32[2,64,512]{2,1,0:T(8,128)S(1)} %copy-done.9, f32[64,512]{1,0:T(8,128)} %collective-permute-done.15.refs_2_, ...), custom_call_target="tpu_custom_call" | custom-call | flops 10000000000 | tf_op jit(solution)/shard_map/pallas_call | solution.py:283
  84.1 4.6 %collective-permute-start.25 = (bf16[128,512]{1,0:T(8,128)(2,1)}, bf16[128,512]{1,0:T(8,128)(2,1)}, u32[]{:S(2)}, u32[]{:S(2)}) collective-permute-start(bf16[128,512]{1,0:T(8,128)(2,1)} %get-tuple-element.165.refs_1_), channel_id=1, source_target_pairs={{0,24},{4,28},{8,16},{12,20},{16,8},{20,12},{24,0},{28,4},{1,25},{... | collective-permute-start | bytes 393224 | tf_op jit(solution)/shard_map/ppermute | solution.py:133
  88.7 6.3 %collective-permute-start.24 = (bf16[128,512]{1,0:T(8,128)(2,1)}, bf16[128,512]{1,0:T(8,128)(2,1)}, u32[]{:S(2)}, u32[]{:S(2)}) collective-permute-start(bf16[128,512]{1,0:T(8,128)(2,1)} %get-tuple-element.165.refs_1_), channel_id=1, source_target_pairs={{0,16},{4,20},{8,24},{12,28},{16,0},{20,4},{24,8},{28,12},{1,17},{... | collective-permute-start | bytes 393224 | tf_op jit(solution)/shard_map/ppermute | solution.py:133
  95.0 0.1 collective-permute-start.23
  95.1 1.5 collective-permute-start.22
  96.6 1.3 all-to-all-done.refs_1_
  97.9 2.5 %shard_map.237 = (f32[3,64,128]{2,1,0:T(8,128)}, bf16[32,64,128]{2,1,0:T(8,128)(2,1)}, bf16[2080,128]{1,0:T(8,128)(2,1)}) custom-call(s32[3]{0:T(128)S(1)} %pad_add_fusion.token_ref.refs_0_, bf16[8,224,128]{2,1,0:T(8,128)(2,1)S(1)} %all-to-all-done.refs_1_, f32[3,64,128]{2,1,0:T(8,128)} %refs_2_.4, f32[8,128]{1,0:T(8,128)} %get-tuple-element.145.refs_3_.refs_10_, ...), custom_call_target="tpu_custom_call" | custom-call | flops 9999999827968 | tf_op jit(solution)/shard_map/pallas_call | solution.py:283
  100.4 4.8 %all-to-all-start.1 = ((bf16[32,64,128]{2,1,0:T(8,128)(2,1)}), bf16[32,64,128]{2,1,0:T(8,128)(2,1)}, u32[]{:S(2)}, u32[]{:S(2)}) async-start(bf16[32,64,128]{2,1,0:T(8,128)(2,1)} %get-tuple-element.151), calls=%async_computation.1 | async-start | bytes 1048576 | tf_op jit(solution)/shard_map/all_to_all | solution.py:917
  105.3 1.2 shard_map.240.refs_2_
  106.5 0.7 collective-permute-start.28
  107.2 0.7 collective-permute-start.27
  107.9 3.3 %collective-permute-start.26 = (bf16[512,512]{1,0:T(8,128)(2,1)S(1)}, bf16[512,512]{1,0:T(8,128)(2,1)S(1)}, u32[]{:S(2)}, u32[]{:S(2)}) collective-permute-start(bf16[512,512]{1,0:T(8,128)(2,1)S(1)} %shard_map.240.refs_2_), channel_id=1, source_target_pairs={{0,1},{7,6},{8,9},{15,14},{16,17},{23,22},{24,25},{31,30}} | collective-permute-start | bytes 1572872 | tf_op jit(solution)/shard_map/ppermute | solution.py:922
  111.2 3.6 %shard_map.238 = (f32[1024,128]{1,0:T(8,128)}, bf16[1024,128]{1,0:T(8,128)(2,1)}) custom-call(s32[3]{0:T(128)S(1)} %pad_add_fusion.token_ref.refs_0_, f32[1024,128]{1,0:T(8,128)S(1)} %get-tuple-element.153.refs_1_, bf16[2080,128]{1,0:T(8,128)(2,1)} %get-tuple-element.154.refs_2_, f32[1024,128]{1,0:T(8,128)S(1)} %get-tuple-element.155.refs_3_, ...), custom_call_target="tpu_custom_call" | custom-call | flops 1000000 | tf_op jit(solution)/shard_map/pallas_call | solution.py:283
  114.8 2.2 %shard_map.239 = f32[2,64,512]{2,1,0:T(8,128)} custom-call(s32[3]{0:T(128)S(1)} %pad_add_fusion.token_ref.refs_0_, f32[64,512]{1,0:T(8,128)} %get-tuple-element.162.refs_1_, f32[64,512]{1,0:T(8,128)} %collective-permute-done.22.refs_2_), custom_call_target="tpu_custom_call" | custom-call | flops 10000000000 | tf_op jit(solution)/shard_map/pallas_call | solution.py:283
  117.2 3.6 %all-to-all-done.1.refs_1_ = bf16[32,64,128]{2,1,0:T(8,128)(2,1)} async-done(((bf16[32,64,128]{2,1,0:T(8,128)(2,1)}), bf16[32,64,128]{2,1,0:T(8,128)(2,1)}, u32[]{:S(2)}, u32[]{:S(2)}) %all-to-all-start.1) | async-done | bytes 524320 | tf_op jit(solution)/shard_map/all_to_all | solution.py:917
  120.8 3.4 %shard_map.241 = (bf16[8,64,512]{2,1,0:T(8,128)(2,1)}, bf16[8,48,128]{2,1,0:T(8,128)(2,1)S(1)}) custom-call(s32[3]{0:T(128)S(1)} %pad_add_fusion.token_ref.refs_0_, bf16[32,64,128]{2,1,0:T(8,128)(2,1)} %all-to-all-done.1.refs_1_, bf16[512,512]{1,0:T(8,128)(2,1)} %copy-done.8, bf16[512,512]{1,0:T(8,128)(2,1)} %copy-done.16, bf16[512,512]{1,0:T(8,128)(2,1)} %copy-done.15, ...), custom_call_target="tpu_custom_call" | custom-call | flops 179999997952 | tf_op jit(solution)/shard_map/pallas_call | solution.py:283
  124.2 23.0 %all-to-all-start.2 = ((bf16[8,64,512]{2,1,0:T(8,128)(2,1)}), bf16[8,64,512]{2,1,0:T(8,128)(2,1)S(1)}, u32[]{:S(2)}, u32[]{:S(2)}) async-start(bf16[8,64,512]{2,1,0:T(8,128)(2,1)} %get-tuple-element.166), calls=%async_computation.2 | async-start | bytes 1048576 | tf_op jit(solution)/shard_map/all_to_all | solution.py:950
  147.2 2.0 %collective-permute-start.29 = (bf16[8,48,128]{2,1,0:T(8,128)(2,1)S(1)}, bf16[8,48,128]{2,1,0:T(8,128)(2,1)S(1)}, u32[]{:S(2)}, u32[]{:S(2)}) collective-permute-start(bf16[8,48,128]{2,1,0:T(8,128)(2,1)S(1)} %get-tuple-element.167.refs_2_), channel_id=1, source_target_pairs={{0,4},{4,0},{8,12},{12,8},{16,20},{20,16},{24,28},{28,24},{1,5},{5... | collective-permute-start | bytes 294920 | tf_op jit(solution)/shard_map/ppermute | solution.py:133
  149.3 2.0 %shard_map.242 = (bf16[3,512,128]{2,1,0:T(8,128)(2,1)S(1)}, bf16[2,512,512]{2,1,0:T(8,128)(2,1)S(1)}, f32[2,512]{1,0:T(2,128)S(1)}, f32[2,512]{1,0:T(2,128)S(1)}...) custom-call(s32[3]{0:T(128)S(1)} %pad_add_fusion.token_ref.refs_0_, bf16[3,512,128]{2,1,0:T(8,128)(2,1)} %refs_0_.2, ...), custom_call_target="tpu_custom_call" | custom-call | flops 1000000 | tf_op jit(solution)/shard_map/pallas_call | solution.py:317
  151.2 7.0 %collective-permute-done.29.refs_3_ = bf16[8,48,128]{2,1,0:T(8,128)(2,1)S(1)} collective-permute-done((bf16[8,48,128]{2,1,0:T(8,128)(2,1)S(1)}, bf16[8,48,128]{2,1,0:T(8,128)(2,1)S(1)}, u32[]{:S(2)}, u32[]{:S(2)}) %collective-permute-start.29) | collective-permute-done | bytes 98336 | tf_op jit(solution)/shard_map/ppermute | solution.py:133
  158.2 2.7 %shard_map.243 = (f32[3,64,128]{2,1,0:T(8,128)}, f32[2,64,512]{2,1,0:T(8,128)}, f32[2,512]{1,0:T(2,128)}, f32[2,512]{1,0:T(2,128)}, f32[160,128]{1,0:T(8,128)}, /*index=5*/f32[160,128]{1,0:T(8,128)}) custom-call(s32[3]{0:T(128)S(1)} %pad_add_fusion.token_ref.refs_0_, bf16[8,64,512]{2,1,0:T(8,128)(2,1)S(1)} %all-to-all-done.2.refs_1_, ...), custom_call_target="tpu_custom_call" | custom-call | flops 1000000 | tf_op jit(solution)/shard_map/pallas_call | solution.py:283
  (59 shorter events, 0.1 us)
Async XLA Ops:
  0.6 10.0 %collective-permute-start.1 = (bf16[1024,128]{1,0:T(8,128)(2,1)}, bf16[1024,128]{1,0:T(8,128)(2,1)S(1)}, u32[]{:S(2)}, u32[]{:S(2)}) collective-permute-start(bf16[1024,128]{1,0:T(8,128)(2,1)} %bitcast.17), channel_id=1, source_target_pairs={{0,2},{1,3},{2,0},{3,1},{4,6},{5,7},{6,4},{7,5},{8,10},{9,11},{10,... | collective-permute-start | bytes 786440 | tf_op jit(solution)/shard_map/ppermute | solution.py:133
  3.6 7.5 %collective-permute-start = (bf16[1024,128]{1,0:T(8,128)(2,1)}, bf16[1024,128]{1,0:T(8,128)(2,1)S(1)}, u32[]{:S(2)}, u32[]{:S(2)}) collective-permute-start(bf16[1024,128]{1,0:T(8,128)(2,1)} %bitcast.18), channel_id=1, source_target_pairs={{0,1},{1,0},{2,3},{3,2},{4,5},{5,4},{6,7},{7,6},{8,9},{9,8},{10,11... | collective-permute-start | bytes 786440 | tf_op jit(solution)/shard_map/ppermute | solution.py:133
  6.5 5.7 %copy-start.2 = (bf16[2,512,256]{2,1,0:T(8,128)(2,1)}, bf16[2,512,256]{2,1,0:T(8,128)(2,1)S(1)}, u32[]{:S(2)}) copy-start(bf16[2,512,256]{2,1,0:T(8,128)(2,1)S(1)} %get-tuple-element.101.refs_7_.refs_13_) | copy-start | bytes 1572868
  6.5 5.7 %copy-start.4 = (bf16[2,256,512]{2,1,0:T(8,128)(2,1)}, bf16[2,256,512]{2,1,0:T(8,128)(2,1)S(1)}, u32[]{:S(2)}) copy-start(bf16[2,256,512]{2,1,0:T(8,128)(2,1)S(1)} %get-tuple-element.102.refs_8_.refs_14_) | copy-start | bytes 1572868
  6.5 5.7 %copy-start.6 = (bf16[3,512,128]{2,1,0:T(8,128)(2,1)}, bf16[3,512,128]{2,1,0:T(8,128)(2,1)S(1)}, u32[]{:S(2)}) copy-start(bf16[3,512,128]{2,1,0:T(8,128)(2,1)S(1)} %get-tuple-element.99.refs_5_) | copy-start | bytes 1179652
  6.5 12.1 %collective-permute-start.6 = (bf16[1536,128]{1,0:T(8,128)(2,1)S(1)}, bf16[1536,128]{1,0:T(8,128)(2,1)S(1)}, u32[]{:S(2)}, u32[]{:S(2)}) collective-permute-start(bf16[1536,128]{1,0:T(8,128)(2,1)S(1)} %get-tuple-element.105.refs_1_), channel_id=1, source_target_pairs={{0,2},{1,3},{2,0},{3,1},{4,6},{5,7},{6,4},{7,5},{8,10},{9,11},{10,... | collective-permute-start | bytes 1179656 | tf_op jit(solution)/shard_map/ppermute | solution.py:133
  9.8 13.5 %copy-start = (f32[2048,128]{1,0:T(8,128)}, f32[2048,128]{1,0:T(8,128)S(1)}, u32[]{:S(2)}) copy-start(f32[2048,128]{1,0:T(8,128)S(1)} %shard_map.223.refs_9_.refs_12_) | copy-start | bytes 3145732
  10.7 1.5 collective-permute-start.2
  10.7 9.9 %collective-permute-start.5 = (bf16[1536,128]{1,0:T(8,128)(2,1)S(1)}, bf16[1536,128]{1,0:T(8,128)(2,1)S(1)}, u32[]{:S(2)}, u32[]{:S(2)}) collective-permute-start(bf16[1536,128]{1,0:T(8,128)(2,1)S(1)} %get-tuple-element.105.refs_1_), channel_id=1, source_target_pairs={{0,1},{1,0},{2,3},{3,2},{4,5},{5,4},{6,7},{7,6},{8,9},{9,8},{10,11... | collective-permute-start | bytes 1179656 | tf_op jit(solution)/shard_map/ppermute | solution.py:133
  15.9 13.0 %copy-start.10 = (f32[2,512]{1,0:T(2,128)}, f32[2,512]{1,0:T(2,128)S(1)}, u32[]{:S(2)}) copy-start(f32[2,512]{1,0:T(2,128)S(1)} %get-tuple-element.111.refs_7_.refs_6_.refs_16_) | copy-start | bytes 12292
  18.6 2.0 %collective-permute-start.7 = (bf16[1536,128]{1,0:T(8,128)(2,1)S(1)}, bf16[1536,128]{1,0:T(8,128)(2,1)S(1)}, u32[]{:S(2)}, u32[]{:S(2)}) collective-permute-start(bf16[1536,128]{1,0:T(8,128)(2,1)S(1)} %collective-permute-done.6.refs_3_), channel_id=1, source_target_pairs={{0,1},{1,0},{2,3},{3,2},{4,5},{5,4},{6,7},{7,6},{8,9},{9,8},{10,11... | collective-permute-start | bytes 1179656 | tf_op jit(solution)/shard_map/ppermute | solution.py:133
  18.6 8.7 %collective-permute-start.4 = (bf16[1024,128]{1,0:T(8,128)(2,1)S(1)}, bf16[1024,128]{1,0:T(8,128)(2,1)S(1)}, u32[]{:S(2)}, u32[]{:S(2)}) collective-permute-start(bf16[1024,128]{1,0:T(8,128)(2,1)S(1)} %get-tuple-element.103.refs_1_.refs_9_), channel_id=1, source_target_pairs={{0,2},{1,3},{2,0},{3,1},{4,6},{5,7},{6,4},{7,5},{8,10},{9,11},{10,... | collective-permute-start | bytes 786440 | tf_op jit(solution)/shard_map/ppermute | solution.py:133
  20.3 7.0 %collective-permute-start.3 = (bf16[1024,128]{1,0:T(8,128)(2,1)S(1)}, bf16[1024,128]{1,0:T(8,128)(2,1)S(1)}, u32[]{:S(2)}, u32[]{:S(2)}) collective-permute-start(bf16[1024,128]{1,0:T(8,128)(2,1)S(1)} %get-tuple-element.103.refs_1_.refs_9_), channel_id=1, source_target_pairs={{0,1},{1,0},{2,3},{3,2},{4,5},{5,4},{6,7},{7,6},{8,9},{9,8},{10,11... | collective-permute-start | bytes 786440 | tf_op jit(solution)/shard_map/ppermute | solution.py:133
  27.3 1.5 collective-permute-start.8
  34.7 9.0 %copy-start.12 = (bf16[1024,512]{1,0:T(8,128)(2,1)}, bf16[1024,512]{1,0:T(8,128)(2,1)S(1)}, u32[]{:S(2)}) copy-start(bf16[1024,512]{1,0:T(8,128)(2,1)S(1)} %get-tuple-element.118.refs_2_.refs_1_) | copy-start | bytes 3145732
  34.7 2.0 %collective-permute-start.9 = (bf16[2,256,512]{2,1,0:T(8,128)(2,1)S(1)}, bf16[2,256,512]{2,1,0:T(8,128)(2,1)S(1)}, u32[]{:S(2)}, u32[]{:S(2)}) collective-permute-start(bf16[2,256,512]{2,1,0:T(8,128)(2,1)S(1)} %bitcast.11), channel_id=1, source_target_pairs={{0,1},{1,0},{2,3},{3,2},{4,5},{5,4},{6,7},{7,6},{8,9},{9,8},{10,11... | collective-permute-start | bytes 1572872 | tf_op jit(solution)/shard_map/ppermute | solution.py:133
  38.0 8.7 %collective-permute-start.11 = (bf16[256,512]{1,0:T(8,128)(2,1)}, bf16[256,512]{1,0:T(8,128)(2,1)}, u32[]{:S(2)}, u32[]{:S(2)}) collective-permute-start(bf16[256,512]{1,0:T(8,128)(2,1)} %get-tuple-element.115), channel_id=1, source_target_pairs={{0,2},{1,3},{2,0},{3,1},{4,6},{5,7},{6,4},{7,5},{8,10},{9,11},{10,... | collective-permute-start | bytes 786440 | tf_op jit(solution)/shard_map/ppermute | solution.py:133
  42.1 14.4 %collective-permute-start.10 = (bf16[528,512]{1,0:T(8,128)(2,1)}, bf16[528,512]{1,0:T(8,128)(2,1)}, u32[]{:S(2)}, u32[]{:S(2)}) collective-permute-start(bf16[528,512]{1,0:T(8,128)(2,1)} %get-tuple-element.121), channel_id=1, source_target_pairs={{0,4},{4,0},{8,12},{12,8},{16,20},{20,16},{24,28},{28,24},{1,5},{5... | collective-permute-start | bytes 1622024 | tf_op jit(solution)/shard_map/ppermute | solution.py:133
  43.7 3.0 %copy-start.11 = (f32[2,512]{1,0:T(2,128)S(1)}, f32[2,512]{1,0:T(2,128)}, u32[]{:S(2)}) copy-start(f32[2,512]{1,0:T(2,128)} %copy-done.10) | copy-start | bytes 12292
  48.0 4.0 %copy-start.13 = (bf16[1024,512]{1,0:T(8,128)(2,1)S(1)}, bf16[1024,512]{1,0:T(8,128)(2,1)}, u32[]{:S(2)}) copy-start(bf16[1024,512]{1,0:T(8,128)(2,1)} %copy-done.12) | copy-start | bytes 3145732
  48.1 7.6 %collective-permute-start.13 = (bf16[256,512]{1,0:T(8,128)(2,1)S(1)}, bf16[256,512]{1,0:T(8,128)(2,1)S(1)}, u32[]{:S(2)}, u32[]{:S(2)}) collective-permute-start(bf16[256,512]{1,0:T(8,128)(2,1)S(1)} %get-tuple-element.129.refs_1_), channel_id=1, source_target_pairs={{0,2},{1,3},{2,0},{3,1},{4,6},{5,7},{6,4},{7,5},{8,10},{9,11},{10,... | collective-permute-start | bytes 786440 | tf_op jit(solution)/shard_map/ppermute | solution.py:133
  49.9 7.9 %collective-permute-start.12 = (bf16[256,512]{1,0:T(8,128)(2,1)S(1)}, bf16[256,512]{1,0:T(8,128)(2,1)S(1)}, u32[]{:S(2)}, u32[]{:S(2)}) collective-permute-start(bf16[256,512]{1,0:T(8,128)(2,1)S(1)} %get-tuple-element.129.refs_1_), channel_id=1, source_target_pairs={{0,1},{1,0},{2,3},{3,2},{4,5},{5,4},{6,7},{7,6},{8,9},{9,8},{10,11... | collective-permute-start | bytes 786440 | tf_op jit(solution)/shard_map/ppermute | solution.py:133
  52.0 5.7 %copy-start.1 = (f32[2048,128]{1,0:T(8,128)S(1)}, f32[2048,128]{1,0:T(8,128)}, u32[]{:S(2)}) copy-start(f32[2048,128]{1,0:T(8,128)} %copy-done) | copy-start | bytes 3145732
  52.0 5.7 %copy-start.3 = (bf16[2,512,256]{2,1,0:T(8,128)(2,1)S(1)}, bf16[2,512,256]{2,1,0:T(8,128)(2,1)}, u32[]{:S(2)}) copy-start(bf16[2,512,256]{2,1,0:T(8,128)(2,1)} %copy-done.2) | copy-start | bytes 1572868
  52.0 5.7 %copy-start.5 = (bf16[2,256,512]{2,1,0:T(8,128)(2,1)S(1)}, bf16[2,256,512]{2,1,0:T(8,128)(2,1)}, u32[]{:S(2)}) copy-start(bf16[2,256,512]{2,1,0:T(8,128)(2,1)} %copy-done.4) | copy-start | bytes 1572868
  52.1 5.7 %copy-start.7 = (bf16[3,512,128]{2,1,0:T(8,128)(2,1)S(1)}, bf16[3,512,128]{2,1,0:T(8,128)(2,1)}, u32[]{:S(2)}) copy-start(bf16[3,512,128]{2,1,0:T(8,128)(2,1)} %copy-done.6) | copy-start | bytes 1179652
  55.7 2.1 %collective-permute-start.14 = (bf16[256,512]{1,0:T(8,128)(2,1)S(1)}, bf16[256,512]{1,0:T(8,128)(2,1)S(1)}, u32[]{:S(2)}, u32[]{:S(2)}) collective-permute-start(bf16[256,512]{1,0:T(8,128)(2,1)S(1)} %collective-permute-done.13.refs_3_), channel_id=1, source_target_pairs={{0,1},{1,0},{2,3},{3,2},{4,5},{5,4},{6,7},{7,6},{8,9},{9,8},{10,11... | collective-permute-start | bytes 786440 | tf_op jit(solution)/shard_map/ppermute | solution.py:133
  55.7 13.8 %collective-permute-start.20 = (bf16[2,1024,128]{2,1,0:T(8,128)(2,1)}, bf16[2,1024,128]{2,1,0:T(8,128)(2,1)}, u32[]{:S(2)}, u32[]{:S(2)}) collective-permute-start(bf16[2,1024,128]{2,1,0:T(8,128)(2,1)} %get-tuple-element.132), channel_id=1, source_target_pairs={{0,1},{1,0},{2,3},{3,2},{4,5},{5,4},{6,7},{7,6},{8,9},{9,8},{10,11... | collective-permute-start | bytes 1572872 | tf_op jit(solution)/shard_map/ppermute | solution.py:133
  64.9 16.5 %copy-start.9 = (f32[2,64,512]{2,1,0:T(8,128)S(1)}, f32[2,64,512]{2,1,0:T(8,128)}, u32[]{:S(2)}) copy-start(f32[2,64,512]{2,1,0:T(8,128)} %refs_1_.5) | copy-start | bytes 786436
  64.9 11.0 %collective-permute-start.19 = (bf16[2,1056,128]{2,1,0:T(8,128)(2,1)}, bf16[2,1056,128]{2,1,0:T(8,128)(2,1)S(1)}, u32[]{:S(2)}, u32[]{:S(2)}) collective-permute-start(bf16[2,1056,128]{2,1,0:T(8,128)(2,1)} %get-tuple-element.147), channel_id=1, source_target_pairs={{0,1},{1,0},{2,3},{3,2},{4,5},{5,4},{6,7},{7,6},{8,9},{9,8},{10,11... | collective-permute-start | bytes 1622024 | tf_op jit(solution)/shard_map/ppermute | solution.py:133
  65.0 15.3 %collective-permute-start.16 = (bf16[144,512]{1,0:T(8,128)(2,1)S(1)}, bf16[144,512]{1,0:T(8,128)(2,1)}, u32[]{:S(2)}, u32[]{:S(2)}) collective-permute-start(bf16[144,512]{1,0:T(8,128)(2,1)S(1)} %get-tuple-element.142), channel_id=1, source_target_pairs={{0,8},{4,12},{8,0},{12,4},{16,24},{20,28},{24,16},{28,20},{1,9},{5... | collective-permute-start | bytes 442376 | tf_op jit(solution)/shard_map/ppermute | solution.py:133
  66.7 14.7 %collective-permute-start.17 = (bf16[144,512]{1,0:T(8,128)(2,1)S(1)}, bf16[144,512]{1,0:T(8,128)(2,1)}, u32[]{:S(2)}, u32[]{:S(2)}) collective-permute-start(bf16[144,512]{1,0:T(8,128)(2,1)S(1)} %get-tuple-element.143), channel_id=1, source_target_pairs={{0,16},{4,20},{8,24},{12,28},{16,0},{20,4},{24,8},{28,12},{1,17},{... | collective-permute-start | bytes 442376 | tf_op jit(solution)/shard_map/ppermute | solution.py:133
  69.2 12.2 %collective-permute-start.18 = (bf16[144,512]{1,0:T(8,128)(2,1)S(1)}, bf16[144,512]{1,0:T(8,128)(2,1)}, u32[]{:S(2)}, u32[]{:S(2)}) collective-permute-start(bf16[144,512]{1,0:T(8,128)(2,1)S(1)} %get-tuple-element.144), channel_id=1, source_target_pairs={{0,24},{4,28},{8,16},{12,20},{16,8},{20,12},{24,0},{28,4},{1,25},{... | collective-permute-start | bytes 442376 | tf_op jit(solution)/shard_map/ppermute | solution.py:133
  69.4 10.8 %collective-permute-start.15 = (f32[64,512]{1,0:T(8,128)}, f32[64,512]{1,0:T(8,128)}, u32[]{:S(2)}, u32[]{:S(2)}) collective-permute-start(f32[64,512]{1,0:T(8,128)} %get-tuple-element.141), channel_id=1, source_target_pairs={{0,4},{4,0},{8,12},{12,8},{16,20},{20,16},{24,28},{28,24},{1,5},{5... | collective-permute-start | bytes 393224 | tf_op jit(solution)/shard_map/ppermute | solution.py:133
  71.0 26.9 %all-to-all-start = ((bf16[8,224,128]{2,1,0:T(8,128)(2,1)}), bf16[8,224,128]{2,1,0:T(8,128)(2,1)S(1)}, u32[]{:S(2)}, u32[]{:S(2)}) async-start(bf16[8,224,128]{2,1,0:T(8,128)(2,1)} %get-tuple-element.140), calls=%async_computation | async-start | bytes 917504 | tf_op jit(solution)/shard_map/all_to_all | solution.py:889
  78.7 19.2 %collective-permute-start.21 = (bf16[2080,128]{1,0:T(8,128)(2,1)S(1)}, bf16[2080,128]{1,0:T(8,128)(2,1)S(1)}, u32[]{:S(2)}, u32[]{:S(2)}) collective-permute-start(bf16[2080,128]{1,0:T(8,128)(2,1)S(1)} %get-tuple-element.150), channel_id=1, source_target_pairs={{0,2},{1,3},{2,0},{3,1},{4,6},{5,7},{6,4},{7,5},{8,10},{9,11},{10,... | collective-permute-start | bytes 1597448 | tf_op jit(solution)/shard_map/ppermute | solution.py:133
  84.1 21.2 %collective-permute-start.25 = (bf16[128,512]{1,0:T(8,128)(2,1)}, bf16[128,512]{1,0:T(8,128)(2,1)}, u32[]{:S(2)}, u32[]{:S(2)}) collective-permute-start(bf16[128,512]{1,0:T(8,128)(2,1)} %get-tuple-element.165.refs_1_), channel_id=1, source_target_pairs={{0,24},{4,28},{8,16},{12,20},{16,8},{20,12},{24,0},{28,4},{1,25},{... | collective-permute-start | bytes 393224 | tf_op jit(solution)/shard_map/ppermute | solution.py:133
  88.7 16.6 %collective-permute-start.24 = (bf16[128,512]{1,0:T(8,128)(2,1)}, bf16[128,512]{1,0:T(8,128)(2,1)}, u32[]{:S(2)}, u32[]{:S(2)}) collective-permute-start(bf16[128,512]{1,0:T(8,128)(2,1)} %get-tuple-element.165.refs_1_), channel_id=1, source_target_pairs={{0,16},{4,20},{8,24},{12,28},{16,0},{20,4},{24,8},{28,12},{1,17},{... | collective-permute-start | bytes 393224 | tf_op jit(solution)/shard_map/ppermute | solution.py:133
  95.0 10.3 %collective-permute-start.23 = (bf16[128,512]{1,0:T(8,128)(2,1)}, bf16[128,512]{1,0:T(8,128)(2,1)}, u32[]{:S(2)}, u32[]{:S(2)}) collective-permute-start(bf16[128,512]{1,0:T(8,128)(2,1)} %get-tuple-element.165.refs_1_), channel_id=1, source_target_pairs={{0,8},{4,12},{8,0},{12,4},{16,24},{20,28},{24,16},{28,20},{1,9},{5... | collective-permute-start | bytes 393224 | tf_op jit(solution)/shard_map/ppermute | solution.py:133
  95.1 19.7 %collective-permute-start.22 = (f32[64,512]{1,0:T(8,128)}, f32[64,512]{1,0:T(8,128)}, u32[]{:S(2)}, u32[]{:S(2)}) collective-permute-start(f32[64,512]{1,0:T(8,128)} %get-tuple-element.163), channel_id=1, source_target_pairs={{0,4},{4,0},{8,12},{12,8},{16,20},{20,16},{24,28},{28,24},{1,5},{5... | collective-permute-start | bytes 393224 | tf_op jit(solution)/shard_map/ppermute | solution.py:133
  100.4 20.3 %all-to-all-start.1 = ((bf16[32,64,128]{2,1,0:T(8,128)(2,1)}), bf16[32,64,128]{2,1,0:T(8,128)(2,1)}, u32[]{:S(2)}, u32[]{:S(2)}) async-start(bf16[32,64,128]{2,1,0:T(8,128)(2,1)} %get-tuple-element.151), calls=%async_computation.1 | async-start | bytes 1048576 | tf_op jit(solution)/shard_map/all_to_all | solution.py:917
  106.5 10.6 %copy-start.8 = (bf16[512,512]{1,0:T(8,128)(2,1)}, bf16[512,512]{1,0:T(8,128)(2,1)S(1)}, u32[]{:S(2)}) copy-start(bf16[512,512]{1,0:T(8,128)(2,1)S(1)} %shard_map.240.refs_2_) | copy-start | bytes 1572868
  106.5 10.6 %collective-permute-start.28 = (bf16[512,512]{1,0:T(8,128)(2,1)S(1)}, bf16[512,512]{1,0:T(8,128)(2,1)S(1)}, u32[]{:S(2)}, u32[]{:S(2)}) collective-permute-start(bf16[512,512]{1,0:T(8,128)(2,1)S(1)} %shard_map.240.refs_2_), channel_id=1, source_target_pairs={{2,1},{5,6},{10,9},{13,14},{18,17},{21,22},{26,25},{29,30}} | collective-permute-start | bytes 1572872 | tf_op jit(solution)/shard_map/ppermute | solution.py:922
  107.2 10.0 %collective-permute-start.27 = (bf16[512,512]{1,0:T(8,128)(2,1)S(1)}, bf16[512,512]{1,0:T(8,128)(2,1)S(1)}, u32[]{:S(2)}, u32[]{:S(2)}) collective-permute-start(bf16[512,512]{1,0:T(8,128)(2,1)S(1)} %shard_map.240.refs_2_), channel_id=1, source_target_pairs={{3,1},{4,6},{11,9},{12,14},{19,17},{20,22},{27,25},{28,30}} | collective-permute-start | bytes 1572872 | tf_op jit(solution)/shard_map/ppermute | solution.py:922
  107.9 9.3 %collective-permute-start.26 = (bf16[512,512]{1,0:T(8,128)(2,1)S(1)}, bf16[512,512]{1,0:T(8,128)(2,1)S(1)}, u32[]{:S(2)}, u32[]{:S(2)}) collective-permute-start(bf16[512,512]{1,0:T(8,128)(2,1)S(1)} %shard_map.240.refs_2_), channel_id=1, source_target_pairs={{0,1},{7,6},{8,9},{15,14},{16,17},{23,22},{24,25},{31,30}} | collective-permute-start | bytes 1572872 | tf_op jit(solution)/shard_map/ppermute | solution.py:922
  117.1 3.7 %copy-start.14 = (bf16[512,512]{1,0:T(8,128)(2,1)}, bf16[512,512]{1,0:T(8,128)(2,1)S(1)}, u32[]{:S(2)}) copy-start(bf16[512,512]{1,0:T(8,128)(2,1)S(1)} %collective-permute-done.28.refs_5_) | copy-start | bytes 1572868
  117.1 3.7 %copy-start.15 = (bf16[512,512]{1,0:T(8,128)(2,1)}, bf16[512,512]{1,0:T(8,128)(2,1)S(1)}, u32[]{:S(2)}) copy-start(bf16[512,512]{1,0:T(8,128)(2,1)S(1)} %collective-permute-done.27.refs_4_) | copy-start | bytes 1572868
  117.2 3.6 %copy-start.16 = (bf16[512,512]{1,0:T(8,128)(2,1)}, bf16[512,512]{1,0:T(8,128)(2,1)S(1)}, u32[]{:S(2)}) copy-start(bf16[512,512]{1,0:T(8,128)(2,1)S(1)} %collective-permute-done.26.refs_3_) | copy-start | bytes 1572868
  124.2 34.0 %all-to-all-start.2 = ((bf16[8,64,512]{2,1,0:T(8,128)(2,1)}), bf16[8,64,512]{2,1,0:T(8,128)(2,1)S(1)}, u32[]{:S(2)}, u32[]{:S(2)}) async-start(bf16[8,64,512]{2,1,0:T(8,128)(2,1)} %get-tuple-element.166), calls=%async_computation.2 | async-start | bytes 1048576 | tf_op jit(solution)/shard_map/all_to_all | solution.py:950
  147.2 11.0 %collective-permute-start.29 = (bf16[8,48,128]{2,1,0:T(8,128)(2,1)S(1)}, bf16[8,48,128]{2,1,0:T(8,128)(2,1)S(1)}, u32[]{:S(2)}, u32[]{:S(2)}) collective-permute-start(bf16[8,48,128]{2,1,0:T(8,128)(2,1)S(1)} %get-tuple-element.167.refs_2_), channel_id=1, source_target_pairs={{0,4},{4,0},{8,12},{12,8},{16,20},{20,16},{24,28},{28,24},{1,5},{5... | collective-permute-start | bytes 294920 | tf_op jit(solution)/shard_map/ppermute | solution.py:133

commit v2 on v1

--- a/solution.py
+++ b/solution.py
@@ -185,15 +185,19 @@
 
 def three_terms(left, right, cut=None):
     right = right if cut is None else [v[:, cut:] for v in right]
-    return dot(left[0], right[0], NN) + (dot(left[0], right[1], NN) + dot(left[1], right[0], NN))
-
-
-def newton_schulz(matrix, a_ref, p_ref, r_ref, start):
+    left = jnp.concatenate([left[0], left[0], left[1]], 1)
+    return dot(left, jnp.concatenate([right[0], right[1], right[0]], 0), NN)
+
+
+def newton_schulz(blocks, a_ref, p_ref, r_ref, start):
     size = a_ref.shape[0]
     row = lax.broadcasted_iota(jnp.int32, (size, size), 0)
     col = lax.broadcasted_iota(jnp.int32, (size, size), 1)
     unit = (row == col).astype(F32)
-    gram = symmetric([matrix], [matrix], lambda a, b, cut: dot(a[0], b[0] if cut is None else b[0][cut:], NT))
+    blocks = [block() for block in blocks]
+    gram = 0.0
+    for block in blocks:
+        gram = gram + symmetric([block], [block], lambda a, b, cut: dot(a[0], b[0] if cut is None else b[0][cut:], NT))
     scale = 1.0 / (jnp.sqrt(jnp.sum(gram * unit)) + 1e-07)
     a_ref[...] = gram * (scale * scale)
 
@@ -216,7 +220,7 @@
     once = three_terms(split(rows), terms)
     rows = NS_COEF_A * rows + NS_COEF_B * once + NS_COEF_C * three_terms(split(once), terms)
     high, low = split(rows)
-    return scale * (dot(high, matrix, NN) + dot(low, matrix, NN))
+    return [scale * (dot(high, block, NN) + dot(low, block, NN)) for block in blocks]
 
 
 VMEM = pl.BlockSpec(memory_space=pltpu.VMEM)
@@ -233,8 +237,8 @@
 
 
 class Store:
-    def __init__(self, shape, dtype):
-        self.shape, self.dtype = shape, dtype
+    def __init__(self, shape, dtype, own=False):
+        self.shape, self.dtype, self.own = shape, dtype, own
 
 
 class Waiting:
@@ -270,7 +274,7 @@
                 passed.append(ref)
                 continue
             passed.append(Waiting(copy, buffers[at]))
-            if isinstance(what, Store):
+            if isinstance(what, Store) and not what.own:
                 stores.append(passed[-1])
             at += 1
         kernel(*passed, *(rest[:-1] if late else rest))
@@ -646,6 +650,8 @@
     for t in range(4):
         for z in range(dp // 2):
             slots.ref[8 * z + (keeper(t) ^ 4), : taps + 16, :] = rest
+            if t == 3:
+                slots.ref[8 * z + keeper(t), : taps + 16, :] = rest
     slots.send()
 
 
@@ -666,40 +672,105 @@
         input_grad.ref[r, :] = delta_own[r, :].astype(F32) + inv[r, :] * back
 
 
-def step_kernel(info, got, m0, m1, m2, m3, out, extra, matrix, large, a, p, r, result):
+def large_kernel(info, m0, m1, m2, m3, out, a, p, r):
+    me, row = info[0], info[2]
+    rows = r.shape[0] // 2
+
+    @pl.when(me == 3)
+    def _():
+        start = pl.multiple_of((row // 2) * (2 * rows), 2 * rows)
+        blocks = [lambda piece=piece: piece[...] for piece in (m0, m1, m2, m3)]
+        for k, steps in enumerate(newton_schulz(blocks, a, p, r, start)):
+            for y in range(2):
+                out.ref[4 * y + (3 ^ k), :rows, :] = steps[y * rows : (y + 1) * rows, :].astype(out.ref.dtype)
+        out.send()
+        out.copy.wait()
+
+
+def gather_extra(got, me, rows, packed, extra):
+    total, dp = packed.shape[0], got.shape[0] // 4
+    part = packed.shape[1]
+    share = -(-total // dp)
+    taps = -(-share // 8) * 8
+    taps += (3 * rows + taps) % 16
+    gain = 0.0
+    for i in range(dp):
+        both = got[4 * i + me, : taps + 16, :].astype(F32)
+        count = min(share, total - i * share)
+        if count > 0:
+            packed[i * share : i * share + count, :] = both[:count, :]
+        gain = gain + (both[taps : taps + 8, :] + both[taps + 8 :, :])
+    high, low = split(gain)
+    extra[...] = jnp.zeros_like(extra)
+    for g in range(-(-total // 64)):
+        count = min(64, total - 64 * g)
+        extra[:count, g * part : (g + 1) * part] = packed[64 * g : 64 * g + count, :].astype(extra.dtype)
+    at = (total // 64) * part
+    extra[32:48, at : at + part] = jnp.concatenate([high.astype(F32), low.astype(F32)], 0).astype(extra.dtype)
+
+
+def small_kernel(info, source, slots, out, got, extra, matrix, a, p, r, packed, steps, semaphore):
     me, row = info[0], info[2]
     side = row % 2
     size, width = matrix.shape
     rows = r.shape[0] // 2
     part = width // 4
-    hidden = m0.ref.shape[1]
     start = pl.multiple_of((row // 2) * (2 * rows), 2 * rows)
-    for i in range(extra.shape[0]):
-        extra[i] = got[4 * i + me, : extra.shape[1], :].astype(BF16)
-
-    @pl.when(jnp.logical_and(side == 1 - me // 2, me < 3))
+    keeps = jnp.logical_and(side == 1 - me // 2, me < 3)
+
+    @pl.when(me < 3)
     def _():
-        for i in range(size // rows):
-            for t in range(4):
-                matrix[i * rows : (i + 1) * rows, t * part : (t + 1) * part] = got[4 * i + t, :rows, :].astype(BF16)
-        result[...] = newton_schulz(matrix[...], a, p, r, start)
-        for q in range(8):
-            lanes = slice((q % 4) * part, (q % 4 + 1) * part)
-            out[q, :, :part] = result[(q // 4) * rows : (q // 4 + 1) * rows, lanes].astype(out.dtype)
-
-    @pl.when(me == side + 1)
-    def _():
-        for k, piece in enumerate((m0, m1, m2, m3)):
-            large[:, block_at(me ^ k, hidden)] = piece.ready()[...]
-        steps = newton_schulz(large[...], a, p, r, start)
-        for q in range(8):
-            lanes = slice((q % 4) * hidden, (q % 4 + 1) * hidden)
-            out[q] = steps[(q // 4) * rows : (q // 4 + 1) * rows, lanes].astype(out.dtype)
-
-    @pl.when(me != side + 1)
-    def _():
-        for piece in (m0, m1, m2, m3):
-            piece.ready()
+        arrive = pltpu.make_async_copy(source, got, semaphore.at[2])
+        arrive.start()
+        arrive.wait()
+
+        @pl.when(keeps)
+        def _():
+            for i in range(size // rows):
+                for t in range(4):
+                    matrix[i * rows : (i + 1) * rows, t * part : (t + 1) * part] = got[4 * i + t, :rows, :].astype(BF16)
+            (result,) = newton_schulz([lambda: matrix[...]], a, p, r, start)
+            for q in range(8):
+                lanes = slice((q % 4) * part, (q % 4 + 1) * part)
+                steps[q] = result[(q // 4) * rows : (q // 4 + 1) * rows, lanes].astype(steps.dtype)
+            copy = pltpu.make_async_copy(steps, out.at[:, pl.ds(0, rows), pl.ds(0, part)], semaphore.at[0])
+            copy.start()
+            copy.wait()
+
+        @pl.when(jnp.logical_not(keeps))
+        def _():
+            gather_extra(got, me, rows, packed, extra)
+            copies = [
+                pltpu.make_async_copy(extra, out.at[4 * y + me, pl.ds(0, 64), pl.ds(0, 3 * part)], semaphore.at[y])
+                for y in range(2)
+            ]
+            for copy in copies:
+                copy.start()
+            for copy in copies:
+                copy.wait()
+
+
+def small_steps(info, got, slots, rows, width, taps):
+    part = width // 4
+    square = pltpu.VMEM((width, width), F32)
+    return pl.pallas_call(
+        small_kernel,
+        out_shape=pltpu.HBM(slots.shape, slots.dtype),
+        in_specs=[SMEM, HBM, HBM],
+        out_specs=HBM,
+        scratch_shapes=[
+            pltpu.VMEM(got.shape, got.dtype), pltpu.VMEM((64, 3 * part), slots.dtype), pltpu.VMEM((width, width), BF16), square,
+            square, pltpu.VMEM((2 * rows, width), F32), pltpu.VMEM((taps, part), F32), pltpu.VMEM((8, rows, part), slots.dtype),
+            pltpu.SemaphoreType.DMA((3,)),
+        ],
+        input_output_aliases={2: 0},
+        compiler_params=pltpu.CompilerParams(vmem_limit_bytes=24 * 2**20),
+        cost_estimate=pl.CostEstimate(flops=18 * SCALE, bytes_accessed=0, transcendentals=0),
+    )(info, pltpu.with_memory_space_constraint(got, pltpu.HBM), pltpu.with_memory_space_constraint(slots, pltpu.HBM))
+
+
+def extra_kernel(rows, info, got, extra, packed):
+    gather_extra(got.ready(), info[0], rows, packed, extra)
 
 
 def aside_kernel(info, moment_mine, moment_back, moment_new):
@@ -708,10 +779,9 @@
     moment_new.ref[1 - side] = moment_back.ready()[...]
 
 
-def final_kernel(info, got, extra_mine, extra_came, mixer_weights, mlp_weights, norm_gains, gain_moment, taps, taps_moment, count,
-                 mixer_new, mlp_new, gain_moment_new, gains_new, taps_moment_new, taps_new, extra, packed):
+def final_kernel(info, got, extra_mine, mixer_weights, mlp_weights, norm_gains, gain_moment, taps, taps_moment, count,
+                 mixer_new, mlp_new, gain_moment_new, gains_new, taps_moment_new, taps_new, extra):
     me, row = info[0], info[2]
-    side = row % 2
     count = count.ready()
     _, rows, part = mixer_new.ref.shape
     hidden = mlp_new.ref.shape[2]
@@ -723,28 +793,21 @@
     rate = MATRIX_RATE * math.sqrt(4 * hidden / width)
     for which in range(2):
         old = mlp_weights[which, block_at(row, rows), :].astype(F32)
-        mlp_new.ref[which] = old - rate * got[4 * which + 1 + which, :rows, :].astype(F32)
+        mlp_new.ref[which] = old - rate * got[4 * which + 3, :rows, :].astype(F32)
     mlp_new.send()
-    here = side != 1 - me // 2
-
-    @pl.when(here)
+    @pl.when(me == 3)
     def _():
         extra[...] = extra_mine[...].astype(F32)
 
-    @pl.when(jnp.logical_not(here))
+    @pl.when(me != 3)
     def _():
-        extra[...] = extra_came[...].astype(F32)
-
-    dp, height, _ = extra.shape
+        extra[...] = got[keeper(me) ^ 4, :64, : 3 * part].astype(F32)
+
     total = taps.shape[0]
-    share = -(-total // dp)
-    gain = 0.0
-    for i in range(dp):
-        size = min(share, total - i * share)
-        if size > 0:
-            packed[i * share : i * share + size, :] = extra[i, :size, :]
-        gain = gain + (extra[i, height - 16 : height - 8, :] + extra[i, height - 8 :, :])
-    new = MOMENT_DECAY * taps_moment[...] + packed[...] / count[0:1, :]
+    grad = [extra[: min(64, total - 64 * g), g * part : (g + 1) * part] for g in range(-(-total // 64))]
+    at = (total // 64) * part
+    gain = extra[32:40, at : at + part] + extra[40:48, at : at + part]
+    new = MOMENT_DECAY * taps_moment[...] + jnp.concatenate(grad, 0) / count[0:1, :]
     taps_moment_new[...] = new
     scale = jnp.sqrt(jnp.mean(new * new, 0, keepdims=True)) + 1e-08
     taps_new[...] = taps[...] - KERNEL_RATE * new / scale
@@ -918,14 +981,7 @@
     (mlp_columns,) = call(
         columns_kernel, [((width, hidden), BF16)], [], (after(info, slots), *pair_pieces), 1000, 4
     )
-    mlp_pieces = [mlp_columns] + [
-        lax.ppermute(
-            mlp_columns,
-            ("dp", "tensor"),
-            [(8 * z + 4 * y + ((1 + y) ^ k), 8 * z + 4 * y + 1 + y) for z in range(pairs) for y in range(2)],
-        )
-        for k in (1, 2, 3)
-    ]
+    mlp_pieces = [mlp_columns] + [lax.ppermute(mlp_columns, "tensor", [(3 ^ k, 3)]) for k in (1, 2, 3)]
     moment_back = swap(moment_other, "dp", 1)
     input_grad, block_out = call(
         output_kernel,
@@ -939,16 +995,20 @@
         aside_kernel, [Store((2, rows, hidden), F32)], [], (after(info, slots), Late(moment_mine), Late(moment_back)), 1, 4
     )
     square = ((width, width), F32)
-    sends, extra = call(
-        step_kernel,
-        [((8, rows, hidden), piece_type), ((dp, slot + 16, part), BF16)],
-        [((width, width), BF16), ((width, 4 * hidden), BF16), square, square, ((2 * rows, width), F32),
-         ((2 * rows, width), F32)],
-        (after(info, block_out, mlp_moment_new), got, *(Late(v) for v in mlp_pieces)),
+    (sends,) = call(
+        large_kernel,
+        [Store((8, max(rows, 64), hidden), piece_type, True)],
+        [square, square, ((2 * rows, width), F32)],
+        (after(info, block_out, mlp_moment_new), *mlp_pieces),
         18, 24,
     )
+    all_got = got
+    sends = small_steps(after(info, sends), got, sends, rows, width, levels * taps)
     got = lax.all_to_all(sends.astype(BF16), ("dp", "tensor"), 0, 0, tiled=True, axis_index_groups=groups)
-    extra_came = swap(extra, "dp", 1)
+    (extra,) = call(
+        functools.partial(extra_kernel, rows), [((64, 3 * part), BF16)], [((levels * taps, part), F32)],
+        (after(info, sends), Late(all_got)), 0, 4,
+    )
     flat = (levels * taps, part)
     old = fetch(
         after(info, extra), 0, mixer_weights, mlp_weights, norm_gains, gain_moment, conv_kernel.reshape(flat),
@@ -958,8 +1018,8 @@
         final_kernel,
         [Store((3, rows, part), F32), Store((2, rows, hidden), F32), ((2, width), F32), ((2, width), F32), (flat, F32),
          (flat, F32)],
-        [((dp, slot + 16, part), F32), (flat, F32)],
-        (info, got.astype(piece_type), extra, extra_came, *old, Late(count)),
+        [((64, 3 * part), F32)],
+        (info, got.astype(piece_type), extra, *old, Late(count)),
         0, 8,
     )
     kernel_moment_new, kernel_new = (v.reshape(conv_kernel.shape) for v in (kernel_moment_new, kernel_new))

time: 162 us -> 158 us (0.975)
  starting transfers between devices: 71.2 us -> 62.4 us
  waiting for transfers between devices: 27.8 us -> 30.4 us
  Pallas kernels: 59.9 us -> 61.8 us
    ppermute x27 -> x26, waiting for transfers between devices: 22.9 us -> 16.1 us  [swap(): return lax.ppermute(value, axis, [(i, i ^ k) for i in range(size)])]
    ppermute x3, waiting for transfers between devices: 0.01 us -> 6.79 us  [per_device(): lax.ppermute(mlp_columns, 'tensor', [(3 ^ k, 3)])]
    all_to_all x1, starting transfers between devices: 23 us -> 16.6 us  [per_device(): lax.all_to_all(sends.astype(BF16), ('dp', 'tensor'), 0, 0, tiled=True, ax...]
    all_to_all x1, waiting for transfers between devices: 0.01 us -> 6.14 us  [per_device(): lax.all_to_all(sends.astype(BF16), ('dp', 'tensor'), 0, 0, tiled=True, ax...]
    all_to_all x1, waiting for transfers between devices: 3.63 us -> 0.01 us  [per_device(): got = lax.all_to_all(slots.astype(BF16), ('dp', 'tensor'), 0, 0, tiled=True)]
    ppermute x27 -> x26, starting transfers between devices: 33.8 us -> 31.4 us  [swap(): return lax.ppermute(value, axis, [(i, i ^ k) for i in range(size)])]
    pallas_call x0 -> x1, Pallas kernels: none -> 2.27 us  [small_steps(): pl.pallas_call(small_kernel, out_shape=pltpu.HBM(slots.shape, slots.dtype...]
    pallas_call x19 -> x20, Pallas kernels: 53.7 us -> 53.3 us  [call(): pl.pallas_call(body, out_shape=tuple((pltpu.HBM(o.shape, o.dtype) if isin...]
  transfers between devices with their start and end apart: 33 -> 32, of which waited for: 13 -> 13; matrix products, arithmetic and copies ran while one was open for 0% -> 0% of each run, Pallas kernels for 29% -> 32%
where the time goes in v2:
time: 158 us; the launch traced here: 157 us
  starting transfers between devices  62.4 us (39%)
  Pallas kernels  61.8 us (39%)
  waiting for transfers between devices  30.4 us (19%)
  between operations  1.89 us (1%)
    pallas_call x20, Pallas kernels, call(): pl.pallas_call(body, out_shape=tuple((pltpu.HBM(o.shape, o.dtype) if isin...  53.3 us
    ppermute x26, starting transfers between devices, swap(): return lax.ppermute(value, axis, [(i, i ^ k) for i in range(size)])  31.4 us
    all_to_all x1, starting transfers between devices, per_device(): lax.all_to_all(sends.astype(BF16), ('dp', 'tensor'), 0, 0, tiled=True, ax...  16.6 us
    ppermute x26, waiting for transfers between devices, swap(): return lax.ppermute(value, axis, [(i, i ^ k) for i in range(size)])  16.1 us
    ppermute x3, waiting for transfers between devices, per_device(): lax.ppermute(mlp_columns, 'tensor', [(3 ^ k, 3)])  6.79 us
    pallas_call x3, Pallas kernels, fetch(): pl.pallas_call(body, out_shape=tuple(shapes), in_specs=[SMEM] + [HBM] * l...  6.23 us
    all_to_all x1, waiting for transfers between devices, per_device(): lax.all_to_all(sends.astype(BF16), ('dp', 'tensor'), 0, 0, tiled=True, ax...  6.14 us
    all_to_all x1, starting transfers between devices, per_device(): arrived = lax.all_to_all(slots.astype(BF16), 'dp', 0, 0, tiled=True)  4.89 us
  transfers between devices with their start and end apart: 32, of which 13 were waited for; matrix products, arithmetic and copies ran while one was open for 0% of the time, Pallas kernels for 32%

profile of v2, /device:TPU:0, one launch (start us, length us, event | category | flops | bytes accessed | tf_op | source)
XLA Modules:
  0.0 156.6 jit_solution(390141938837641352)
XLA Ops:
  0.6 3.0 %collective-permute-start.1 = (bf16[1024,128]{1,0:T(8,128)(2,1)}, bf16[1024,128]{1,0:T(8,128)(2,1)S(1)}, u32[]{:S(2)}, u32[]{:S(2)}) collective-permute-start(bf16[1024,128]{1,0:T(8,128)(2,1)} %bitcast.17), channel_id=1, source_target_pairs={{0,2},{1,3},{2,0},{3,1},{4,6},{5,7},{6,4},{7,5},{8,10},{9,11},{10,... | collective-permute-start | bytes 786440 | tf_op jit(solution)/shard_map/ppermute | solution.py:133
  4.3 0.1 pad_add_fusion.token_ref.refs_0_.info
  4.4 2.1 %shard_map.222 = (bf16[1024,128]{1,0:T(8,128)(2,1)S(1)}, bf16[3,512,128]{2,1,0:T(8,128)(2,1)S(1)}, f32[2,512]{1,0:T(2,128)S(1)}, bf16[2,512,256]{2,1,0:T(8,128)(...) custom-call(s32[3]{0:T(128)S(1)} %pad_add_fusion.token_ref.refs_0_.info, ...), custom_call_target="tpu_custom_call" | custom-call | flops 10000000000 | tf_op jit(solution)/shard_map/pallas_call | solution.py:321
  6.5 0.2 collective-permute-start.6
  6.7 3.1 %shard_map.223.refs_9_.refs_12_ = f32[2048,128]{1,0:T(8,128)S(1)} custom-call(s32[3]{0:T(128)S(1)} %pad_add_fusion.token_ref.refs_0_.info, bf16[2,2048,160]{2,1,0:T(8,128)(2,1)} %constant.19.clone.refs_1_, f32[160,128]{1,0:T(8,128)} %bitcast.13), custom_call_target="tpu_custom_call" | custom-call | flops 20000000000 | tf_op jit(solution)/shard_map/pallas_call | solution.py:287
  9.8 0.8 collective-permute-done.1.refs_3_
  10.7 0.5 collective-permute-start.5
  11.2 1.0 collective-permute-done.2.refs_4_
  12.2 3.6 %shard_map.224 = (bf16[1024,512]{1,0:T(8,128)(2,1)S(1)}, bf16[1024,512]{1,0:T(8,128)(2,1)S(1)}, f32[1024,128]{1,0:T(8,128)}, f32[1024,1]{1,0:T(8,128)}, f32[512,...) custom-call(s32[3]{0:T(128)S(1)} %pad_add_fusion.token_ref.refs_0_.i, ...), custom_call_target="tpu_custom_call" | custom-call | flops 1000000 | tf_op jit(solution)/shard_map/pallas_call | solution.py:287
  15.9 2.7 %collective-permute-done.6.refs_3_ = bf16[1536,128]{1,0:T(8,128)(2,1)S(1)} collective-permute-done((bf16[1536,128]{1,0:T(8,128)(2,1)S(1)}, bf16[1536,128]{1,0:T(8,128)(2,1)S(1)}, u32[]{:S(2)}, u32[]{:S(2)}) %collective-permute-start.6) | collective-permute-done | bytes 393248 | tf_op jit(solution)/shard_map/ppermute | solution.py:133
  18.6 1.7 %collective-permute-start.4 = (bf16[1024,128]{1,0:T(8,128)(2,1)S(1)}, bf16[1024,128]{1,0:T(8,128)(2,1)S(1)}, u32[]{:S(2)}, u32[]{:S(2)}) collective-permute-start(bf16[1024,128]{1,0:T(8,128)(2,1)S(1)} %get-tuple-element.103.refs_1_.refs_9_), channel_id=1, source_target_pairs={{0,2},{1,3},{2,0},{3,1},{4,6},{5,7},{6,4},{7,5},{8,10},{9,11},{10,... | collective-permute-start | bytes 786440 | tf_op jit(solution)/shard_map/ppermute | solution.py:133
  20.3 0.2 collective-permute-start.3
  20.6 2.7 %shard_map.225 = (bf16[1024,512]{1,0:T(8,128)(2,1)S(1)}, bf16[512,512]{1,0:T(8,128)(2,1)S(1)}, f32[1024,512]{1,0:T(8,128)S(1)}, bf16[2,512,512]{2,1,0:T(8,128)(2,1)S(1)}) custom-call(s32[3]{0:T(128)S(1)} %pad_add_fusion.token_ref.refs_0_.info, bf16[1536,128]{1,0:T(8,128)(2,1)S(1)} %get-tuple-element.105.refs_1_, ...), custom_call_target="tpu_custom_call" | custom-call | flops 30000001024 | tf_op jit(solution)/shard_map/pallas_call | solution.py:287
  23.3 4.0 %collective-permute-done.4.refs_3_ = bf16[1024,128]{1,0:T(8,128)(2,1)S(1)} collective-permute-done((bf16[1024,128]{1,0:T(8,128)(2,1)S(1)}, bf16[1024,128]{1,0:T(8,128)(2,1)S(1)}, u32[]{:S(2)}, u32[]{:S(2)}) %collective-permute-start.4) | collective-permute-done | bytes 262176 | tf_op jit(solution)/shard_map/ppermute | solution.py:133
  27.3 1.5 collective-permute-done.8.refs_4_
  28.9 5.9 %shard_map.226 = (bf16[512,512]{1,0:T(8,128)(2,1)S(1)}, f32[512,512]{1,0:T(8,128)S(1)}, bf16[1024,512]{1,0:T(8,128)(2,1)S(1)}, bf16[1024,512]{1,0:T(8,128)(2,1)S...) custom-call(s32[3]{0:T(128)S(1)} %pad_add_fusion.token_ref.refs_0_.inf, ...), custom_call_target="tpu_custom_call" | custom-call | flops 60000002048 | tf_op jit(solution)/shard_map/pallas_call | solution.py:287
  34.8 0.2 collective-permute-start.9
  35.0 1.8 %collective-permute-done.9.refs_2_ = bf16[2,256,512]{2,1,0:T(8,128)(2,1)S(1)} collective-permute-done((bf16[2,256,512]{2,1,0:T(8,128)(2,1)S(1)}, bf16[2,256,512]{2,1,0:T(8,128)(2,1)S(1)}, u32[]{:S(2)}, u32[]{:S(2)}) %collective-permute-start.9) | collective-permute-done | bytes 524320 | tf_op jit(solution)/shard_map/ppermute | solution.py:133
  36.7 1.3 shard_map.227
  38.0 1.7 %collective-permute-start.11 = (bf16[256,512]{1,0:T(8,128)(2,1)}, bf16[256,512]{1,0:T(8,128)(2,1)}, u32[]{:S(2)}, u32[]{:S(2)}) collective-permute-start(bf16[256,512]{1,0:T(8,128)(2,1)} %get-tuple-element.115), channel_id=1, source_target_pairs={{0,2},{1,3},{2,0},{3,1},{4,6},{5,7},{6,4},{7,5},{8,10},{9,11},{10,... | collective-permute-start | bytes 786440 | tf_op jit(solution)/shard_map/ppermute | solution.py:133
  39.8 2.3 %shard_map.228 = (bf16[528,512]{1,0:T(8,128)(2,1)}, f32[64,512]{1,0:T(8,128)S(1)}) custom-call(s32[3]{0:T(128)S(1)} %pad_add_fusion.token_ref.refs_0_.info, bf16[1024,512]{1,0:T(8,128)(2,1)S(1)} %get-tuple-element.117.refs_1_, bf16[1024,512]{1,0:T(8,128)(2,1)S(1)} %get-tuple-element.118.refs_2_.refs_1_, bf16[1024,512]{1,0:T(8,128)(2,1)S(1)} %get-tuple-element.119.refs_3_, ...), custom_call_target="tpu_custom_call" | custom-call | flops 20000000000 | tf_op jit(solution)/shard_map/pallas_call | solution.py:287
  42.1 1.6 %collective-permute-start.10 = (bf16[528,512]{1,0:T(8,128)(2,1)}, bf16[528,512]{1,0:T(8,128)(2,1)}, u32[]{:S(2)}, u32[]{:S(2)}) collective-permute-start(bf16[528,512]{1,0:T(8,128)(2,1)} %get-tuple-element.121), channel_id=1, source_target_pairs={{0,4},{4,0},{8,12},{12,8},{16,20},{20,16},{24,28},{28,24},{1,5},{5... | collective-permute-start | bytes 1622024 | tf_op jit(solution)/shard_map/ppermute | solution.py:133
  43.7 1.5 shard_map.229.refs_1_
  45.2 1.5 collective-permute-done.11.refs_2_
  46.7 1.3 shard_map.231
  48.0 1.8 %collective-permute-start.13 = (bf16[256,512]{1,0:T(8,128)(2,1)S(1)}, bf16[256,512]{1,0:T(8,128)(2,1)S(1)}, u32[]{:S(2)}, u32[]{:S(2)}) collective-permute-start(bf16[256,512]{1,0:T(8,128)(2,1)S(1)} %get-tuple-element.129.refs_1_), channel_id=1, source_target_pairs={{0,2},{1,3},{2,0},{3,1},{4,6},{5,7},{6,4},{7,5},{8,10},{9,11},{10,... | collective-permute-start | bytes 786440 | tf_op jit(solution)/shard_map/ppermute | solution.py:133
  49.8 2.1 %shard_map.232.refs_15_ = bf16[2,256,2048]{2,1,0:T(8,128)(2,1)S(1)} custom-call(s32[3]{0:T(128)S(1)} %pad_add_fusion.token_ref.refs_0_.info, bf16[2,256,2048]{2,1,0:T(8,128)(2,1)} %constant.20.clone.refs_0_), custom_call_target="tpu_custom_call" | custom-call | flops 1000000 | tf_op jit(solution)/shard_map/pallas_call | solution.py:321
  52.0 2.6 %shard_map.233 = (bf16[2,1024,128]{2,1,0:T(8,128)(2,1)}, f32[2,1024,128]{2,1,0:T(8,128)}) custom-call(s32[3]{0:T(128)S(1)} %pad_add_fusion.token_ref.refs_0_.info, bf16[1024,512]{1,0:T(8,128)(2,1)S(1)} %copy-done.12, bf16[2,512,512]{2,1,0:T(8,128)(2,1)S(1)} %get-tuple-element.112.refs_8_.refs_2_), custom_call_target="tpu_custom_call" | custom-call | flops 10000000000 | tf_op jit(solution)/shard_map/pallas_call | solution.py:287
  54.6 1.0 collective-permute-done.13.refs_3_
  55.6 0.5 collective-permute-start.20
  56.1 0.4 collective-permute-done.10.refs_2_
  56.5 1.8 %shard_map.230 = (bf16[144,512]{1,0:T(8,128)(2,1)S(1)}, bf16[144,512]{1,0:T(8,128)(2,1)}, bf16[144,512]{1,0:T(8,128)(2,1)S(1)}, bf16[144,512]{1,0:T(8,128)(2,1)S(1)}) custom-call(s32[3]{0:T(128)S(1)} %pad_add_fusion.token_ref.refs_0_.info, f32[528,512]{1,0:T(8,128)S(1)} %shard_map.229.refs_1_, bf16[528,512]{1,0:T(8,128)(2,1)} %collective-permute-done.10.refs_2_), custom_call_target="tpu_custom_call" | custom-call | flops 1000000 | tf_op jit(solution)/shard_map/pallas_call | solution.py:287
  58.4 7.1 %shard_map.234 = (bf16[8,224,128]{2,1,0:T(8,128)(2,1)}, bf16[2,1056,128]{2,1,0:T(8,128)(2,1)}, f32[2,1056,128]{2,1,0:T(8,128)}, bf16[1024,128]{1,0:T(8,128)(2,1)}) custom-call(s32[3]{0:T(128)S(1)} %pad_add_fusion.token_ref.refs_0_.info, bf16[256,512]{1,0:T(8,128)(2,1)S(1)} %get-tuple-element.129.refs_1_, ...), custom_call_target="tpu_custom_call" | custom-call | flops 9999999827968 | tf_op jit(solution)/shard_map/pallas_call | solution.py:287
  65.5 0.1 collective-permute-start.19
  65.5 1.6 %collective-permute-start.16 = (bf16[144,512]{1,0:T(8,128)(2,1)}, bf16[144,512]{1,0:T(8,128)(2,1)}, u32[]{:S(2)}, u32[]{:S(2)}) collective-permute-start(bf16[144,512]{1,0:T(8,128)(2,1)} %get-tuple-element.142), channel_id=1, source_target_pairs={{0,8},{4,12},{8,0},{12,4},{16,24},{20,28},{24,16},{28,20},{1,9},{5... | collective-permute-start | bytes 442376 | tf_op jit(solution)/shard_map/ppermute | solution.py:133
  67.2 2.6 %collective-permute-start.17 = (bf16[144,512]{1,0:T(8,128)(2,1)S(1)}, bf16[144,512]{1,0:T(8,128)(2,1)}, u32[]{:S(2)}, u32[]{:S(2)}) collective-permute-start(bf16[144,512]{1,0:T(8,128)(2,1)S(1)} %get-tuple-element.143), channel_id=1, source_target_pairs={{0,16},{4,20},{8,24},{12,28},{16,0},{20,4},{24,8},{28,12},{1,17},{... | collective-permute-start | bytes 442376 | tf_op jit(solution)/shard_map/ppermute | solution.py:133
  69.8 0.2 collective-permute-start.18
  70.0 1.5 collective-permute-start.15
  71.5 4.9 %all-to-all-start = ((bf16[8,224,128]{2,1,0:T(8,128)(2,1)}), bf16[8,224,128]{2,1,0:T(8,128)(2,1)S(1)}, u32[]{:S(2)}, u32[]{:S(2)}) async-start(bf16[8,224,128]{2,1,0:T(8,128)(2,1)} %get-tuple-element.140), calls=%async_computation | async-start | bytes 917504 | tf_op jit(solution)/shard_map/all_to_all | solution.py:952
  76.4 2.8 %shard_map.236 = (f32[1024,128]{1,0:T(8,128)S(1)}, f32[32,128]{1,0:T(8,128)S(1)}, f32[1024,128]{1,0:T(8,128)S(1)}, bf16[2080,128]{1,0:T(8,128)(2,1)S(1)}) custom-call(s32[3]{0:T(128)S(1)} %pad_add_fusion.token_ref.refs_0_.info, f32[2,1056,128]{2,1,0:T(8,128)} %get-tuple-element.146.refs_1_, bf16[2,1056,128]{2,1,0:T(8,128)(2,1)S(1)} %collective-permute-done.19.refs_2_, ...), custom_call_target="tpu_custom_call" | custom-call | flops 1000000 | tf_op jit(solution)/shard_map/pallas_call | solution.py:287
  79.2 1.4 collective-permute-start.21
  80.6 1.2 collective-permute-done.17.refs_5_
  81.9 2.7 %shard_map.235 = (bf16[128,512]{1,0:T(8,128)(2,1)}, f32[64,512]{1,0:T(8,128)}, f32[64,512]{1,0:T(8,128)}, f32[8,128]{1,0:T(8,128)}) custom-call(s32[3]{0:T(128)S(1)} %pad_add_fusion.token_ref.refs_0_.info, f32[2,64,512]{2,1,0:T(8,128)S(1)} %copy-done.8, f32[64,512]{1,0:T(8,128)} %collective-permute-done.15.refs_2_, ...), custom_call_target="tpu_custom_call" | custom-call | flops 10000000000 | tf_op jit(solution)/shard_map/pallas_call | solution.py:287
  84.6 4.4 %collective-permute-start.25 = (bf16[128,512]{1,0:T(8,128)(2,1)}, bf16[128,512]{1,0:T(8,128)(2,1)}, u32[]{:S(2)}, u32[]{:S(2)}) collective-permute-start(bf16[128,512]{1,0:T(8,128)(2,1)} %get-tuple-element.165.refs_1_), channel_id=1, source_target_pairs={{0,24},{4,28},{8,16},{12,20},{16,8},{20,12},{24,0},{28,4},{1,25},{... | collective-permute-start | bytes 393224 | tf_op jit(solution)/shard_map/ppermute | solution.py:133
  89.0 6.6 %collective-permute-start.24 = (bf16[128,512]{1,0:T(8,128)(2,1)}, bf16[128,512]{1,0:T(8,128)(2,1)}, u32[]{:S(2)}, u32[]{:S(2)}) collective-permute-start(bf16[128,512]{1,0:T(8,128)(2,1)} %get-tuple-element.165.refs_1_), channel_id=1, source_target_pairs={{0,16},{4,20},{8,24},{12,28},{16,0},{20,4},{24,8},{28,12},{1,17},{... | collective-permute-start | bytes 393224 | tf_op jit(solution)/shard_map/ppermute | solution.py:133
  95.5 0.1 collective-permute-start.23
  95.6 1.4 collective-permute-start.22
  97.0 1.3 all-to-all-done.refs_1_
  98.4 2.5 %shard_map.237 = (f32[3,64,128]{2,1,0:T(8,128)}, bf16[32,64,128]{2,1,0:T(8,128)(2,1)}, bf16[2080,128]{1,0:T(8,128)(2,1)}) custom-call(s32[3]{0:T(128)S(1)} %pad_add_fusion.token_ref.refs_0_.info, bf16[8,224,128]{2,1,0:T(8,128)(2,1)S(1)} %all-to-all-done.refs_1_, f32[3,64,128]{2,1,0:T(8,128)} %refs_2_.4, f32[8,128]{1,0:T(8,128)} %get-tuple-element.145.refs_3_.refs_9_, ...), custom_call_target="tpu_custom_call" | custom-call | flops 9999999827968 | tf_op jit(solution)/shard_map/pallas_call | solution.py:287
  100.9 4.7 %all-to-all-start.1 = ((bf16[32,64,128]{2,1,0:T(8,128)(2,1)}), bf16[32,64,128]{2,1,0:T(8,128)(2,1)}, u32[]{:S(2)}, u32[]{:S(2)}) async-start(bf16[32,64,128]{2,1,0:T(8,128)(2,1)} %get-tuple-element.151), calls=%async_computation.1 | async-start | bytes 1048576 | tf_op jit(solution)/shard_map/all_to_all | solution.py:980
  105.6 1.2 shard_map.240.refs_1_
  106.8 3.4 %collective-permute-start.28 = (bf16[512,512]{1,0:T(8,128)(2,1)S(1)}, bf16[512,512]{1,0:T(8,128)(2,1)S(1)}, u32[]{:S(2)}, u32[]{:S(2)}) collective-permute-start(bf16[512,512]{1,0:T(8,128)(2,1)S(1)} %shard_map.240.refs_1_), channel_id=1, source_target_pairs={{0,3},{4,7},{8,11},{12,15},{16,19},{20,23},{24,27},{28,31}} | collective-permute-start | bytes 1572872 | tf_op jit(solution)/shard_map/ppermute | solution.py:984
  110.2 0.7 collective-permute-start.27
  110.9 0.7 collective-permute-start.26
  111.6 3.6 %shard_map.238 = (f32[1024,128]{1,0:T(8,128)}, bf16[1024,128]{1,0:T(8,128)(2,1)}) custom-call(s32[3]{0:T(128)S(1)} %pad_add_fusion.token_ref.refs_0_.info, f32[1024,128]{1,0:T(8,128)S(1)} %get-tuple-element.153.refs_1_, bf16[2080,128]{1,0:T(8,128)(2,1)} %get-tuple-element.154.refs_2_, f32[1024,128]{1,0:T(8,128)S(1)} %get-tuple-element.155.refs_3_, ...), custom_call_target="tpu_custom_call" | custom-call | flops 1000000 | tf_op jit(solution)/shard_map/pallas_call | solution.py:287
  115.2 2.2 %shard_map.239 = f32[2,64,512]{2,1,0:T(8,128)} custom-call(s32[3]{0:T(128)S(1)} %pad_add_fusion.token_ref.refs_0_.info, f32[64,512]{1,0:T(8,128)} %get-tuple-element.162.refs_1_, f32[64,512]{1,0:T(8,128)} %collective-permute-done.22.refs_2_), custom_call_target="tpu_custom_call" | custom-call | flops 10000000000 | tf_op jit(solution)/shard_map/pallas_call | solution.py:287
  117.5 6.8 %collective-permute-done.28.refs_4_ = bf16[512,512]{1,0:T(8,128)(2,1)S(1)} collective-permute-done((bf16[512,512]{1,0:T(8,128)(2,1)S(1)}, bf16[512,512]{1,0:T(8,128)(2,1)S(1)}, u32[]{:S(2)}, u32[]{:S(2)}) %collective-permute-start.28) | collective-permute-done | bytes 524320 | tf_op jit(solution)/shard_map/ppermute | solution.py:984
  124.3 0.8 shard_map.241.slots
  125.1 2.3 %shard_map.242 = bf16[8,64,512]{2,1,0:T(8,128)(2,1)} custom-call(s32[3]{0:T(128)S(1)} %pad_add_fusion.token_ref.refs_0_.info, bf16[32,64,128]{2,1,0:T(8,128)(2,1)} %all-to-all-done.1.source.refs_1_, bf16[8,64,512]{2,1,0:T(8,128)(2,1)} %shard_map.241.slots), custom_call_target="tpu_custom_call", output_to_operand_aliasing={{}: (2, {})} | custom-call | flops 179999997952 | tf_op jit(solution)/shard_map/pallas_call | solution.py:756
  127.4 16.6 %all-to-all-start.2 = ((bf16[8,64,512]{2,1,0:T(8,128)(2,1)}), bf16[8,64,512]{2,1,0:T(8,128)(2,1)S(1)}, u32[]{:S(2)}, u32[]{:S(2)}) async-start(bf16[8,64,512]{2,1,0:T(8,128)(2,1)} %shard_map.242), calls=%async_computation.2 | async-start | bytes 1048576 | tf_op jit(solution)/shard_map/all_to_all | solution.py:1007
  144.0 1.6 %shard_map.243.refs_2_ = bf16[64,384]{1,0:T(8,128)(2,1)S(1)} custom-call(s32[3]{0:T(128)S(1)} %pad_add_fusion.token_ref.refs_0_.info, bf16[32,64,128]{2,1,0:T(8,128)(2,1)} %all-to-all-done.1.source.refs_1_), custom_call_target="tpu_custom_call" | custom-call | flops 1000000 | tf_op jit(solution)/shard_map/pallas_call | solution.py:287
  145.6 2.0 %shard_map.244 = (bf16[3,512,128]{2,1,0:T(8,128)(2,1)S(1)}, bf16[2,512,512]{2,1,0:T(8,128)(2,1)S(1)}, f32[2,512]{1,0:T(2,128)S(1)}, f32[2,512]{1,0:T(2,128)S(1)}...) custom-call(s32[3]{0:T(128)S(1)} %pad_add_fusion.token_ref.refs_0_.info, bf16[3,512,128]{2,1,0:T(8,128)(2,1)} %refs_0_.2, ...), custom_call_target="tpu_custom_call" | custom-call | flops 1000000 | tf_op jit(solution)/shard_map/pallas_call | solution.py:321
  147.6 6.1 %all-to-all-done.2.refs_1_ = bf16[8,64,512]{2,1,0:T(8,128)(2,1)S(1)} async-done(((bf16[8,64,512]{2,1,0:T(8,128)(2,1)}), bf16[8,64,512]{2,1,0:T(8,128)(2,1)S(1)}, u32[]{:S(2)}, u32[]{:S(2)}) %all-to-all-start.2) | async-done | bytes 524320 | tf_op jit(solution)/shard_map/all_to_all | solution.py:1007
  153.7 2.7 %shard_map.245 = (f32[3,64,128]{2,1,0:T(8,128)}, f32[2,64,512]{2,1,0:T(8,128)}, f32[2,512]{1,0:T(2,128)}, f32[2,512]{1,0:T(2,128)}, f32[160,128]{1,0:T(8,128)}, /*index=5*/f32[160,128]{1,0:T(8,128)}) custom-call(s32[3]{0:T(128)S(1)} %pad_add_fusion.token_ref.refs_0_.info, bf16[8,64,512]{2,1,0:T(8,128)(2,1)S(1)} %all-to-all-done.2.refs_1_, ...), custom_call_target="tpu_custom_call" | custom-call | flops 1000000 | tf_op jit(solution)/shard_map/pallas_call | solution.py:287
  (51 shorter events, 0.1 us)
Async XLA Ops:
  0.6 10.0 %collective-permute-start.1 = (bf16[1024,128]{1,0:T(8,128)(2,1)}, bf16[1024,128]{1,0:T(8,128)(2,1)S(1)}, u32[]{:S(2)}, u32[]{:S(2)}) collective-permute-start(bf16[1024,128]{1,0:T(8,128)(2,1)} %bitcast.17), channel_id=1, source_target_pairs={{0,2},{1,3},{2,0},{3,1},{4,6},{5,7},{6,4},{7,5},{8,10},{9,11},{10,... | collective-permute-start | bytes 786440 | tf_op jit(solution)/shard_map/ppermute | solution.py:133
  3.6 7.5 %collective-permute-start = (bf16[1024,128]{1,0:T(8,128)(2,1)}, bf16[1024,128]{1,0:T(8,128)(2,1)S(1)}, u32[]{:S(2)}, u32[]{:S(2)}) collective-permute-start(bf16[1024,128]{1,0:T(8,128)(2,1)} %bitcast.18), channel_id=1, source_target_pairs={{0,1},{1,0},{2,3},{3,2},{4,5},{5,4},{6,7},{7,6},{8,9},{9,8},{10,11... | collective-permute-start | bytes 786440 | tf_op jit(solution)/shard_map/ppermute | solution.py:133
  6.5 5.7 %copy-start.2 = (bf16[2,512,256]{2,1,0:T(8,128)(2,1)}, bf16[2,512,256]{2,1,0:T(8,128)(2,1)S(1)}, u32[]{:S(2)}) copy-start(bf16[2,512,256]{2,1,0:T(8,128)(2,1)S(1)} %get-tuple-element.101.refs_7_.refs_13_) | copy-start | bytes 1572868
  6.5 5.7 %copy-start.4 = (bf16[2,256,512]{2,1,0:T(8,128)(2,1)}, bf16[2,256,512]{2,1,0:T(8,128)(2,1)S(1)}, u32[]{:S(2)}) copy-start(bf16[2,256,512]{2,1,0:T(8,128)(2,1)S(1)} %get-tuple-element.102.refs_8_.refs_14_) | copy-start | bytes 1572868
  6.5 5.7 %copy-start.6 = (bf16[3,512,128]{2,1,0:T(8,128)(2,1)}, bf16[3,512,128]{2,1,0:T(8,128)(2,1)S(1)}, u32[]{:S(2)}) copy-start(bf16[3,512,128]{2,1,0:T(8,128)(2,1)S(1)} %get-tuple-element.99.refs_5_) | copy-start | bytes 1179652
  6.5 12.1 %collective-permute-start.6 = (bf16[1536,128]{1,0:T(8,128)(2,1)S(1)}, bf16[1536,128]{1,0:T(8,128)(2,1)S(1)}, u32[]{:S(2)}, u32[]{:S(2)}) collective-permute-start(bf16[1536,128]{1,0:T(8,128)(2,1)S(1)} %get-tuple-element.105.refs_1_), channel_id=1, source_target_pairs={{0,2},{1,3},{2,0},{3,1},{4,6},{5,7},{6,4},{7,5},{8,10},{9,11},{10,... | collective-permute-start | bytes 1179656 | tf_op jit(solution)/shard_map/ppermute | solution.py:133
  9.8 13.5 %copy-start = (f32[2048,128]{1,0:T(8,128)}, f32[2048,128]{1,0:T(8,128)S(1)}, u32[]{:S(2)}) copy-start(f32[2048,128]{1,0:T(8,128)S(1)} %shard_map.223.refs_9_.refs_12_) | copy-start | bytes 3145732
  10.7 1.5 collective-permute-start.2
  10.7 9.9 %collective-permute-start.5 = (bf16[1536,128]{1,0:T(8,128)(2,1)S(1)}, bf16[1536,128]{1,0:T(8,128)(2,1)S(1)}, u32[]{:S(2)}, u32[]{:S(2)}) collective-permute-start(bf16[1536,128]{1,0:T(8,128)(2,1)S(1)} %get-tuple-element.105.refs_1_), channel_id=1, source_target_pairs={{0,1},{1,0},{2,3},{3,2},{4,5},{5,4},{6,7},{7,6},{8,9},{9,8},{10,11... | collective-permute-start | bytes 1179656 | tf_op jit(solution)/shard_map/ppermute | solution.py:133
  15.9 13.0 %copy-start.9 = (f32[2,512]{1,0:T(2,128)}, f32[2,512]{1,0:T(2,128)S(1)}, u32[]{:S(2)}) copy-start(f32[2,512]{1,0:T(2,128)S(1)} %get-tuple-element.111.refs_7_.refs_6_.refs_16_) | copy-start | bytes 12292
  18.6 2.0 %collective-permute-start.7 = (bf16[1536,128]{1,0:T(8,128)(2,1)S(1)}, bf16[1536,128]{1,0:T(8,128)(2,1)S(1)}, u32[]{:S(2)}, u32[]{:S(2)}) collective-permute-start(bf16[1536,128]{1,0:T(8,128)(2,1)S(1)} %collective-permute-done.6.refs_3_), channel_id=1, source_target_pairs={{0,1},{1,0},{2,3},{3,2},{4,5},{5,4},{6,7},{7,6},{8,9},{9,8},{10,11... | collective-permute-start | bytes 1179656 | tf_op jit(solution)/shard_map/ppermute | solution.py:133
  18.6 8.7 %collective-permute-start.4 = (bf16[1024,128]{1,0:T(8,128)(2,1)S(1)}, bf16[1024,128]{1,0:T(8,128)(2,1)S(1)}, u32[]{:S(2)}, u32[]{:S(2)}) collective-permute-start(bf16[1024,128]{1,0:T(8,128)(2,1)S(1)} %get-tuple-element.103.refs_1_.refs_9_), channel_id=1, source_target_pairs={{0,2},{1,3},{2,0},{3,1},{4,6},{5,7},{6,4},{7,5},{8,10},{9,11},{10,... | collective-permute-start | bytes 786440 | tf_op jit(solution)/shard_map/ppermute | solution.py:133
  20.3 7.0 %collective-permute-start.3 = (bf16[1024,128]{1,0:T(8,128)(2,1)S(1)}, bf16[1024,128]{1,0:T(8,128)(2,1)S(1)}, u32[]{:S(2)}, u32[]{:S(2)}) collective-permute-start(bf16[1024,128]{1,0:T(8,128)(2,1)S(1)} %get-tuple-element.103.refs_1_.refs_9_), channel_id=1, source_target_pairs={{0,1},{1,0},{2,3},{3,2},{4,5},{5,4},{6,7},{7,6},{8,9},{9,8},{10,11... | collective-permute-start | bytes 786440 | tf_op jit(solution)/shard_map/ppermute | solution.py:133
  27.3 1.5 collective-permute-start.8
  34.7 8.9 %copy-start.11 = (bf16[1024,512]{1,0:T(8,128)(2,1)}, bf16[1024,512]{1,0:T(8,128)(2,1)S(1)}, u32[]{:S(2)}) copy-start(bf16[1024,512]{1,0:T(8,128)(2,1)S(1)} %get-tuple-element.118.refs_2_.refs_1_) | copy-start | bytes 3145732
  34.8 2.0 %collective-permute-start.9 = (bf16[2,256,512]{2,1,0:T(8,128)(2,1)S(1)}, bf16[2,256,512]{2,1,0:T(8,128)(2,1)S(1)}, u32[]{:S(2)}, u32[]{:S(2)}) collective-permute-start(bf16[2,256,512]{2,1,0:T(8,128)(2,1)S(1)} %bitcast.11), channel_id=1, source_target_pairs={{0,1},{1,0},{2,3},{3,2},{4,5},{5,4},{6,7},{7,6},{8,9},{9,8},{10,11... | collective-permute-start | bytes 1572872 | tf_op jit(solution)/shard_map/ppermute | solution.py:133
  38.0 8.7 %collective-permute-start.11 = (bf16[256,512]{1,0:T(8,128)(2,1)}, bf16[256,512]{1,0:T(8,128)(2,1)}, u32[]{:S(2)}, u32[]{:S(2)}) collective-permute-start(bf16[256,512]{1,0:T(8,128)(2,1)} %get-tuple-element.115), channel_id=1, source_target_pairs={{0,2},{1,3},{2,0},{3,1},{4,6},{5,7},{6,4},{7,5},{8,10},{9,11},{10,... | collective-permute-start | bytes 786440 | tf_op jit(solution)/shard_map/ppermute | solution.py:133
  42.1 14.4 %collective-permute-start.10 = (bf16[528,512]{1,0:T(8,128)(2,1)}, bf16[528,512]{1,0:T(8,128)(2,1)}, u32[]{:S(2)}, u32[]{:S(2)}) collective-permute-start(bf16[528,512]{1,0:T(8,128)(2,1)} %get-tuple-element.121), channel_id=1, source_target_pairs={{0,4},{4,0},{8,12},{12,8},{16,20},{20,16},{24,28},{28,24},{1,5},{5... | collective-permute-start | bytes 1622024 | tf_op jit(solution)/shard_map/ppermute | solution.py:133
  43.7 3.0 %copy-start.10 = (f32[2,512]{1,0:T(2,128)S(1)}, f32[2,512]{1,0:T(2,128)}, u32[]{:S(2)}) copy-start(f32[2,512]{1,0:T(2,128)} %copy-done.9) | copy-start | bytes 12292
  48.0 4.0 %copy-start.12 = (bf16[1024,512]{1,0:T(8,128)(2,1)S(1)}, bf16[1024,512]{1,0:T(8,128)(2,1)}, u32[]{:S(2)}) copy-start(bf16[1024,512]{1,0:T(8,128)(2,1)} %copy-done.11) | copy-start | bytes 3145732
  48.0 7.6 %collective-permute-start.13 = (bf16[256,512]{1,0:T(8,128)(2,1)S(1)}, bf16[256,512]{1,0:T(8,128)(2,1)S(1)}, u32[]{:S(2)}, u32[]{:S(2)}) collective-permute-start(bf16[256,512]{1,0:T(8,128)(2,1)S(1)} %get-tuple-element.129.refs_1_), channel_id=1, source_target_pairs={{0,2},{1,3},{2,0},{3,1},{4,6},{5,7},{6,4},{7,5},{8,10},{9,11},{10,... | collective-permute-start | bytes 786440 | tf_op jit(solution)/shard_map/ppermute | solution.py:133
  49.8 8.5 %collective-permute-start.12 = (bf16[256,512]{1,0:T(8,128)(2,1)S(1)}, bf16[256,512]{1,0:T(8,128)(2,1)S(1)}, u32[]{:S(2)}, u32[]{:S(2)}) collective-permute-start(bf16[256,512]{1,0:T(8,128)(2,1)S(1)} %get-tuple-element.129.refs_1_), channel_id=1, source_target_pairs={{0,1},{1,0},{2,3},{3,2},{4,5},{5,4},{6,7},{7,6},{8,9},{9,8},{10,11... | collective-permute-start | bytes 786440 | tf_op jit(solution)/shard_map/ppermute | solution.py:133
  52.0 6.3 %copy-start.1 = (f32[2048,128]{1,0:T(8,128)S(1)}, f32[2048,128]{1,0:T(8,128)}, u32[]{:S(2)}) copy-start(f32[2048,128]{1,0:T(8,128)} %copy-done) | copy-start | bytes 3145732
  52.0 6.3 %copy-start.3 = (bf16[2,512,256]{2,1,0:T(8,128)(2,1)S(1)}, bf16[2,512,256]{2,1,0:T(8,128)(2,1)}, u32[]{:S(2)}) copy-start(bf16[2,512,256]{2,1,0:T(8,128)(2,1)} %copy-done.2) | copy-start | bytes 1572868
  52.0 6.3 %copy-start.5 = (bf16[2,256,512]{2,1,0:T(8,128)(2,1)S(1)}, bf16[2,256,512]{2,1,0:T(8,128)(2,1)}, u32[]{:S(2)}) copy-start(bf16[2,256,512]{2,1,0:T(8,128)(2,1)} %copy-done.4) | copy-start | bytes 1572868
  52.0 6.3 %copy-start.7 = (bf16[3,512,128]{2,1,0:T(8,128)(2,1)S(1)}, bf16[3,512,128]{2,1,0:T(8,128)(2,1)}, u32[]{:S(2)}) copy-start(bf16[3,512,128]{2,1,0:T(8,128)(2,1)} %copy-done.6) | copy-start | bytes 1179652
  55.6 2.7 %collective-permute-start.14 = (bf16[256,512]{1,0:T(8,128)(2,1)S(1)}, bf16[256,512]{1,0:T(8,128)(2,1)S(1)}, u32[]{:S(2)}, u32[]{:S(2)}) collective-permute-start(bf16[256,512]{1,0:T(8,128)(2,1)S(1)} %collective-permute-done.13.refs_3_), channel_id=1, source_target_pairs={{0,1},{1,0},{2,3},{3,2},{4,5},{5,4},{6,7},{7,6},{8,9},{9,8},{10,11... | collective-permute-start | bytes 786440 | tf_op jit(solution)/shard_map/ppermute | solution.py:133
  55.6 14.4 %collective-permute-start.20 = (bf16[2,1024,128]{2,1,0:T(8,128)(2,1)}, bf16[2,1024,128]{2,1,0:T(8,128)(2,1)}, u32[]{:S(2)}, u32[]{:S(2)}) collective-permute-start(bf16[2,1024,128]{2,1,0:T(8,128)(2,1)} %get-tuple-element.132), channel_id=1, source_target_pairs={{0,1},{1,0},{2,3},{3,2},{4,5},{5,4},{6,7},{7,6},{8,9},{9,8},{10,11... | collective-permute-start | bytes 1572872 | tf_op jit(solution)/shard_map/ppermute | solution.py:133
  65.4 16.5 %copy-start.8 = (f32[2,64,512]{2,1,0:T(8,128)S(1)}, f32[2,64,512]{2,1,0:T(8,128)}, u32[]{:S(2)}) copy-start(f32[2,64,512]{2,1,0:T(8,128)} %refs_1_.5) | copy-start | bytes 786436
  65.5 10.9 %collective-permute-start.19 = (bf16[2,1056,128]{2,1,0:T(8,128)(2,1)}, bf16[2,1056,128]{2,1,0:T(8,128)(2,1)S(1)}, u32[]{:S(2)}, u32[]{:S(2)}) collective-permute-start(bf16[2,1056,128]{2,1,0:T(8,128)(2,1)} %get-tuple-element.147), channel_id=1, source_target_pairs={{0,1},{1,0},{2,3},{3,2},{4,5},{5,4},{6,7},{7,6},{8,9},{9,8},{10,11... | collective-permute-start | bytes 1622024 | tf_op jit(solution)/shard_map/ppermute | solution.py:133
  65.5 15.1 %collective-permute-start.16 = (bf16[144,512]{1,0:T(8,128)(2,1)}, bf16[144,512]{1,0:T(8,128)(2,1)}, u32[]{:S(2)}, u32[]{:S(2)}) collective-permute-start(bf16[144,512]{1,0:T(8,128)(2,1)} %get-tuple-element.142), channel_id=1, source_target_pairs={{0,8},{4,12},{8,0},{12,4},{16,24},{20,28},{24,16},{28,20},{1,9},{5... | collective-permute-start | bytes 442376 | tf_op jit(solution)/shard_map/ppermute | solution.py:133
  67.2 14.7 %collective-permute-start.17 = (bf16[144,512]{1,0:T(8,128)(2,1)S(1)}, bf16[144,512]{1,0:T(8,128)(2,1)}, u32[]{:S(2)}, u32[]{:S(2)}) collective-permute-start(bf16[144,512]{1,0:T(8,128)(2,1)S(1)} %get-tuple-element.143), channel_id=1, source_target_pairs={{0,16},{4,20},{8,24},{12,28},{16,0},{20,4},{24,8},{28,12},{1,17},{... | collective-permute-start | bytes 442376 | tf_op jit(solution)/shard_map/ppermute | solution.py:133
  69.8 12.1 %collective-permute-start.18 = (bf16[144,512]{1,0:T(8,128)(2,1)S(1)}, bf16[144,512]{1,0:T(8,128)(2,1)}, u32[]{:S(2)}, u32[]{:S(2)}) collective-permute-start(bf16[144,512]{1,0:T(8,128)(2,1)S(1)} %get-tuple-element.144), channel_id=1, source_target_pairs={{0,24},{4,28},{8,16},{12,20},{16,8},{20,12},{24,0},{28,4},{1,25},{... | collective-permute-start | bytes 442376 | tf_op jit(solution)/shard_map/ppermute | solution.py:133
  70.0 10.7 %collective-permute-start.15 = (f32[64,512]{1,0:T(8,128)S(1)}, f32[64,512]{1,0:T(8,128)}, u32[]{:S(2)}, u32[]{:S(2)}) collective-permute-start(f32[64,512]{1,0:T(8,128)S(1)} %get-tuple-element.141), channel_id=1, source_target_pairs={{0,4},{4,0},{8,12},{12,8},{16,20},{20,16},{24,28},{28,24},{1,5},{5... | collective-permute-start | bytes 393224 | tf_op jit(solution)/shard_map/ppermute | solution.py:133
  71.5 26.9 %all-to-all-start = ((bf16[8,224,128]{2,1,0:T(8,128)(2,1)}), bf16[8,224,128]{2,1,0:T(8,128)(2,1)S(1)}, u32[]{:S(2)}, u32[]{:S(2)}) async-start(bf16[8,224,128]{2,1,0:T(8,128)(2,1)} %get-tuple-element.140), calls=%async_computation | async-start | bytes 917504 | tf_op jit(solution)/shard_map/all_to_all | solution.py:952
  79.2 19.2 %collective-permute-start.21 = (bf16[2080,128]{1,0:T(8,128)(2,1)S(1)}, bf16[2080,128]{1,0:T(8,128)(2,1)S(1)}, u32[]{:S(2)}, u32[]{:S(2)}) collective-permute-start(bf16[2080,128]{1,0:T(8,128)(2,1)S(1)} %get-tuple-element.150), channel_id=1, source_target_pairs={{0,2},{1,3},{2,0},{3,1},{4,6},{5,7},{6,4},{7,5},{8,10},{9,11},{10,... | collective-permute-start | bytes 1597448 | tf_op jit(solution)/shard_map/ppermute | solution.py:133
  84.6 21.0 %collective-permute-start.25 = (bf16[128,512]{1,0:T(8,128)(2,1)}, bf16[128,512]{1,0:T(8,128)(2,1)}, u32[]{:S(2)}, u32[]{:S(2)}) collective-permute-start(bf16[128,512]{1,0:T(8,128)(2,1)} %get-tuple-element.165.refs_1_), channel_id=1, source_target_pairs={{0,24},{4,28},{8,16},{12,20},{16,8},{20,12},{24,0},{28,4},{1,25},{... | collective-permute-start | bytes 393224 | tf_op jit(solution)/shard_map/ppermute | solution.py:133
  89.0 16.7 %collective-permute-start.24 = (bf16[128,512]{1,0:T(8,128)(2,1)}, bf16[128,512]{1,0:T(8,128)(2,1)}, u32[]{:S(2)}, u32[]{:S(2)}) collective-permute-start(bf16[128,512]{1,0:T(8,128)(2,1)} %get-tuple-element.165.refs_1_), channel_id=1, source_target_pairs={{0,16},{4,20},{8,24},{12,28},{16,0},{20,4},{24,8},{28,12},{1,17},{... | collective-permute-start | bytes 393224 | tf_op jit(solution)/shard_map/ppermute | solution.py:133
  95.5 10.1 %collective-permute-start.23 = (bf16[128,512]{1,0:T(8,128)(2,1)}, bf16[128,512]{1,0:T(8,128)(2,1)}, u32[]{:S(2)}, u32[]{:S(2)}) collective-permute-start(bf16[128,512]{1,0:T(8,128)(2,1)} %get-tuple-element.165.refs_1_), channel_id=1, source_target_pairs={{0,8},{4,12},{8,0},{12,4},{16,24},{20,28},{24,16},{28,20},{1,9},{5... | collective-permute-start | bytes 393224 | tf_op jit(solution)/shard_map/ppermute | solution.py:133
  95.6 19.6 %collective-permute-start.22 = (f32[64,512]{1,0:T(8,128)}, f32[64,512]{1,0:T(8,128)}, u32[]{:S(2)}, u32[]{:S(2)}) collective-permute-start(f32[64,512]{1,0:T(8,128)} %get-tuple-element.163), channel_id=1, source_target_pairs={{0,4},{4,0},{8,12},{12,8},{16,20},{20,16},{24,28},{28,24},{1,5},{5... | collective-permute-start | bytes 393224 | tf_op jit(solution)/shard_map/ppermute | solution.py:133
  100.9 24.2 %all-to-all-start.1 = ((bf16[32,64,128]{2,1,0:T(8,128)(2,1)}), bf16[32,64,128]{2,1,0:T(8,128)(2,1)}, u32[]{:S(2)}, u32[]{:S(2)}) async-start(bf16[32,64,128]{2,1,0:T(8,128)(2,1)} %get-tuple-element.151), calls=%async_computation.1 | async-start | bytes 1048576 | tf_op jit(solution)/shard_map/all_to_all | solution.py:980
  106.8 17.5 %collective-permute-start.28 = (bf16[512,512]{1,0:T(8,128)(2,1)S(1)}, bf16[512,512]{1,0:T(8,128)(2,1)S(1)}, u32[]{:S(2)}, u32[]{:S(2)}) collective-permute-start(bf16[512,512]{1,0:T(8,128)(2,1)S(1)} %shard_map.240.refs_1_), channel_id=1, source_target_pairs={{0,3},{4,7},{8,11},{12,15},{16,19},{20,23},{24,27},{28,31}} | collective-permute-start | bytes 1572872 | tf_op jit(solution)/shard_map/ppermute | solution.py:984
  110.2 14.1 %collective-permute-start.27 = (bf16[512,512]{1,0:T(8,128)(2,1)S(1)}, bf16[512,512]{1,0:T(8,128)(2,1)S(1)}, u32[]{:S(2)}, u32[]{:S(2)}) collective-permute-start(bf16[512,512]{1,0:T(8,128)(2,1)S(1)} %shard_map.240.refs_1_), channel_id=1, source_target_pairs={{1,3},{5,7},{9,11},{13,15},{17,19},{21,23},{25,27},{29,31}} | collective-permute-start | bytes 1572872 | tf_op jit(solution)/shard_map/ppermute | solution.py:984
  110.9 13.4 %collective-permute-start.26 = (bf16[512,512]{1,0:T(8,128)(2,1)S(1)}, bf16[512,512]{1,0:T(8,128)(2,1)S(1)}, u32[]{:S(2)}, u32[]{:S(2)}) collective-permute-start(bf16[512,512]{1,0:T(8,128)(2,1)S(1)} %shard_map.240.refs_1_), channel_id=1, source_target_pairs={{2,3},{6,7},{10,11},{14,15},{18,19},{22,23},{26,27},{30,31}} | collective-permute-start | bytes 1572872 | tf_op jit(solution)/shard_map/ppermute | solution.py:984
  127.4 26.4 %all-to-all-start.2 = ((bf16[8,64,512]{2,1,0:T(8,128)(2,1)}), bf16[8,64,512]{2,1,0:T(8,128)(2,1)S(1)}, u32[]{:S(2)}, u32[]{:S(2)}) async-start(bf16[8,64,512]{2,1,0:T(8,128)(2,1)} %shard_map.242), calls=%async_computation.2 | async-start | bytes 1048576 | tf_op jit(solution)/shard_map/all_to_all | solution.py:1007

commit v3 on v2

--- a/solution.py
+++ b/solution.py
@@ -241,6 +241,11 @@
         self.shape, self.dtype, self.own = shape, dtype, own
 
 
+class Bare:
+    def __init__(self, shape, dtype):
+        self.shape, self.dtype = shape, dtype
+
+
 class Waiting:
     def __init__(self, copy, ref):
         self.copy, self.ref, self.started = copy, ref, False
@@ -255,7 +260,7 @@
 
 
 def call(kernel, outs, scratch, args, time, limit):
-    outs = [o if isinstance(o, Store) else jax.ShapeDtypeStruct(*o) for o in outs]
+    outs = [o if isinstance(o, (Store, Bare)) else jax.ShapeDtypeStruct(*o) for o in outs]
     late = [a for a in (*args, *outs) if isinstance(a, (Late, Store))]
     n_in, n_out = len(args), len(outs)
 
@@ -286,11 +291,11 @@
 
     return pl.pallas_call(
         body,
-        out_shape=tuple(pltpu.HBM(o.shape, o.dtype) if isinstance(o, Store) else o for o in outs),
+        out_shape=tuple(pltpu.HBM(o.shape, o.dtype) if isinstance(o, (Store, Bare)) else o for o in outs),
         in_specs=[SMEM] + [HBM if isinstance(a, Late) else VMEM for a in args[1:]],
-        out_specs=tuple(HBM if isinstance(o, Store) else VMEM for o in outs),
+        out_specs=tuple(HBM if isinstance(o, (Store, Bare)) else VMEM for o in outs),
         scratch_shapes=[pltpu.VMEM(a.shape, a.dtype) for a in late]
-        + [pltpu.VMEM(shape, dtype) for shape, dtype in scratch]
+        + [pltpu.VMEM(*what) if isinstance(what, tuple) else what for what in scratch]
         + ([pltpu.SemaphoreType.DMA((len(late),))] if late else []),
         compiler_params=pltpu.CompilerParams(vmem_limit_bytes=limit * 2**20),
         cost_estimate=pl.CostEstimate(flops=max(time * SCALE, 10**6), bytes_accessed=0, transcendentals=0),
@@ -530,14 +535,10 @@
     one_kept, out_kept = one_kept.ready(), out_kept.ready()
     size = out_mine.shape[0]
     one_mine[...] = one_kept[0, :size, :] + one_came[0, :size, :].astype(F32)
-    far[:size, :] = (one_kept[1, :size, :] + one_came[1, :size, :].astype(F32)).astype(BF16)
-    below = one_kept[0, size:, :] + one_came[0, size:, :].astype(F32)
-    high, low = split(below[16:24, :] + below[24:, :])
-    below = jnp.concatenate([below[:16, :], high.astype(F32), low.astype(F32)], 0)
-    tail[...] = below
-    far[size : size + 32, :] = below.astype(BF16)
+    tail[...] = one_kept[0, size:, :] + one_came[0, size:, :].astype(F32)
+    far[: size + 16, :] = (one_kept[1] + one_came[1].astype(F32)).astype(BF16)
     out_mine[...] = out_kept[0] + out_came[0].astype(F32)
-    far[size + 32 :, :] = (out_kept[1] + out_came[1].astype(F32)).astype(BF16)
+    far[size + 16 :, :] = (out_kept[1] + out_came[1].astype(F32)).astype(BF16)
 
 
 def norm_back_kernel(info, mine, came, cot, n_mine, inv_mine, gains, delta, grad_gain):
@@ -552,11 +553,11 @@
 
 def mixer_back_kernel(info, d0, d1, d2, d3, weights, act, slope, conv, branch, normed, spec_v, spec_k, forward, inverse,
                       kernel_inverse, gains, gain_two,
-                      slots, near, kept, delta_own,
-                      delta, wide, spec_d, spec_y, spec_u, back, share):
+                      keep, send, near, kept, delta_own, gain_part,
+                      slots, semaphores, delta, wide, spec_d, spec_y, spec_u, back, share):
     me = info[0]
     step, width = d0.shape
-    part = slots.ref.shape[2]
+    part = slots.shape[3]
     half = step
     for k, piece in enumerate((d0, d1, d2, d3)):
         block = me ^ k
@@ -585,16 +586,22 @@
     grad_kernel = table_dot(kernel_inverse, spec_u[...])
     grads = dot(normed[...], back[...], TN)
     grad_out = dot(delta[...], branch[...], TN)
-    dp = slots.ref.shape[0]
+    dp = 2 * slots.shape[1]
     rows = width // dp
     taps = grad_kernel.shape[0] // dp
     for i in range(dp):
         r = slice(i * rows, (i + 1) * rows)
-        slots.ref[i, :rows, :] = grads[r, :part].astype(slots.ref.dtype)
-        slots.ref[i, rows : 2 * rows, :] = grads[r, part:].astype(slots.ref.dtype)
-        slots.ref[i, 2 * rows : 3 * rows, :] = grad_out[r, :].astype(slots.ref.dtype)
-        slots.ref[i, 3 * rows :, :] = grad_kernel[i * taps : (i + 1) * taps, :].astype(slots.ref.dtype)
-    slots.send()
+        slots[i % 2, i // 2, :rows, :] = grads[r, :part].astype(slots.dtype)
+        slots[i % 2, i // 2, rows : 2 * rows, :] = grads[r, part:].astype(slots.dtype)
+        slots[i % 2, i // 2, 2 * rows : 3 * rows, :] = grad_out[r, :].astype(slots.dtype)
+        slots[i % 2, i // 2, 3 * rows :, :] = grad_kernel[i * taps : (i + 1) * taps, :].astype(slots.dtype)
+    side = info[2] % 2
+    copies = [
+        pltpu.make_async_copy(slots.at[side], keep, semaphores.at[0]),
+        pltpu.make_async_copy(slots.at[1 - side], send, semaphores.at[1]),
+    ]
+    for copy in copies:
+        copy.start()
     ones = jnp.ones((8, width), BF16)
     gain_one = jnp.zeros((1, width), F32)
     sums = [[], []]
@@ -612,8 +619,8 @@
             sums[1].append(second[0:1, h * part : (h + 1) * part])
     gain_one = gain_one / gains[0:1, :]
     gain = [g[:, q * part : (q + 1) * part] for g in (gain_one, gain_two[...]) for q in range(4)]
-    gain_high, gain_low = split(jnp.concatenate(gain, 0))
-    tail = jnp.concatenate([*sums[0], *sums[1], gain_high.astype(F32), gain_low.astype(F32)], 0)
+    gain_part.ref[...] = jnp.concatenate(gain, 0)
+    tail = jnp.concatenate([*sums[0], *sums[1]], 0)
     for k in range(4):
         block = share[:, block_at(me ^ k, part)]
         if k % 2:
@@ -622,33 +629,38 @@
         else:
             kept.ref[k // 2, : share.shape[0], :] = block
             kept.ref[k // 2, share.shape[0] :, :] = tail
+    for copy in copies:
+        copy.wait()
+
+
+def pair_sum_kernel(info, keep, came, out):
+    keep, came = keep.ready(), came.ready()
+    for z in range(keep.shape[0]):
+        out.ref[z] = (keep[z].astype(F32) + came[z].astype(F32)).astype(out.ref.dtype)
 
 
 def keeper(t):
     return 4 * (1 - t // 2) + t
 
 
-def moment_kernel(info, arrived, moment, count, tail, came, moment_new, slots, came_kept):
+def moment_kernel(info, arrived, moment, count, gain_part, moment_new, slots):
     me = info[0]
-    dp = arrived.shape[0]
+    pairs = arrived.shape[0]
     _, rows, part = moment.ref.shape
     taps = arrived.shape[1] - 3 * rows
     total = arrived[0].astype(F32)
-    for i in range(1, dp):
+    for i in range(1, pairs):
         total = total + arrived[i].astype(F32)
-    size = (came.shape[0] - 32) // 2
-    below = tail[16:, :] + came[size + 16 : size + 32, :].astype(F32)
-    came_kept.ref[...] = came[...]
-    high, low = split(below[:8, :] + below[8:, :])
+    high, low = split(gain_part.ready()[...])
     rest = jnp.concatenate([total[3 * rows :, :], high.astype(F32), low.astype(F32)], 0).astype(slots.ref.dtype)
     moment, count = moment.ready(), count.ready()
     for which in range(3):
         value = MOMENT_DECAY * moment[which] + total[which * rows : (which + 1) * rows, :] / count[0:1, :]
         moment_new.ref[which] = value
-        for z in range(dp // 2):
+        for z in range(pairs):
             slots.ref[8 * z + keeper(which), :rows, :] = value.astype(slots.ref.dtype)
     for t in range(4):
-        for z in range(dp // 2):
+        for z in range(pairs):
             slots.ref[8 * z + (keeper(t) ^ 4), : taps + 16, :] = rest
             if t == 3:
                 slots.ref[8 * z + keeper(t), : taps + 16, :] = rest
@@ -660,12 +672,12 @@
     came = came.ready()
     gain = gains.ready()[0:1, block_at(info[0], part)]
     size = mine.shape[0]
-    sums = (tail[:16, :] + came[size : size + 16, :].astype(F32)) / (4 * part)
+    sums = (tail[...] + came[size : size + 16, :].astype(F32)) / (4 * part)
     middle_own = middle_own.ready()
     n_own, inv, delta_own = n_own.ready(), inv.ready(), delta_own.ready()
     for h in range(mine.shape[0] // part):
         r = slice(h * part, (h + 1) * part)
-        block_out.ref[r, :] = (middle_own[r, :] + (out_mine[r, :] + came[size + 32 + h * part : size + 32 + (h + 1) * part, :].astype(F32))).astype(BF16)
+        block_out.ref[r, :] = (middle_own[r, :] + (out_mine[r, :] + came[size + 16 + h * part : size + 16 + (h + 1) * part, :].astype(F32))).astype(BF16)
         column = lambda at: jnp.broadcast_to(sums[at : at + 1, :], (part, part)).T
         total = mine[r, :] + came[r, :].astype(F32)
         back = total * gain - column(h) - n_own[r, :] * column(8 + h)
@@ -699,7 +711,9 @@
         count = min(share, total - i * share)
         if count > 0:
             packed[i * share : i * share + count, :] = both[:count, :]
-        gain = gain + (both[taps : taps + 8, :] + both[taps + 8 :, :])
+        for t in range(4):
+            both = got[4 * i + t, taps : taps + 16, :].astype(F32)
+            gain = gain + (both[:8, :] + both[8:, :])
     high, low = split(gain)
     extra[...] = jnp.zeros_like(extra)
     for g in range(-(-total // 64)):
@@ -939,20 +953,23 @@
         (blocks,) = call(mlp_rows_kernel, [((pairs, *block), BF16)], [], (info, mlp_keep, mlp_came), 0, 6)
         blocks = [lax.all_to_all(blocks, "dp", 0, 0, tiled=True, axis_index_groups=parities)]
 
-    slots, one_near, one_kept, delta_own = call(
+    piece = (pairs, 3 * rows + slot, part)
+    slots_keep, slots_send, one_near, one_kept, delta_own, gain_part = call(
         mixer_back_kernel,
-        [Store((dp, 3 * rows + slot, part), piece_type), Store((2, bucket + 32, part), BF16),
-         Store((2, bucket + 32, part), F32), Store((bucket, part), BF16)],
-        [whole_like, wide_like, spec_like, spec_like, ((8 * half, part), F32), ((bucket, 2 * part), BF16),
-         ((bucket, width), F32)],
+        [Bare(piece, piece_type), Bare(piece, piece_type), Store((2, bucket + 16, part), BF16),
+         Store((2, bucket + 16, part), F32), Store((bucket, part), BF16), Store((8, part), F32)],
+        [((2, *piece), piece_type), pltpu.SemaphoreType.DMA((2,)), whole_like, wide_like, spec_like, spec_like,
+         ((8 * half, part), F32), ((bucket, 2 * part), BF16), ((bucket, width), F32)],
         (after(info, blocks[0]), *delta_pieces, in_weights, gate_act, gate_slope, conv, branch, normed, spec_v, spec_k, forward_one, inverse_one,
          kernel_inverse_one, gains, grad_gain_two),
         1000, 18,
     )
-    arrived = lax.all_to_all(slots.astype(BF16), "dp", 0, 0, tiled=True)
+    slots_came = swap(slots_send.astype(BF16), "dp", 1).astype(piece_type)
+    (slots,) = call(pair_sum_kernel, [Store(piece, piece_type)], [], (info, Late(slots_keep), Late(slots_came)), 0, 6)
+    arrived = lax.all_to_all(slots.astype(BF16), "dp", 0, 0, tiled=True, axis_index_groups=parities)
     one_mine, one_tail, out_mine, far = call(
         join_late_kernel,
-        [act_like, ((32, part), F32), act_like, ((2 * bucket + 32, part), BF16)],
+        [act_like, ((16, part), F32), act_like, ((2 * bucket + 16, part), BF16)],
         [],
         (info, Late(one_kept), swap(one_near, "tensor", 1), Late(out_kept), swap(out_near, "tensor", 1)),
         0, 6,
@@ -962,7 +979,7 @@
         mlp_moment_kernel,
         [((2 * rows, hidden), BF16), Store((rows, hidden), F32), Store((rows, hidden), F32), Store((8, part), F32)],
         [],
-        (info, mlp_moment, moment_came, *blocks),
+        (after(info, far), mlp_moment, moment_came, *blocks),
         1, 8,
     )
     if dp == 8:
@@ -970,12 +987,12 @@
     else:
         pair_pieces = [lax.all_gather(pair, "dp", axis=0, tiled=True, axis_index_groups=parities)]
     height = -(-max(rows, slot + 16) // 16) * 16
-    mixer_moment_new, slots, far_kept = call(
+    mixer_moment_new, slots = call(
         moment_kernel,
-        [Store((3, rows, part), F32), Store((4 * dp, height, part), piece_type), Store((2 * bucket + 32, part), BF16)],
+        [Store((3, rows, part), F32), Store((4 * dp, height, part), piece_type)],
         [],
-        (info, arrived, Late(mixer_moment), Late(count), one_tail, far_came),
-        1000, 8,
+        (info, arrived, Late(mixer_moment), Late(count), Late(gain_part)),
+        0, 8,
     )
     got = lax.all_to_all(slots.astype(BF16), ("dp", "tensor"), 0, 0, tiled=True)
     (mlp_columns,) = call(
@@ -987,7 +1004,7 @@
         output_kernel,
         [Store(*act_like), Store((bucket, part), BF16)],
         [],
-        (after(info, slots), one_mine, Late(far_kept), out_mine, Late(delta_own), Late(n_own), Late(inv_one),
+        (after(info, slots), one_mine, Late(far_came), out_mine, Late(delta_own), Late(n_own), Late(inv_one),
          Late(middle_own), Late(norm_gains), one_tail),
         0, 8,
     )

time: 158 us -> 153 us (0.968)
  starting transfers between devices: 62.4 us -> 57.2 us
    ppermute x26 -> x27, starting transfers between devices: 31.4 us -> 25.9 us  [swap(): return lax.ppermute(value, axis, [(i, i ^ k) for i in range(size)])]
    pallas_call x20 -> x21, Pallas kernels: 53.3 us -> 54.4 us  [call(): pl.pallas_call(body, out_shape=tuple((pltpu.HBM(o.shape, o.dtype) if isin...]
    ppermute x26 -> x27, waiting for transfers between devices: 16.1 us -> 17 us  [swap(): return lax.ppermute(value, axis, [(i, i ^ k) for i in range(size)])]
  transfers between devices with their start and end apart: 32 -> 33, of which waited for: 13 -> 12; matrix products, arithmetic and copies ran while one was open for 0% -> 0% of each run, Pallas kernels for 32% -> 33%
where the time goes in v3:
time: 153 us; the launch traced here: 152 us
  Pallas kernels  62.9 us (41%)
  starting transfers between devices  57.2 us (37%)
  waiting for transfers between devices  30.2 us (20%)
  between operations  1.97 us (1%)
    pallas_call x21, Pallas kernels, call(): pl.pallas_call(body, out_shape=tuple((pltpu.HBM(o.shape, o.dtype) if isin...  54.4 us
    ppermute x27, starting transfers between devices, swap(): return lax.ppermute(value, axis, [(i, i ^ k) for i in range(size)])  25.9 us
    ppermute x27, waiting for transfers between devices, swap(): return lax.ppermute(value, axis, [(i, i ^ k) for i in range(size)])  17 us
    all_to_all x1, starting transfers between devices, per_device(): lax.all_to_all(sends.astype(BF16), ('dp', 'tensor'), 0, 0, tiled=True, ax...  16.7 us
    ppermute x3, waiting for transfers between devices, per_device(): lax.ppermute(mlp_columns, 'tensor', [(3 ^ k, 3)])  7.11 us
    pallas_call x3, Pallas kernels, fetch(): pl.pallas_call(body, out_shape=tuple(shapes), in_specs=[SMEM] + [HBM] * l...  6.23 us
    all_to_all x1, waiting for transfers between devices, per_device(): lax.all_to_all(sends.astype(BF16), ('dp', 'tensor'), 0, 0, tiled=True, ax...  6.12 us
    all_to_all x1, starting transfers between devices, per_device(): got = lax.all_to_all(slots.astype(BF16), ('dp', 'tensor'), 0, 0, tiled=True)  5.02 us
  transfers between devices with their start and end apart: 33, of which 12 were waited for; matrix products, arithmetic and copies ran while one was open for 0% of the time, Pallas kernels for 33%

profile of v3, /device:TPU:0, one launch (start us, length us, event | category | flops | bytes accessed | tf_op | source)
XLA Modules:
  0.0 152.4 jit_solution(2072849105718821378)
XLA Ops:
  0.6 3.0 %collective-permute-start.1 = (bf16[1024,128]{1,0:T(8,128)(2,1)}, bf16[1024,128]{1,0:T(8,128)(2,1)S(1)}, u32[]{:S(2)}, u32[]{:S(2)}) collective-permute-start(bf16[1024,128]{1,0:T(8,128)(2,1)} %bitcast.17), channel_id=1, source_target_pairs={{0,2},{1,3},{2,0},{3,1},{4,6},{5,7},{6,4},{7,5},{8,10},{9,11},{10,... | collective-permute-start | bytes 786440 | tf_op jit(solution)/shard_map/ppermute | solution.py:133
  4.3 0.1 pad_add_fusion.token_ref.refs_0_.info
  4.4 2.1 %shard_map.222 = (bf16[1024,128]{1,0:T(8,128)(2,1)S(1)}, bf16[3,512,128]{2,1,0:T(8,128)(2,1)S(1)}, f32[2,512]{1,0:T(2,128)S(1)}, bf16[2,512,256]{2,1,0:T(8,128)(...) custom-call(s32[3]{0:T(128)S(1)} %pad_add_fusion.token_ref.refs_0_.info, ...), custom_call_target="tpu_custom_call" | custom-call | flops 10000000000 | tf_op jit(solution)/shard_map/pallas_call | solution.py:326
  6.5 0.2 collective-permute-start.6
  6.7 3.1 %shard_map.223.refs_9_.refs_12_ = f32[2048,128]{1,0:T(8,128)S(1)} custom-call(s32[3]{0:T(128)S(1)} %pad_add_fusion.token_ref.refs_0_.info, bf16[2,2048,160]{2,1,0:T(8,128)(2,1)} %constant.19.clone.refs_1_, f32[160,128]{1,0:T(8,128)} %bitcast.13), custom_call_target="tpu_custom_call" | custom-call | flops 20000000000 | tf_op jit(solution)/shard_map/pallas_call | solution.py:292
  9.8 0.8 collective-permute-done.1.refs_3_
  10.7 0.5 collective-permute-start.5
  11.2 1.0 collective-permute-done.2.refs_4_
  12.2 3.6 %shard_map.224 = (bf16[1024,512]{1,0:T(8,128)(2,1)S(1)}, bf16[1024,512]{1,0:T(8,128)(2,1)S(1)}, f32[1024,128]{1,0:T(8,128)}, f32[1024,1]{1,0:T(8,128)}, f32[512,...) custom-call(s32[3]{0:T(128)S(1)} %pad_add_fusion.token_ref.refs_0_.i, ...), custom_call_target="tpu_custom_call" | custom-call | flops 1000000 | tf_op jit(solution)/shard_map/pallas_call | solution.py:292
  15.9 2.7 %collective-permute-done.6.refs_3_ = bf16[1536,128]{1,0:T(8,128)(2,1)S(1)} collective-permute-done((bf16[1536,128]{1,0:T(8,128)(2,1)S(1)}, bf16[1536,128]{1,0:T(8,128)(2,1)S(1)}, u32[]{:S(2)}, u32[]{:S(2)}) %collective-permute-start.6) | collective-permute-done | bytes 393248 | tf_op jit(solution)/shard_map/ppermute | solution.py:133
  18.6 1.7 %collective-permute-start.4 = (bf16[1024,128]{1,0:T(8,128)(2,1)S(1)}, bf16[1024,128]{1,0:T(8,128)(2,1)S(1)}, u32[]{:S(2)}, u32[]{:S(2)}) collective-permute-start(bf16[1024,128]{1,0:T(8,128)(2,1)S(1)} %get-tuple-element.105.refs_1_.refs_9_), channel_id=1, source_target_pairs={{0,2},{1,3},{2,0},{3,1},{4,6},{5,7},{6,4},{7,5},{8,10},{9,11},{10,... | collective-permute-start | bytes 786440 | tf_op jit(solution)/shard_map/ppermute | solution.py:133
  20.3 0.2 collective-permute-start.3
  20.6 2.7 %shard_map.225 = (bf16[1024,512]{1,0:T(8,128)(2,1)S(1)}, bf16[512,512]{1,0:T(8,128)(2,1)S(1)}, f32[1024,512]{1,0:T(8,128)S(1)}, bf16[2,512,512]{2,1,0:T(8,128)(2,1)S(1)}) custom-call(s32[3]{0:T(128)S(1)} %pad_add_fusion.token_ref.refs_0_.info, bf16[1536,128]{1,0:T(8,128)(2,1)S(1)} %get-tuple-element.107.refs_1_, ...), custom_call_target="tpu_custom_call" | custom-call | flops 30000001024 | tf_op jit(solution)/shard_map/pallas_call | solution.py:292
  23.3 4.0 %collective-permute-done.4.refs_3_ = bf16[1024,128]{1,0:T(8,128)(2,1)S(1)} collective-permute-done((bf16[1024,128]{1,0:T(8,128)(2,1)S(1)}, bf16[1024,128]{1,0:T(8,128)(2,1)S(1)}, u32[]{:S(2)}, u32[]{:S(2)}) %collective-permute-start.4) | collective-permute-done | bytes 262176 | tf_op jit(solution)/shard_map/ppermute | solution.py:133
  27.3 1.5 %collective-permute-done.8.refs_4_ = bf16[1024,128]{1,0:T(8,128)(2,1)S(1)} collective-permute-done((bf16[1024,128]{1,0:T(8,128)(2,1)S(1)}, bf16[1024,128]{1,0:T(8,128)(2,1)S(1)}, u32[]{:S(2)}, u32[]{:S(2)}) %collective-permute-start.8) | collective-permute-done | bytes 262176 | tf_op jit(solution)/shard_map/ppermute | solution.py:133
  28.9 5.9 %shard_map.226 = (bf16[512,512]{1,0:T(8,128)(2,1)S(1)}, f32[512,512]{1,0:T(8,128)S(1)}, bf16[1024,512]{1,0:T(8,128)(2,1)S(1)}, bf16[1024,512]{1,0:T(8,128)(2,1)S...) custom-call(s32[3]{0:T(128)S(1)} %pad_add_fusion.token_ref.refs_0_.inf, ...), custom_call_target="tpu_custom_call" | custom-call | flops 60000002048 | tf_op jit(solution)/shard_map/pallas_call | solution.py:292
  34.8 0.2 collective-permute-start.9
  35.0 1.8 %collective-permute-done.9.refs_2_ = bf16[2,256,512]{2,1,0:T(8,128)(2,1)S(1)} collective-permute-done((bf16[2,256,512]{2,1,0:T(8,128)(2,1)S(1)}, bf16[2,256,512]{2,1,0:T(8,128)(2,1)S(1)}, u32[]{:S(2)}, u32[]{:S(2)}) %collective-permute-start.9) | collective-permute-done | bytes 524320 | tf_op jit(solution)/shard_map/ppermute | solution.py:133
  36.7 1.3 shard_map.227
  38.0 1.7 %collective-permute-start.11 = (bf16[256,512]{1,0:T(8,128)(2,1)}, bf16[256,512]{1,0:T(8,128)(2,1)}, u32[]{:S(2)}, u32[]{:S(2)}) collective-permute-start(bf16[256,512]{1,0:T(8,128)(2,1)} %get-tuple-element.117), channel_id=1, source_target_pairs={{0,2},{1,3},{2,0},{3,1},{4,6},{5,7},{6,4},{7,5},{8,10},{9,11},{10,... | collective-permute-start | bytes 786440 | tf_op jit(solution)/shard_map/ppermute | solution.py:133
  39.8 2.3 %shard_map.228 = (bf16[528,512]{1,0:T(8,128)(2,1)}, f32[64,512]{1,0:T(8,128)S(1)}) custom-call(s32[3]{0:T(128)S(1)} %pad_add_fusion.token_ref.refs_0_.info, bf16[1024,512]{1,0:T(8,128)(2,1)S(1)} %get-tuple-element.119.refs_1_, bf16[1024,512]{1,0:T(8,128)(2,1)S(1)} %get-tuple-element.120.refs_2_.refs_1_, bf16[1024,512]{1,0:T(8,128)(2,1)S(1)} %get-tuple-element.121.refs_3_, ...), custom_call_target="tpu_custom_call" | custom-call | flops 20000000000 | tf_op jit(solution)/shard_map/pallas_call | solution.py:292
  42.1 1.6 %collective-permute-start.10 = (bf16[528,512]{1,0:T(8,128)(2,1)}, bf16[528,512]{1,0:T(8,128)(2,1)}, u32[]{:S(2)}, u32[]{:S(2)}) collective-permute-start(bf16[528,512]{1,0:T(8,128)(2,1)} %get-tuple-element.123), channel_id=1, source_target_pairs={{0,4},{4,0},{8,12},{12,8},{16,20},{20,16},{24,28},{28,24},{1,5},{5... | collective-permute-start | bytes 1622024 | tf_op jit(solution)/shard_map/ppermute | solution.py:133
  43.7 1.5 shard_map.229.refs_1_
  45.2 1.6 %collective-permute-done.11.refs_2_ = bf16[256,512]{1,0:T(8,128)(2,1)} collective-permute-done((bf16[256,512]{1,0:T(8,128)(2,1)}, bf16[256,512]{1,0:T(8,128)(2,1)}, u32[]{:S(2)}, u32[]{:S(2)}) %collective-permute-start.11) | collective-permute-done | bytes 262176 | tf_op jit(solution)/shard_map/ppermute | solution.py:133
  46.7 1.3 shard_map.231
  48.0 1.8 %collective-permute-start.13 = (bf16[256,512]{1,0:T(8,128)(2,1)S(1)}, bf16[256,512]{1,0:T(8,128)(2,1)S(1)}, u32[]{:S(2)}, u32[]{:S(2)}) collective-permute-start(bf16[256,512]{1,0:T(8,128)(2,1)S(1)} %get-tuple-element.131.refs_1_), channel_id=1, source_target_pairs={{0,2},{1,3},{2,0},{3,1},{4,6},{5,7},{6,4},{7,5},{8,10},{9,11},{10,... | collective-permute-start | bytes 786440 | tf_op jit(solution)/shard_map/ppermute | solution.py:133
  49.8 2.1 %shard_map.232.refs_15_ = bf16[2,256,2048]{2,1,0:T(8,128)(2,1)S(1)} custom-call(s32[3]{0:T(128)S(1)} %pad_add_fusion.token_ref.refs_0_.info, bf16[2,256,2048]{2,1,0:T(8,128)(2,1)} %constant.20.clone.refs_0_), custom_call_target="tpu_custom_call" | custom-call | flops 1000000 | tf_op jit(solution)/shard_map/pallas_call | solution.py:326
  52.0 2.6 %shard_map.233 = (bf16[2,1024,128]{2,1,0:T(8,128)(2,1)}, f32[2,1024,128]{2,1,0:T(8,128)}) custom-call(s32[3]{0:T(128)S(1)} %pad_add_fusion.token_ref.refs_0_.info, bf16[1024,512]{1,0:T(8,128)(2,1)S(1)} %copy-done.12, bf16[2,512,512]{2,1,0:T(8,128)(2,1)S(1)} %get-tuple-element.114.refs_8_.refs_2_), custom_call_target="tpu_custom_call" | custom-call | flops 10000000000 | tf_op jit(solution)/shard_map/pallas_call | solution.py:292
  54.6 1.0 collective-permute-done.13.refs_3_
  55.6 0.5 collective-permute-start.17
  56.1 0.4 collective-permute-done.10.refs_2_
  56.5 1.2 shard_map.230
  57.7 7.7 %shard_map.234 = (bf16[4,224,128]{2,1,0:T(8,128)(2,1)}, bf16[4,224,128]{2,1,0:T(8,128)(2,1)}, bf16[2,1040,128]{2,1,0:T(8,128)(2,1)}, f32[2,1040,128]{2,1,0:T(8,1...) custom-call(s32[3]{0:T(128)S(1)} %pad_add_fusion.token_ref.refs_0_.info, ...), custom_call_target="tpu_custom_call" | custom-call | flops 9999999827968 | tf_op jit(solution)/shard_map/pallas_call | solution.py:292
  65.4 0.1 collective-permute-start.16
  65.5 1.7 %collective-permute-start.15 = (bf16[4,224,128]{2,1,0:T(8,128)(2,1)}, bf16[4,224,128]{2,1,0:T(8,128)(2,1)S(1)}, u32[]{:S(2)}, u32[]{:S(2)}) collective-permute-start(bf16[4,224,128]{2,1,0:T(8,128)(2,1)} %get-tuple-element.143), channel_id=1, source_target_pairs={{0,4},{4,0},{8,12},{12,8},{16,20},{20,16},{24,28},{28,24},{1,5},{5... | collective-permute-start | bytes 688136 | tf_op jit(solution)/shard_map/ppermute | solution.py:133
  67.2 1.6 %collective-permute-start.19 = (bf16[144,512]{1,0:T(8,128)(2,1)S(1)}, bf16[144,512]{1,0:T(8,128)(2,1)S(1)}, u32[]{:S(2)}, u32[]{:S(2)}) collective-permute-start(bf16[144,512]{1,0:T(8,128)(2,1)S(1)} %get-tuple-element.150), channel_id=1, source_target_pairs={{0,8},{4,12},{8,0},{12,4},{16,24},{20,28},{24,16},{28,20},{1,9},{5... | collective-permute-start | bytes 442376 | tf_op jit(solution)/shard_map/ppermute | solution.py:133
  68.8 2.6 %collective-permute-start.20 = (bf16[144,512]{1,0:T(8,128)(2,1)S(1)}, bf16[144,512]{1,0:T(8,128)(2,1)S(1)}, u32[]{:S(2)}, u32[]{:S(2)}) collective-permute-start(bf16[144,512]{1,0:T(8,128)(2,1)S(1)} %get-tuple-element.151), channel_id=1, source_target_pairs={{0,16},{4,20},{8,24},{12,28},{16,0},{20,4},{24,8},{28,12},{1,17},{... | collective-permute-start | bytes 442376 | tf_op jit(solution)/shard_map/ppermute | solution.py:133
  71.4 0.2 collective-permute-start.21
  71.6 2.1 %collective-permute-done.15.refs_2_ = bf16[4,224,128]{2,1,0:T(8,128)(2,1)S(1)} collective-permute-done((bf16[4,224,128]{2,1,0:T(8,128)(2,1)}, bf16[4,224,128]{2,1,0:T(8,128)(2,1)S(1)}, u32[]{:S(2)}, u32[]{:S(2)}) %collective-permute-start.15) | collective-permute-done | bytes 229408 | tf_op jit(solution)/shard_map/ppermute | solution.py:133
  73.7 1.5 %collective-permute-start.18 = (f32[64,512]{1,0:T(8,128)S(1)}, f32[64,512]{1,0:T(8,128)S(1)}, u32[]{:S(2)}, u32[]{:S(2)}) collective-permute-start(f32[64,512]{1,0:T(8,128)S(1)} %get-tuple-element.149), channel_id=1, source_target_pairs={{0,4},{4,0},{8,12},{12,8},{16,20},{20,16},{24,28},{28,24},{1,5},{5... | collective-permute-start | bytes 393224 | tf_op jit(solution)/shard_map/ppermute | solution.py:133
  75.3 2.4 %shard_map.235 = bf16[4,224,128]{2,1,0:T(8,128)(2,1)} custom-call(s32[3]{0:T(128)S(1)} %pad_add_fusion.token_ref.refs_0_.info, bf16[4,224,128]{2,1,0:T(8,128)(2,1)} %get-tuple-element.142.refs_1_, bf16[4,224,128]{2,1,0:T(8,128)(2,1)} %copy-done.13), custom_call_target="tpu_custom_call" | custom-call | flops 1000000 | tf_op jit(solution)/shard_map/pallas_call | solution.py:292
  77.6 4.9 %all-to-all-start = ((bf16[4,224,128]{2,1,0:T(8,128)(2,1)}), bf16[4,224,128]{2,1,0:T(8,128)(2,1)S(1)}, u32[]{:S(2)}, u32[]{:S(2)}) async-start(bf16[4,224,128]{2,1,0:T(8,128)(2,1)} %shard_map.235), calls=%async_computation | async-start | bytes 458752 | tf_op jit(solution)/shard_map/all_to_all | solution.py:969
  82.5 3.5 %shard_map.236 = (f32[1024,128]{1,0:T(8,128)S(1)}, f32[16,128]{1,0:T(8,128)S(1)}, f32[1024,128]{1,0:T(8,128)S(1)}, bf16[2064,128]{1,0:T(8,128)(2,1)}) custom-call(s32[3]{0:T(128)S(1)} %pad_add_fusion.token_ref.refs_0_.info, f32[2,1040,128]{2,1,0:T(8,128)} %get-tuple-element.144.refs_1_, bf16[2,1040,128]{2,1,0:T(8,128)(2,1)S(1)} %collective-permute-done.16.refs_2_, ...), custom_call_target="tpu_custom_call" | custom-call | flops 1000000 | tf_op jit(solution)/shard_map/pallas_call | solution.py:292
  86.1 1.4 shard_map.237
  87.5 3.9 %collective-permute-start.26 = (bf16[128,512]{1,0:T(8,128)(2,1)S(1)}, bf16[128,512]{1,0:T(8,128)(2,1)S(1)}, u32[]{:S(2)}, u32[]{:S(2)}) collective-permute-start(bf16[128,512]{1,0:T(8,128)(2,1)S(1)} %get-tuple-element.169.refs_1_), channel_id=1, source_target_pairs={{0,24},{4,28},{8,16},{12,20},{16,8},{20,12},{24,0},{28,4},{1,25},{... | collective-permute-start | bytes 393224 | tf_op jit(solution)/shard_map/ppermute | solution.py:133
  91.4 0.6 collective-permute-start.24
  92.1 1.5 collective-permute-start.22
  93.6 0.7 collective-permute-start.23
  94.3 2.3 %shard_map.238 = (f32[3,64,128]{2,1,0:T(8,128)}, bf16[32,64,128]{2,1,0:T(8,128)(2,1)}) custom-call(s32[3]{0:T(128)S(1)} %pad_add_fusion.token_ref.refs_0_.info, bf16[4,224,128]{2,1,0:T(8,128)(2,1)S(1)} %all-to-all-done.refs_1_, f32[3,64,128]{2,1,0:T(8,128)} %refs_2_.4, f32[8,128]{1,0:T(8,128)} %get-tuple-element.153.refs_3_.refs_9_, ...), custom_call_target="tpu_custom_call" | custom-call | flops 1000000 | tf_op jit(solution)/shard_map/pallas_call | solution.py:292
  96.6 5.0 %all-to-all-start.1 = ((bf16[32,64,128]{2,1,0:T(8,128)(2,1)}), bf16[32,64,128]{2,1,0:T(8,128)(2,1)}, u32[]{:S(2)}, u32[]{:S(2)}) async-start(bf16[32,64,128]{2,1,0:T(8,128)(2,1)} %get-tuple-element.155), calls=%async_computation.1 | async-start | bytes 1048576 | tf_op jit(solution)/shard_map/all_to_all | solution.py:997
  101.7 0.6 shard_map.241.refs_1_
  102.3 3.4 %collective-permute-start.29 = (bf16[512,512]{1,0:T(8,128)(2,1)S(1)}, bf16[512,512]{1,0:T(8,128)(2,1)S(1)}, u32[]{:S(2)}, u32[]{:S(2)}) collective-permute-start(bf16[512,512]{1,0:T(8,128)(2,1)S(1)} %shard_map.241.refs_1_), channel_id=1, source_target_pairs={{0,3},{4,7},{8,11},{12,15},{16,19},{20,23},{24,27},{28,31}} | collective-permute-start | bytes 1572872 | tf_op jit(solution)/shard_map/ppermute | solution.py:1001
  105.7 0.7 collective-permute-start.28
  106.4 0.7 collective-permute-start.27
  107.1 2.2 %shard_map.240 = f32[2,64,512]{2,1,0:T(8,128)} custom-call(s32[3]{0:T(128)S(1)} %pad_add_fusion.token_ref.refs_0_.info, f32[64,512]{1,0:T(8,128)} %get-tuple-element.166.refs_1_, f32[64,512]{1,0:T(8,128)} %collective-permute-done.23.refs_2_), custom_call_target="tpu_custom_call" | custom-call | flops 10000000000 | tf_op jit(solution)/shard_map/pallas_call | solution.py:292
  109.3 3.6 %shard_map.239 = (f32[1024,128]{1,0:T(8,128)}, bf16[1024,128]{1,0:T(8,128)(2,1)}) custom-call(s32[3]{0:T(128)S(1)} %pad_add_fusion.token_ref.refs_0_.info, f32[1024,128]{1,0:T(8,128)S(1)} %get-tuple-element.157.refs_1_, bf16[2064,128]{1,0:T(8,128)(2,1)} %collective-permute-done.22.refs_2_, f32[1024,128]{1,0:T(8,128)S(1)} %get-tuple-element.158.refs_3_, ...), custom_call_target="tpu_custom_call" | custom-call | flops 1000000 | tf_op jit(solution)/shard_map/pallas_call | solution.py:292
  113.0 7.1 %collective-permute-done.29.refs_4_ = bf16[512,512]{1,0:T(8,128)(2,1)S(1)} collective-permute-done((bf16[512,512]{1,0:T(8,128)(2,1)S(1)}, bf16[512,512]{1,0:T(8,128)(2,1)S(1)}, u32[]{:S(2)}, u32[]{:S(2)}) %collective-permute-start.29) | collective-permute-done | bytes 524320 | tf_op jit(solution)/shard_map/ppermute | solution.py:1001
  120.1 0.8 shard_map.242.slots
  120.9 2.3 %shard_map.243 = bf16[8,64,512]{2,1,0:T(8,128)(2,1)} custom-call(s32[3]{0:T(128)S(1)} %pad_add_fusion.token_ref.refs_0_.info, bf16[32,64,128]{2,1,0:T(8,128)(2,1)} %all-to-all-done.1.source.refs_1_, bf16[8,64,512]{2,1,0:T(8,128)(2,1)} %shard_map.242.slots), custom_call_target="tpu_custom_call", output_to_operand_aliasing={{}: (2, {})} | custom-call | flops 179999997952 | tf_op jit(solution)/shard_map/pallas_call | solution.py:770
  123.2 16.7 %all-to-all-start.2 = ((bf16[8,64,512]{2,1,0:T(8,128)(2,1)}), bf16[8,64,512]{2,1,0:T(8,128)(2,1)S(1)}, u32[]{:S(2)}, u32[]{:S(2)}) async-start(bf16[8,64,512]{2,1,0:T(8,128)(2,1)} %shard_map.243), calls=%async_computation.2 | async-start | bytes 1048576 | tf_op jit(solution)/shard_map/all_to_all | solution.py:1024
  139.8 1.6 %shard_map.244.refs_2_ = bf16[64,384]{1,0:T(8,128)(2,1)S(1)} custom-call(s32[3]{0:T(128)S(1)} %pad_add_fusion.token_ref.refs_0_.info, bf16[32,64,128]{2,1,0:T(8,128)(2,1)} %all-to-all-done.1.source.refs_1_), custom_call_target="tpu_custom_call" | custom-call | flops 1000000 | tf_op jit(solution)/shard_map/pallas_call | solution.py:292
  141.5 2.0 %shard_map.245 = (bf16[3,512,128]{2,1,0:T(8,128)(2,1)S(1)}, bf16[2,512,512]{2,1,0:T(8,128)(2,1)S(1)}, f32[2,512]{1,0:T(2,128)S(1)}, f32[2,512]{1,0:T(2,128)S(1)}...) custom-call(s32[3]{0:T(128)S(1)} %pad_add_fusion.token_ref.refs_0_.info, bf16[3,512,128]{2,1,0:T(8,128)(2,1)} %refs_0_.2, ...), custom_call_target="tpu_custom_call" | custom-call | flops 1000000 | tf_op jit(solution)/shard_map/pallas_call | solution.py:326
  143.5 6.1 %all-to-all-done.2.refs_1_ = bf16[8,64,512]{2,1,0:T(8,128)(2,1)S(1)} async-done(((bf16[8,64,512]{2,1,0:T(8,128)(2,1)}), bf16[8,64,512]{2,1,0:T(8,128)(2,1)S(1)}, u32[]{:S(2)}, u32[]{:S(2)}) %all-to-all-start.2) | async-done | bytes 524320 | tf_op jit(solution)/shard_map/all_to_all | solution.py:1024
  149.6 2.7 %shard_map.246 = (f32[3,64,128]{2,1,0:T(8,128)}, f32[2,64,512]{2,1,0:T(8,128)}, f32[2,512]{1,0:T(2,128)}, f32[2,512]{1,0:T(2,128)}, f32[160,128]{1,0:T(8,128)}, /*index=5*/f32[160,128]{1,0:T(8,128)}) custom-call(s32[3]{0:T(128)S(1)} %pad_add_fusion.token_ref.refs_0_.info, bf16[8,64,512]{2,1,0:T(8,128)(2,1)S(1)} %all-to-all-done.2.refs_1_, ...), custom_call_target="tpu_custom_call" | custom-call | flops 1000000 | tf_op jit(solution)/shard_map/pallas_call | solution.py:292
  (56 shorter events, 0.1 us)
Async XLA Ops:
  0.6 10.0 %collective-permute-start.1 = (bf16[1024,128]{1,0:T(8,128)(2,1)}, bf16[1024,128]{1,0:T(8,128)(2,1)S(1)}, u32[]{:S(2)}, u32[]{:S(2)}) collective-permute-start(bf16[1024,128]{1,0:T(8,128)(2,1)} %bitcast.17), channel_id=1, source_target_pairs={{0,2},{1,3},{2,0},{3,1},{4,6},{5,7},{6,4},{7,5},{8,10},{9,11},{10,... | collective-permute-start | bytes 786440 | tf_op jit(solution)/shard_map/ppermute | solution.py:133
  3.6 7.5 %collective-permute-start = (bf16[1024,128]{1,0:T(8,128)(2,1)}, bf16[1024,128]{1,0:T(8,128)(2,1)S(1)}, u32[]{:S(2)}, u32[]{:S(2)}) collective-permute-start(bf16[1024,128]{1,0:T(8,128)(2,1)} %bitcast.18), channel_id=1, source_target_pairs={{0,1},{1,0},{2,3},{3,2},{4,5},{5,4},{6,7},{7,6},{8,9},{9,8},{10,11... | collective-permute-start | bytes 786440 | tf_op jit(solution)/shard_map/ppermute | solution.py:133
  6.5 5.7 %copy-start.2 = (bf16[2,512,256]{2,1,0:T(8,128)(2,1)}, bf16[2,512,256]{2,1,0:T(8,128)(2,1)S(1)}, u32[]{:S(2)}) copy-start(bf16[2,512,256]{2,1,0:T(8,128)(2,1)S(1)} %get-tuple-element.103.refs_7_.refs_13_) | copy-start | bytes 1572868
  6.5 5.7 %copy-start.4 = (bf16[2,256,512]{2,1,0:T(8,128)(2,1)}, bf16[2,256,512]{2,1,0:T(8,128)(2,1)S(1)}, u32[]{:S(2)}) copy-start(bf16[2,256,512]{2,1,0:T(8,128)(2,1)S(1)} %get-tuple-element.104.refs_8_.refs_14_) | copy-start | bytes 1572868
  6.5 5.7 %copy-start.6 = (bf16[3,512,128]{2,1,0:T(8,128)(2,1)}, bf16[3,512,128]{2,1,0:T(8,128)(2,1)S(1)}, u32[]{:S(2)}) copy-start(bf16[3,512,128]{2,1,0:T(8,128)(2,1)S(1)} %get-tuple-element.101.refs_5_) | copy-start | bytes 1179652
  6.5 12.1 %collective-permute-start.6 = (bf16[1536,128]{1,0:T(8,128)(2,1)S(1)}, bf16[1536,128]{1,0:T(8,128)(2,1)S(1)}, u32[]{:S(2)}, u32[]{:S(2)}) collective-permute-start(bf16[1536,128]{1,0:T(8,128)(2,1)S(1)} %get-tuple-element.107.refs_1_), channel_id=1, source_target_pairs={{0,2},{1,3},{2,0},{3,1},{4,6},{5,7},{6,4},{7,5},{8,10},{9,11},{10,... | collective-permute-start | bytes 1179656 | tf_op jit(solution)/shard_map/ppermute | solution.py:133
  9.8 13.5 %copy-start = (f32[2048,128]{1,0:T(8,128)}, f32[2048,128]{1,0:T(8,128)S(1)}, u32[]{:S(2)}) copy-start(f32[2048,128]{1,0:T(8,128)S(1)} %shard_map.223.refs_9_.refs_12_) | copy-start | bytes 3145732
  10.7 1.5 %collective-permute-start.2 = (bf16[1024,128]{1,0:T(8,128)(2,1)S(1)}, bf16[1024,128]{1,0:T(8,128)(2,1)S(1)}, u32[]{:S(2)}, u32[]{:S(2)}) collective-permute-start(bf16[1024,128]{1,0:T(8,128)(2,1)S(1)} %collective-permute-done.1.refs_3_), channel_id=1, source_target_pairs={{0,1},{1,0},{2,3},{3,2},{4,5},{5,4},{6,7},{7,6},{8,9},{9,8},{10,11... | collective-permute-start | bytes 786440 | tf_op jit(solution)/shard_map/ppermute | solution.py:133
  10.7 9.9 %collective-permute-start.5 = (bf16[1536,128]{1,0:T(8,128)(2,1)S(1)}, bf16[1536,128]{1,0:T(8,128)(2,1)S(1)}, u32[]{:S(2)}, u32[]{:S(2)}) collective-permute-start(bf16[1536,128]{1,0:T(8,128)(2,1)S(1)} %get-tuple-element.107.refs_1_), channel_id=1, source_target_pairs={{0,1},{1,0},{2,3},{3,2},{4,5},{5,4},{6,7},{7,6},{8,9},{9,8},{10,11... | collective-permute-start | bytes 1179656 | tf_op jit(solution)/shard_map/ppermute | solution.py:133
  15.9 13.0 %copy-start.9 = (f32[2,512]{1,0:T(2,128)}, f32[2,512]{1,0:T(2,128)S(1)}, u32[]{:S(2)}) copy-start(f32[2,512]{1,0:T(2,128)S(1)} %get-tuple-element.113.refs_7_.refs_6_.refs_16_) | copy-start | bytes 12292
  18.6 2.0 %collective-permute-start.7 = (bf16[1536,128]{1,0:T(8,128)(2,1)S(1)}, bf16[1536,128]{1,0:T(8,128)(2,1)S(1)}, u32[]{:S(2)}, u32[]{:S(2)}) collective-permute-start(bf16[1536,128]{1,0:T(8,128)(2,1)S(1)} %collective-permute-done.6.refs_3_), channel_id=1, source_target_pairs={{0,1},{1,0},{2,3},{3,2},{4,5},{5,4},{6,7},{7,6},{8,9},{9,8},{10,11... | collective-permute-start | bytes 1179656 | tf_op jit(solution)/shard_map/ppermute | solution.py:133
  18.6 8.7 %collective-permute-start.4 = (bf16[1024,128]{1,0:T(8,128)(2,1)S(1)}, bf16[1024,128]{1,0:T(8,128)(2,1)S(1)}, u32[]{:S(2)}, u32[]{:S(2)}) collective-permute-start(bf16[1024,128]{1,0:T(8,128)(2,1)S(1)} %get-tuple-element.105.refs_1_.refs_9_), channel_id=1, source_target_pairs={{0,2},{1,3},{2,0},{3,1},{4,6},{5,7},{6,4},{7,5},{8,10},{9,11},{10,... | collective-permute-start | bytes 786440 | tf_op jit(solution)/shard_map/ppermute | solution.py:133
  20.3 7.0 %collective-permute-start.3 = (bf16[1024,128]{1,0:T(8,128)(2,1)S(1)}, bf16[1024,128]{1,0:T(8,128)(2,1)S(1)}, u32[]{:S(2)}, u32[]{:S(2)}) collective-permute-start(bf16[1024,128]{1,0:T(8,128)(2,1)S(1)} %get-tuple-element.105.refs_1_.refs_9_), channel_id=1, source_target_pairs={{0,1},{1,0},{2,3},{3,2},{4,5},{5,4},{6,7},{7,6},{8,9},{9,8},{10,11... | collective-permute-start | bytes 786440 | tf_op jit(solution)/shard_map/ppermute | solution.py:133
  27.3 1.5 %collective-permute-start.8 = (bf16[1024,128]{1,0:T(8,128)(2,1)S(1)}, bf16[1024,128]{1,0:T(8,128)(2,1)S(1)}, u32[]{:S(2)}, u32[]{:S(2)}) collective-permute-start(bf16[1024,128]{1,0:T(8,128)(2,1)S(1)} %collective-permute-done.4.refs_3_), channel_id=1, source_target_pairs={{0,1},{1,0},{2,3},{3,2},{4,5},{5,4},{6,7},{7,6},{8,9},{9,8},{10,11... | collective-permute-start | bytes 786440 | tf_op jit(solution)/shard_map/ppermute | solution.py:133
  34.7 8.9 %copy-start.11 = (bf16[1024,512]{1,0:T(8,128)(2,1)}, bf16[1024,512]{1,0:T(8,128)(2,1)S(1)}, u32[]{:S(2)}) copy-start(bf16[1024,512]{1,0:T(8,128)(2,1)S(1)} %get-tuple-element.120.refs_2_.refs_1_) | copy-start | bytes 3145732
  34.8 2.0 %collective-permute-start.9 = (bf16[2,256,512]{2,1,0:T(8,128)(2,1)S(1)}, bf16[2,256,512]{2,1,0:T(8,128)(2,1)S(1)}, u32[]{:S(2)}, u32[]{:S(2)}) collective-permute-start(bf16[2,256,512]{2,1,0:T(8,128)(2,1)S(1)} %bitcast.11), channel_id=1, source_target_pairs={{0,1},{1,0},{2,3},{3,2},{4,5},{5,4},{6,7},{7,6},{8,9},{9,8},{10,11... | collective-permute-start | bytes 1572872 | tf_op jit(solution)/shard_map/ppermute | solution.py:133
  38.0 8.7 %collective-permute-start.11 = (bf16[256,512]{1,0:T(8,128)(2,1)}, bf16[256,512]{1,0:T(8,128)(2,1)}, u32[]{:S(2)}, u32[]{:S(2)}) collective-permute-start(bf16[256,512]{1,0:T(8,128)(2,1)} %get-tuple-element.117), channel_id=1, source_target_pairs={{0,2},{1,3},{2,0},{3,1},{4,6},{5,7},{6,4},{7,5},{8,10},{9,11},{10,... | collective-permute-start | bytes 786440 | tf_op jit(solution)/shard_map/ppermute | solution.py:133
  42.1 14.4 %collective-permute-start.10 = (bf16[528,512]{1,0:T(8,128)(2,1)}, bf16[528,512]{1,0:T(8,128)(2,1)}, u32[]{:S(2)}, u32[]{:S(2)}) collective-permute-start(bf16[528,512]{1,0:T(8,128)(2,1)} %get-tuple-element.123), channel_id=1, source_target_pairs={{0,4},{4,0},{8,12},{12,8},{16,20},{20,16},{24,28},{28,24},{1,5},{5... | collective-permute-start | bytes 1622024 | tf_op jit(solution)/shard_map/ppermute | solution.py:133
  43.7 3.0 %copy-start.10 = (f32[2,512]{1,0:T(2,128)S(1)}, f32[2,512]{1,0:T(2,128)}, u32[]{:S(2)}) copy-start(f32[2,512]{1,0:T(2,128)} %copy-done.9) | copy-start | bytes 12292
  48.0 4.0 %copy-start.12 = (bf16[1024,512]{1,0:T(8,128)(2,1)S(1)}, bf16[1024,512]{1,0:T(8,128)(2,1)}, u32[]{:S(2)}) copy-start(bf16[1024,512]{1,0:T(8,128)(2,1)} %copy-done.11) | copy-start | bytes 3145732
  48.0 7.6 %collective-permute-start.13 = (bf16[256,512]{1,0:T(8,128)(2,1)S(1)}, bf16[256,512]{1,0:T(8,128)(2,1)S(1)}, u32[]{:S(2)}, u32[]{:S(2)}) collective-permute-start(bf16[256,512]{1,0:T(8,128)(2,1)S(1)} %get-tuple-element.131.refs_1_), channel_id=1, source_target_pairs={{0,2},{1,3},{2,0},{3,1},{4,6},{5,7},{6,4},{7,5},{8,10},{9,11},{10,... | collective-permute-start | bytes 786440 | tf_op jit(solution)/shard_map/ppermute | solution.py:133
  49.8 7.8 %collective-permute-start.12 = (bf16[256,512]{1,0:T(8,128)(2,1)S(1)}, bf16[256,512]{1,0:T(8,128)(2,1)S(1)}, u32[]{:S(2)}, u32[]{:S(2)}) collective-permute-start(bf16[256,512]{1,0:T(8,128)(2,1)S(1)} %get-tuple-element.131.refs_1_), channel_id=1, source_target_pairs={{0,1},{1,0},{2,3},{3,2},{4,5},{5,4},{6,7},{7,6},{8,9},{9,8},{10,11... | collective-permute-start | bytes 786440 | tf_op jit(solution)/shard_map/ppermute | solution.py:133
  52.0 5.7 %copy-start.1 = (f32[2048,128]{1,0:T(8,128)S(1)}, f32[2048,128]{1,0:T(8,128)}, u32[]{:S(2)}) copy-start(f32[2048,128]{1,0:T(8,128)} %copy-done) | copy-start | bytes 3145732
  52.0 5.7 %copy-start.3 = (bf16[2,512,256]{2,1,0:T(8,128)(2,1)S(1)}, bf16[2,512,256]{2,1,0:T(8,128)(2,1)}, u32[]{:S(2)}) copy-start(bf16[2,512,256]{2,1,0:T(8,128)(2,1)} %copy-done.2) | copy-start | bytes 1572868
  52.0 5.7 %copy-start.5 = (bf16[2,256,512]{2,1,0:T(8,128)(2,1)S(1)}, bf16[2,256,512]{2,1,0:T(8,128)(2,1)}, u32[]{:S(2)}) copy-start(bf16[2,256,512]{2,1,0:T(8,128)(2,1)} %copy-done.4) | copy-start | bytes 1572868
  52.0 5.7 %copy-start.7 = (bf16[3,512,128]{2,1,0:T(8,128)(2,1)S(1)}, bf16[3,512,128]{2,1,0:T(8,128)(2,1)}, u32[]{:S(2)}) copy-start(bf16[3,512,128]{2,1,0:T(8,128)(2,1)} %copy-done.6) | copy-start | bytes 1179652
  55.6 2.1 %collective-permute-start.14 = (bf16[256,512]{1,0:T(8,128)(2,1)S(1)}, bf16[256,512]{1,0:T(8,128)(2,1)S(1)}, u32[]{:S(2)}, u32[]{:S(2)}) collective-permute-start(bf16[256,512]{1,0:T(8,128)(2,1)S(1)} %collective-permute-done.13.refs_3_), channel_id=1, source_target_pairs={{0,1},{1,0},{2,3},{3,2},{4,5},{5,4},{6,7},{7,6},{8,9},{9,8},{10,11... | collective-permute-start | bytes 786440 | tf_op jit(solution)/shard_map/ppermute | solution.py:133
  55.6 15.7 %collective-permute-start.17 = (bf16[2,1024,128]{2,1,0:T(8,128)(2,1)}, bf16[2,1024,128]{2,1,0:T(8,128)(2,1)}, u32[]{:S(2)}, u32[]{:S(2)}) collective-permute-start(bf16[2,1024,128]{2,1,0:T(8,128)(2,1)} %get-tuple-element.134), channel_id=1, source_target_pairs={{0,1},{1,0},{2,3},{3,2},{4,5},{5,4},{6,7},{7,6},{8,9},{9,8},{10,11... | collective-permute-start | bytes 1572872 | tf_op jit(solution)/shard_map/ppermute | solution.py:133
  65.4 20.7 %copy-start.8 = (f32[2,64,512]{2,1,0:T(8,128)S(1)}, f32[2,64,512]{2,1,0:T(8,128)}, u32[]{:S(2)}) copy-start(f32[2,64,512]{2,1,0:T(8,128)} %refs_1_.5) | copy-start | bytes 786436
  65.4 17.1 %collective-permute-start.16 = (bf16[2,1040,128]{2,1,0:T(8,128)(2,1)}, bf16[2,1040,128]{2,1,0:T(8,128)(2,1)S(1)}, u32[]{:S(2)}, u32[]{:S(2)}) collective-permute-start(bf16[2,1040,128]{2,1,0:T(8,128)(2,1)} %get-tuple-element.145), channel_id=1, source_target_pairs={{0,1},{1,0},{2,3},{3,2},{4,5},{5,4},{6,7},{7,6},{8,9},{9,8},{10,11... | collective-permute-start | bytes 1597448 | tf_op jit(solution)/shard_map/ppermute | solution.py:133
  65.5 8.2 %collective-permute-start.15 = (bf16[4,224,128]{2,1,0:T(8,128)(2,1)}, bf16[4,224,128]{2,1,0:T(8,128)(2,1)S(1)}, u32[]{:S(2)}, u32[]{:S(2)}) collective-permute-start(bf16[4,224,128]{2,1,0:T(8,128)(2,1)} %get-tuple-element.143), channel_id=1, source_target_pairs={{0,4},{4,0},{8,12},{12,8},{16,20},{20,16},{24,28},{28,24},{1,5},{5... | collective-permute-start | bytes 688136 | tf_op jit(solution)/shard_map/ppermute | solution.py:133
  67.2 18.9 %collective-permute-start.19 = (bf16[144,512]{1,0:T(8,128)(2,1)S(1)}, bf16[144,512]{1,0:T(8,128)(2,1)S(1)}, u32[]{:S(2)}, u32[]{:S(2)}) collective-permute-start(bf16[144,512]{1,0:T(8,128)(2,1)S(1)} %get-tuple-element.150), channel_id=1, source_target_pairs={{0,8},{4,12},{8,0},{12,4},{16,24},{20,28},{24,16},{28,20},{1,9},{5... | collective-permute-start | bytes 442376 | tf_op jit(solution)/shard_map/ppermute | solution.py:133
  68.8 17.3 %collective-permute-start.20 = (bf16[144,512]{1,0:T(8,128)(2,1)S(1)}, bf16[144,512]{1,0:T(8,128)(2,1)S(1)}, u32[]{:S(2)}, u32[]{:S(2)}) collective-permute-start(bf16[144,512]{1,0:T(8,128)(2,1)S(1)} %get-tuple-element.151), channel_id=1, source_target_pairs={{0,16},{4,20},{8,24},{12,28},{16,0},{20,4},{24,8},{28,12},{1,17},{... | collective-permute-start | bytes 442376 | tf_op jit(solution)/shard_map/ppermute | solution.py:133
  71.4 14.7 %collective-permute-start.21 = (bf16[144,512]{1,0:T(8,128)(2,1)S(1)}, bf16[144,512]{1,0:T(8,128)(2,1)S(1)}, u32[]{:S(2)}, u32[]{:S(2)}) collective-permute-start(bf16[144,512]{1,0:T(8,128)(2,1)S(1)} %get-tuple-element.152), channel_id=1, source_target_pairs={{0,24},{4,28},{8,16},{12,20},{16,8},{20,12},{24,0},{28,4},{1,25},{... | collective-permute-start | bytes 442376 | tf_op jit(solution)/shard_map/ppermute | solution.py:133
  73.7 1.6 %copy-start.13 = (bf16[4,224,128]{2,1,0:T(8,128)(2,1)}, bf16[4,224,128]{2,1,0:T(8,128)(2,1)S(1)}, u32[]{:S(2)}) copy-start(bf16[4,224,128]{2,1,0:T(8,128)(2,1)S(1)} %collective-permute-done.15.refs_2_) | copy-start | bytes 688132
  73.7 12.3 %collective-permute-start.18 = (f32[64,512]{1,0:T(8,128)S(1)}, f32[64,512]{1,0:T(8,128)S(1)}, u32[]{:S(2)}, u32[]{:S(2)}) collective-permute-start(f32[64,512]{1,0:T(8,128)S(1)} %get-tuple-element.149), channel_id=1, source_target_pairs={{0,4},{4,0},{8,12},{12,8},{16,20},{20,16},{24,28},{28,24},{1,5},{5... | collective-permute-start | bytes 393224 | tf_op jit(solution)/shard_map/ppermute | solution.py:133
  77.6 16.6 %all-to-all-start = ((bf16[4,224,128]{2,1,0:T(8,128)(2,1)}), bf16[4,224,128]{2,1,0:T(8,128)(2,1)S(1)}, u32[]{:S(2)}, u32[]{:S(2)}) async-start(bf16[4,224,128]{2,1,0:T(8,128)(2,1)} %shard_map.235), calls=%async_computation | async-start | bytes 458752 | tf_op jit(solution)/shard_map/all_to_all | solution.py:969
  87.5 14.1 %collective-permute-start.26 = (bf16[128,512]{1,0:T(8,128)(2,1)S(1)}, bf16[128,512]{1,0:T(8,128)(2,1)S(1)}, u32[]{:S(2)}, u32[]{:S(2)}) collective-permute-start(bf16[128,512]{1,0:T(8,128)(2,1)S(1)} %get-tuple-element.169.refs_1_), channel_id=1, source_target_pairs={{0,24},{4,28},{8,16},{12,20},{16,8},{20,12},{24,0},{28,4},{1,25},{... | collective-permute-start | bytes 393224 | tf_op jit(solution)/shard_map/ppermute | solution.py:133
  91.4 10.2 %collective-permute-start.25 = (bf16[128,512]{1,0:T(8,128)(2,1)S(1)}, bf16[128,512]{1,0:T(8,128)(2,1)S(1)}, u32[]{:S(2)}, u32[]{:S(2)}) collective-permute-start(bf16[128,512]{1,0:T(8,128)(2,1)S(1)} %get-tuple-element.169.refs_1_), channel_id=1, source_target_pairs={{0,16},{4,20},{8,24},{12,28},{16,0},{20,4},{24,8},{28,12},{1,17},{... | collective-permute-start | bytes 393224 | tf_op jit(solution)/shard_map/ppermute | solution.py:133
  91.4 10.2 %collective-permute-start.24 = (bf16[128,512]{1,0:T(8,128)(2,1)S(1)}, bf16[128,512]{1,0:T(8,128)(2,1)S(1)}, u32[]{:S(2)}, u32[]{:S(2)}) collective-permute-start(bf16[128,512]{1,0:T(8,128)(2,1)S(1)} %get-tuple-element.169.refs_1_), channel_id=1, source_target_pairs={{0,8},{4,12},{8,0},{12,4},{16,24},{20,28},{24,16},{28,20},{1,9},{5... | collective-permute-start | bytes 393224 | tf_op jit(solution)/shard_map/ppermute | solution.py:133
  92.1 17.3 %collective-permute-start.22 = (bf16[2064,128]{1,0:T(8,128)(2,1)}, bf16[2064,128]{1,0:T(8,128)(2,1)}, u32[]{:S(2)}, u32[]{:S(2)}) collective-permute-start(bf16[2064,128]{1,0:T(8,128)(2,1)} %get-tuple-element.147), channel_id=1, source_target_pairs={{0,2},{1,3},{2,0},{3,1},{4,6},{5,7},{6,4},{7,5},{8,10},{9,11},{10,... | collective-permute-start | bytes 1585160 | tf_op jit(solution)/shard_map/ppermute | solution.py:133
  93.6 13.5 %collective-permute-start.23 = (f32[64,512]{1,0:T(8,128)}, f32[64,512]{1,0:T(8,128)}, u32[]{:S(2)}, u32[]{:S(2)}) collective-permute-start(f32[64,512]{1,0:T(8,128)} %get-tuple-element.167), channel_id=1, source_target_pairs={{0,4},{4,0},{8,12},{12,8},{16,20},{20,16},{24,28},{28,24},{1,5},{5... | collective-permute-start | bytes 393224 | tf_op jit(solution)/shard_map/ppermute | solution.py:133
  96.6 24.3 %all-to-all-start.1 = ((bf16[32,64,128]{2,1,0:T(8,128)(2,1)}), bf16[32,64,128]{2,1,0:T(8,128)(2,1)}, u32[]{:S(2)}, u32[]{:S(2)}) async-start(bf16[32,64,128]{2,1,0:T(8,128)(2,1)} %get-tuple-element.155), calls=%async_computation.1 | async-start | bytes 1048576 | tf_op jit(solution)/shard_map/all_to_all | solution.py:997
  102.3 17.8 %collective-permute-start.29 = (bf16[512,512]{1,0:T(8,128)(2,1)S(1)}, bf16[512,512]{1,0:T(8,128)(2,1)S(1)}, u32[]{:S(2)}, u32[]{:S(2)}) collective-permute-start(bf16[512,512]{1,0:T(8,128)(2,1)S(1)} %shard_map.241.refs_1_), channel_id=1, source_target_pairs={{0,3},{4,7},{8,11},{12,15},{16,19},{20,23},{24,27},{28,31}} | collective-permute-start | bytes 1572872 | tf_op jit(solution)/shard_map/ppermute | solution.py:1001
  105.7 14.4 %collective-permute-start.28 = (bf16[512,512]{1,0:T(8,128)(2,1)S(1)}, bf16[512,512]{1,0:T(8,128)(2,1)S(1)}, u32[]{:S(2)}, u32[]{:S(2)}) collective-permute-start(bf16[512,512]{1,0:T(8,128)(2,1)S(1)} %shard_map.241.refs_1_), channel_id=1, source_target_pairs={{1,3},{5,7},{9,11},{13,15},{17,19},{21,23},{25,27},{29,31}} | collective-permute-start | bytes 1572872 | tf_op jit(solution)/shard_map/ppermute | solution.py:1001
  106.4 13.7 %collective-permute-start.27 = (bf16[512,512]{1,0:T(8,128)(2,1)S(1)}, bf16[512,512]{1,0:T(8,128)(2,1)S(1)}, u32[]{:S(2)}, u32[]{:S(2)}) collective-permute-start(bf16[512,512]{1,0:T(8,128)(2,1)S(1)} %shard_map.241.refs_1_), channel_id=1, source_target_pairs={{2,3},{6,7},{10,11},{14,15},{18,19},{22,23},{26,27},{30,31}} | collective-permute-start | bytes 1572872 | tf_op jit(solution)/shard_map/ppermute | solution.py:1001
  123.2 26.4 %all-to-all-start.2 = ((bf16[8,64,512]{2,1,0:T(8,128)(2,1)}), bf16[8,64,512]{2,1,0:T(8,128)(2,1)S(1)}, u32[]{:S(2)}, u32[]{:S(2)}) async-start(bf16[8,64,512]{2,1,0:T(8,128)(2,1)} %shard_map.243), calls=%async_computation.2 | async-start | bytes 1048576 | tf_op jit(solution)/shard_map/all_to_all | solution.py:1024

commit v4 on v3

--- a/solution.py
+++ b/solution.py
@@ -241,11 +241,6 @@
         self.shape, self.dtype, self.own = shape, dtype, own
 
 
-class Bare:
-    def __init__(self, shape, dtype):
-        self.shape, self.dtype = shape, dtype
-
-
 class Waiting:
     def __init__(self, copy, ref):
         self.copy, self.ref, self.started = copy, ref, False
@@ -260,7 +255,7 @@
 
 
 def call(kernel, outs, scratch, args, time, limit):
-    outs = [o if isinstance(o, (Store, Bare)) else jax.ShapeDtypeStruct(*o) for o in outs]
+    outs = [o if isinstance(o, Store) else jax.ShapeDtypeStruct(*o) for o in outs]
     late = [a for a in (*args, *outs) if isinstance(a, (Late, Store))]
     n_in, n_out = len(args), len(outs)
 
@@ -291,9 +286,9 @@
 
     return pl.pallas_call(
         body,
-        out_shape=tuple(pltpu.HBM(o.shape, o.dtype) if isinstance(o, (Store, Bare)) else o for o in outs),
+        out_shape=tuple(pltpu.HBM(o.shape, o.dtype) if isinstance(o, Store) else o for o in outs),
         in_specs=[SMEM] + [HBM if isinstance(a, Late) else VMEM for a in args[1:]],
-        out_specs=tuple(HBM if isinstance(o, (Store, Bare)) else VMEM for o in outs),
+        out_specs=tuple(HBM if isinstance(o, Store) else VMEM for o in outs),
         scratch_shapes=[pltpu.VMEM(a.shape, a.dtype) for a in late]
         + [pltpu.VMEM(*what) if isinstance(what, tuple) else what for what in scratch]
         + ([pltpu.SemaphoreType.DMA((len(late),))] if late else []),
@@ -634,7 +629,6 @@
 
 
 def pair_sum_kernel(info, keep, came, out):
-    keep, came = keep.ready(), came.ready()
     for z in range(keep.shape[0]):
         out.ref[z] = (keep[z].astype(F32) + came[z].astype(F32)).astype(out.ref.dtype)
 
@@ -956,7 +950,7 @@
     piece = (pairs, 3 * rows + slot, part)
     slots_keep, slots_send, one_near, one_kept, delta_own, gain_part = call(
         mixer_back_kernel,
-        [Bare(piece, piece_type), Bare(piece, piece_type), Store((2, bucket + 16, part), BF16),
+        [(piece, piece_type), (piece, piece_type), Store((2, bucket + 16, part), BF16),
          Store((2, bucket + 16, part), F32), Store((bucket, part), BF16), Store((8, part), F32)],
         [((2, *piece), piece_type), pltpu.SemaphoreType.DMA((2,)), whole_like, wide_like, spec_like, spec_like,
          ((8 * half, part), F32), ((bucket, 2 * part), BF16), ((bucket, width), F32)],
@@ -965,7 +959,7 @@
         1000, 18,
     )
     slots_came = swap(slots_send.astype(BF16), "dp", 1).astype(piece_type)
-    (slots,) = call(pair_sum_kernel, [Store(piece, piece_type)], [], (info, Late(slots_keep), Late(slots_came)), 0, 6)
+    (slots,) = call(pair_sum_kernel, [Store(piece, piece_type)], [], (info, slots_keep, slots_came), 0, 6)
     arrived = lax.all_to_all(slots.astype(BF16), "dp", 0, 0, tiled=True, axis_index_groups=parities)
     one_mine, one_tail, out_mine, far = call(
         join_late_kernel,

time: 153 us -> 153 us (level)
  transfers between devices with their start and end apart: 33 -> 33, of which waited for: 12 -> 14; matrix products, arithmetic and copies ran while one was open for 0% -> 0% of each run, Pallas kernels for 33% -> 33%
where the time goes in v4:
time: 153 us; the launch traced here: 152 us
  Pallas kernels  62.2 us (41%)
  starting transfers between devices  56.9 us (37%)
  waiting for transfers between devices  30.6 us (20%)
  between operations  1.95 us (1%)
    pallas_call x21, Pallas kernels, call(): pl.pallas_call(body, out_shape=tuple((pltpu.HBM(o.shape, o.dtype) if isin...  53.6 us
    ppermute x27, starting transfers between devices, swap(): return lax.ppermute(value, axis, [(i, i ^ k) for i in range(size)])  26.8 us
    ppermute x27, waiting for transfers between devices, swap(): return lax.ppermute(value, axis, [(i, i ^ k) for i in range(size)])  17 us
    all_to_all x1, starting transfers between devices, per_device(): lax.all_to_all(sends.astype(BF16), ('dp', 'tensor'), 0, 0, tiled=True, ax...  16.6 us
    ppermute x3, waiting for transfers between devices, per_device(): lax.ppermute(mlp_columns, 'tensor', [(3 ^ k, 3)])  7.11 us
    pallas_call x3, Pallas kernels, fetch(): pl.pallas_call(body, out_shape=tuple(shapes), in_specs=[SMEM] + [HBM] * l...  6.23 us
    all_to_all x1, waiting for transfers between devices, per_device(): lax.all_to_all(sends.astype(BF16), ('dp', 'tensor'), 0, 0, tiled=True, ax...  6.12 us
    all_to_all x1, starting transfers between devices, per_device(): lax.all_to_all(slots.astype(BF16), 'dp', 0, 0, tiled=True, axis_index_gro...  4.88 us
  transfers between devices with their start and end apart: 33, of which 14 were waited for; matrix products, arithmetic and copies ran while one was open for 0% of the time, Pallas kernels for 33%

profile of v4, /device:TPU:0, one launch (start us, length us, event | category | flops | bytes accessed | tf_op | source)
XLA Modules:
  0.0 151.8 jit_solution(12459689345747485090)
XLA Ops:
  0.6 3.0 %collective-permute-start.1 = (bf16[1024,128]{1,0:T(8,128)(2,1)}, bf16[1024,128]{1,0:T(8,128)(2,1)S(1)}, u32[]{:S(2)}, u32[]{:S(2)}) collective-permute-start(bf16[1024,128]{1,0:T(8,128)(2,1)} %bitcast.17), channel_id=1, source_target_pairs={{0,2},{1,3},{2,0},{3,1},{4,6},{5,7},{6,4},{7,5},{8,10},{9,11},{10,... | collective-permute-start | bytes 786440 | tf_op jit(solution)/shard_map/ppermute | solution.py:133
  4.4 2.1 %shard_map.222 = (bf16[1024,128]{1,0:T(8,128)(2,1)S(1)}, bf16[3,512,128]{2,1,0:T(8,128)(2,1)S(1)}, f32[2,512]{1,0:T(2,128)S(1)}, bf16[2,512,256]{2,1,0:T(8,128)(...) custom-call(s32[3]{0:T(128)S(1)} %pad_add_fusion.token_ref.refs_0_.info, ...), custom_call_target="tpu_custom_call" | custom-call | flops 10000000000 | tf_op jit(solution)/shard_map/pallas_call | solution.py:321
  6.7 3.1 %shard_map.223.refs_9_.refs_12_ = f32[2048,128]{1,0:T(8,128)S(1)} custom-call(s32[3]{0:T(128)S(1)} %pad_add_fusion.token_ref.refs_0_.info, bf16[2,2048,160]{2,1,0:T(8,128)(2,1)} %constant.19.clone.refs_1_, f32[160,128]{1,0:T(8,128)} %bitcast.13), custom_call_target="tpu_custom_call" | custom-call | flops 20000000000 | tf_op jit(solution)/shard_map/pallas_call | solution.py:287
  9.8 0.8 collective-permute-done.1.refs_3_
  10.7 0.5 collective-permute-start.5
  11.2 1.0 collective-permute-done.2.refs_4_
  12.2 3.6 %shard_map.224 = (bf16[1024,512]{1,0:T(8,128)(2,1)S(1)}, bf16[1024,512]{1,0:T(8,128)(2,1)S(1)}, f32[1024,128]{1,0:T(8,128)}, f32[1024,1]{1,0:T(8,128)}, f32[512,...) custom-call(s32[3]{0:T(128)S(1)} %pad_add_fusion.token_ref.refs_0_.i, ...), custom_call_target="tpu_custom_call" | custom-call | flops 1000000 | tf_op jit(solution)/shard_map/pallas_call | solution.py:287
  15.9 2.7 %collective-permute-done.6.refs_3_ = bf16[1536,128]{1,0:T(8,128)(2,1)S(1)} collective-permute-done((bf16[1536,128]{1,0:T(8,128)(2,1)S(1)}, bf16[1536,128]{1,0:T(8,128)(2,1)S(1)}, u32[]{:S(2)}, u32[]{:S(2)}) %collective-permute-start.6) | collective-permute-done | bytes 393248 | tf_op jit(solution)/shard_map/ppermute | solution.py:133
  18.6 1.7 %collective-permute-start.4 = (bf16[1024,128]{1,0:T(8,128)(2,1)S(1)}, bf16[1024,128]{1,0:T(8,128)(2,1)S(1)}, u32[]{:S(2)}, u32[]{:S(2)}) collective-permute-start(bf16[1024,128]{1,0:T(8,128)(2,1)S(1)} %get-tuple-element.105.refs_1_.refs_9_), channel_id=1, source_target_pairs={{0,2},{1,3},{2,0},{3,1},{4,6},{5,7},{6,4},{7,5},{8,10},{9,11},{10,... | collective-permute-start | bytes 786440 | tf_op jit(solution)/shard_map/ppermute | solution.py:133
  20.3 0.2 collective-permute-start.3
  20.6 2.7 %shard_map.225 = (bf16[1024,512]{1,0:T(8,128)(2,1)S(1)}, bf16[512,512]{1,0:T(8,128)(2,1)S(1)}, f32[1024,512]{1,0:T(8,128)S(1)}, bf16[2,512,512]{2,1,0:T(8,128)(2,1)S(1)}) custom-call(s32[3]{0:T(128)S(1)} %pad_add_fusion.token_ref.refs_0_.info, bf16[1536,128]{1,0:T(8,128)(2,1)S(1)} %get-tuple-element.107.refs_1_, ...), custom_call_target="tpu_custom_call" | custom-call | flops 30000001024 | tf_op jit(solution)/shard_map/pallas_call | solution.py:287
  23.3 4.0 %collective-permute-done.4.refs_3_ = bf16[1024,128]{1,0:T(8,128)(2,1)S(1)} collective-permute-done((bf16[1024,128]{1,0:T(8,128)(2,1)S(1)}, bf16[1024,128]{1,0:T(8,128)(2,1)S(1)}, u32[]{:S(2)}, u32[]{:S(2)}) %collective-permute-start.4) | collective-permute-done | bytes 262176 | tf_op jit(solution)/shard_map/ppermute | solution.py:133
  27.3 1.5 %collective-permute-done.8.refs_4_ = bf16[1024,128]{1,0:T(8,128)(2,1)S(1)} collective-permute-done((bf16[1024,128]{1,0:T(8,128)(2,1)S(1)}, bf16[1024,128]{1,0:T(8,128)(2,1)S(1)}, u32[]{:S(2)}, u32[]{:S(2)}) %collective-permute-start.8) | collective-permute-done | bytes 262176 | tf_op jit(solution)/shard_map/ppermute | solution.py:133
  28.9 5.9 %shard_map.226 = (bf16[512,512]{1,0:T(8,128)(2,1)S(1)}, f32[512,512]{1,0:T(8,128)S(1)}, bf16[1024,512]{1,0:T(8,128)(2,1)S(1)}, bf16[1024,512]{1,0:T(8,128)(2,1)S...) custom-call(s32[3]{0:T(128)S(1)} %pad_add_fusion.token_ref.refs_0_.inf, ...), custom_call_target="tpu_custom_call" | custom-call | flops 60000002048 | tf_op jit(solution)/shard_map/pallas_call | solution.py:287
  34.8 0.2 collective-permute-start.9
  35.0 1.8 %collective-permute-done.9.refs_2_ = bf16[2,256,512]{2,1,0:T(8,128)(2,1)S(1)} collective-permute-done((bf16[2,256,512]{2,1,0:T(8,128)(2,1)S(1)}, bf16[2,256,512]{2,1,0:T(8,128)(2,1)S(1)}, u32[]{:S(2)}, u32[]{:S(2)}) %collective-permute-start.9) | collective-permute-done | bytes 524320 | tf_op jit(solution)/shard_map/ppermute | solution.py:133
  36.7 1.3 shard_map.227
  38.0 1.7 %collective-permute-start.11 = (bf16[256,512]{1,0:T(8,128)(2,1)}, bf16[256,512]{1,0:T(8,128)(2,1)}, u32[]{:S(2)}, u32[]{:S(2)}) collective-permute-start(bf16[256,512]{1,0:T(8,128)(2,1)} %get-tuple-element.117), channel_id=1, source_target_pairs={{0,2},{1,3},{2,0},{3,1},{4,6},{5,7},{6,4},{7,5},{8,10},{9,11},{10,... | collective-permute-start | bytes 786440 | tf_op jit(solution)/shard_map/ppermute | solution.py:133
  39.8 2.3 %shard_map.228 = (bf16[528,512]{1,0:T(8,128)(2,1)}, f32[64,512]{1,0:T(8,128)S(1)}) custom-call(s32[3]{0:T(128)S(1)} %pad_add_fusion.token_ref.refs_0_.info, bf16[1024,512]{1,0:T(8,128)(2,1)S(1)} %get-tuple-element.119.refs_1_, bf16[1024,512]{1,0:T(8,128)(2,1)S(1)} %get-tuple-element.120.refs_2_.refs_1_, bf16[1024,512]{1,0:T(8,128)(2,1)S(1)} %get-tuple-element.121.refs_3_, ...), custom_call_target="tpu_custom_call" | custom-call | flops 20000000000 | tf_op jit(solution)/shard_map/pallas_call | solution.py:287
  42.1 1.6 %collective-permute-start.10 = (bf16[528,512]{1,0:T(8,128)(2,1)}, bf16[528,512]{1,0:T(8,128)(2,1)}, u32[]{:S(2)}, u32[]{:S(2)}) collective-permute-start(bf16[528,512]{1,0:T(8,128)(2,1)} %get-tuple-element.123), channel_id=1, source_target_pairs={{0,4},{4,0},{8,12},{12,8},{16,20},{20,16},{24,28},{28,24},{1,5},{5... | collective-permute-start | bytes 1622024 | tf_op jit(solution)/shard_map/ppermute | solution.py:133
  43.7 1.5 shard_map.229.refs_1_
  45.2 1.5 %collective-permute-done.11.refs_2_ = bf16[256,512]{1,0:T(8,128)(2,1)} collective-permute-done((bf16[256,512]{1,0:T(8,128)(2,1)}, bf16[256,512]{1,0:T(8,128)(2,1)}, u32[]{:S(2)}, u32[]{:S(2)}) %collective-permute-start.11) | collective-permute-done | bytes 262176 | tf_op jit(solution)/shard_map/ppermute | solution.py:133
  46.7 1.3 shard_map.231
  48.0 1.8 %collective-permute-start.13 = (bf16[256,512]{1,0:T(8,128)(2,1)S(1)}, bf16[256,512]{1,0:T(8,128)(2,1)S(1)}, u32[]{:S(2)}, u32[]{:S(2)}) collective-permute-start(bf16[256,512]{1,0:T(8,128)(2,1)S(1)} %get-tuple-element.131.refs_1_), channel_id=1, source_target_pairs={{0,2},{1,3},{2,0},{3,1},{4,6},{5,7},{6,4},{7,5},{8,10},{9,11},{10,... | collective-permute-start | bytes 786440 | tf_op jit(solution)/shard_map/ppermute | solution.py:133
  49.8 2.1 %shard_map.232.refs_15_ = bf16[2,256,2048]{2,1,0:T(8,128)(2,1)S(1)} custom-call(s32[3]{0:T(128)S(1)} %pad_add_fusion.token_ref.refs_0_.info, bf16[2,256,2048]{2,1,0:T(8,128)(2,1)} %constant.20.clone.refs_0_), custom_call_target="tpu_custom_call" | custom-call | flops 1000000 | tf_op jit(solution)/shard_map/pallas_call | solution.py:321
  52.0 2.6 %shard_map.233 = (bf16[2,1024,128]{2,1,0:T(8,128)(2,1)}, f32[2,1024,128]{2,1,0:T(8,128)}) custom-call(s32[3]{0:T(128)S(1)} %pad_add_fusion.token_ref.refs_0_.info, bf16[1024,512]{1,0:T(8,128)(2,1)S(1)} %copy-done.12, bf16[2,512,512]{2,1,0:T(8,128)(2,1)S(1)} %get-tuple-element.114.refs_8_.refs_2_), custom_call_target="tpu_custom_call" | custom-call | flops 10000000000 | tf_op jit(solution)/shard_map/pallas_call | solution.py:287
  54.6 1.0 collective-permute-done.13.refs_3_
  55.6 0.5 collective-permute-start.17
  56.1 0.4 collective-permute-done.10.refs_2_
  56.5 1.2 shard_map.230
  57.7 8.0 %shard_map.234 = (bf16[4,224,128]{2,1,0:T(8,128)(2,1)S(1)}, bf16[4,224,128]{2,1,0:T(8,128)(2,1)S(1)}, bf16[2,1040,128]{2,1,0:T(8,128)(2,1)}, f32[2,1040,128]{2,1...) custom-call(s32[3]{0:T(128)S(1)} %pad_add_fusion.token_ref.refs_0_.info, ...), custom_call_target="tpu_custom_call" | custom-call | flops 9999999827968 | tf_op jit(solution)/shard_map/pallas_call | solution.py:287
  65.8 1.7 %collective-permute-start.15 = (bf16[4,224,128]{2,1,0:T(8,128)(2,1)S(1)}, bf16[4,224,128]{2,1,0:T(8,128)(2,1)S(1)}, u32[]{:S(2)}, u32[]{:S(2)}) collective-permute-start(bf16[4,224,128]{2,1,0:T(8,128)(2,1)S(1)} %get-tuple-element.143), channel_id=1, source_target_pairs={{0,4},{4,0},{8,12},{12,8},{16,20},{20,16},{24,28},{28,24},{1,5},{5... | collective-permute-start | bytes 688136 | tf_op jit(solution)/shard_map/ppermute | solution.py:133
  67.5 1.6 %collective-permute-start.19 = (bf16[144,512]{1,0:T(8,128)(2,1)S(1)}, bf16[144,512]{1,0:T(8,128)(2,1)S(1)}, u32[]{:S(2)}, u32[]{:S(2)}) collective-permute-start(bf16[144,512]{1,0:T(8,128)(2,1)S(1)} %get-tuple-element.150), channel_id=1, source_target_pairs={{0,8},{4,12},{8,0},{12,4},{16,24},{20,28},{24,16},{28,20},{1,9},{5... | collective-permute-start | bytes 442376 | tf_op jit(solution)/shard_map/ppermute | solution.py:133
  69.1 2.6 %collective-permute-start.20 = (bf16[144,512]{1,0:T(8,128)(2,1)S(1)}, bf16[144,512]{1,0:T(8,128)(2,1)S(1)}, u32[]{:S(2)}, u32[]{:S(2)}) collective-permute-start(bf16[144,512]{1,0:T(8,128)(2,1)S(1)} %get-tuple-element.151), channel_id=1, source_target_pairs={{0,16},{4,20},{8,24},{12,28},{16,0},{20,4},{24,8},{28,12},{1,17},{... | collective-permute-start | bytes 442376 | tf_op jit(solution)/shard_map/ppermute | solution.py:133
  71.7 0.2 collective-permute-start.21
  71.9 1.9 %collective-permute-done.15.refs_2_ = bf16[4,224,128]{2,1,0:T(8,128)(2,1)S(1)} collective-permute-done((bf16[4,224,128]{2,1,0:T(8,128)(2,1)S(1)}, bf16[4,224,128]{2,1,0:T(8,128)(2,1)S(1)}, u32[]{:S(2)}, u32[]{:S(2)}) %collective-permute-start.15) | collective-permute-done | bytes 229408 | tf_op jit(solution)/shard_map/ppermute | solution.py:133
  73.9 1.5 %collective-permute-start.18 = (f32[64,512]{1,0:T(8,128)S(1)}, f32[64,512]{1,0:T(8,128)S(1)}, u32[]{:S(2)}, u32[]{:S(2)}) collective-permute-start(f32[64,512]{1,0:T(8,128)S(1)} %get-tuple-element.149), channel_id=1, source_target_pairs={{0,4},{4,0},{8,12},{12,8},{16,20},{20,16},{24,28},{28,24},{1,5},{5... | collective-permute-start | bytes 393224 | tf_op jit(solution)/shard_map/ppermute | solution.py:133
  75.4 1.3 shard_map.235
  76.7 4.9 %all-to-all-start = ((bf16[4,224,128]{2,1,0:T(8,128)(2,1)}), bf16[4,224,128]{2,1,0:T(8,128)(2,1)S(1)}, u32[]{:S(2)}, u32[]{:S(2)}) async-start(bf16[4,224,128]{2,1,0:T(8,128)(2,1)} %shard_map.235), calls=%async_computation | async-start | bytes 458752 | tf_op jit(solution)/shard_map/all_to_all | solution.py:963
  81.6 3.5 %shard_map.236 = (f32[1024,128]{1,0:T(8,128)S(1)}, f32[16,128]{1,0:T(8,128)S(1)}, f32[1024,128]{1,0:T(8,128)S(1)}, bf16[2064,128]{1,0:T(8,128)(2,1)}) custom-call(s32[3]{0:T(128)S(1)} %pad_add_fusion.token_ref.refs_0_.info, f32[2,1040,128]{2,1,0:T(8,128)} %get-tuple-element.144.refs_1_, bf16[2,1040,128]{2,1,0:T(8,128)(2,1)S(1)} %collective-permute-done.16.refs_2_, ...), custom_call_target="tpu_custom_call" | custom-call | flops 1000000 | tf_op jit(solution)/shard_map/pallas_call | solution.py:287
  85.2 1.4 shard_map.237
  86.6 3.9 %collective-permute-start.26 = (bf16[128,512]{1,0:T(8,128)(2,1)S(1)}, bf16[128,512]{1,0:T(8,128)(2,1)S(1)}, u32[]{:S(2)}, u32[]{:S(2)}) collective-permute-start(bf16[128,512]{1,0:T(8,128)(2,1)S(1)} %get-tuple-element.169.refs_1_), channel_id=1, source_target_pairs={{0,24},{4,28},{8,16},{12,20},{16,8},{20,12},{24,0},{28,4},{1,25},{... | collective-permute-start | bytes 393224 | tf_op jit(solution)/shard_map/ppermute | solution.py:133
  90.5 1.3 collective-permute-start.25
  91.8 0.5 collective-permute-start.24
  92.3 1.5 collective-permute-start.22
  93.7 0.5 collective-permute-start.23
  94.2 0.4 all-to-all-done.refs_1_
  94.6 2.3 %shard_map.238 = (f32[3,64,128]{2,1,0:T(8,128)}, bf16[32,64,128]{2,1,0:T(8,128)(2,1)}) custom-call(s32[3]{0:T(128)S(1)} %pad_add_fusion.token_ref.refs_0_.info, bf16[4,224,128]{2,1,0:T(8,128)(2,1)S(1)} %all-to-all-done.refs_1_, f32[3,64,128]{2,1,0:T(8,128)} %refs_2_.4, f32[8,128]{1,0:T(8,128)} %get-tuple-element.153.refs_3_.refs_9_, ...), custom_call_target="tpu_custom_call" | custom-call | flops 1000000 | tf_op jit(solution)/shard_map/pallas_call | solution.py:287
  97.0 4.0 %all-to-all-start.1 = ((bf16[32,64,128]{2,1,0:T(8,128)(2,1)}), bf16[32,64,128]{2,1,0:T(8,128)(2,1)}, u32[]{:S(2)}, u32[]{:S(2)}) async-start(bf16[32,64,128]{2,1,0:T(8,128)(2,1)} %get-tuple-element.155), calls=%async_computation.1 | async-start | bytes 1048576 | tf_op jit(solution)/shard_map/all_to_all | solution.py:991
  101.0 0.2 collective-permute-done.25.refs_3_
  101.2 0.6 shard_map.241.refs_1_
  101.8 3.2 %collective-permute-start.29 = (bf16[512,512]{1,0:T(8,128)(2,1)S(1)}, bf16[512,512]{1,0:T(8,128)(2,1)S(1)}, u32[]{:S(2)}, u32[]{:S(2)}) collective-permute-start(bf16[512,512]{1,0:T(8,128)(2,1)S(1)} %shard_map.241.refs_1_), channel_id=1, source_target_pairs={{0,3},{4,7},{8,11},{12,15},{16,19},{20,23},{24,27},{28,31}} | collective-permute-start | bytes 1572872 | tf_op jit(solution)/shard_map/ppermute | solution.py:995
  105.0 0.7 collective-permute-start.28
  105.7 0.7 collective-permute-start.27
  106.4 2.2 %shard_map.240 = f32[2,64,512]{2,1,0:T(8,128)} custom-call(s32[3]{0:T(128)S(1)} %pad_add_fusion.token_ref.refs_0_.info, f32[64,512]{1,0:T(8,128)} %get-tuple-element.166.refs_1_, f32[64,512]{1,0:T(8,128)} %collective-permute-done.23.refs_2_), custom_call_target="tpu_custom_call" | custom-call | flops 10000000000 | tf_op jit(solution)/shard_map/pallas_call | solution.py:287
  108.7 3.6 %shard_map.239 = (f32[1024,128]{1,0:T(8,128)}, bf16[1024,128]{1,0:T(8,128)(2,1)}) custom-call(s32[3]{0:T(128)S(1)} %pad_add_fusion.token_ref.refs_0_.info, f32[1024,128]{1,0:T(8,128)S(1)} %get-tuple-element.157.refs_1_, bf16[2064,128]{1,0:T(8,128)(2,1)} %collective-permute-done.22.refs_2_, f32[1024,128]{1,0:T(8,128)S(1)} %get-tuple-element.158.refs_3_, ...), custom_call_target="tpu_custom_call" | custom-call | flops 1000000 | tf_op jit(solution)/shard_map/pallas_call | solution.py:287
  112.3 7.1 %collective-permute-done.29.refs_4_ = bf16[512,512]{1,0:T(8,128)(2,1)S(1)} collective-permute-done((bf16[512,512]{1,0:T(8,128)(2,1)S(1)}, bf16[512,512]{1,0:T(8,128)(2,1)S(1)}, u32[]{:S(2)}, u32[]{:S(2)}) %collective-permute-start.29) | collective-permute-done | bytes 524320 | tf_op jit(solution)/shard_map/ppermute | solution.py:995
  119.4 0.8 shard_map.242.slots
  120.2 2.3 %shard_map.243 = bf16[8,64,512]{2,1,0:T(8,128)(2,1)} custom-call(s32[3]{0:T(128)S(1)} %pad_add_fusion.token_ref.refs_0_.info, bf16[32,64,128]{2,1,0:T(8,128)(2,1)} %all-to-all-done.1.source.refs_1_, bf16[8,64,512]{2,1,0:T(8,128)(2,1)} %shard_map.242.slots), custom_call_target="tpu_custom_call", output_to_operand_aliasing={{}: (2, {})} | custom-call | flops 179999997952 | tf_op jit(solution)/shard_map/pallas_call | solution.py:764
  122.5 16.6 %all-to-all-start.2 = ((bf16[8,64,512]{2,1,0:T(8,128)(2,1)}), bf16[8,64,512]{2,1,0:T(8,128)(2,1)S(1)}, u32[]{:S(2)}, u32[]{:S(2)}) async-start(bf16[8,64,512]{2,1,0:T(8,128)(2,1)} %shard_map.243), calls=%async_computation.2 | async-start | bytes 1048576 | tf_op jit(solution)/shard_map/all_to_all | solution.py:1018
  139.2 1.6 %shard_map.244.refs_2_ = bf16[64,384]{1,0:T(8,128)(2,1)S(1)} custom-call(s32[3]{0:T(128)S(1)} %pad_add_fusion.token_ref.refs_0_.info, bf16[32,64,128]{2,1,0:T(8,128)(2,1)} %all-to-all-done.1.source.refs_1_), custom_call_target="tpu_custom_call" | custom-call | flops 1000000 | tf_op jit(solution)/shard_map/pallas_call | solution.py:287
  140.8 2.0 %shard_map.245 = (bf16[3,512,128]{2,1,0:T(8,128)(2,1)S(1)}, bf16[2,512,512]{2,1,0:T(8,128)(2,1)S(1)}, f32[2,512]{1,0:T(2,128)S(1)}, f32[2,512]{1,0:T(2,128)S(1)}...) custom-call(s32[3]{0:T(128)S(1)} %pad_add_fusion.token_ref.refs_0_.info, bf16[3,512,128]{2,1,0:T(8,128)(2,1)} %refs_0_.2, ...), custom_call_target="tpu_custom_call" | custom-call | flops 1000000 | tf_op jit(solution)/shard_map/pallas_call | solution.py:321
  142.8 6.1 %all-to-all-done.2.refs_1_ = bf16[8,64,512]{2,1,0:T(8,128)(2,1)S(1)} async-done(((bf16[8,64,512]{2,1,0:T(8,128)(2,1)}), bf16[8,64,512]{2,1,0:T(8,128)(2,1)S(1)}, u32[]{:S(2)}, u32[]{:S(2)}) %all-to-all-start.2) | async-done | bytes 524320 | tf_op jit(solution)/shard_map/all_to_all | solution.py:1018
  148.9 2.7 %shard_map.246 = (f32[3,64,128]{2,1,0:T(8,128)}, f32[2,64,512]{2,1,0:T(8,128)}, f32[2,512]{1,0:T(2,128)}, f32[2,512]{1,0:T(2,128)}, f32[160,128]{1,0:T(8,128)}, /*index=5*/f32[160,128]{1,0:T(8,128)}) custom-call(s32[3]{0:T(128)S(1)} %pad_add_fusion.token_ref.refs_0_.info, bf16[8,64,512]{2,1,0:T(8,128)(2,1)S(1)} %all-to-all-done.2.refs_1_, ...), custom_call_target="tpu_custom_call" | custom-call | flops 1000000 | tf_op jit(solution)/shard_map/pallas_call | solution.py:287
  (54 shorter events, 0.4 us)
Async XLA Ops:
  0.6 10.0 %collective-permute-start.1 = (bf16[1024,128]{1,0:T(8,128)(2,1)}, bf16[1024,128]{1,0:T(8,128)(2,1)S(1)}, u32[]{:S(2)}, u32[]{:S(2)}) collective-permute-start(bf16[1024,128]{1,0:T(8,128)(2,1)} %bitcast.17), channel_id=1, source_target_pairs={{0,2},{1,3},{2,0},{3,1},{4,6},{5,7},{6,4},{7,5},{8,10},{9,11},{10,... | collective-permute-start | bytes 786440 | tf_op jit(solution)/shard_map/ppermute | solution.py:133
  3.6 7.5 %collective-permute-start = (bf16[1024,128]{1,0:T(8,128)(2,1)}, bf16[1024,128]{1,0:T(8,128)(2,1)S(1)}, u32[]{:S(2)}, u32[]{:S(2)}) collective-permute-start(bf16[1024,128]{1,0:T(8,128)(2,1)} %bitcast.18), channel_id=1, source_target_pairs={{0,1},{1,0},{2,3},{3,2},{4,5},{5,4},{6,7},{7,6},{8,9},{9,8},{10,11... | collective-permute-start | bytes 786440 | tf_op jit(solution)/shard_map/ppermute | solution.py:133
  6.5 5.7 %copy-start.2 = (bf16[2,512,256]{2,1,0:T(8,128)(2,1)}, bf16[2,512,256]{2,1,0:T(8,128)(2,1)S(1)}, u32[]{:S(2)}) copy-start(bf16[2,512,256]{2,1,0:T(8,128)(2,1)S(1)} %get-tuple-element.103.refs_7_.refs_13_) | copy-start | bytes 1572868
  6.5 5.7 %copy-start.4 = (bf16[2,256,512]{2,1,0:T(8,128)(2,1)}, bf16[2,256,512]{2,1,0:T(8,128)(2,1)S(1)}, u32[]{:S(2)}) copy-start(bf16[2,256,512]{2,1,0:T(8,128)(2,1)S(1)} %get-tuple-element.104.refs_8_.refs_14_) | copy-start | bytes 1572868
  6.5 5.7 %copy-start.6 = (bf16[3,512,128]{2,1,0:T(8,128)(2,1)}, bf16[3,512,128]{2,1,0:T(8,128)(2,1)S(1)}, u32[]{:S(2)}) copy-start(bf16[3,512,128]{2,1,0:T(8,128)(2,1)S(1)} %get-tuple-element.101.refs_5_) | copy-start | bytes 1179652
  6.5 12.1 %collective-permute-start.6 = (bf16[1536,128]{1,0:T(8,128)(2,1)S(1)}, bf16[1536,128]{1,0:T(8,128)(2,1)S(1)}, u32[]{:S(2)}, u32[]{:S(2)}) collective-permute-start(bf16[1536,128]{1,0:T(8,128)(2,1)S(1)} %get-tuple-element.107.refs_1_), channel_id=1, source_target_pairs={{0,2},{1,3},{2,0},{3,1},{4,6},{5,7},{6,4},{7,5},{8,10},{9,11},{10,... | collective-permute-start | bytes 1179656 | tf_op jit(solution)/shard_map/ppermute | solution.py:133
  9.8 13.5 %copy-start = (f32[2048,128]{1,0:T(8,128)}, f32[2048,128]{1,0:T(8,128)S(1)}, u32[]{:S(2)}) copy-start(f32[2048,128]{1,0:T(8,128)S(1)} %shard_map.223.refs_9_.refs_12_) | copy-start | bytes 3145732
  10.7 1.5 %collective-permute-start.2 = (bf16[1024,128]{1,0:T(8,128)(2,1)S(1)}, bf16[1024,128]{1,0:T(8,128)(2,1)S(1)}, u32[]{:S(2)}, u32[]{:S(2)}) collective-permute-start(bf16[1024,128]{1,0:T(8,128)(2,1)S(1)} %collective-permute-done.1.refs_3_), channel_id=1, source_target_pairs={{0,1},{1,0},{2,3},{3,2},{4,5},{5,4},{6,7},{7,6},{8,9},{9,8},{10,11... | collective-permute-start | bytes 786440 | tf_op jit(solution)/shard_map/ppermute | solution.py:133
  10.7 9.9 %collective-permute-start.5 = (bf16[1536,128]{1,0:T(8,128)(2,1)S(1)}, bf16[1536,128]{1,0:T(8,128)(2,1)S(1)}, u32[]{:S(2)}, u32[]{:S(2)}) collective-permute-start(bf16[1536,128]{1,0:T(8,128)(2,1)S(1)} %get-tuple-element.107.refs_1_), channel_id=1, source_target_pairs={{0,1},{1,0},{2,3},{3,2},{4,5},{5,4},{6,7},{7,6},{8,9},{9,8},{10,11... | collective-permute-start | bytes 1179656 | tf_op jit(solution)/shard_map/ppermute | solution.py:133
  15.9 13.0 %copy-start.9 = (f32[2,512]{1,0:T(2,128)}, f32[2,512]{1,0:T(2,128)S(1)}, u32[]{:S(2)}) copy-start(f32[2,512]{1,0:T(2,128)S(1)} %get-tuple-element.113.refs_7_.refs_6_.refs_16_) | copy-start | bytes 12292
  18.6 2.0 %collective-permute-start.7 = (bf16[1536,128]{1,0:T(8,128)(2,1)S(1)}, bf16[1536,128]{1,0:T(8,128)(2,1)S(1)}, u32[]{:S(2)}, u32[]{:S(2)}) collective-permute-start(bf16[1536,128]{1,0:T(8,128)(2,1)S(1)} %collective-permute-done.6.refs_3_), channel_id=1, source_target_pairs={{0,1},{1,0},{2,3},{3,2},{4,5},{5,4},{6,7},{7,6},{8,9},{9,8},{10,11... | collective-permute-start | bytes 1179656 | tf_op jit(solution)/shard_map/ppermute | solution.py:133
  18.6 8.7 %collective-permute-start.4 = (bf16[1024,128]{1,0:T(8,128)(2,1)S(1)}, bf16[1024,128]{1,0:T(8,128)(2,1)S(1)}, u32[]{:S(2)}, u32[]{:S(2)}) collective-permute-start(bf16[1024,128]{1,0:T(8,128)(2,1)S(1)} %get-tuple-element.105.refs_1_.refs_9_), channel_id=1, source_target_pairs={{0,2},{1,3},{2,0},{3,1},{4,6},{5,7},{6,4},{7,5},{8,10},{9,11},{10,... | collective-permute-start | bytes 786440 | tf_op jit(solution)/shard_map/ppermute | solution.py:133
  20.3 7.0 %collective-permute-start.3 = (bf16[1024,128]{1,0:T(8,128)(2,1)S(1)}, bf16[1024,128]{1,0:T(8,128)(2,1)S(1)}, u32[]{:S(2)}, u32[]{:S(2)}) collective-permute-start(bf16[1024,128]{1,0:T(8,128)(2,1)S(1)} %get-tuple-element.105.refs_1_.refs_9_), channel_id=1, source_target_pairs={{0,1},{1,0},{2,3},{3,2},{4,5},{5,4},{6,7},{7,6},{8,9},{9,8},{10,11... | collective-permute-start | bytes 786440 | tf_op jit(solution)/shard_map/ppermute | solution.py:133
  27.3 1.5 %collective-permute-start.8 = (bf16[1024,128]{1,0:T(8,128)(2,1)S(1)}, bf16[1024,128]{1,0:T(8,128)(2,1)S(1)}, u32[]{:S(2)}, u32[]{:S(2)}) collective-permute-start(bf16[1024,128]{1,0:T(8,128)(2,1)S(1)} %collective-permute-done.4.refs_3_), channel_id=1, source_target_pairs={{0,1},{1,0},{2,3},{3,2},{4,5},{5,4},{6,7},{7,6},{8,9},{9,8},{10,11... | collective-permute-start | bytes 786440 | tf_op jit(solution)/shard_map/ppermute | solution.py:133
  34.7 8.9 %copy-start.11 = (bf16[1024,512]{1,0:T(8,128)(2,1)}, bf16[1024,512]{1,0:T(8,128)(2,1)S(1)}, u32[]{:S(2)}) copy-start(bf16[1024,512]{1,0:T(8,128)(2,1)S(1)} %get-tuple-element.120.refs_2_.refs_1_) | copy-start | bytes 3145732
  34.8 2.0 %collective-permute-start.9 = (bf16[2,256,512]{2,1,0:T(8,128)(2,1)S(1)}, bf16[2,256,512]{2,1,0:T(8,128)(2,1)S(1)}, u32[]{:S(2)}, u32[]{:S(2)}) collective-permute-start(bf16[2,256,512]{2,1,0:T(8,128)(2,1)S(1)} %bitcast.11), channel_id=1, source_target_pairs={{0,1},{1,0},{2,3},{3,2},{4,5},{5,4},{6,7},{7,6},{8,9},{9,8},{10,11... | collective-permute-start | bytes 1572872 | tf_op jit(solution)/shard_map/ppermute | solution.py:133
  38.0 8.7 %collective-permute-start.11 = (bf16[256,512]{1,0:T(8,128)(2,1)}, bf16[256,512]{1,0:T(8,128)(2,1)}, u32[]{:S(2)}, u32[]{:S(2)}) collective-permute-start(bf16[256,512]{1,0:T(8,128)(2,1)} %get-tuple-element.117), channel_id=1, source_target_pairs={{0,2},{1,3},{2,0},{3,1},{4,6},{5,7},{6,4},{7,5},{8,10},{9,11},{10,... | collective-permute-start | bytes 786440 | tf_op jit(solution)/shard_map/ppermute | solution.py:133
  42.1 14.4 %collective-permute-start.10 = (bf16[528,512]{1,0:T(8,128)(2,1)}, bf16[528,512]{1,0:T(8,128)(2,1)}, u32[]{:S(2)}, u32[]{:S(2)}) collective-permute-start(bf16[528,512]{1,0:T(8,128)(2,1)} %get-tuple-element.123), channel_id=1, source_target_pairs={{0,4},{4,0},{8,12},{12,8},{16,20},{20,16},{24,28},{28,24},{1,5},{5... | collective-permute-start | bytes 1622024 | tf_op jit(solution)/shard_map/ppermute | solution.py:133
  43.7 3.0 %copy-start.10 = (f32[2,512]{1,0:T(2,128)S(1)}, f32[2,512]{1,0:T(2,128)}, u32[]{:S(2)}) copy-start(f32[2,512]{1,0:T(2,128)} %copy-done.9) | copy-start | bytes 12292
  48.0 4.0 %copy-start.12 = (bf16[1024,512]{1,0:T(8,128)(2,1)S(1)}, bf16[1024,512]{1,0:T(8,128)(2,1)}, u32[]{:S(2)}) copy-start(bf16[1024,512]{1,0:T(8,128)(2,1)} %copy-done.11) | copy-start | bytes 3145732
  48.0 7.6 %collective-permute-start.13 = (bf16[256,512]{1,0:T(8,128)(2,1)S(1)}, bf16[256,512]{1,0:T(8,128)(2,1)S(1)}, u32[]{:S(2)}, u32[]{:S(2)}) collective-permute-start(bf16[256,512]{1,0:T(8,128)(2,1)S(1)} %get-tuple-element.131.refs_1_), channel_id=1, source_target_pairs={{0,2},{1,3},{2,0},{3,1},{4,6},{5,7},{6,4},{7,5},{8,10},{9,11},{10,... | collective-permute-start | bytes 786440 | tf_op jit(solution)/shard_map/ppermute | solution.py:133
  49.8 7.8 %collective-permute-start.12 = (bf16[256,512]{1,0:T(8,128)(2,1)S(1)}, bf16[256,512]{1,0:T(8,128)(2,1)S(1)}, u32[]{:S(2)}, u32[]{:S(2)}) collective-permute-start(bf16[256,512]{1,0:T(8,128)(2,1)S(1)} %get-tuple-element.131.refs_1_), channel_id=1, source_target_pairs={{0,1},{1,0},{2,3},{3,2},{4,5},{5,4},{6,7},{7,6},{8,9},{9,8},{10,11... | collective-permute-start | bytes 786440 | tf_op jit(solution)/shard_map/ppermute | solution.py:133
  52.0 5.7 %copy-start.1 = (f32[2048,128]{1,0:T(8,128)S(1)}, f32[2048,128]{1,0:T(8,128)}, u32[]{:S(2)}) copy-start(f32[2048,128]{1,0:T(8,128)} %copy-done) | copy-start | bytes 3145732
  52.0 5.7 %copy-start.3 = (bf16[2,512,256]{2,1,0:T(8,128)(2,1)S(1)}, bf16[2,512,256]{2,1,0:T(8,128)(2,1)}, u32[]{:S(2)}) copy-start(bf16[2,512,256]{2,1,0:T(8,128)(2,1)} %copy-done.2) | copy-start | bytes 1572868
  52.0 5.7 %copy-start.5 = (bf16[2,256,512]{2,1,0:T(8,128)(2,1)S(1)}, bf16[2,256,512]{2,1,0:T(8,128)(2,1)}, u32[]{:S(2)}) copy-start(bf16[2,256,512]{2,1,0:T(8,128)(2,1)} %copy-done.4) | copy-start | bytes 1572868
  52.0 5.7 %copy-start.7 = (bf16[3,512,128]{2,1,0:T(8,128)(2,1)S(1)}, bf16[3,512,128]{2,1,0:T(8,128)(2,1)}, u32[]{:S(2)}) copy-start(bf16[3,512,128]{2,1,0:T(8,128)(2,1)} %copy-done.6) | copy-start | bytes 1179652
  55.6 2.1 %collective-permute-start.14 = (bf16[256,512]{1,0:T(8,128)(2,1)S(1)}, bf16[256,512]{1,0:T(8,128)(2,1)S(1)}, u32[]{:S(2)}, u32[]{:S(2)}) collective-permute-start(bf16[256,512]{1,0:T(8,128)(2,1)S(1)} %collective-permute-done.13.refs_3_), channel_id=1, source_target_pairs={{0,1},{1,0},{2,3},{3,2},{4,5},{5,4},{6,7},{7,6},{8,9},{9,8},{10,11... | collective-permute-start | bytes 786440 | tf_op jit(solution)/shard_map/ppermute | solution.py:133
  55.6 16.1 %collective-permute-start.17 = (bf16[2,1024,128]{2,1,0:T(8,128)(2,1)}, bf16[2,1024,128]{2,1,0:T(8,128)(2,1)}, u32[]{:S(2)}, u32[]{:S(2)}) collective-permute-start(bf16[2,1024,128]{2,1,0:T(8,128)(2,1)} %get-tuple-element.134), channel_id=1, source_target_pairs={{0,1},{1,0},{2,3},{3,2},{4,5},{5,4},{6,7},{7,6},{8,9},{9,8},{10,11... | collective-permute-start | bytes 1572872 | tf_op jit(solution)/shard_map/ppermute | solution.py:133
  65.7 19.4 %copy-start.8 = (f32[2,64,512]{2,1,0:T(8,128)S(1)}, f32[2,64,512]{2,1,0:T(8,128)}, u32[]{:S(2)}) copy-start(f32[2,64,512]{2,1,0:T(8,128)} %refs_1_.5) | copy-start | bytes 786436
  65.8 15.8 %collective-permute-start.16 = (bf16[2,1040,128]{2,1,0:T(8,128)(2,1)}, bf16[2,1040,128]{2,1,0:T(8,128)(2,1)S(1)}, u32[]{:S(2)}, u32[]{:S(2)}) collective-permute-start(bf16[2,1040,128]{2,1,0:T(8,128)(2,1)} %get-tuple-element.145), channel_id=1, source_target_pairs={{0,1},{1,0},{2,3},{3,2},{4,5},{5,4},{6,7},{7,6},{8,9},{9,8},{10,11... | collective-permute-start | bytes 1597448 | tf_op jit(solution)/shard_map/ppermute | solution.py:133
  65.8 8.0 %collective-permute-start.15 = (bf16[4,224,128]{2,1,0:T(8,128)(2,1)S(1)}, bf16[4,224,128]{2,1,0:T(8,128)(2,1)S(1)}, u32[]{:S(2)}, u32[]{:S(2)}) collective-permute-start(bf16[4,224,128]{2,1,0:T(8,128)(2,1)S(1)} %get-tuple-element.143), channel_id=1, source_target_pairs={{0,4},{4,0},{8,12},{12,8},{16,20},{20,16},{24,28},{28,24},{1,5},{5... | collective-permute-start | bytes 688136 | tf_op jit(solution)/shard_map/ppermute | solution.py:133
  67.5 17.6 %collective-permute-start.19 = (bf16[144,512]{1,0:T(8,128)(2,1)S(1)}, bf16[144,512]{1,0:T(8,128)(2,1)S(1)}, u32[]{:S(2)}, u32[]{:S(2)}) collective-permute-start(bf16[144,512]{1,0:T(8,128)(2,1)S(1)} %get-tuple-element.150), channel_id=1, source_target_pairs={{0,8},{4,12},{8,0},{12,4},{16,24},{20,28},{24,16},{28,20},{1,9},{5... | collective-permute-start | bytes 442376 | tf_op jit(solution)/shard_map/ppermute | solution.py:133
  69.1 16.1 %collective-permute-start.20 = (bf16[144,512]{1,0:T(8,128)(2,1)S(1)}, bf16[144,512]{1,0:T(8,128)(2,1)S(1)}, u32[]{:S(2)}, u32[]{:S(2)}) collective-permute-start(bf16[144,512]{1,0:T(8,128)(2,1)S(1)} %get-tuple-element.151), channel_id=1, source_target_pairs={{0,16},{4,20},{8,24},{12,28},{16,0},{20,4},{24,8},{28,12},{1,17},{... | collective-permute-start | bytes 442376 | tf_op jit(solution)/shard_map/ppermute | solution.py:133
  71.7 13.5 %collective-permute-start.21 = (bf16[144,512]{1,0:T(8,128)(2,1)S(1)}, bf16[144,512]{1,0:T(8,128)(2,1)S(1)}, u32[]{:S(2)}, u32[]{:S(2)}) collective-permute-start(bf16[144,512]{1,0:T(8,128)(2,1)S(1)} %get-tuple-element.152), channel_id=1, source_target_pairs={{0,24},{4,28},{8,16},{12,20},{16,8},{20,12},{24,0},{28,4},{1,25},{... | collective-permute-start | bytes 442376 | tf_op jit(solution)/shard_map/ppermute | solution.py:133
  73.9 11.3 %collective-permute-start.18 = (f32[64,512]{1,0:T(8,128)S(1)}, f32[64,512]{1,0:T(8,128)S(1)}, u32[]{:S(2)}, u32[]{:S(2)}) collective-permute-start(f32[64,512]{1,0:T(8,128)S(1)} %get-tuple-element.149), channel_id=1, source_target_pairs={{0,4},{4,0},{8,12},{12,8},{16,20},{20,16},{24,28},{28,24},{1,5},{5... | collective-permute-start | bytes 393224 | tf_op jit(solution)/shard_map/ppermute | solution.py:133
  76.7 17.9 %all-to-all-start = ((bf16[4,224,128]{2,1,0:T(8,128)(2,1)}), bf16[4,224,128]{2,1,0:T(8,128)(2,1)S(1)}, u32[]{:S(2)}, u32[]{:S(2)}) async-start(bf16[4,224,128]{2,1,0:T(8,128)(2,1)} %shard_map.235), calls=%async_computation | async-start | bytes 458752 | tf_op jit(solution)/shard_map/all_to_all | solution.py:963
  86.6 14.4 %collective-permute-start.26 = (bf16[128,512]{1,0:T(8,128)(2,1)S(1)}, bf16[128,512]{1,0:T(8,128)(2,1)S(1)}, u32[]{:S(2)}, u32[]{:S(2)}) collective-permute-start(bf16[128,512]{1,0:T(8,128)(2,1)S(1)} %get-tuple-element.169.refs_1_), channel_id=1, source_target_pairs={{0,24},{4,28},{8,16},{12,20},{16,8},{20,12},{24,0},{28,4},{1,25},{... | collective-permute-start | bytes 393224 | tf_op jit(solution)/shard_map/ppermute | solution.py:133
  90.5 10.7 %collective-permute-start.25 = (bf16[128,512]{1,0:T(8,128)(2,1)S(1)}, bf16[128,512]{1,0:T(8,128)(2,1)S(1)}, u32[]{:S(2)}, u32[]{:S(2)}) collective-permute-start(bf16[128,512]{1,0:T(8,128)(2,1)S(1)} %get-tuple-element.169.refs_1_), channel_id=1, source_target_pairs={{0,16},{4,20},{8,24},{12,28},{16,0},{20,4},{24,8},{28,12},{1,17},{... | collective-permute-start | bytes 393224 | tf_op jit(solution)/shard_map/ppermute | solution.py:133
  91.8 9.5 %collective-permute-start.24 = (bf16[128,512]{1,0:T(8,128)(2,1)S(1)}, bf16[128,512]{1,0:T(8,128)(2,1)S(1)}, u32[]{:S(2)}, u32[]{:S(2)}) collective-permute-start(bf16[128,512]{1,0:T(8,128)(2,1)S(1)} %get-tuple-element.169.refs_1_), channel_id=1, source_target_pairs={{0,8},{4,12},{8,0},{12,4},{16,24},{20,28},{24,16},{28,20},{1,9},{5... | collective-permute-start | bytes 393224 | tf_op jit(solution)/shard_map/ppermute | solution.py:133
  92.3 16.4 %collective-permute-start.22 = (bf16[2064,128]{1,0:T(8,128)(2,1)}, bf16[2064,128]{1,0:T(8,128)(2,1)}, u32[]{:S(2)}, u32[]{:S(2)}) collective-permute-start(bf16[2064,128]{1,0:T(8,128)(2,1)} %get-tuple-element.147), channel_id=1, source_target_pairs={{0,2},{1,3},{2,0},{3,1},{4,6},{5,7},{6,4},{7,5},{8,10},{9,11},{10,... | collective-permute-start | bytes 1585160 | tf_op jit(solution)/shard_map/ppermute | solution.py:133
  93.7 12.7 %collective-permute-start.23 = (f32[64,512]{1,0:T(8,128)}, f32[64,512]{1,0:T(8,128)}, u32[]{:S(2)}, u32[]{:S(2)}) collective-permute-start(f32[64,512]{1,0:T(8,128)} %get-tuple-element.167), channel_id=1, source_target_pairs={{0,4},{4,0},{8,12},{12,8},{16,20},{20,16},{24,28},{28,24},{1,5},{5... | collective-permute-start | bytes 393224 | tf_op jit(solution)/shard_map/ppermute | solution.py:133
  97.0 23.2 %all-to-all-start.1 = ((bf16[32,64,128]{2,1,0:T(8,128)(2,1)}), bf16[32,64,128]{2,1,0:T(8,128)(2,1)}, u32[]{:S(2)}, u32[]{:S(2)}) async-start(bf16[32,64,128]{2,1,0:T(8,128)(2,1)} %get-tuple-element.155), calls=%async_computation.1 | async-start | bytes 1048576 | tf_op jit(solution)/shard_map/all_to_all | solution.py:991
  101.8 17.6 %collective-permute-start.29 = (bf16[512,512]{1,0:T(8,128)(2,1)S(1)}, bf16[512,512]{1,0:T(8,128)(2,1)S(1)}, u32[]{:S(2)}, u32[]{:S(2)}) collective-permute-start(bf16[512,512]{1,0:T(8,128)(2,1)S(1)} %shard_map.241.refs_1_), channel_id=1, source_target_pairs={{0,3},{4,7},{8,11},{12,15},{16,19},{20,23},{24,27},{28,31}} | collective-permute-start | bytes 1572872 | tf_op jit(solution)/shard_map/ppermute | solution.py:995
  105.0 14.4 %collective-permute-start.28 = (bf16[512,512]{1,0:T(8,128)(2,1)S(1)}, bf16[512,512]{1,0:T(8,128)(2,1)S(1)}, u32[]{:S(2)}, u32[]{:S(2)}) collective-permute-start(bf16[512,512]{1,0:T(8,128)(2,1)S(1)} %shard_map.241.refs_1_), channel_id=1, source_target_pairs={{1,3},{5,7},{9,11},{13,15},{17,19},{21,23},{25,27},{29,31}} | collective-permute-start | bytes 1572872 | tf_op jit(solution)/shard_map/ppermute | solution.py:995
  105.7 13.7 %collective-permute-start.27 = (bf16[512,512]{1,0:T(8,128)(2,1)S(1)}, bf16[512,512]{1,0:T(8,128)(2,1)S(1)}, u32[]{:S(2)}, u32[]{:S(2)}) collective-permute-start(bf16[512,512]{1,0:T(8,128)(2,1)S(1)} %shard_map.241.refs_1_), channel_id=1, source_target_pairs={{2,3},{6,7},{10,11},{14,15},{18,19},{22,23},{26,27},{30,31}} | collective-permute-start | bytes 1572872 | tf_op jit(solution)/shard_map/ppermute | solution.py:995
  122.5 26.4 %all-to-all-start.2 = ((bf16[8,64,512]{2,1,0:T(8,128)(2,1)}), bf16[8,64,512]{2,1,0:T(8,128)(2,1)S(1)}, u32[]{:S(2)}, u32[]{:S(2)}) async-start(bf16[8,64,512]{2,1,0:T(8,128)(2,1)} %shard_map.243), calls=%async_computation.2 | async-start | bytes 1048576 | tf_op jit(solution)/shard_map/all_to_all | solution.py:1018

commit v5 on v4

--- a/solution.py
+++ b/solution.py
@@ -195,9 +195,8 @@
     col = lax.broadcasted_iota(jnp.int32, (size, size), 1)
     unit = (row == col).astype(F32)
     blocks = [block() for block in blocks]
-    gram = 0.0
-    for block in blocks:
-        gram = gram + symmetric([block], [block], lambda a, b, cut: dot(a[0], b[0] if cut is None else b[0][cut:], NT))
+    whole = jnp.concatenate(blocks, 1) if len(blocks) > 1 else blocks[0]
+    gram = symmetric([whole], [whole], lambda a, b, cut: dot(a[0], b[0] if cut is None else b[0][cut:], NT))
     scale = 1.0 / (jnp.sqrt(jnp.sum(gram * unit)) + 1e-07)
     a_ref[...] = gram * (scale * scale)
 
@@ -219,8 +218,10 @@
     rows, terms = r_ref[...], split(a_ref[...])
     once = three_terms(split(rows), terms)
     rows = NS_COEF_A * rows + NS_COEF_B * once + NS_COEF_C * three_terms(split(once), terms)
-    high, low = split(rows)
-    return [scale * (dot(high, block, NN) + dot(low, block, NN)) for block in blocks]
+    count = rows.shape[0]
+    terms = jnp.concatenate(split(rows), 0)
+    both = [dot(terms, block, NN) for block in blocks]
+    return [scale * (v[:count] + v[count:]) for v in both]
 
 
 VMEM = pl.BlockSpec(memory_space=pltpu.VMEM)
@@ -469,7 +470,7 @@
         if k % 2:
             near.ref[k // 2] = share.astype(BF16)
         else:
-            kept.ref[k // 2] = share
+            kept.ref[k // 2] = share.astype(BF16)
 
 
 def mlp_rows_kernel(info, keep, came, *outs):
@@ -532,8 +533,8 @@
     one_mine[...] = one_kept[0, :size, :] + one_came[0, :size, :].astype(F32)
     tail[...] = one_kept[0, size:, :] + one_came[0, size:, :].astype(F32)
     far[: size + 16, :] = (one_kept[1] + one_came[1].astype(F32)).astype(BF16)
-    out_mine[...] = out_kept[0] + out_came[0].astype(F32)
-    far[size + 16 :, :] = (out_kept[1] + out_came[1].astype(F32)).astype(BF16)
+    out_mine[...] = out_kept[0].astype(F32) + out_came[0].astype(F32)
+    far[size + 16 :, :] = (out_kept[1].astype(F32) + out_came[1].astype(F32)).astype(BF16)
 
 
 def norm_back_kernel(info, mine, came, cot, n_mine, inv_mine, gains, delta, grad_gain):
@@ -929,7 +930,7 @@
     (kernel_inverse_one,) = fetch(after(info, delta_mid), 0, kernel_inverse)
     out_near, out_kept = call(
         mlp_out_kernel,
-        [Store((2, bucket, part), BF16), Store((2, bucket, part), F32)],
+        [Store((2, bucket, part), BF16), Store((2, bucket, part), BF16)],
         [((bucket, width), F32)],
         (after(info, kernel_inverse_one), active, mlp_kept),
         1, 8,

time: 153 us -> 153 us (level)
  no operation moved by 1% of the time
where the time goes in v5:
time: 153 us; the launch traced here: 152 us
  Pallas kernels  61.8 us (40%)
  starting transfers between devices  56.8 us (37%)
  waiting for transfers between devices  31 us (20%)
  between operations  1.95 us (1%)
    pallas_call x21, Pallas kernels, call(): pl.pallas_call(body, out_shape=tuple((pltpu.HBM(o.shape, o.dtype) if isin...  53.3 us
    ppermute x27, starting transfers between devices, swap(): return lax.ppermute(value, axis, [(i, i ^ k) for i in range(size)])  27 us
    ppermute x27, waiting for transfers between devices, swap(): return lax.ppermute(value, axis, [(i, i ^ k) for i in range(size)])  17.2 us
    all_to_all x1, starting transfers between devices, per_device(): lax.all_to_all(sends.astype(BF16), ('dp', 'tensor'), 0, 0, tiled=True, ax...  16.6 us
    ppermute x3, waiting for transfers between devices, per_device(): lax.ppermute(mlp_columns, 'tensor', [(3 ^ k, 3)])  7.11 us
    pallas_call x3, Pallas kernels, fetch(): pl.pallas_call(body, out_shape=tuple(shapes), in_specs=[SMEM] + [HBM] * l...  6.23 us
    all_to_all x1, waiting for transfers between devices, per_device(): lax.all_to_all(sends.astype(BF16), ('dp', 'tensor'), 0, 0, tiled=True, ax...  6.12 us
    all_to_all x1, starting transfers between devices, per_device(): lax.all_to_all(slots.astype(BF16), 'dp', 0, 0, tiled=True, axis_index_gro...  4.88 us
  transfers between devices with their start and end apart: 33, of which 14 were waited for; matrix products, arithmetic and copies ran while one was open for 0% of the time, Pallas kernels for 33%

profile of v5, /device:TPU:0, one launch (start us, length us, event | category | flops | bytes accessed | tf_op | source)
XLA Modules:
  0.0 151.8 jit_solution(14527398901873728239)
XLA Ops:
  0.6 3.0 %collective-permute-start.1 = (bf16[1024,128]{1,0:T(8,128)(2,1)}, bf16[1024,128]{1,0:T(8,128)(2,1)S(1)}, u32[]{:S(2)}, u32[]{:S(2)}) collective-permute-start(bf16[1024,128]{1,0:T(8,128)(2,1)} %bitcast.17), channel_id=1, source_target_pairs={{0,2},{1,3},{2,0},{3,1},{4,6},{5,7},{6,4},{7,5},{8,10},{9,11},{10,... | collective-permute-start | bytes 786440 | tf_op jit(solution)/shard_map/ppermute | solution.py:133
  4.4 2.1 %shard_map.222 = (bf16[1024,128]{1,0:T(8,128)(2,1)S(1)}, bf16[3,512,128]{2,1,0:T(8,128)(2,1)S(1)}, f32[2,512]{1,0:T(2,128)S(1)}, bf16[2,512,256]{2,1,0:T(8,128)(...) custom-call(s32[3]{0:T(128)S(1)} %pad_add_fusion.token_ref.refs_0_.info, ...), custom_call_target="tpu_custom_call" | custom-call | flops 10000000000 | tf_op jit(solution)/shard_map/pallas_call | solution.py:322
  6.7 3.1 %shard_map.223.refs_9_.refs_12_ = f32[2048,128]{1,0:T(8,128)S(1)} custom-call(s32[3]{0:T(128)S(1)} %pad_add_fusion.token_ref.refs_0_.info, bf16[2,2048,160]{2,1,0:T(8,128)(2,1)} %constant.19.clone.refs_1_, f32[160,128]{1,0:T(8,128)} %bitcast.13), custom_call_target="tpu_custom_call" | custom-call | flops 20000000000 | tf_op jit(solution)/shard_map/pallas_call | solution.py:288
  9.8 0.8 collective-permute-done.1.refs_3_
  10.7 0.5 collective-permute-start.5
  11.2 1.0 collective-permute-done.2.refs_4_
  12.2 3.6 %shard_map.224 = (bf16[1024,512]{1,0:T(8,128)(2,1)S(1)}, bf16[1024,512]{1,0:T(8,128)(2,1)S(1)}, f32[1024,128]{1,0:T(8,128)}, f32[1024,1]{1,0:T(8,128)}, f32[512,...) custom-call(s32[3]{0:T(128)S(1)} %pad_add_fusion.token_ref.refs_0_.i, ...), custom_call_target="tpu_custom_call" | custom-call | flops 1000000 | tf_op jit(solution)/shard_map/pallas_call | solution.py:288
  15.9 2.7 %collective-permute-done.6.refs_3_ = bf16[1536,128]{1,0:T(8,128)(2,1)S(1)} collective-permute-done((bf16[1536,128]{1,0:T(8,128)(2,1)S(1)}, bf16[1536,128]{1,0:T(8,128)(2,1)S(1)}, u32[]{:S(2)}, u32[]{:S(2)}) %collective-permute-start.6) | collective-permute-done | bytes 393248 | tf_op jit(solution)/shard_map/ppermute | solution.py:133
  18.6 1.7 %collective-permute-start.4 = (bf16[1024,128]{1,0:T(8,128)(2,1)S(1)}, bf16[1024,128]{1,0:T(8,128)(2,1)S(1)}, u32[]{:S(2)}, u32[]{:S(2)}) collective-permute-start(bf16[1024,128]{1,0:T(8,128)(2,1)S(1)} %get-tuple-element.105.refs_1_.refs_9_), channel_id=1, source_target_pairs={{0,2},{1,3},{2,0},{3,1},{4,6},{5,7},{6,4},{7,5},{8,10},{9,11},{10,... | collective-permute-start | bytes 786440 | tf_op jit(solution)/shard_map/ppermute | solution.py:133
  20.3 0.2 collective-permute-start.3
  20.6 2.7 %shard_map.225 = (bf16[1024,512]{1,0:T(8,128)(2,1)S(1)}, bf16[512,512]{1,0:T(8,128)(2,1)S(1)}, f32[1024,512]{1,0:T(8,128)S(1)}, bf16[2,512,512]{2,1,0:T(8,128)(2,1)S(1)}) custom-call(s32[3]{0:T(128)S(1)} %pad_add_fusion.token_ref.refs_0_.info, bf16[1536,128]{1,0:T(8,128)(2,1)S(1)} %get-tuple-element.107.refs_1_, ...), custom_call_target="tpu_custom_call" | custom-call | flops 30000001024 | tf_op jit(solution)/shard_map/pallas_call | solution.py:288
  23.3 4.0 %collective-permute-done.4.refs_3_ = bf16[1024,128]{1,0:T(8,128)(2,1)S(1)} collective-permute-done((bf16[1024,128]{1,0:T(8,128)(2,1)S(1)}, bf16[1024,128]{1,0:T(8,128)(2,1)S(1)}, u32[]{:S(2)}, u32[]{:S(2)}) %collective-permute-start.4) | collective-permute-done | bytes 262176 | tf_op jit(solution)/shard_map/ppermute | solution.py:133
  27.3 1.5 %collective-permute-done.8.refs_4_ = bf16[1024,128]{1,0:T(8,128)(2,1)S(1)} collective-permute-done((bf16[1024,128]{1,0:T(8,128)(2,1)S(1)}, bf16[1024,128]{1,0:T(8,128)(2,1)S(1)}, u32[]{:S(2)}, u32[]{:S(2)}) %collective-permute-start.8) | collective-permute-done | bytes 262176 | tf_op jit(solution)/shard_map/ppermute | solution.py:133
  28.9 5.9 %shard_map.226 = (bf16[512,512]{1,0:T(8,128)(2,1)S(1)}, f32[512,512]{1,0:T(8,128)S(1)}, bf16[1024,512]{1,0:T(8,128)(2,1)S(1)}, bf16[1024,512]{1,0:T(8,128)(2,1)S...) custom-call(s32[3]{0:T(128)S(1)} %pad_add_fusion.token_ref.refs_0_.inf, ...), custom_call_target="tpu_custom_call" | custom-call | flops 60000002048 | tf_op jit(solution)/shard_map/pallas_call | solution.py:288
  34.8 0.2 collective-permute-start.9
  35.0 1.8 %collective-permute-done.9.refs_2_ = bf16[2,256,512]{2,1,0:T(8,128)(2,1)S(1)} collective-permute-done((bf16[2,256,512]{2,1,0:T(8,128)(2,1)S(1)}, bf16[2,256,512]{2,1,0:T(8,128)(2,1)S(1)}, u32[]{:S(2)}, u32[]{:S(2)}) %collective-permute-start.9) | collective-permute-done | bytes 524320 | tf_op jit(solution)/shard_map/ppermute | solution.py:133
  36.7 1.3 shard_map.227
  38.0 1.7 %collective-permute-start.11 = (bf16[256,512]{1,0:T(8,128)(2,1)}, bf16[256,512]{1,0:T(8,128)(2,1)}, u32[]{:S(2)}, u32[]{:S(2)}) collective-permute-start(bf16[256,512]{1,0:T(8,128)(2,1)} %get-tuple-element.117), channel_id=1, source_target_pairs={{0,2},{1,3},{2,0},{3,1},{4,6},{5,7},{6,4},{7,5},{8,10},{9,11},{10,... | collective-permute-start | bytes 786440 | tf_op jit(solution)/shard_map/ppermute | solution.py:133
  39.8 2.3 %shard_map.228 = (bf16[528,512]{1,0:T(8,128)(2,1)}, f32[64,512]{1,0:T(8,128)S(1)}) custom-call(s32[3]{0:T(128)S(1)} %pad_add_fusion.token_ref.refs_0_.info, bf16[1024,512]{1,0:T(8,128)(2,1)S(1)} %get-tuple-element.119.refs_1_, bf16[1024,512]{1,0:T(8,128)(2,1)S(1)} %get-tuple-element.120.refs_2_.refs_1_, bf16[1024,512]{1,0:T(8,128)(2,1)S(1)} %get-tuple-element.121.refs_3_, ...), custom_call_target="tpu_custom_call" | custom-call | flops 20000000000 | tf_op jit(solution)/shard_map/pallas_call | solution.py:288
  42.1 1.6 %collective-permute-start.10 = (bf16[528,512]{1,0:T(8,128)(2,1)}, bf16[528,512]{1,0:T(8,128)(2,1)}, u32[]{:S(2)}, u32[]{:S(2)}) collective-permute-start(bf16[528,512]{1,0:T(8,128)(2,1)} %get-tuple-element.123), channel_id=1, source_target_pairs={{0,4},{4,0},{8,12},{12,8},{16,20},{20,16},{24,28},{28,24},{1,5},{5... | collective-permute-start | bytes 1622024 | tf_op jit(solution)/shard_map/ppermute | solution.py:133
  43.7 1.5 shard_map.229.refs_1_
  45.2 1.5 %collective-permute-done.11.refs_2_ = bf16[256,512]{1,0:T(8,128)(2,1)} collective-permute-done((bf16[256,512]{1,0:T(8,128)(2,1)}, bf16[256,512]{1,0:T(8,128)(2,1)}, u32[]{:S(2)}, u32[]{:S(2)}) %collective-permute-start.11) | collective-permute-done | bytes 262176 | tf_op jit(solution)/shard_map/ppermute | solution.py:133
  46.7 1.3 shard_map.231
  48.0 1.8 %collective-permute-start.13 = (bf16[256,512]{1,0:T(8,128)(2,1)S(1)}, bf16[256,512]{1,0:T(8,128)(2,1)S(1)}, u32[]{:S(2)}, u32[]{:S(2)}) collective-permute-start(bf16[256,512]{1,0:T(8,128)(2,1)S(1)} %get-tuple-element.131.refs_1_), channel_id=1, source_target_pairs={{0,2},{1,3},{2,0},{3,1},{4,6},{5,7},{6,4},{7,5},{8,10},{9,11},{10,... | collective-permute-start | bytes 786440 | tf_op jit(solution)/shard_map/ppermute | solution.py:133
  49.8 2.1 %shard_map.232.refs_15_ = bf16[2,256,2048]{2,1,0:T(8,128)(2,1)S(1)} custom-call(s32[3]{0:T(128)S(1)} %pad_add_fusion.token_ref.refs_0_.info, bf16[2,256,2048]{2,1,0:T(8,128)(2,1)} %constant.20.clone.refs_0_), custom_call_target="tpu_custom_call" | custom-call | flops 1000000 | tf_op jit(solution)/shard_map/pallas_call | solution.py:322
  52.0 2.4 %shard_map.233 = (bf16[2,1024,128]{2,1,0:T(8,128)(2,1)}, bf16[2,1024,128]{2,1,0:T(8,128)(2,1)}) custom-call(s32[3]{0:T(128)S(1)} %pad_add_fusion.token_ref.refs_0_.info, bf16[1024,512]{1,0:T(8,128)(2,1)S(1)} %copy-done.12, bf16[2,512,512]{2,1,0:T(8,128)(2,1)S(1)} %get-tuple-element.114.refs_8_.refs_2_), custom_call_target="tpu_custom_call" | custom-call | flops 10000000000 | tf_op jit(solution)/shard_map/pallas_call | solution.py:288
  54.5 1.2 collective-permute-done.13.refs_3_
  55.6 0.5 collective-permute-start.17
  56.1 0.4 collective-permute-done.10.refs_2_
  56.5 1.2 shard_map.230
  57.7 8.0 %shard_map.234 = (bf16[4,224,128]{2,1,0:T(8,128)(2,1)S(1)}, bf16[4,224,128]{2,1,0:T(8,128)(2,1)S(1)}, bf16[2,1040,128]{2,1,0:T(8,128)(2,1)}, f32[2,1040,128]{2,1...) custom-call(s32[3]{0:T(128)S(1)} %pad_add_fusion.token_ref.refs_0_.info, ...), custom_call_target="tpu_custom_call" | custom-call | flops 9999999827968 | tf_op jit(solution)/shard_map/pallas_call | solution.py:288
  65.9 1.7 %collective-permute-start.15 = (bf16[4,224,128]{2,1,0:T(8,128)(2,1)S(1)}, bf16[4,224,128]{2,1,0:T(8,128)(2,1)S(1)}, u32[]{:S(2)}, u32[]{:S(2)}) collective-permute-start(bf16[4,224,128]{2,1,0:T(8,128)(2,1)S(1)} %get-tuple-element.143), channel_id=1, source_target_pairs={{0,4},{4,0},{8,12},{12,8},{16,20},{20,16},{24,28},{28,24},{1,5},{5... | collective-permute-start | bytes 688136 | tf_op jit(solution)/shard_map/ppermute | solution.py:133
  67.6 1.6 %collective-permute-start.19 = (bf16[144,512]{1,0:T(8,128)(2,1)S(1)}, bf16[144,512]{1,0:T(8,128)(2,1)S(1)}, u32[]{:S(2)}, u32[]{:S(2)}) collective-permute-start(bf16[144,512]{1,0:T(8,128)(2,1)S(1)} %get-tuple-element.150), channel_id=1, source_target_pairs={{0,8},{4,12},{8,0},{12,4},{16,24},{20,28},{24,16},{28,20},{1,9},{5... | collective-permute-start | bytes 442376 | tf_op jit(solution)/shard_map/ppermute | solution.py:133
  69.1 2.6 %collective-permute-start.20 = (bf16[144,512]{1,0:T(8,128)(2,1)S(1)}, bf16[144,512]{1,0:T(8,128)(2,1)S(1)}, u32[]{:S(2)}, u32[]{:S(2)}) collective-permute-start(bf16[144,512]{1,0:T(8,128)(2,1)S(1)} %get-tuple-element.151), channel_id=1, source_target_pairs={{0,16},{4,20},{8,24},{12,28},{16,0},{20,4},{24,8},{28,12},{1,17},{... | collective-permute-start | bytes 442376 | tf_op jit(solution)/shard_map/ppermute | solution.py:133
  71.7 0.2 collective-permute-start.21
  71.9 1.9 %collective-permute-done.15.refs_2_ = bf16[4,224,128]{2,1,0:T(8,128)(2,1)S(1)} collective-permute-done((bf16[4,224,128]{2,1,0:T(8,128)(2,1)S(1)}, bf16[4,224,128]{2,1,0:T(8,128)(2,1)S(1)}, u32[]{:S(2)}, u32[]{:S(2)}) %collective-permute-start.15) | collective-permute-done | bytes 229408 | tf_op jit(solution)/shard_map/ppermute | solution.py:133
  73.9 1.5 %collective-permute-start.18 = (f32[64,512]{1,0:T(8,128)S(1)}, f32[64,512]{1,0:T(8,128)S(1)}, u32[]{:S(2)}, u32[]{:S(2)}) collective-permute-start(f32[64,512]{1,0:T(8,128)S(1)} %get-tuple-element.149), channel_id=1, source_target_pairs={{0,4},{4,0},{8,12},{12,8},{16,20},{20,16},{24,28},{28,24},{1,5},{5... | collective-permute-start | bytes 393224 | tf_op jit(solution)/shard_map/ppermute | solution.py:133
  75.4 1.3 shard_map.235
  76.7 4.9 %all-to-all-start = ((bf16[4,224,128]{2,1,0:T(8,128)(2,1)}), bf16[4,224,128]{2,1,0:T(8,128)(2,1)S(1)}, u32[]{:S(2)}, u32[]{:S(2)}) async-start(bf16[4,224,128]{2,1,0:T(8,128)(2,1)} %shard_map.235), calls=%async_computation | async-start | bytes 458752 | tf_op jit(solution)/shard_map/all_to_all | solution.py:964
  81.6 3.4 %shard_map.236 = (f32[1024,128]{1,0:T(8,128)S(1)}, f32[16,128]{1,0:T(8,128)S(1)}, f32[1024,128]{1,0:T(8,128)S(1)}, bf16[2064,128]{1,0:T(8,128)(2,1)}) custom-call(s32[3]{0:T(128)S(1)} %pad_add_fusion.token_ref.refs_0_.info, f32[2,1040,128]{2,1,0:T(8,128)} %get-tuple-element.144.refs_1_, bf16[2,1040,128]{2,1,0:T(8,128)(2,1)S(1)} %collective-permute-done.16.refs_2_, ...), custom_call_target="tpu_custom_call" | custom-call | flops 1000000 | tf_op jit(solution)/shard_map/pallas_call | solution.py:288
  85.0 1.4 shard_map.237
  86.4 3.9 %collective-permute-start.26 = (bf16[128,512]{1,0:T(8,128)(2,1)S(1)}, bf16[128,512]{1,0:T(8,128)(2,1)S(1)}, u32[]{:S(2)}, u32[]{:S(2)}) collective-permute-start(bf16[128,512]{1,0:T(8,128)(2,1)S(1)} %get-tuple-element.169.refs_1_), channel_id=1, source_target_pairs={{0,24},{4,28},{8,16},{12,20},{16,8},{20,12},{24,0},{28,4},{1,25},{... | collective-permute-start | bytes 393224 | tf_op jit(solution)/shard_map/ppermute | solution.py:133
  90.3 1.5 collective-permute-start.25
  91.8 0.5 collective-permute-start.24
  92.3 1.5 collective-permute-start.22
  93.8 0.5 collective-permute-start.23
  94.3 0.6 all-to-all-done.refs_1_
  94.9 2.3 %shard_map.238 = (f32[3,64,128]{2,1,0:T(8,128)}, bf16[32,64,128]{2,1,0:T(8,128)(2,1)}) custom-call(s32[3]{0:T(128)S(1)} %pad_add_fusion.token_ref.refs_0_.info, bf16[4,224,128]{2,1,0:T(8,128)(2,1)S(1)} %all-to-all-done.refs_1_, f32[3,64,128]{2,1,0:T(8,128)} %refs_2_.4, f32[8,128]{1,0:T(8,128)} %get-tuple-element.153.refs_3_.refs_9_, ...), custom_call_target="tpu_custom_call" | custom-call | flops 1000000 | tf_op jit(solution)/shard_map/pallas_call | solution.py:288
  97.2 3.8 %all-to-all-start.1 = ((bf16[32,64,128]{2,1,0:T(8,128)(2,1)}), bf16[32,64,128]{2,1,0:T(8,128)(2,1)}, u32[]{:S(2)}, u32[]{:S(2)}) async-start(bf16[32,64,128]{2,1,0:T(8,128)(2,1)} %get-tuple-element.155), calls=%async_computation.1 | async-start | bytes 1048576 | tf_op jit(solution)/shard_map/all_to_all | solution.py:992
  101.0 0.2 collective-permute-done.25.refs_3_
  101.2 0.6 shard_map.241.refs_1_
  101.8 3.2 %collective-permute-start.29 = (bf16[512,512]{1,0:T(8,128)(2,1)S(1)}, bf16[512,512]{1,0:T(8,128)(2,1)S(1)}, u32[]{:S(2)}, u32[]{:S(2)}) collective-permute-start(bf16[512,512]{1,0:T(8,128)(2,1)S(1)} %shard_map.241.refs_1_), channel_id=1, source_target_pairs={{0,3},{4,7},{8,11},{12,15},{16,19},{20,23},{24,27},{28,31}} | collective-permute-start | bytes 1572872 | tf_op jit(solution)/shard_map/ppermute | solution.py:996
  105.0 0.7 collective-permute-start.28
  105.7 0.7 collective-permute-start.27
  106.4 2.2 %shard_map.240 = f32[2,64,512]{2,1,0:T(8,128)} custom-call(s32[3]{0:T(128)S(1)} %pad_add_fusion.token_ref.refs_0_.info, f32[64,512]{1,0:T(8,128)} %get-tuple-element.166.refs_1_, f32[64,512]{1,0:T(8,128)} %collective-permute-done.23.refs_2_), custom_call_target="tpu_custom_call" | custom-call | flops 10000000000 | tf_op jit(solution)/shard_map/pallas_call | solution.py:288
  108.7 3.6 %shard_map.239 = (f32[1024,128]{1,0:T(8,128)}, bf16[1024,128]{1,0:T(8,128)(2,1)}) custom-call(s32[3]{0:T(128)S(1)} %pad_add_fusion.token_ref.refs_0_.info, f32[1024,128]{1,0:T(8,128)S(1)} %get-tuple-element.157.refs_1_, bf16[2064,128]{1,0:T(8,128)(2,1)} %collective-permute-done.22.refs_2_, f32[1024,128]{1,0:T(8,128)S(1)} %get-tuple-element.158.refs_3_, ...), custom_call_target="tpu_custom_call" | custom-call | flops 1000000 | tf_op jit(solution)/shard_map/pallas_call | solution.py:288
  112.3 7.1 %collective-permute-done.29.refs_4_ = bf16[512,512]{1,0:T(8,128)(2,1)S(1)} collective-permute-done((bf16[512,512]{1,0:T(8,128)(2,1)S(1)}, bf16[512,512]{1,0:T(8,128)(2,1)S(1)}, u32[]{:S(2)}, u32[]{:S(2)}) %collective-permute-start.29) | collective-permute-done | bytes 524320 | tf_op jit(solution)/shard_map/ppermute | solution.py:996
  119.4 0.8 shard_map.242.slots
  120.2 2.3 %shard_map.243 = bf16[8,64,512]{2,1,0:T(8,128)(2,1)} custom-call(s32[3]{0:T(128)S(1)} %pad_add_fusion.token_ref.refs_0_.info, bf16[32,64,128]{2,1,0:T(8,128)(2,1)} %all-to-all-done.1.source.refs_1_, bf16[8,64,512]{2,1,0:T(8,128)(2,1)} %shard_map.242.slots), custom_call_target="tpu_custom_call", output_to_operand_aliasing={{}: (2, {})} | custom-call | flops 179999997952 | tf_op jit(solution)/shard_map/pallas_call | solution.py:765
  122.6 16.6 %all-to-all-start.2 = ((bf16[8,64,512]{2,1,0:T(8,128)(2,1)}), bf16[8,64,512]{2,1,0:T(8,128)(2,1)S(1)}, u32[]{:S(2)}, u32[]{:S(2)}) async-start(bf16[8,64,512]{2,1,0:T(8,128)(2,1)} %shard_map.243), calls=%async_computation.2 | async-start | bytes 1048576 | tf_op jit(solution)/shard_map/all_to_all | solution.py:1019
  139.2 1.6 %shard_map.244.refs_2_ = bf16[64,384]{1,0:T(8,128)(2,1)S(1)} custom-call(s32[3]{0:T(128)S(1)} %pad_add_fusion.token_ref.refs_0_.info, bf16[32,64,128]{2,1,0:T(8,128)(2,1)} %all-to-all-done.1.source.refs_1_), custom_call_target="tpu_custom_call" | custom-call | flops 1000000 | tf_op jit(solution)/shard_map/pallas_call | solution.py:288
  140.8 2.0 %shard_map.245 = (bf16[3,512,128]{2,1,0:T(8,128)(2,1)S(1)}, bf16[2,512,512]{2,1,0:T(8,128)(2,1)S(1)}, f32[2,512]{1,0:T(2,128)S(1)}, f32[2,512]{1,0:T(2,128)S(1)}...) custom-call(s32[3]{0:T(128)S(1)} %pad_add_fusion.token_ref.refs_0_.info, bf16[3,512,128]{2,1,0:T(8,128)(2,1)} %refs_0_.2, ...), custom_call_target="tpu_custom_call" | custom-call | flops 1000000 | tf_op jit(solution)/shard_map/pallas_call | solution.py:322
  142.8 6.1 %all-to-all-done.2.refs_1_ = bf16[8,64,512]{2,1,0:T(8,128)(2,1)S(1)} async-done(((bf16[8,64,512]{2,1,0:T(8,128)(2,1)}), bf16[8,64,512]{2,1,0:T(8,128)(2,1)S(1)}, u32[]{:S(2)}, u32[]{:S(2)}) %all-to-all-start.2) | async-done | bytes 524320 | tf_op jit(solution)/shard_map/all_to_all | solution.py:1019
  148.9 2.7 %shard_map.246 = (f32[3,64,128]{2,1,0:T(8,128)}, f32[2,64,512]{2,1,0:T(8,128)}, f32[2,512]{1,0:T(2,128)}, f32[2,512]{1,0:T(2,128)}, f32[160,128]{1,0:T(8,128)}, /*index=5*/f32[160,128]{1,0:T(8,128)}) custom-call(s32[3]{0:T(128)S(1)} %pad_add_fusion.token_ref.refs_0_.info, bf16[8,64,512]{2,1,0:T(8,128)(2,1)S(1)} %all-to-all-done.2.refs_1_, ...), custom_call_target="tpu_custom_call" | custom-call | flops 1000000 | tf_op jit(solution)/shard_map/pallas_call | solution.py:288
  (54 shorter events, 0.4 us)
Async XLA Ops:
  0.6 10.0 %collective-permute-start.1 = (bf16[1024,128]{1,0:T(8,128)(2,1)}, bf16[1024,128]{1,0:T(8,128)(2,1)S(1)}, u32[]{:S(2)}, u32[]{:S(2)}) collective-permute-start(bf16[1024,128]{1,0:T(8,128)(2,1)} %bitcast.17), channel_id=1, source_target_pairs={{0,2},{1,3},{2,0},{3,1},{4,6},{5,7},{6,4},{7,5},{8,10},{9,11},{10,... | collective-permute-start | bytes 786440 | tf_op jit(solution)/shard_map/ppermute | solution.py:133
  3.6 7.5 %collective-permute-start = (bf16[1024,128]{1,0:T(8,128)(2,1)}, bf16[1024,128]{1,0:T(8,128)(2,1)S(1)}, u32[]{:S(2)}, u32[]{:S(2)}) collective-permute-start(bf16[1024,128]{1,0:T(8,128)(2,1)} %bitcast.18), channel_id=1, source_target_pairs={{0,1},{1,0},{2,3},{3,2},{4,5},{5,4},{6,7},{7,6},{8,9},{9,8},{10,11... | collective-permute-start | bytes 786440 | tf_op jit(solution)/shard_map/ppermute | solution.py:133
  6.5 5.7 %copy-start.2 = (bf16[2,512,256]{2,1,0:T(8,128)(2,1)}, bf16[2,512,256]{2,1,0:T(8,128)(2,1)S(1)}, u32[]{:S(2)}) copy-start(bf16[2,512,256]{2,1,0:T(8,128)(2,1)S(1)} %get-tuple-element.103.refs_7_.refs_13_) | copy-start | bytes 1572868
  6.5 5.7 %copy-start.4 = (bf16[2,256,512]{2,1,0:T(8,128)(2,1)}, bf16[2,256,512]{2,1,0:T(8,128)(2,1)S(1)}, u32[]{:S(2)}) copy-start(bf16[2,256,512]{2,1,0:T(8,128)(2,1)S(1)} %get-tuple-element.104.refs_8_.refs_14_) | copy-start | bytes 1572868
  6.5 5.7 %copy-start.6 = (bf16[3,512,128]{2,1,0:T(8,128)(2,1)}, bf16[3,512,128]{2,1,0:T(8,128)(2,1)S(1)}, u32[]{:S(2)}) copy-start(bf16[3,512,128]{2,1,0:T(8,128)(2,1)S(1)} %get-tuple-element.101.refs_5_) | copy-start | bytes 1179652
  6.5 12.1 %collective-permute-start.6 = (bf16[1536,128]{1,0:T(8,128)(2,1)S(1)}, bf16[1536,128]{1,0:T(8,128)(2,1)S(1)}, u32[]{:S(2)}, u32[]{:S(2)}) collective-permute-start(bf16[1536,128]{1,0:T(8,128)(2,1)S(1)} %get-tuple-element.107.refs_1_), channel_id=1, source_target_pairs={{0,2},{1,3},{2,0},{3,1},{4,6},{5,7},{6,4},{7,5},{8,10},{9,11},{10,... | collective-permute-start | bytes 1179656 | tf_op jit(solution)/shard_map/ppermute | solution.py:133
  9.8 13.5 %copy-start = (f32[2048,128]{1,0:T(8,128)}, f32[2048,128]{1,0:T(8,128)S(1)}, u32[]{:S(2)}) copy-start(f32[2048,128]{1,0:T(8,128)S(1)} %shard_map.223.refs_9_.refs_12_) | copy-start | bytes 3145732
  10.7 1.5 %collective-permute-start.2 = (bf16[1024,128]{1,0:T(8,128)(2,1)S(1)}, bf16[1024,128]{1,0:T(8,128)(2,1)S(1)}, u32[]{:S(2)}, u32[]{:S(2)}) collective-permute-start(bf16[1024,128]{1,0:T(8,128)(2,1)S(1)} %collective-permute-done.1.refs_3_), channel_id=1, source_target_pairs={{0,1},{1,0},{2,3},{3,2},{4,5},{5,4},{6,7},{7,6},{8,9},{9,8},{10,11... | collective-permute-start | bytes 786440 | tf_op jit(solution)/shard_map/ppermute | solution.py:133
  10.7 9.9 %collective-permute-start.5 = (bf16[1536,128]{1,0:T(8,128)(2,1)S(1)}, bf16[1536,128]{1,0:T(8,128)(2,1)S(1)}, u32[]{:S(2)}, u32[]{:S(2)}) collective-permute-start(bf16[1536,128]{1,0:T(8,128)(2,1)S(1)} %get-tuple-element.107.refs_1_), channel_id=1, source_target_pairs={{0,1},{1,0},{2,3},{3,2},{4,5},{5,4},{6,7},{7,6},{8,9},{9,8},{10,11... | collective-permute-start | bytes 1179656 | tf_op jit(solution)/shard_map/ppermute | solution.py:133
  15.9 13.0 %copy-start.9 = (f32[2,512]{1,0:T(2,128)}, f32[2,512]{1,0:T(2,128)S(1)}, u32[]{:S(2)}) copy-start(f32[2,512]{1,0:T(2,128)S(1)} %get-tuple-element.113.refs_7_.refs_6_.refs_16_) | copy-start | bytes 12292
  18.6 2.0 %collective-permute-start.7 = (bf16[1536,128]{1,0:T(8,128)(2,1)S(1)}, bf16[1536,128]{1,0:T(8,128)(2,1)S(1)}, u32[]{:S(2)}, u32[]{:S(2)}) collective-permute-start(bf16[1536,128]{1,0:T(8,128)(2,1)S(1)} %collective-permute-done.6.refs_3_), channel_id=1, source_target_pairs={{0,1},{1,0},{2,3},{3,2},{4,5},{5,4},{6,7},{7,6},{8,9},{9,8},{10,11... | collective-permute-start | bytes 1179656 | tf_op jit(solution)/shard_map/ppermute | solution.py:133
  18.6 8.7 %collective-permute-start.4 = (bf16[1024,128]{1,0:T(8,128)(2,1)S(1)}, bf16[1024,128]{1,0:T(8,128)(2,1)S(1)}, u32[]{:S(2)}, u32[]{:S(2)}) collective-permute-start(bf16[1024,128]{1,0:T(8,128)(2,1)S(1)} %get-tuple-element.105.refs_1_.refs_9_), channel_id=1, source_target_pairs={{0,2},{1,3},{2,0},{3,1},{4,6},{5,7},{6,4},{7,5},{8,10},{9,11},{10,... | collective-permute-start | bytes 786440 | tf_op jit(solution)/shard_map/ppermute | solution.py:133
  20.3 7.0 %collective-permute-start.3 = (bf16[1024,128]{1,0:T(8,128)(2,1)S(1)}, bf16[1024,128]{1,0:T(8,128)(2,1)S(1)}, u32[]{:S(2)}, u32[]{:S(2)}) collective-permute-start(bf16[1024,128]{1,0:T(8,128)(2,1)S(1)} %get-tuple-element.105.refs_1_.refs_9_), channel_id=1, source_target_pairs={{0,1},{1,0},{2,3},{3,2},{4,5},{5,4},{6,7},{7,6},{8,9},{9,8},{10,11... | collective-permute-start | bytes 786440 | tf_op jit(solution)/shard_map/ppermute | solution.py:133
  27.3 1.5 %collective-permute-start.8 = (bf16[1024,128]{1,0:T(8,128)(2,1)S(1)}, bf16[1024,128]{1,0:T(8,128)(2,1)S(1)}, u32[]{:S(2)}, u32[]{:S(2)}) collective-permute-start(bf16[1024,128]{1,0:T(8,128)(2,1)S(1)} %collective-permute-done.4.refs_3_), channel_id=1, source_target_pairs={{0,1},{1,0},{2,3},{3,2},{4,5},{5,4},{6,7},{7,6},{8,9},{9,8},{10,11... | collective-permute-start | bytes 786440 | tf_op jit(solution)/shard_map/ppermute | solution.py:133
  34.7 8.9 %copy-start.11 = (bf16[1024,512]{1,0:T(8,128)(2,1)}, bf16[1024,512]{1,0:T(8,128)(2,1)S(1)}, u32[]{:S(2)}) copy-start(bf16[1024,512]{1,0:T(8,128)(2,1)S(1)} %get-tuple-element.120.refs_2_.refs_1_) | copy-start | bytes 3145732
  34.8 2.0 %collective-permute-start.9 = (bf16[2,256,512]{2,1,0:T(8,128)(2,1)S(1)}, bf16[2,256,512]{2,1,0:T(8,128)(2,1)S(1)}, u32[]{:S(2)}, u32[]{:S(2)}) collective-permute-start(bf16[2,256,512]{2,1,0:T(8,128)(2,1)S(1)} %bitcast.11), channel_id=1, source_target_pairs={{0,1},{1,0},{2,3},{3,2},{4,5},{5,4},{6,7},{7,6},{8,9},{9,8},{10,11... | collective-permute-start | bytes 1572872 | tf_op jit(solution)/shard_map/ppermute | solution.py:133
  38.0 8.7 %collective-permute-start.11 = (bf16[256,512]{1,0:T(8,128)(2,1)}, bf16[256,512]{1,0:T(8,128)(2,1)}, u32[]{:S(2)}, u32[]{:S(2)}) collective-permute-start(bf16[256,512]{1,0:T(8,128)(2,1)} %get-tuple-element.117), channel_id=1, source_target_pairs={{0,2},{1,3},{2,0},{3,1},{4,6},{5,7},{6,4},{7,5},{8,10},{9,11},{10,... | collective-permute-start | bytes 786440 | tf_op jit(solution)/shard_map/ppermute | solution.py:133
  42.1 14.4 %collective-permute-start.10 = (bf16[528,512]{1,0:T(8,128)(2,1)}, bf16[528,512]{1,0:T(8,128)(2,1)}, u32[]{:S(2)}, u32[]{:S(2)}) collective-permute-start(bf16[528,512]{1,0:T(8,128)(2,1)} %get-tuple-element.123), channel_id=1, source_target_pairs={{0,4},{4,0},{8,12},{12,8},{16,20},{20,16},{24,28},{28,24},{1,5},{5... | collective-permute-start | bytes 1622024 | tf_op jit(solution)/shard_map/ppermute | solution.py:133
  43.7 3.0 %copy-start.10 = (f32[2,512]{1,0:T(2,128)S(1)}, f32[2,512]{1,0:T(2,128)}, u32[]{:S(2)}) copy-start(f32[2,512]{1,0:T(2,128)} %copy-done.9) | copy-start | bytes 12292
  48.0 4.0 %copy-start.12 = (bf16[1024,512]{1,0:T(8,128)(2,1)S(1)}, bf16[1024,512]{1,0:T(8,128)(2,1)}, u32[]{:S(2)}) copy-start(bf16[1024,512]{1,0:T(8,128)(2,1)} %copy-done.11) | copy-start | bytes 3145732
  48.0 7.6 %collective-permute-start.13 = (bf16[256,512]{1,0:T(8,128)(2,1)S(1)}, bf16[256,512]{1,0:T(8,128)(2,1)S(1)}, u32[]{:S(2)}, u32[]{:S(2)}) collective-permute-start(bf16[256,512]{1,0:T(8,128)(2,1)S(1)} %get-tuple-element.131.refs_1_), channel_id=1, source_target_pairs={{0,2},{1,3},{2,0},{3,1},{4,6},{5,7},{6,4},{7,5},{8,10},{9,11},{10,... | collective-permute-start | bytes 786440 | tf_op jit(solution)/shard_map/ppermute | solution.py:133
  49.8 7.9 %collective-permute-start.12 = (bf16[256,512]{1,0:T(8,128)(2,1)S(1)}, bf16[256,512]{1,0:T(8,128)(2,1)S(1)}, u32[]{:S(2)}, u32[]{:S(2)}) collective-permute-start(bf16[256,512]{1,0:T(8,128)(2,1)S(1)} %get-tuple-element.131.refs_1_), channel_id=1, source_target_pairs={{0,1},{1,0},{2,3},{3,2},{4,5},{5,4},{6,7},{7,6},{8,9},{9,8},{10,11... | collective-permute-start | bytes 786440 | tf_op jit(solution)/shard_map/ppermute | solution.py:133
  52.0 5.7 %copy-start.1 = (f32[2048,128]{1,0:T(8,128)S(1)}, f32[2048,128]{1,0:T(8,128)}, u32[]{:S(2)}) copy-start(f32[2048,128]{1,0:T(8,128)} %copy-done) | copy-start | bytes 3145732
  52.0 5.7 %copy-start.3 = (bf16[2,512,256]{2,1,0:T(8,128)(2,1)S(1)}, bf16[2,512,256]{2,1,0:T(8,128)(2,1)}, u32[]{:S(2)}) copy-start(bf16[2,512,256]{2,1,0:T(8,128)(2,1)} %copy-done.2) | copy-start | bytes 1572868
  52.0 5.7 %copy-start.5 = (bf16[2,256,512]{2,1,0:T(8,128)(2,1)S(1)}, bf16[2,256,512]{2,1,0:T(8,128)(2,1)}, u32[]{:S(2)}) copy-start(bf16[2,256,512]{2,1,0:T(8,128)(2,1)} %copy-done.4) | copy-start | bytes 1572868
  52.0 5.7 %copy-start.7 = (bf16[3,512,128]{2,1,0:T(8,128)(2,1)S(1)}, bf16[3,512,128]{2,1,0:T(8,128)(2,1)}, u32[]{:S(2)}) copy-start(bf16[3,512,128]{2,1,0:T(8,128)(2,1)} %copy-done.6) | copy-start | bytes 1179652
  55.6 2.1 %collective-permute-start.14 = (bf16[256,512]{1,0:T(8,128)(2,1)S(1)}, bf16[256,512]{1,0:T(8,128)(2,1)S(1)}, u32[]{:S(2)}, u32[]{:S(2)}) collective-permute-start(bf16[256,512]{1,0:T(8,128)(2,1)S(1)} %collective-permute-done.13.refs_3_), channel_id=1, source_target_pairs={{0,1},{1,0},{2,3},{3,2},{4,5},{5,4},{6,7},{7,6},{8,9},{9,8},{10,11... | collective-permute-start | bytes 786440 | tf_op jit(solution)/shard_map/ppermute | solution.py:133
  55.6 16.1 %collective-permute-start.17 = (bf16[2,1024,128]{2,1,0:T(8,128)(2,1)}, bf16[2,1024,128]{2,1,0:T(8,128)(2,1)}, u32[]{:S(2)}, u32[]{:S(2)}) collective-permute-start(bf16[2,1024,128]{2,1,0:T(8,128)(2,1)} %get-tuple-element.134), channel_id=1, source_target_pairs={{0,1},{1,0},{2,3},{3,2},{4,5},{5,4},{6,7},{7,6},{8,9},{9,8},{10,11... | collective-permute-start | bytes 1572872 | tf_op jit(solution)/shard_map/ppermute | solution.py:133
  65.8 19.2 %copy-start.8 = (f32[2,64,512]{2,1,0:T(8,128)S(1)}, f32[2,64,512]{2,1,0:T(8,128)}, u32[]{:S(2)}) copy-start(f32[2,64,512]{2,1,0:T(8,128)} %refs_1_.5) | copy-start | bytes 786436
  65.8 15.8 %collective-permute-start.16 = (bf16[2,1040,128]{2,1,0:T(8,128)(2,1)}, bf16[2,1040,128]{2,1,0:T(8,128)(2,1)S(1)}, u32[]{:S(2)}, u32[]{:S(2)}) collective-permute-start(bf16[2,1040,128]{2,1,0:T(8,128)(2,1)} %get-tuple-element.145), channel_id=1, source_target_pairs={{0,1},{1,0},{2,3},{3,2},{4,5},{5,4},{6,7},{7,6},{8,9},{9,8},{10,11... | collective-permute-start | bytes 1597448 | tf_op jit(solution)/shard_map/ppermute | solution.py:133
  65.9 8.0 %collective-permute-start.15 = (bf16[4,224,128]{2,1,0:T(8,128)(2,1)S(1)}, bf16[4,224,128]{2,1,0:T(8,128)(2,1)S(1)}, u32[]{:S(2)}, u32[]{:S(2)}) collective-permute-start(bf16[4,224,128]{2,1,0:T(8,128)(2,1)S(1)} %get-tuple-element.143), channel_id=1, source_target_pairs={{0,4},{4,0},{8,12},{12,8},{16,20},{20,16},{24,28},{28,24},{1,5},{5... | collective-permute-start | bytes 688136 | tf_op jit(solution)/shard_map/ppermute | solution.py:133
  67.6 17.4 %collective-permute-start.19 = (bf16[144,512]{1,0:T(8,128)(2,1)S(1)}, bf16[144,512]{1,0:T(8,128)(2,1)S(1)}, u32[]{:S(2)}, u32[]{:S(2)}) collective-permute-start(bf16[144,512]{1,0:T(8,128)(2,1)S(1)} %get-tuple-element.150), channel_id=1, source_target_pairs={{0,8},{4,12},{8,0},{12,4},{16,24},{20,28},{24,16},{28,20},{1,9},{5... | collective-permute-start | bytes 442376 | tf_op jit(solution)/shard_map/ppermute | solution.py:133
  69.1 15.9 %collective-permute-start.20 = (bf16[144,512]{1,0:T(8,128)(2,1)S(1)}, bf16[144,512]{1,0:T(8,128)(2,1)S(1)}, u32[]{:S(2)}, u32[]{:S(2)}) collective-permute-start(bf16[144,512]{1,0:T(8,128)(2,1)S(1)} %get-tuple-element.151), channel_id=1, source_target_pairs={{0,16},{4,20},{8,24},{12,28},{16,0},{20,4},{24,8},{28,12},{1,17},{... | collective-permute-start | bytes 442376 | tf_op jit(solution)/shard_map/ppermute | solution.py:133
  71.7 13.3 %collective-permute-start.21 = (bf16[144,512]{1,0:T(8,128)(2,1)S(1)}, bf16[144,512]{1,0:T(8,128)(2,1)S(1)}, u32[]{:S(2)}, u32[]{:S(2)}) collective-permute-start(bf16[144,512]{1,0:T(8,128)(2,1)S(1)} %get-tuple-element.152), channel_id=1, source_target_pairs={{0,24},{4,28},{8,16},{12,20},{16,8},{20,12},{24,0},{28,4},{1,25},{... | collective-permute-start | bytes 442376 | tf_op jit(solution)/shard_map/ppermute | solution.py:133
  73.9 11.1 %collective-permute-start.18 = (f32[64,512]{1,0:T(8,128)S(1)}, f32[64,512]{1,0:T(8,128)S(1)}, u32[]{:S(2)}, u32[]{:S(2)}) collective-permute-start(f32[64,512]{1,0:T(8,128)S(1)} %get-tuple-element.149), channel_id=1, source_target_pairs={{0,4},{4,0},{8,12},{12,8},{16,20},{20,16},{24,28},{28,24},{1,5},{5... | collective-permute-start | bytes 393224 | tf_op jit(solution)/shard_map/ppermute | solution.py:133
  76.7 18.2 %all-to-all-start = ((bf16[4,224,128]{2,1,0:T(8,128)(2,1)}), bf16[4,224,128]{2,1,0:T(8,128)(2,1)S(1)}, u32[]{:S(2)}, u32[]{:S(2)}) async-start(bf16[4,224,128]{2,1,0:T(8,128)(2,1)} %shard_map.235), calls=%async_computation | async-start | bytes 458752 | tf_op jit(solution)/shard_map/all_to_all | solution.py:964
  86.4 14.6 %collective-permute-start.26 = (bf16[128,512]{1,0:T(8,128)(2,1)S(1)}, bf16[128,512]{1,0:T(8,128)(2,1)S(1)}, u32[]{:S(2)}, u32[]{:S(2)}) collective-permute-start(bf16[128,512]{1,0:T(8,128)(2,1)S(1)} %get-tuple-element.169.refs_1_), channel_id=1, source_target_pairs={{0,24},{4,28},{8,16},{12,20},{16,8},{20,12},{24,0},{28,4},{1,25},{... | collective-permute-start | bytes 393224 | tf_op jit(solution)/shard_map/ppermute | solution.py:133
  90.3 10.9 %collective-permute-start.25 = (bf16[128,512]{1,0:T(8,128)(2,1)S(1)}, bf16[128,512]{1,0:T(8,128)(2,1)S(1)}, u32[]{:S(2)}, u32[]{:S(2)}) collective-permute-start(bf16[128,512]{1,0:T(8,128)(2,1)S(1)} %get-tuple-element.169.refs_1_), channel_id=1, source_target_pairs={{0,16},{4,20},{8,24},{12,28},{16,0},{20,4},{24,8},{28,12},{1,17},{... | collective-permute-start | bytes 393224 | tf_op jit(solution)/shard_map/ppermute | solution.py:133
  91.8 9.5 %collective-permute-start.24 = (bf16[128,512]{1,0:T(8,128)(2,1)S(1)}, bf16[128,512]{1,0:T(8,128)(2,1)S(1)}, u32[]{:S(2)}, u32[]{:S(2)}) collective-permute-start(bf16[128,512]{1,0:T(8,128)(2,1)S(1)} %get-tuple-element.169.refs_1_), channel_id=1, source_target_pairs={{0,8},{4,12},{8,0},{12,4},{16,24},{20,28},{24,16},{28,20},{1,9},{5... | collective-permute-start | bytes 393224 | tf_op jit(solution)/shard_map/ppermute | solution.py:133
  92.3 16.4 %collective-permute-start.22 = (bf16[2064,128]{1,0:T(8,128)(2,1)}, bf16[2064,128]{1,0:T(8,128)(2,1)}, u32[]{:S(2)}, u32[]{:S(2)}) collective-permute-start(bf16[2064,128]{1,0:T(8,128)(2,1)} %get-tuple-element.147), channel_id=1, source_target_pairs={{0,2},{1,3},{2,0},{3,1},{4,6},{5,7},{6,4},{7,5},{8,10},{9,11},{10,... | collective-permute-start | bytes 1585160 | tf_op jit(solution)/shard_map/ppermute | solution.py:133
  93.8 12.7 %collective-permute-start.23 = (f32[64,512]{1,0:T(8,128)}, f32[64,512]{1,0:T(8,128)}, u32[]{:S(2)}, u32[]{:S(2)}) collective-permute-start(f32[64,512]{1,0:T(8,128)} %get-tuple-element.167), channel_id=1, source_target_pairs={{0,4},{4,0},{8,12},{12,8},{16,20},{20,16},{24,28},{28,24},{1,5},{5... | collective-permute-start | bytes 393224 | tf_op jit(solution)/shard_map/ppermute | solution.py:133
  97.2 23.0 %all-to-all-start.1 = ((bf16[32,64,128]{2,1,0:T(8,128)(2,1)}), bf16[32,64,128]{2,1,0:T(8,128)(2,1)}, u32[]{:S(2)}, u32[]{:S(2)}) async-start(bf16[32,64,128]{2,1,0:T(8,128)(2,1)} %get-tuple-element.155), calls=%async_computation.1 | async-start | bytes 1048576 | tf_op jit(solution)/shard_map/all_to_all | solution.py:992
  101.8 17.6 %collective-permute-start.29 = (bf16[512,512]{1,0:T(8,128)(2,1)S(1)}, bf16[512,512]{1,0:T(8,128)(2,1)S(1)}, u32[]{:S(2)}, u32[]{:S(2)}) collective-permute-start(bf16[512,512]{1,0:T(8,128)(2,1)S(1)} %shard_map.241.refs_1_), channel_id=1, source_target_pairs={{0,3},{4,7},{8,11},{12,15},{16,19},{20,23},{24,27},{28,31}} | collective-permute-start | bytes 1572872 | tf_op jit(solution)/shard_map/ppermute | solution.py:996
  105.0 14.4 %collective-permute-start.28 = (bf16[512,512]{1,0:T(8,128)(2,1)S(1)}, bf16[512,512]{1,0:T(8,128)(2,1)S(1)}, u32[]{:S(2)}, u32[]{:S(2)}) collective-permute-start(bf16[512,512]{1,0:T(8,128)(2,1)S(1)} %shard_map.241.refs_1_), channel_id=1, source_target_pairs={{1,3},{5,7},{9,11},{13,15},{17,19},{21,23},{25,27},{29,31}} | collective-permute-start | bytes 1572872 | tf_op jit(solution)/shard_map/ppermute | solution.py:996
  105.7 13.7 %collective-permute-start.27 = (bf16[512,512]{1,0:T(8,128)(2,1)S(1)}, bf16[512,512]{1,0:T(8,128)(2,1)S(1)}, u32[]{:S(2)}, u32[]{:S(2)}) collective-permute-start(bf16[512,512]{1,0:T(8,128)(2,1)S(1)} %shard_map.241.refs_1_), channel_id=1, source_target_pairs={{2,3},{6,7},{10,11},{14,15},{18,19},{22,23},{26,27},{30,31}} | collective-permute-start | bytes 1572872 | tf_op jit(solution)/shard_map/ppermute | solution.py:996
  122.6 26.4 %all-to-all-start.2 = ((bf16[8,64,512]{2,1,0:T(8,128)(2,1)}), bf16[8,64,512]{2,1,0:T(8,128)(2,1)S(1)}, u32[]{:S(2)}, u32[]{:S(2)}) async-start(bf16[8,64,512]{2,1,0:T(8,128)(2,1)} %shard_map.243), calls=%async_computation.2 | async-start | bytes 1048576 | tf_op jit(solution)/shard_map/all_to_all | solution.py:1019
